TPU v7x, 32 devices: a whole 2x2x4 slice. The times are simulated.
32 devices in a mesh: wide: 16 (over z, y, core), narrow: 2 (over x).
Axes of the slice: x: 2, y: 2, z: 4, core: 2. Of those that a mesh axis runs over, the one named last changes fastest.
Arguments:
- tokens: bfloat16 [32, 1024, 768], P(('wide', 'narrow')), may hold values from -6 to 6
- doc_ids: int32 [32, 1024], P(('wide', 'narrow')), may hold values from 0 to 5, never falling along the last dimension, each value on 1 to 512 neighbouring positions
- cotangent: bfloat16 [32, 1024, 768], P(('wide', 'narrow')), may hold values from -6 to 6
- owner: int32 [1], replicated, may hold values from 0 to 15
- ln1_gain: bfloat16 [16, 768], P('wide', 'narrow'), may hold values from 0.25 to 1.75
- ln1_bias: bfloat16 [16, 768], P('wide', 'narrow'), may hold values from -2 to 2
- qkv_weight: bfloat16 [16, 768, 2304], P('wide', 'narrow'), may hold values from -0.21875 to 0.21875
- qv_bias: bfloat16 [16, 1536], P('wide', 'narrow'), may hold values from -2 to 2
- out_weight: bfloat16 [16, 768, 768], P('wide', 'narrow'), may hold values from -1.75 to 1.75
- out_bias: bfloat16 [16, 768], P('wide', 'narrow'), may hold values from -2 to 2
- ln2_gain: bfloat16 [16, 768], P('wide', 'narrow'), may hold values from 0.25 to 1.75
- ln2_bias: bfloat16 [16, 768], P('wide', 'narrow'), may hold values from -2 to 2
- fc_weight: bfloat16 [16, 768, 3072], P('wide', 'narrow'), may hold values from -0.21875 to 0.21875
- fc_bias: bfloat16 [16, 3072], P('wide', 'narrow'), may hold values from -3 to 3
- proj_weight: bfloat16 [16, 3072, 768], P('wide', 'narrow'), may hold values from -0.109375 to 0.109375
- proj_bias: bfloat16 [16, 768], P('wide', 'narrow'), may hold values from -2 to 2
Outputs:
- block_out: bfloat16 [32, 1024, 768], P(('wide', 'narrow'))
- tokens_grad: bfloat16 [32, 1024, 768], P(('wide', 'narrow'))
- ln1_gain_grad: float32 [16, 768], P('wide', 'narrow')
- ln1_bias_grad: float32 [16, 768], P('wide', 'narrow')
- qkv_weight_grad: float32 [16, 768, 2304], P('wide', 'narrow')
- qv_bias_grad: float32 [16, 1536], P('wide', 'narrow')
- out_weight_grad: float32 [16, 768, 768], P('wide', 'narrow')
- out_bias_grad: float32 [16, 768], P('wide', 'narrow')
- ln2_gain_grad: float32 [16, 768], P('wide', 'narrow')
- ln2_bias_grad: float32 [16, 768], P('wide', 'narrow')
- fc_weight_grad: float32 [16, 768, 3072], P('wide', 'narrow')
- fc_bias_grad: float32 [16, 3072], P('wide', 'narrow')
- proj_weight_grad: float32 [16, 3072, 768], P('wide', 'narrow')
- proj_bias_grad: float32 [16, 768], P('wide', 'narrow')
Inputs may be any that keep to these rules, and one draw needn't show every extreme that they name: `owner`: the slot that holds the source layer. `doc_ids`: along each row the numbers never fall; equal numbers mark one document.
All inputs are finite; a program needn't handle non-finite values.
Results may differ from a plain program's by a relative error of at most 0.019.
Values may be sent and summed in bfloat16 or wider, within the bound.
No kernel may reach another device: no remote copies, remote signals or barrier semaphores. Data moves between devices by JAX's collectives and lax.ppermute only.
A program may use at most 192 MiB of HBM per device.

v0:
```python
import math

import jax
import jax.numpy as jnp
from jax import lax
from jax.sharding import PartitionSpec as P

H = 12
HD = 64


epsilon = 1e-05


def broadcast(x, axis, root):
    mine = lax.axis_index(axis) == root
    return lax.psum(jnp.where(mine, x, jnp.zeros_like(x)), axis)


def norm_rows(values, gain, shift):
    center = values - jnp.mean(values, axis=-1, keepdims=True)
    spread = jnp.mean(center * center, axis=-1, keepdims=True)
    return center * lax.rsqrt(spread + epsilon) * gain + shift


def gelu_tanh(values):
    inner = math.sqrt(2.0 / math.pi) * (values + 0.044715 * values * values * values)
    return 0.5 * values * (1.0 + jnp.tanh(inner))


def doc_mask(doc_row):
    places = jnp.arange(doc_row.shape[0])
    return (places[:, None] >= places[None, :]) & (doc_row[:, None] == doc_row[None, :])


def head_scores(queries, keys, doc_row):
    scores = jnp.dot(queries, keys.T, preferred_element_type=jnp.float32) * HD ** (-0.5)
    return jnp.where(doc_mask(doc_row), scores, -1000000000.0)


def head_forward(pieces):
    queries, keys, values, doc_row = pieces
    scores = head_scores(queries, keys, doc_row)
    row_max = jnp.max(scores, axis=-1, keepdims=True)
    expon = jnp.exp(scores - row_max)
    totals = jnp.sum(expon, axis=-1, keepdims=True)
    soft = (expon / totals).astype(jnp.bfloat16)
    mixed = jnp.dot(soft, values, preferred_element_type=jnp.float32)
    return (mixed, row_max[:, 0] + jnp.log(totals[:, 0]))


def head_backward(pieces):
    queries, keys, values, doc_row, log_total, grad_out = pieces
    scores = head_scores(queries, keys, doc_row)
    soft = jnp.where(doc_mask(doc_row), jnp.exp(scores - log_total[:, None]), 0.0)
    grad_values = jnp.einsum(
        "lm,ld->md", soft.astype(jnp.bfloat16), grad_out, preferred_element_type=jnp.float32
    )
    grad_soft = jnp.einsum("ld,md->lm", grad_out, values, preferred_element_type=jnp.float32)
    center = jnp.sum(soft * grad_soft, axis=-1, keepdims=True)
    grad_scores = (soft * (grad_soft - center)).astype(jnp.bfloat16)
    grad_queries = jnp.dot(grad_scores, keys, preferred_element_type=jnp.float32) * HD ** (-0.5)
    grad_keys = jnp.einsum(
        "lm,ld->md", grad_scores, queries, preferred_element_type=jnp.float32
    ) * HD ** (-0.5)
    return (grad_queries, grad_keys, grad_values)


def fetch(
    owner,
    ln1_gain,
    ln1_bias,
    qkv_weight,
    qv_bias,
    out_weight,
    out_bias,
    ln2_gain,
    ln2_bias,
    fc_weight,
    fc_bias,
    proj_weight,
    proj_bias,
):
    joined = (
        lax.all_gather(ln1_gain, "narrow", axis=1, tiled=True),
        lax.all_gather(ln1_bias, "narrow", axis=1, tiled=True),
        lax.all_gather(qkv_weight, "narrow", axis=1, tiled=True),
        lax.all_gather(qv_bias, "narrow", axis=1, tiled=True),
        lax.all_gather(out_weight, "narrow", axis=1, tiled=True),
        lax.all_gather(out_bias, "narrow", axis=1, tiled=True),
        lax.all_gather(ln2_gain, "narrow", axis=1, tiled=True),
        lax.all_gather(ln2_bias, "narrow", axis=1, tiled=True),
        lax.all_gather(fc_weight, "narrow", axis=1, tiled=True),
        lax.all_gather(fc_bias, "narrow", axis=1, tiled=True),
        lax.all_gather(proj_weight, "narrow", axis=1, tiled=True),
        lax.all_gather(proj_bias, "narrow", axis=1, tiled=True),
    )
    (
        j_gain1,
        j_shift1,
        j_qkv,
        j_qv,
        j_out,
        j_outb,
        j_gain2,
        j_shift2,
        j_fc,
        j_fcb,
        j_proj,
        j_projb,
    ) = joined
    whole = (
        broadcast(j_gain1, "wide", owner[0]),
        broadcast(j_shift1, "wide", owner[0]),
        broadcast(j_qkv, "wide", owner[0]),
        broadcast(j_qv, "wide", owner[0]),
        broadcast(j_out, "wide", owner[0]),
        broadcast(j_outb, "wide", owner[0]),
        broadcast(j_gain2, "wide", owner[0]),
        broadcast(j_shift2, "wide", owner[0]),
        broadcast(j_fc, "wide", owner[0]),
        broadcast(j_fcb, "wide", owner[0]),
        broadcast(j_proj, "wide", owner[0]),
        broadcast(j_projb, "wide", owner[0]),
    )
    return tuple((member[0] for member in whole))


def on_device(
    tokens,
    doc_ids,
    cotangent,
    owner,
    ln1_gain,
    ln1_bias,
    qkv_weight,
    qv_bias,
    out_weight,
    out_bias,
    ln2_gain,
    ln2_bias,
    fc_weight,
    fc_bias,
    proj_weight,
    proj_bias,
):
    stacked = (
        owner,
        ln1_gain,
        ln1_bias,
        qkv_weight,
        qv_bias,
        out_weight,
        out_bias,
        ln2_gain,
        ln2_bias,
        fc_weight,
        fc_bias,
        proj_weight,
        proj_bias,
    )
    rows_here, length, width = tokens.shape
    count = rows_here * length
    inputs = tokens.astype(jnp.float32).reshape(count, width)
    (
        gain_first,
        shift_first,
        weight_qkv,
        bias_qv,
        weight_out,
        bias_out,
        gain_second,
        shift_second,
        weight_fc,
        bias_fc,
        weight_proj,
        bias_proj,
    ) = fetch(*stacked)
    gain_one = gain_first.astype(jnp.float32)
    shift_one = shift_first.astype(jnp.float32)
    gain_two = gain_second.astype(jnp.float32)
    shift_two = shift_second.astype(jnp.float32)
    normed = norm_rows(inputs, gain_one, shift_one).astype(jnp.bfloat16)
    bias_float = bias_qv.astype(jnp.float32)
    bias_full = jnp.concatenate(
        [bias_float[:width], jnp.zeros((width,), jnp.float32), bias_float[width:]]
    )
    packed = (jnp.dot(normed, weight_qkv, preferred_element_type=jnp.float32) + bias_full).astype(
        jnp.bfloat16
    )
    heads = (
        packed.reshape(rows_here, length, 3, H, HD)
        .transpose(2, 0, 3, 1, 4)
        .reshape(3, rows_here * H, length, HD)
    )
    doc_heads = jnp.repeat(doc_ids, H, axis=0)
    head_out, log_totals = lax.map(head_forward, (heads[0], heads[1], heads[2], doc_heads))
    mixed = (
        head_out.reshape(rows_here, H, length, HD)
        .transpose(0, 2, 1, 3)
        .reshape(count, width)
        .astype(jnp.bfloat16)
    )
    middle = (
        inputs
        + jnp.dot(mixed, weight_out, preferred_element_type=jnp.float32)
        + bias_out.astype(jnp.float32)
    )
    second = norm_rows(middle, gain_two, shift_two).astype(jnp.bfloat16)
    hidden = jnp.dot(second, weight_fc, preferred_element_type=jnp.float32) + bias_fc.astype(
        jnp.float32
    )
    active = gelu_tanh(hidden).astype(jnp.bfloat16)
    result = (
        middle
        + jnp.dot(active, weight_proj, preferred_element_type=jnp.float32)
        + bias_proj.astype(jnp.float32)
    )
    (
        gain_first,
        shift_first,
        weight_qkv,
        bias_qv,
        weight_out,
        bias_out,
        gain_second,
        shift_second,
        weight_fc,
        bias_fc,
        weight_proj,
        bias_proj,
    ) = fetch(*stacked)
    gain_one = gain_first.astype(jnp.float32)
    shift_one = shift_first.astype(jnp.float32)
    gain_two = gain_second.astype(jnp.float32)
    shift_two = shift_second.astype(jnp.float32)
    grad_result = cotangent.astype(jnp.float32).reshape(count, width)
    grad_branch_two = grad_result.astype(jnp.bfloat16)
    grad_proj = jnp.einsum("nf,nd->fd", active, grad_branch_two, preferred_element_type=jnp.float32)
    grad_projb = jnp.sum(grad_branch_two.astype(jnp.float32), axis=0)
    grad_active = jnp.einsum(
        "nd,fd->nf", grad_branch_two, weight_proj, preferred_element_type=jnp.float32
    )
    _, gelu_pull = jax.vjp(gelu_tanh, hidden)
    grad_hidden = gelu_pull(grad_active)[0].astype(jnp.bfloat16)
    grad_fc = jnp.einsum("nd,nf->df", second, grad_hidden, preferred_element_type=jnp.float32)
    grad_fcb = jnp.sum(grad_hidden.astype(jnp.float32), axis=0)
    grad_second = jnp.einsum(
        "nf,df->nd", grad_hidden, weight_fc, preferred_element_type=jnp.float32
    )
    _, norm_pull_two = jax.vjp(norm_rows, middle, gain_two, shift_two)
    grad_middle_part, grad_gain_two, grad_shift_two = norm_pull_two(grad_second)
    grad_middle = grad_result + grad_middle_part
    grad_branch_one = grad_middle.astype(jnp.bfloat16)
    grad_out = jnp.einsum("ne,nd->ed", mixed, grad_branch_one, preferred_element_type=jnp.float32)
    grad_outb = jnp.sum(grad_branch_one.astype(jnp.float32), axis=0)
    grad_mixed = jnp.einsum(
        "nd,ed->ne", grad_branch_one, weight_out, preferred_element_type=jnp.float32
    ).astype(jnp.bfloat16)
    grad_heads = (
        grad_mixed.reshape(rows_here, length, H, HD)
        .transpose(0, 2, 1, 3)
        .reshape(rows_here * H, length, HD)
    )
    grad_queries, grad_keys, grad_values = lax.map(
        head_backward, (heads[0], heads[1], heads[2], doc_heads, log_totals, grad_heads)
    )
    grad_packed = jnp.stack([grad_queries, grad_keys, grad_values]).reshape(
        3, rows_here, H, length, HD
    )
    grad_packed = (
        grad_packed.transpose(1, 3, 0, 2, 4).reshape(count, 3 * width).astype(jnp.bfloat16)
    )
    grad_qkv = jnp.einsum("nd,ne->de", normed, grad_packed, preferred_element_type=jnp.float32)
    packed_sums = jnp.sum(grad_packed.astype(jnp.float32), axis=0)
    grad_qvb = jnp.concatenate([packed_sums[:width], packed_sums[2 * width :]])
    grad_normed = jnp.einsum(
        "ne,de->nd", grad_packed, weight_qkv, preferred_element_type=jnp.float32
    )
    _, norm_pull_one = jax.vjp(norm_rows, inputs, gain_one, shift_one)
    grad_input_part, grad_gain_one, grad_shift_one = norm_pull_one(grad_normed)
    grad_inputs = (grad_middle + grad_input_part).astype(jnp.bfloat16).reshape(tokens.shape)
    shares = (
        lax.psum_scatter(
            grad_gain_one.astype(jnp.bfloat16), "narrow", scatter_dimension=0, tiled=True
        ).astype(jnp.float32),
        lax.psum_scatter(
            grad_shift_one.astype(jnp.bfloat16), "narrow", scatter_dimension=0, tiled=True
        ).astype(jnp.float32),
        lax.psum_scatter(
            grad_qkv.astype(jnp.bfloat16), "narrow", scatter_dimension=0, tiled=True
        ).astype(jnp.float32),
        lax.psum_scatter(
            grad_qvb.astype(jnp.bfloat16), "narrow", scatter_dimension=0, tiled=True
        ).astype(jnp.float32),
        lax.psum_scatter(
            grad_out.astype(jnp.bfloat16), "narrow", scatter_dimension=0, tiled=True
        ).astype(jnp.float32),
        lax.psum_scatter(
            grad_outb.astype(jnp.bfloat16), "narrow", scatter_dimension=0, tiled=True
        ).astype(jnp.float32),
        lax.psum_scatter(
            grad_gain_two.astype(jnp.bfloat16), "narrow", scatter_dimension=0, tiled=True
        ).astype(jnp.float32),
        lax.psum_scatter(
            grad_shift_two.astype(jnp.bfloat16), "narrow", scatter_dimension=0, tiled=True
        ).astype(jnp.float32),
        lax.psum_scatter(
            grad_fc.astype(jnp.bfloat16), "narrow", scatter_dimension=0, tiled=True
        ).astype(jnp.float32),
        lax.psum_scatter(
            grad_fcb.astype(jnp.bfloat16), "narrow", scatter_dimension=0, tiled=True
        ).astype(jnp.float32),
        lax.psum_scatter(
            grad_proj.astype(jnp.bfloat16), "narrow", scatter_dimension=0, tiled=True
        ).astype(jnp.float32),
        lax.psum_scatter(
            grad_projb.astype(jnp.bfloat16), "narrow", scatter_dimension=0, tiled=True
        ).astype(jnp.float32),
    )
    (
        share_gain1,
        share_shift1,
        share_qkv,
        share_qv,
        share_out,
        share_outb,
        share_gain2,
        share_shift2,
        share_fc,
        share_fcb,
        share_proj,
        share_projb,
    ) = shares
    summed = (
        lax.psum(share_gain1.astype(jnp.bfloat16), "wide").astype(jnp.float32),
        lax.psum(share_shift1.astype(jnp.bfloat16), "wide").astype(jnp.float32),
        lax.psum(share_qkv.astype(jnp.bfloat16), "wide").astype(jnp.float32),
        lax.psum(share_qv.astype(jnp.bfloat16), "wide").astype(jnp.float32),
        lax.psum(share_out.astype(jnp.bfloat16), "wide").astype(jnp.float32),
        lax.psum(share_outb.astype(jnp.bfloat16), "wide").astype(jnp.float32),
        lax.psum(share_gain2.astype(jnp.bfloat16), "wide").astype(jnp.float32),
        lax.psum(share_shift2.astype(jnp.bfloat16), "wide").astype(jnp.float32),
        lax.psum(share_fc.astype(jnp.bfloat16), "wide").astype(jnp.float32),
        lax.psum(share_fcb.astype(jnp.bfloat16), "wide").astype(jnp.float32),
        lax.psum(share_proj.astype(jnp.bfloat16), "wide").astype(jnp.float32),
        lax.psum(share_projb.astype(jnp.bfloat16), "wide").astype(jnp.float32),
    )
    holder = (lax.axis_index("wide") == owner[0]).astype(jnp.float32)
    placed = tuple((holder * member[None] for member in summed))
    return (
        result.astype(jnp.bfloat16).reshape(tokens.shape),
        grad_inputs,
        placed[0],
        placed[1],
        placed[2],
        placed[3],
        placed[4],
        placed[5],
        placed[6],
        placed[7],
        placed[8],
        placed[9],
        placed[10],
        placed[11],
    )


def solution(mesh):
    in_specs = (
        P(("wide", "narrow"), None, None),
        P(("wide", "narrow"), None),
        P(("wide", "narrow"), None, None),
        P(),
        P("wide", "narrow"),
        P("wide", "narrow"),
        P("wide", "narrow", None),
        P("wide", "narrow"),
        P("wide", "narrow", None),
        P("wide", "narrow"),
        P("wide", "narrow"),
        P("wide", "narrow"),
        P("wide", "narrow", None),
        P("wide", "narrow"),
        P("wide", "narrow", None),
        P("wide", "narrow"),
    )
    out_specs = (
        P(("wide", "narrow"), None, None),
        P(("wide", "narrow"), None, None),
        P("wide", "narrow"),
        P("wide", "narrow"),
        P("wide", "narrow", None),
        P("wide", "narrow"),
        P("wide", "narrow", None),
        P("wide", "narrow"),
        P("wide", "narrow"),
        P("wide", "narrow"),
        P("wide", "narrow", None),
        P("wide", "narrow"),
        P("wide", "narrow", None),
        P("wide", "narrow"),
    )
    return jax.shard_map(
        on_device, mesh=mesh, in_specs=in_specs, out_specs=out_specs, check_vma=False
    )
```

profile of v0, /device:TPU:0, one launch (start us, length us, event | category | flops | bytes accessed | tf_op | source)
XLA Modules:
  0.0 1152.7 jit_solution(14246586460051045269)
XLA Ops:
  10.7 24.4 %all-gather.7.cloned.1.call-done = bf16[1,768,768]{2,1,0:T(8,128)(2,1)} async-done(((bf16[1,384,768]{2,1,0:T(8,128)(2,1)}), bf16[1,768,768]{2,1,0:T(8,128)(2,1)}) %all-gather.7.cloned.1.call-update) | async-done | bytes 1179664 | tf_op jit(solution)/shard_map/all_gather | solution.py:89
  36.2 49.8 %all-gather.5.cloned.1.call-done = bf16[1,768,2304]{2,1,0:T(8,128)(2,1)} async-done(((bf16[1,384,2304]{2,1,0:T(8,128)(2,1)}), bf16[1,768,2304]{2,1,0:T(8,128)(2,1)}) %all-gather.5.cloned.1.call-update) | async-done | bytes 3538960 | tf_op jit(solution)/shard_map/all_gather | solution.py:87
  88.0 62.2 %all-gather.9.cloned.1.call-done = bf16[1,768,3072]{2,1,0:T(8,128)(2,1)} async-done(((bf16[1,384,3072]{2,1,0:T(8,128)(2,1)}), bf16[1,768,3072]{2,1,0:T(8,128)(2,1)}) %all-gather.9.cloned.1.call-update) | async-done | bytes 4718608 | tf_op jit(solution)/shard_map/all_gather | solution.py:93
  150.2 2.5 select_bitcast_fusion.1
  152.7 61.6 %all-gather.11.cloned.1.call-done = bf16[1,3072,768]{2,1,0:T(8,128)(2,1)} async-done(((bf16[1,1536,768]{2,1,0:T(8,128)(2,1)}), bf16[1,3072,768]{2,1,0:T(8,128)(2,1)}) %all-gather.11.cloned.1.call-update) | async-done | bytes 4718608 | tf_op jit(solution)/shard_map/all_gather | solution.py:95
  214.3 2.5 select_bitcast_fusion
  217.5 4.3 all_gather.42
  221.8 4.3 all_gather.43
  226.2 4.3 all_gather.47
  230.5 4.3 all_gather.48
  234.8 4.3 all_gather.49
  239.1 4.3 all_gather.45
  243.5 4.4 all_gather.51
  248.0 61.5 %all-reduce.9 = (bf16[1,1536]{1,0:T(2,128)(2,1)S(1)}, bf16[768]{0:T(1024)(128)(2,1)S(1)}, bf16[768]{0:T(1024)(128)(2,1)S(1)}, bf16[768]{0:T(1024)(128)(2,1)S(1)}...) all-reduce(bf16[1,1536]{1,0:T(2,128)(2,1)S(1)} %broadcast_select_fu, ...), channel_id=1, replica_groups=mesh['wide'=16,'narrow'=2] {'wide'}, use_global_device_ids=true, to_apply=%region_5.6 | all-reduce | flops 8448 | bytes 33792 | tf_op jit(solution)/shard_map/psum | solution.py:17
  313.4 165.8 %all-reduce.18.cloned.1.call-done = (bf16[768,2304]{1,0:T(8,128)(2,1)}, bf16[768,768]{1,0:T(8,128)(2,1)}, bf16[768,3072]{1,0:T(8,128)(2,1)}, bf16[3072,768]{1,0:T(8,128)(2,1)}) async-done(((bf16[768,2304]{1,0:T(8,128)(2,1)}, bf16[768,768]{1,0:T(8,128)(2,1)}, bf16[768,3072]{1,0:T(8,128)(2,1)}, bf16[3072,768]{1,0:T(8,128)(2,1)}), (bf16[768,2304]{1,0:T(8,128)(2,1)}, bf16[768,768]{1,0:T(8,128)(2,1)}, ...) | async-done | bytes 14155792 | tf_op jit(solution)/shard_map/psum | solution.py:17
  479.3 7.8 add_convert_fusion
  487.1 6.6 copy.59
  493.7 4.7 slice_bitcast_fusion
  498.3 4.1 copy.62
  502.4 4.1 copy.61
  506.5 4.1 copy.60
  512.0 63.2 %while.26 = (s32[]{:T(128)}, bf16[12,1024,64]{1,2,0:T(8,128)(2,1)}, f32[12,1024]{1,0:T(8,128)S(1)}, s32[12,1024]{1,0:T(8,128)S(1)}, bf16[12,1024,64]{2,1,0:T(8,1...) while((s32[]{:T(128)}, bf16[12,1024,64]{1,2,0:T(8,128)(2,1)}, ...), condition=%wide.region_9.10_spmd, body=%wide.region_6.9_spmd.sunk | while | flops 279968768 | bytes 13690989 | solution.py:197
  514.7 2.5 fusion.137
  519.9 2.5 fusion.137
  575.3 3.5 fusion.96
  579.3 5.6 fusion.90
  584.9 18.5 %fusion.99 = (bf16[3072]{0:T(1024)(128)(2,1)S(1)}, bf16[1024,3072]{1,0:T(8,128)(2,1)}) fusion(f32[1024,3072]{1,0:T(8,128)S(1)} %fusion.90, f32[3072]{0:T(1024)S(1)} %add.232, bf16[3072,768]{1,0:T(8,128)(2,1)} %get-tuple-element.250, bf16[1,1024,768]{2,1,0:T(8,128)(2,1)S(1)} %copy-done.6), kind=kOutput, calls=%fused_computation.174 | convolution fusion | flops 4913624064 | bytes 25184256 | tf_op jit(solution)/shard_map/nd,fd->nf/dot_general | solution.py:241
  603.4 8.9 fusion.98
  612.3 3.6 copy.65
  615.9 3.9 multiply_reduce_fusion.1
  626.7 4.3 convolution_convert_fusion.3
  631.0 4.3 copy.66
  639.4 155.7 %while.27 = (s32[]{:T(128)}, bf16[12,1024,64]{1,2,0:T(8,128)(2,1)}, bf16[12,1024,64]{1,2,0:T(8,128)(2,1)}, bf16[12,1024,64]{1,2,0:T(8,128)(2,1)}, s32[12,1024]{1...) while((s32[]{:T(128)}, bf16[12,1024,64]{1,2,0:T(8,128)(2,1)}, ...), condition=%wide.region_24.25_spmd, body=%wide.region_22.24_spmd.sunk | while | flops 684850176 | bytes 34120828 | solution.py:265
  641.2 3.2 multiply_reduce_fusion.5
  654.1 3.1 multiply_reduce_fusion.5
  667.1 3.1 multiply_reduce_fusion.5
  680.0 3.2 multiply_reduce_fusion.5
  693.0 3.2 multiply_reduce_fusion.5
  706.0 3.2 multiply_reduce_fusion.5
  719.0 3.1 multiply_reduce_fusion.5
  731.9 3.2 multiply_reduce_fusion.5
  744.9 3.2 multiply_reduce_fusion.5
  757.9 3.2 multiply_reduce_fusion.5
  770.9 3.2 multiply_reduce_fusion.5
  783.9 3.2 multiply_reduce_fusion.5
  795.1 2.7 bitcast_reduce_fusion
  800.0 5.7 convolution_convert_fusion.2
  805.8 12.6 %convolution_convert_fusion = bf16[3072,768]{1,0:T(8,128)(2,1)} fusion(bf16[1,1024,768]{2,1,0:T(8,128)(2,1)} %param.22, f32[1024,3072]{1,0:T(8,128)} %copy-done.5, f32[3072]{0:T(1024)S(1)} %add.232), kind=kOutput, calls=%fused_computation.74 | convolution fusion | flops 4865654784 | bytes 18886656 | tf_op jit(solution)/shard_map/nf,nd->fd/dot_general | solution.py:239
  818.5 9.9 convolution_convert_fusion.1
  833.3 4.3 all_gather.53
  837.9 9.0 fusion.97
  846.8 3.5 copy.70
  850.4 2.6 fusion.64
  854.6 8.4 all-reduce.12
  863.6 57.9 %all-reduce.8 = (bf16[768]{0:T(1024)(128)(2,1)S(1)}, bf16[384]{0:T(512)(128)(2,1)S(1)}, bf16[384]{0:T(512)(128)(2,1)S(1)}, bf16[768]{0:T(1024)(128)(2,1)S(1)}, b...) all-reduce(bf16[768]{0:T(1024)(128)(2,1)S(1)} %fusion.87, ...), channel_id=1, replica_groups=mesh['wide'=16,'narrow'=2] {'wide'}, use_global_device_ids=true, to_apply=%region_19.20 | all-reduce | flops 5376 | bytes 21504 | tf_op jit(solution)/shard_map/psum | solution.py:17
  921.5 57.4 %reduce-scatter.9.cloned.1.call-done = bf16[384,3072]{1,0:T(8,128)(2,1)} async-done(((bf16[768,3072]{1,0:T(8,128)(2,1)}), bf16[384,3072]{1,0:T(8,128)(2,1)}) %reduce-scatter.9.cloned.1.call-update) | async-done | bytes 2359312 | tf_op jit(solution)/shard_map/reduce_scatter | solution.py:308
  979.0 12.0 %fusion.77 = bf16[1,1024,768]{1,2,0:T(8,128)(2,1)} fusion(f32[768]{0:T(1024)S(1)} %add.239, f32[1024,768]{0,1:T(8,128)} %copy-done, bf16[3072,768]{1,0:T(8,128)(2,1)} %get-tuple-element.250, f32[1024,3072]{1,0:T(8,128)} %copy-done.5, f32[3072]{0:T(1024)S(1)} %add.232), kind=kOutput, calls=%fused_computation.125 | convolution fusion | flops 4865654784 | bytes 22035456 | tf_op jit(solution)/shard_map/dot_general | solution.py:216
  990.9 2.6 copy.73
  994.1 5.5 fusion.73
  999.7 2.6 copy.74
  1006.3 128.1 %all-reduce.16.cloned.1.call-done = (bf16[384,2304]{1,0:T(8,128)(2,1)}, bf16[384,768]{1,0:T(8,128)(2,1)}, bf16[384,3072]{1,0:T(8,128)(2,1)}, bf16[1536,768]{1,0:T(8,128)(2,1)}) async-done(((bf16[384,2304]{1,0:T(8,128)(2,1)}, bf16[384,768]{1,0:T(8,128)(2,1)}, bf16[384,3072]{1,0:T(8,128)(2,1)}, bf16[1536,768]{1,0:T(8,128)(2,1)}), (bf16[384,2304]{1,0:T(8,128)(2,1)}, bf16[384,768]{1,0:T(8,128)(2,1)}, ...) | async-done | bytes 7077904 | tf_op jit(solution)/shard_map/psum | solution.py:338
  1136.7 3.5 multiply_bitcast_fusion.2
  1140.2 2.7 multiply_bitcast_fusion.1
  1142.9 2.5 multiply_bitcast_fusion
  (320 shorter events, 212.9 us)
Async XLA Ops:
  7.2 27.9 %all-gather.7.cloned.1.call-start = ((), (), s32[]{:S(2)}) async-start(), calls=%async_computation.5 | async-start | bytes 1769472 | tf_op jit(solution)/shard_map/all_gather | solution.py:89
  7.9 78.1 %all-gather.5.cloned.1.call-start = ((), (), s32[]{:S(2)}) async-start(), calls=%async_computation.4 | async-start | bytes 5308416 | tf_op jit(solution)/shard_map/all_gather | solution.py:87
  8.7 141.6 %all-gather.9.cloned.1.call-start = ((), (), s32[]{:S(2)}) async-start(), calls=%async_computation.6 | async-start | bytes 7077888 | tf_op jit(solution)/shard_map/all_gather | solution.py:93
  9.4 204.9 %all-gather.11.cloned.1.call-start = ((), (), s32[]{:S(2)}) async-start(), calls=%async_computation.7 | async-start | bytes 7077888 | tf_op jit(solution)/shard_map/all_gather | solution.py:95
  10.0 469.3 %all-reduce.18.cloned.1.call-start = ((), (), s32[]{:S(2)}) async-start(), calls=%async_computation.13 | async-start | bytes 28311552 | tf_op jit(solution)/shard_map/psum | solution.py:17
  216.8 0.7 copy-start.26
  216.8 5.0 copy-start.27
  216.8 9.3 copy-start.28
  216.8 13.6 %copy-start.29 = (bf16[1,384]{1,0:T(2,128)(2,1)S(1)}, bf16[1,384]{1,0:T(2,128)(2,1)}, u32[]{:S(2)}) copy-start(bf16[1,384]{1,0:T(2,128)(2,1)} %param.30) | copy-start | bytes 2308
  216.8 18.0 %copy-start.30 = (bf16[1,384]{1,0:T(2,128)(2,1)S(1)}, bf16[1,384]{1,0:T(2,128)(2,1)}, u32[]{:S(2)}) copy-start(bf16[1,384]{1,0:T(2,128)(2,1)} %param.31) | copy-start | bytes 2308
  216.9 22.3 %copy-start.25 = (bf16[1,768]{1,0:T(2,128)(2,1)S(1)}, bf16[1,768]{1,0:T(2,128)(2,1)}, u32[]{:S(2)}) copy-start(bf16[1,768]{1,0:T(2,128)(2,1)} %param.27) | copy-start | bytes 4612
  216.9 26.6 %copy-start.21 = (bf16[1,1536]{1,0:T(2,128)(2,1)S(1)}, bf16[1,1536]{1,0:T(2,128)(2,1)}, u32[]{:S(2)}) copy-start(bf16[1,1536]{1,0:T(2,128)(2,1)} %param.33) | copy-start | bytes 9220
  216.9 92.7 %copy-start.10 = (bf16[1,1024,768]{2,1,0:T(8,128)(2,1)S(1)}, bf16[1,1024,768]{2,1,0:T(8,128)(2,1)}, u32[]{:S(2)}) copy-start(bf16[1,1024,768]{2,1,0:T(8,128)(2,1)} %param.20) | copy-start | bytes 4718596
  216.9 704.6 %reduce-scatter.7.cloned.1.call-start = ((), (), s32[]{:S(2)}) async-start(), calls=%async_computation.9 | async-start | bytes 1769472 | tf_op jit(solution)/shard_map/reduce_scatter | solution.py:296
  309.5 169.8 %copy-start.15 = (f32[768]{0:T(1024)}, f32[768]{0:T(1024)S(1)}, u32[]{:S(2)}) copy-start(f32[768]{0:T(1024)S(1)} %mul.311) | copy-start | bytes 9220
  309.5 169.8 %copy-start.23 = (f32[768]{0:T(1024)}, f32[768]{0:T(1024)S(1)}, u32[]{:S(2)}) copy-start(f32[768]{0:T(1024)S(1)} %add.216) | copy-start | bytes 9220
  312.4 174.7 %copy-start.13 = (f32[1024]{0:T(1024)}, f32[1024]{0:T(1024)S(1)}, u32[]{:S(2)}) copy-start(f32[1024]{0:T(1024)S(1)} %broadcast_multiply_fusion.1) | copy-start | bytes 12292
  312.8 0.6 copy-start.19
  313.4 173.6 %copy-start.17 = (f32[1024]{0:T(1024)}, f32[1024]{0:T(1024)S(1)}, u32[]{:S(2)}) copy-start(f32[1024]{0:T(1024)S(1)} %fusion.80) | copy-start | bytes 12292
  506.5 4.1 copy-start.22
  575.2 4.0 slice-start
  575.3 4.0 slice-start.1
  578.8 6.0 copy-start
  579.3 5.6 copy-start.6
  584.9 18.5 %copy-start.5 = (f32[1024,3072]{1,0:T(8,128)}, f32[1024,3072]{1,0:T(8,128)S(1)}, u32[]{:S(2)}) copy-start(f32[1024,3072]{1,0:T(8,128)S(1)} %fusion.90) | copy-start | bytes 37748740
  615.9 3.9 copy-start.1
  615.9 4.7 copy-start.3
  621.4 1.7 copy-start.4
  621.4 2.8 copy-start.11
  623.1 1.1 copy-start.12
  631.0 290.5 %reduce-scatter.5.cloned.1.call-start = ((), (), s32[]{:S(2)}) async-start(), calls=%async_computation.8 | async-start | bytes 5308416 | tf_op jit(solution)/shard_map/reduce_scatter | solution.py:290
  795.1 4.9 copy-start.14
  795.1 4.9 copy-start.16
  795.1 4.9 copy-start.18
  795.1 4.9 copy-start.24
  797.8 2.2 copy-start.7
  805.7 115.8 %reduce-scatter.11.cloned.1.call-start = ((), (), s32[]{:S(2)}) async-start(), calls=%async_computation.11 | async-start | bytes 7077888 | tf_op jit(solution)/shard_map/reduce_scatter | solution.py:314
  818.4 160.5 %reduce-scatter.9.cloned.1.call-start = ((), (), s32[]{:S(2)}) async-start(), calls=%async_computation.10 | async-start | bytes 7077888 | tf_op jit(solution)/shard_map/reduce_scatter | solution.py:308
  828.4 0.7 copy-start.32
  828.4 4.9 copy-start.31
  828.5 305.9 %all-reduce.16.cloned.1.call-start = ((), (), s32[]{:S(2)}) async-start(), calls=%async_computation.12 | async-start | bytes 14155776 | tf_op jit(solution)/shard_map/psum | solution.py:338
  850.4 2.6 copy-start.20
  850.4 2.8 copy-start.2
  1134.4 5.8 copy-start.9
  1140.2 2.8 copy-start.8
Sparse Core Ops, SparseCore 0:
  9.6 25.4 all-gather.6
  36.6 49.3 all-gather.4
  87.6 62.6 all-gather.8
  151.6 62.6 all-gather.10
  219.9 259.3 all-reduce.17
  631.1 21.7 reduce-scatter.6
  805.8 47.7 reduce-scatter.4
  855.9 59.9 reduce-scatter.10
  918.9 59.9 reduce-scatter.8
  982.8 151.4 all-reduce.15
where the time goes:
time: 1160 us; the launch traced here: 1150 us
  waiting for transfers between devices  552 us (48%)
  matrix products  296 us (26%)
  blocking collectives  162 us (14%)
  local copies, waits for them, and re-layouts  62.6 us (5%)
  other arithmetic  60.9 us (5%)
  between operations  17.7 us (2%)
    psum x1, waiting for transfers between devices, broadcast(): return lax.psum(jnp.where(mine, x, jnp.zeros_like(x)), axis)  166 us
    psum x1, waiting for transfers between devices, on_device(): lax.psum(share_qkv.astype(jnp.bfloat16), 'wide').astype(jnp.float32)  128 us
    psum x2, blocking collectives, broadcast(): return lax.psum(jnp.where(mine, x, jnp.zeros_like(x)), axis)  119 us
    all_gather x1, waiting for transfers between devices, fetch(): lax.all_gather(fc_weight, 'narrow', axis=1, tiled=True)  62.2 us
    dot_general x24, matrix products, head_scores(): jnp.dot(queries, keys.T, preferred_element_type=jnp.float32) * HD ** (-0.5)  62.1 us
    all_gather x1, waiting for transfers between devices, fetch(): lax.all_gather(proj_weight, 'narrow', axis=1, tiled=True)  61.6 us
    reduce_scatter x1, waiting for transfers between devices, on_device(): lax.psum_scatter(grad_fc.astype(jnp.bfloat16), 'narrow', scatter_dimensio...  57.4 us
    all_gather x1, waiting for transfers between devices, fetch(): lax.all_gather(qkv_weight, 'narrow', axis=1, tiled=True)  49.8 us
  transfers between devices with their start and end apart: 10, of which 7 were waited for; matrix products, arithmetic and copies ran while one was open for 22% of the time, Pallas kernels for 0%

commit v1 on v0

v1 whole, which is shorter than its diff:
```python
import functools
import math

import jax
import jax.numpy as jnp
from jax import lax
from jax.experimental import pallas as pl
from jax.experimental.pallas import tpu as pltpu
from jax.sharding import PartitionSpec as P

H = 12
HD = 64
QB = 256
REACH = 512

epsilon = 1e-05
AXES = ("wide", "narrow")
VMEM = 56 * 1024 * 1024
f32 = jnp.float32
bf16 = jnp.bfloat16


def spans(length):
    out = []
    for b in range(length // QB):
        low = max(0, (b * QB - (REACH - 1)) // QB * QB)
        out.append((low, (b + 1) * QB))
    return out


def attend_kernel(doc_ref, q_ref, k_ref, v_ref, o_ref, p_ref, *, length):
    lane = lax.broadcasted_iota(jnp.int32, (length, 128), 1)
    low = lane < HD
    hot = (lane & (HD - 1)) == doc_ref[...]
    q_side = jnp.where(hot, 1.0, 0.0)
    k_side = jnp.where(hot, 0.0, -1e9)
    q = q_ref[...].astype(f32) * HD ** (-0.5)
    k = k_ref[...].astype(f32)
    v_t = v_ref[...].T
    sides = []
    for h in range(2):
        mine = low if h == 0 else jnp.logical_not(low)
        sides.append(
            (jnp.where(mine, q, q_side).astype(bf16), jnp.where(mine, k, k_side).astype(bf16))
        )
    rows = lax.broadcasted_iota(jnp.int32, (QB, QB), 0)
    tri = rows <= lax.broadcasted_iota(jnp.int32, (QB, QB), 1)
    at = 0
    for b, (lo, hi) in enumerate(spans(length)):
        n = hi - lo
        outs = []
        for h in range(2):
            qa, ka = sides[h]
            s = lax.dot_general(
                ka[lo:hi],
                qa[b * QB : (b + 1) * QB],
                (((1,), (1,)), ((), ())),
                preferred_element_type=f32,
            )
            last = jnp.where(tri, s[n - QB :], -1e9)
            s = last if n == QB else jnp.concatenate([s[: n - QB], last], axis=0)
            e = jnp.exp(s - jnp.max(s, axis=0, keepdims=True))
            p = (e * (1.0 / jnp.sum(e, axis=0, keepdims=True))).astype(bf16)
            p_ref[h, at : at + n, :] = p
            outs.append(
                jnp.dot(v_t[h * HD : (h + 1) * HD, lo:hi], p, preferred_element_type=f32)
            )
        o_ref[b * QB : (b + 1) * QB, :] = jnp.concatenate(outs, axis=0).T.astype(bf16)
        at += n


def attend(qkv, doc):
    length = qkv.shape[0]
    pairs = H // 2
    rows = sum(hi - lo for lo, hi in spans(length))
    col = lambda off: pl.BlockSpec((length, 128), lambda i: (0, off + i))
    return pl.pallas_call(
        functools.partial(attend_kernel, length=length),
        grid=(pairs,),
        in_specs=[
            pl.BlockSpec((length, 1), lambda i: (0, 0)),
            col(0),
            col(pairs),
            col(2 * pairs),
        ],
        out_specs=[col(0), pl.BlockSpec((2, rows, QB), lambda i: (i, 0, 0))],
        out_shape=[
            jax.ShapeDtypeStruct((length, pairs * 128), bf16),
            jax.ShapeDtypeStruct((2 * pairs, rows, QB), bf16),
        ],
        compiler_params=pltpu.CompilerParams(vmem_limit_bytes=VMEM),
        name="attend",
    )(doc, qkv, qkv, qkv)


def attend_back_kernel(
    q_ref, k_ref, v_ref, o_ref, do_ref, p_ref, dq_ref, dk_ref, dv_ref, dk_acc, dv_acc, *, length
):
    lane = lax.broadcasted_iota(jnp.int32, (length, 128), 1)
    low = lane < HD
    spot = lane & (HD - 1)
    q = q_ref[...].astype(f32) * HD ** (-0.5)
    do = do_ref[...].astype(f32)
    v = v_ref[...].astype(f32)
    product = do * o_ref[...].astype(f32)
    k_t = k_ref[...].T
    sides = []
    for h in range(2):
        mine = low if h == 0 else jnp.logical_not(low)
        center = jnp.sum(jnp.where(mine, product, 0.0), axis=1, keepdims=True)
        first = center.astype(bf16).astype(f32)
        second = (center - first).astype(bf16).astype(f32)
        third = center - first - second
        extra = jnp.where(
            spot == 0, -first, jnp.where(spot == 1, -second, jnp.where(spot == 2, -third, 0.0))
        )
        sides.append(
            (
                jnp.where(mine, do, extra).astype(bf16),
                jnp.where(mine, v, jnp.where(spot < 3, 1.0, 0.0)).astype(bf16),
                jnp.where(mine, do, 0.0).astype(bf16),
                jnp.where(mine, q, 0.0).astype(bf16),
            )
        )
    dk_acc[...] = jnp.zeros_like(dk_acc)
    dv_acc[...] = jnp.zeros_like(dv_acc)
    at = 0
    for b, (lo, hi) in enumerate(spans(length)):
        n = hi - lo
        here = slice(b * QB, (b + 1) * QB)
        dqs = []
        dk = dv = None
        for h in range(2):
            do_more, v_more, do_own, q_own = sides[h]
            p = p_ref[h, at : at + n, :]
            dp = lax.dot_general(
                v_more[lo:hi],
                do_more[here],
                (((1,), (1,)), ((), ())),
                preferred_element_type=f32,
            )
            ds = (p.astype(f32) * dp).astype(bf16)
            dv_part = jnp.dot(p, do_own[here], preferred_element_type=f32)
            dk_part = jnp.dot(ds, q_own[here], preferred_element_type=f32)
            dv = dv_part if dv is None else dv + dv_part
            dk = dk_part if dk is None else dk + dk_part
            dqs.append(
                jnp.dot(k_t[h * HD : (h + 1) * HD, lo:hi], ds, preferred_element_type=f32)
            )
        dv_acc[lo:hi, :] += dv
        dk_acc[lo:hi, :] += dk
        dq_ref[here, :] = (jnp.concatenate(dqs, axis=0) * HD ** (-0.5)).T.astype(bf16)
        at += n
    dk_ref[...] = dk_acc[...].astype(bf16)
    dv_ref[...] = dv_acc[...].astype(bf16)


def attend_back(qkv, mixed, grad_mixed, soft):
    length = qkv.shape[0]
    pairs = H // 2
    rows = soft.shape[1]
    col = lambda off: pl.BlockSpec((length, 128), lambda i: (0, off + i))
    out = jax.ShapeDtypeStruct((length, pairs * 128), bf16)
    return pl.pallas_call(
        functools.partial(attend_back_kernel, length=length),
        grid=(pairs,),
        in_specs=[
            col(0),
            col(pairs),
            col(2 * pairs),
            col(0),
            col(0),
            pl.BlockSpec((2, rows, QB), lambda i: (i, 0, 0)),
        ],
        out_specs=[col(0)] * 3,
        out_shape=[out] * 3,
        scratch_shapes=[pltpu.VMEM((length, 128), f32)] * 2,
        compiler_params=pltpu.CompilerParams(vmem_limit_bytes=VMEM),
        name="attend_back",
    )(qkv, qkv, qkv, mixed, grad_mixed, soft)


class Place:
    def __init__(self, owner, wide, narrow):
        self.wide, self.narrow = wide, narrow
        self.deep = wide // 4
        mine = lax.axis_index("wide")
        self.core, self.y, self.z = mine & 1, (mine >> 1) & 1, mine >> 2
        self.o_core, self.o_y, self.o_z = owner & 1, (owner >> 1) & 1, owner >> 2
        self.x = lax.axis_index("narrow")
        self.holder = mine == owner

    def swap(self, value, flip):
        return lax.ppermute(value, "wide", [(i, i ^ flip) for i in range(self.wide)])

    def z_flips(self):
        step = self.deep // 2
        while step:
            yield step
            step //= 2


def pick(parts, index):
    return lax.dynamic_index_in_dim(parts, index, axis=0, keepdims=False)


def ordered(mine, other, index):
    first = index == 0
    return jnp.stack([jnp.where(first, mine, other), jnp.where(first, other, mine)])


def spread(place, shard):
    rows, width = shard.shape
    cut = rows % 64 == 0
    now = shard
    if cut:
        halves = shard.reshape(2, rows // 2, width)
        other = place.swap(pick(halves, 1 - place.core), 1)
        now = jnp.where(place.core == place.o_core, pick(halves, place.core), other)
        halves = now.reshape(2, rows // 4, width)
        other = place.swap(pick(halves, 1 - place.y), 2)
        now = jnp.where(place.y == place.o_y, pick(halves, place.y), other)
    else:
        now = jnp.where(place.core == place.o_core, now, place.swap(now, 1))
        now = jnp.where(place.y == place.o_y, now, place.swap(now, 2))
    for step in place.z_flips():
        other = place.swap(now, 4 * step)
        now = jnp.where((place.z & step) == (place.o_z & step), now, other)
    if cut:
        now = ordered(now, place.swap(now, 2), place.y)
        if place.narrow == 2:
            other = lax.ppermute(now, "narrow", [(0, 1), (1, 0)])
            now = ordered(now, other, place.x)
        else:
            now = lax.all_gather(now, "narrow", axis=0)
        other = place.swap(now, 1)
        first = place.core == 0
        now = jnp.stack([jnp.where(first, now, other), jnp.where(first, other, now)], axis=1)
        return now.reshape(place.narrow * rows, width)
    return lax.all_gather(now, "narrow", axis=0, tiled=True)


def collect(place, terms):
    total, width = terms.shape
    rows = total // place.narrow
    cut = rows % 64 == 0
    now = terms.astype(bf16)
    add = lambda a, b: (a.astype(f32) + b.astype(f32)).astype(bf16)
    if cut:
        now = now.reshape(place.narrow, 2, rows // 2, width)
        take = lambda i: lax.dynamic_index_in_dim(now, i, axis=1, keepdims=False)
        other = place.swap(take(1 - place.core), 1)
        now = add(take(place.core), other)
        if place.narrow == 2:
            other = lax.ppermute(pick(now, 1 - place.x), "narrow", [(0, 1), (1, 0)])
            now = add(pick(now, place.x), other)
        else:
            now = lax.psum_scatter(now, "narrow", scatter_dimension=0, tiled=False)
        now = now.reshape(2, rows // 4, width)
        other = place.swap(pick(now, 1 - place.y), 2)
        now = add(pick(now, place.y), other)
        for step in place.z_flips():
            now = add(now, place.swap(now, 4 * step))
        now = ordered(now, place.swap(now, 2), place.y)
        now = ordered(now, place.swap(now, 1), place.core)
        return now.reshape(rows, width)
    now = lax.psum_scatter(now, "narrow", scatter_dimension=0, tiled=True)
    return lax.psum(now, "wide")


VECTORS = (
    "ln1_gain",
    "ln1_bias",
    "qv_bias",
    "out_bias",
    "ln2_gain",
    "ln2_bias",
    "fc_bias",
    "proj_bias",
)


def spread_vectors(place, vectors):
    sizes = [v.shape[-1] for v in vectors]
    now = jnp.concatenate([v.reshape(-1) for v in vectors]).reshape(-1, 128)
    now = jnp.where(place.core == place.o_core, now, place.swap(now, 1))
    now = jnp.where(place.y == place.o_y, now, place.swap(now, 2))
    for step in place.z_flips():
        now = jnp.where((place.z & step) == (place.o_z & step), now, place.swap(now, 4 * step))
    if place.narrow == 2:
        now = ordered(now, lax.ppermute(now, "narrow", [(0, 1), (1, 0)]), place.x)
    else:
        now = lax.all_gather(now, "narrow", axis=0)
    now = now.reshape(place.narrow, -1).astype(f32)
    out, at = [], 0
    for size in sizes:
        out.append(now[:, at : at + size].reshape(-1))
        at += size
    return out


def collect_vectors(place, vectors):
    sizes = [v.shape[0] // place.narrow for v in vectors]
    now = jnp.concatenate([v.reshape(place.narrow, -1) for v in vectors], axis=1)
    now = now.reshape(place.narrow, -1, 128)
    now = now + place.swap(now, 1)
    if place.narrow == 2:
        now = pick(now, place.x) + lax.ppermute(
            pick(now, 1 - place.x), "narrow", [(0, 1), (1, 0)]
        )
    else:
        now = lax.psum_scatter(now, "narrow", scatter_dimension=0, tiled=False)
    now = now + place.swap(now, 2)
    for step in place.z_flips():
        now = now + place.swap(now, 4 * step)
    now = now.reshape(-1)
    out, at = [], 0
    for size in sizes:
        out.append(now[at : at + size])
        at += size
    return out


def norm_rows(values, gain, shift):
    center = values - jnp.mean(values, axis=-1, keepdims=True)
    spread_of = jnp.mean(center * center, axis=-1, keepdims=True)
    return center * lax.rsqrt(spread_of + epsilon) * gain + shift


def norm_back(values, gain, grad):
    center = values - jnp.mean(values, axis=-1, keepdims=True)
    inverse = lax.rsqrt(jnp.mean(center * center, axis=-1, keepdims=True) + epsilon)
    hat = center * inverse
    scaled = grad * gain
    inner = jnp.mean(scaled * hat, axis=-1, keepdims=True)
    back = inverse * (scaled - jnp.mean(scaled, axis=-1, keepdims=True) - hat * inner)
    return back, jnp.sum(grad * hat, axis=0), jnp.sum(grad, axis=0)


def gelu_both(u):
    c = math.sqrt(2.0 / math.pi)
    t = jnp.tanh(c * (u + 0.044715 * u * u * u))
    slope = 0.5 * (1.0 + t) + 0.5 * u * (1.0 - t * t) * c * (1.0 + 3 * 0.044715 * u * u)
    return 0.5 * u * (1.0 + t), slope


def dot(a, b, dims=((1,), (0,))):
    return lax.dot_general(a, b, (dims, ((), ())), preferred_element_type=f32)


def on_device(
    wide,
    narrow,
    tokens,
    doc_ids,
    cotangent,
    owner,
    ln1_gain,
    ln1_bias,
    qkv_weight,
    qv_bias,
    out_weight,
    out_bias,
    ln2_gain,
    ln2_bias,
    fc_weight,
    fc_bias,
    proj_weight,
    proj_bias,
):
    _, length, width = tokens.shape
    place = Place(owner[0], wide, narrow)
    x = tokens[0].astype(f32)
    dout = cotangent[0]

    gain1, shift1, qv, outb, gain2, shift2, fcb, projb = spread_vectors(
        place, (ln1_gain, ln1_bias, qv_bias, out_bias, ln2_gain, ln2_bias, fc_bias, proj_bias)
    )
    w_qkv = spread(place, qkv_weight[0])
    w_out = spread(place, out_weight[0])
    w_fc = spread(place, fc_weight[0])
    w_proj = spread(place, proj_weight[0])

    h1 = norm_rows(x, gain1, shift1).astype(bf16)
    bias = jnp.concatenate([qv[:width], jnp.zeros((width,), f32), qv[width:]])
    qkv = (dot(h1, w_qkv) + bias).astype(bf16)
    mixed, soft = attend(qkv, doc_ids[0][:, None])
    y1 = x + dot(mixed, w_out) + outb
    h2 = norm_rows(y1, gain2, shift2).astype(bf16)
    g, slope = gelu_both(dot(h2, w_fc) + fcb)
    g, slope = g.astype(bf16), slope.astype(bf16)
    block_out = (y1 + dot(g, w_proj) + projb).astype(bf16)

    d_proj = dot(g, dout, ((0,), (0,)))
    d_projb = jnp.sum(dout.astype(f32), axis=0)
    du = (dot(dout, w_proj, ((1,), (1,))) * slope.astype(f32)).astype(bf16)
    d_fc = dot(h2, du, ((0,), (0,)))
    d_fcb = jnp.sum(du.astype(f32), axis=0)
    dh2 = dot(du, w_fc, ((1,), (1,)))
    back, d_gain2, d_shift2 = norm_back(y1, gain2, dh2)
    dy1 = dout.astype(f32) + back
    db1 = dy1.astype(bf16)
    d_out = dot(mixed, db1, ((0,), (0,)))
    d_outb = jnp.sum(db1.astype(f32), axis=0)
    dmixed = dot(db1, w_out, ((1,), (1,))).astype(bf16)
    dqkv = jnp.concatenate(attend_back(qkv, mixed, dmixed, soft), axis=1)
    d_qkv = dot(h1, dqkv, ((0,), (0,)))
    sums = jnp.sum(dqkv.astype(f32), axis=0)
    d_qv = jnp.concatenate([sums[:width], sums[2 * width :]])
    dh1 = dot(dqkv, w_qkv, ((1,), (1,)))
    back, d_gain1, d_shift1 = norm_back(x, gain1, dh1)
    tokens_grad = (dy1 + back).astype(bf16)

    grads = [collect(place, g) for g in (d_proj, d_fc, d_out, d_qkv)]
    small = collect_vectors(
        place, (d_gain1, d_shift1, d_qv, d_outb, d_gain2, d_shift2, d_fcb, d_projb)
    )
    put = lambda v: jnp.where(place.holder, v.astype(f32), 0.0)[None]
    s_proj, s_fc, s_out, s_qkv = [put(v) for v in grads]
    s_gain1, s_shift1, s_qv, s_outb, s_gain2, s_shift2, s_fcb, s_projb = [put(v) for v in small]
    return (
        block_out[None],
        tokens_grad[None],
        s_gain1,
        s_shift1,
        s_qkv,
        s_qv,
        s_out,
        s_outb,
        s_gain2,
        s_shift2,
        s_fc,
        s_fcb,
        s_proj,
        s_projb,
    )


def solution(mesh):
    rows = P(AXES, None, None)
    flat, deep = P("wide", "narrow"), P("wide", "narrow", None)
    in_specs = (
        rows,
        P(AXES, None),
        rows,
        P(),
        flat,
        flat,
        deep,
        flat,
        deep,
        flat,
        flat,
        flat,
        deep,
        flat,
        deep,
        flat,
    )
    out_specs = (
        rows,
        rows,
        flat,
        flat,
        deep,
        flat,
        deep,
        flat,
        flat,
        flat,
        deep,
        flat,
        deep,
        flat,
    )
    body = functools.partial(on_device, mesh.shape["wide"], mesh.shape["narrow"])
    return jax.shard_map(
        body, mesh=mesh, in_specs=in_specs, out_specs=out_specs, check_vma=False
    )
```

time: 1160 us -> 647 us (0.56)
  matrix products: 296 us -> 83.5 us
  waiting for transfers between devices: 552 us -> 341 us
  blocking collectives: 162 us -> 0 us
  starting transfers between devices: 0.4 us -> 54.2 us
  Pallas kernels: 0 us -> 51.4 us
  local copies, waits for them, and re-layouts: 62.6 us -> 46.8 us
  between operations: 17.7 us -> 3.86 us
    ppermute x0 -> x66, waiting for transfers between devices: none -> 341 us  [the longest x56 229 us: swap(): lax.ppermute(value, 'wide', [(i, i ^ flip) for i in range(self.wide)])]
    psum x2 -> x0, waiting for transfers between devices: 294 us -> none  [the longest x1 166 us: broadcast(): return lax.psum(jnp.where(mine, x, jnp.zeros_like(x)), axis)]
    dot_general x96 -> x12, matrix products: 296 us -> 83.5 us  [dot(): return lax.dot_general(a, b, (dims, ((), ())), preferred_element_type=f32)]
    all_gather x4 -> x0, waiting for transfers between devices: 198 us -> none  [the longest x1 62.2 us: fetch(): lax.all_gather(fc_weight, 'narrow', axis=1, tiled=True)]
    psum x2 -> x0, blocking collectives: 119 us -> none  [broadcast(): return lax.psum(jnp.where(mine, x, jnp.zeros_like(x)), axis)]
    reduce_scatter x4 -> x0, waiting for transfers between devices: 57.4 us -> none  [the longest x1 57.4 us: on_device(): lax.psum_scatter(grad_fc.astype(jnp.bfloat16), 'narrow', scatter_dimensio...]
    ppermute x0 -> x66, starting transfers between devices: none -> 54.2 us  [the longest x56 44.1 us: swap(): lax.ppermute(value, 'wide', [(i, i ^ flip) for i in range(self.wide)])]
    pallas_call x0 -> x2, Pallas kernels: none -> 51.4 us  [the longest x1 29.6 us: attend(): pl.pallas_call(functools.partial(attend_kernel, length=length), grid=(pai...]
  transfers between devices with their start and end apart: 10 -> 66, of which waited for: 7 -> 37; matrix products, arithmetic and copies ran while one was open for 22% -> 12% of each run, Pallas kernels for 0% -> 5%
where the time goes in v1:
time: 647 us; the launch traced here: 638 us
  waiting for transfers between devices  341 us (53%)
  matrix products  83.5 us (13%)
  other arithmetic  57.4 us (9%)
  starting transfers between devices  54.2 us (8%)
  Pallas kernels  51.4 us (8%)
  local copies, waits for them, and re-layouts  46.8 us (7%)
    ppermute x56, waiting for transfers between devices, swap(): lax.ppermute(value, 'wide', [(i, i ^ flip) for i in range(self.wide)])  229 us
    dot_general x12, matrix products, dot(): return lax.dot_general(a, b, (dims, ((), ())), preferred_element_type=f32)  83.5 us
    ppermute x4, waiting for transfers between devices, spread(): other = lax.ppermute(now, 'narrow', [(0, 1), (1, 0)])  58.5 us
    ppermute x4, waiting for transfers between devices, collect(): other = lax.ppermute(pick(now, 1 - place.x), 'narrow', [(0, 1), (1, 0)])  52.6 us
    ppermute x56, starting transfers between devices, swap(): lax.ppermute(value, 'wide', [(i, i ^ flip) for i in range(self.wide)])  44.1 us
    pallas_call x1, Pallas kernels, attend(): pl.pallas_call(functools.partial(attend_kernel, length=length), grid=(pai...  29.6 us
    pallas_call x1, Pallas kernels, attend_back(): pl.pallas_call(functools.partial(attend_back_kernel, length=length), grid...  21.8 us
    unnamed x122, local copies, waits for them, and re-layouts  19.4 us
  transfers between devices with their start and end apart: 66, of which 37 were waited for; matrix products, arithmetic and copies ran while one was open for 12% of the time, Pallas kernels for 5%

profile of v1, /device:TPU:0, one launch (start us, length us, event | category | flops | bytes accessed | tf_op | source)
XLA Modules:
  0.0 637.8 jit_solution(8412046909326083349)
XLA Ops:
  8.6 2.3 dynamic-slice_bitcast_fusion.8
  18.5 2.4 collective-permute-start.1
  22.7 3.1 collective-permute-start.2
  36.9 3.6 collective-permute-done.13
  40.6 2.7 collective-permute-start.14
  43.2 5.0 collective-permute-done.14
  48.4 5.1 collective-permute-done.15
  65.1 4.2 collective-permute-done.17
  72.9 2.5 collective-permute-start.7
  77.5 15.1 %collective-permute-done.7 = bf16[96,2304]{1,0:T(8,128)(2,1)S(1)} collective-permute-done((bf16[96,2304]{1,0:T(8,128)(2,1)S(1)}, bf16[96,2304]{1,0:T(8,128)(2,1)S(1)}, u32[]{:S(2)}, u32[]{:S(2)}) %collective-permute-start.7) | collective-permute-done | bytes 442400 | tf_op jit(solution)/shard_map/ppermute | solution.py:194
  92.7 3.0 collective-permute-start.28
  95.7 2.4 collective-permute-done.20
  98.2 2.5 collective-permute-start.21
  100.8 11.5 %collective-permute-done.8 = bf16[96,2304]{1,0:T(8,128)(2,1)S(1)} collective-permute-done((bf16[96,2304]{1,0:T(8,128)(2,1)S(1)}, bf16[96,2304]{1,0:T(8,128)(2,1)S(1)}, u32[]{:S(2)}, u32[]{:S(2)}) %collective-permute-start.8) | collective-permute-done | bytes 442400 | tf_op jit(solution)/shard_map/ppermute | solution.py:194
  113.9 21.3 %collective-permute-done.28 = bf16[384,768]{1,0:T(8,128)(2,1)S(1)} collective-permute-done((bf16[384,768]{1,0:T(8,128)(2,1)S(1)}, bf16[384,768]{1,0:T(8,128)(2,1)S(1)}, u32[]{:S(2)}, u32[]{:S(2)}) %collective-permute-start.28) | collective-permute-done | bytes 589856 | tf_op jit(solution)/shard_map/ppermute | solution.py:194
  135.4 11.7 %collective-permute-done.21 = bf16[96,3072]{1,0:T(8,128)(2,1)S(1)} collective-permute-done((bf16[96,3072]{1,0:T(8,128)(2,1)S(1)}, bf16[96,3072]{1,0:T(8,128)(2,1)S(1)}, u32[]{:S(2)}, u32[]{:S(2)}) %collective-permute-start.21) | collective-permute-done | bytes 589856 | tf_op jit(solution)/shard_map/ppermute | solution.py:194
  147.3 12.4 %collective-permute-done.29 = bf16[384,768]{1,0:T(8,128)(2,1)S(1)} collective-permute-done((bf16[384,768]{1,0:T(8,128)(2,1)S(1)}, bf16[384,768]{1,0:T(8,128)(2,1)S(1)}, u32[]{:S(2)}, u32[]{:S(2)}) %collective-permute-start.29) | collective-permute-done | bytes 589856 | tf_op jit(solution)/shard_map/ppermute | solution.py:194
  161.3 10.9 %collective-permute-done.22 = bf16[96,3072]{1,0:T(8,128)(2,1)S(1)} collective-permute-done((bf16[96,3072]{1,0:T(8,128)(2,1)S(1)}, bf16[96,3072]{1,0:T(8,128)(2,1)S(1)}, u32[]{:S(2)}, u32[]{:S(2)}) %collective-permute-start.22) | collective-permute-done | bytes 589856 | tf_op jit(solution)/shard_map/ppermute | solution.py:194
  176.4 11.2 %collective-permute-done.23 = bf16[96,3072]{1,0:T(8,128)(2,1)S(1)} collective-permute-done((bf16[96,3072]{1,0:T(8,128)(2,1)S(1)}, bf16[96,3072]{1,0:T(8,128)(2,1)S(1)}, u32[]{:S(2)}, u32[]{:S(2)}) %collective-permute-start.23) | collective-permute-done | bytes 589856 | tf_op jit(solution)/shard_map/ppermute | solution.py:194
  188.2 8.3 %collective-permute-done.10 = bf16[2,96,2304]{2,1,0:T(8,128)(2,1)S(1)} collective-permute-done((bf16[2,96,2304]{2,1,0:T(8,128)(2,1)S(1)}, bf16[2,96,2304]{2,1,0:T(8,128)(2,1)S(1)}, u32[]{:S(2)}, u32[]{:S(2)}) %collective-permute-start.10) | collective-permute-done | bytes 884768 | tf_op jit(solution)/shard_map/ppermute | solution.py:232
  198.1 23.8 %collective-permute-done.31 = bf16[2,384,768]{2,1,0:T(8,128)(2,1)S(1)} collective-permute-done((bf16[2,384,768]{2,1,0:T(8,128)(2,1)S(1)}, bf16[2,384,768]{2,1,0:T(8,128)(2,1)S(1)}, u32[]{:S(2)}, u32[]{:S(2)}) %collective-permute-start.31) | collective-permute-done | bytes 1179680 | tf_op jit(solution)/shard_map/ppermute | solution.py:232
  223.6 22.2 %collective-permute-done.24 = bf16[2,96,3072]{2,1,0:T(8,128)(2,1)S(1)} collective-permute-done((bf16[2,96,3072]{2,1,0:T(8,128)(2,1)S(1)}, bf16[2,96,3072]{2,1,0:T(8,128)(2,1)S(1)}, u32[]{:S(2)}, u32[]{:S(2)}) %collective-permute-start.24) | collective-permute-done | bytes 1179680 | tf_op jit(solution)/shard_map/ppermute | solution.py:232
  250.6 6.1 add_convert_fusion.q_ref.k_ref.v_ref
  256.7 29.6 %attend.1 = (bf16[1024,768]{1,0:T(8,128)(2,1)}, bf16[12,2304,256]{2,1,0:T(8,128)(2,1)}) custom-call(s32[1024,1]{1,0:T(8,128)} %copy.41.doc_ref, bf16[1024,2304]{1,0:T(8,128)(2,1)} %add_convert_fusion.q_ref.k_ref.v_ref, bf16[1024,2304]{1,0:T(8,128)(2,1)} %add_convert_fusion.q_ref.k_ref.v_ref, bf16[1024,2304]{1,0:T(8,128)(2,1)} %add_convert_fusion.q_ref.k_ref.v_ref), custom_call_target="tpu_custom_call" | custom-call | tf_op jit(solution)/shard_map/attend/pallas_call | solution.py:77
  286.3 3.3 fusion.69
  292.0 2.6 pad_maximum_fusion.1
  297.1 5.5 fusion.67
  302.6 16.9 %convert_reduce_fusion = (f32[3072]{0:T(1024)S(1)}, bf16[1024,3072]{1,0:T(8,128)(2,1)}) fusion(f32[1024,3072]{1,0:T(8,128)S(1)} %fusion.67, f32[3072]{0:T(1024)S(1)} %copy-done.33, bf16[3072,768]{1,0:T(8,128)(2,1)} %bitcast.366, bf16[1,1024,768]{2,1,0:T(8,128)(2,1)S(1)} %copy-done.23), kind=kOutput, calls=%fused_computation.10 | convolution fusion | flops 4907332608 | bytes 25190400 | tf_op jit(solution)/shard_map/dot_general | solution.py:348
  319.5 8.5 %fusion.71 = (f32[768]{0:T(1024)S(1)}, f32[1024,768]{1,0:T(8,128)}) fusion(bf16[1024,3072]{1,0:T(8,128)(2,1)} %get-tuple-element.126, bf16[768,3072]{1,0:T(8,128)(2,1)S(1)} %bitcast.355), kind=kOutput, calls=%fused_computation.267 | convolution fusion | flops 4832623616 | bytes 14158848 | tf_op jit(solution)/shard_map/dot_general | solution.py:348
  328.0 3.9 copy.47
  332.0 3.0 multiply_reduce_fusion
  337.1 2.6 convolution_convert_fusion.3.do_ref
  339.7 21.8 %attend_back.1 = (bf16[1024,768]{1,0:T(8,128)(2,1)}, bf16[1024,768]{1,0:T(8,128)(2,1)}, bf16[1024,768]{1,0:T(8,128)(2,1)}) custom-call(bf16[1024,2304]{1,0:T(8,128)(2,1)} %add_convert_fusion.q_ref.k_ref.v_ref, bf16[1024,2304]{1,0:T(8,128)(2,1)} %add_convert_fusion.q_ref.k_ref.v_ref, bf16[1024,2304]{1,0:T(8,128)(2,1)} %add_convert_fusion.q_ref.k_ref.v_ref, ...), custom_call_target="tpu_custom_call" | custom-call | tf_op jit(solution)/shard_map/attend_back/pallas_call | solution.py:164
  365.7 5.6 fusion.70
  372.7 5.8 convolution_convert_fusion.2
  378.5 2.5 convolution_convert_fusion.4
  381.1 7.0 %convolution_convert_fusion.1 = bf16[768,3072]{1,0:T(8,128)(2,1)} fusion(bf16[1024,3072]{1,0:T(8,128)(2,1)S(1)} %bitcast.415, f32[1024,768]{0,1:T(8,128)S(1)} %get-tuple-element.120, f32[768]{0:T(1024)S(1)} %add.266, f32[768]{0:T(1024)S(1)} %mul.172, f32[1024]{0:T(1024)S(1)} %add_rsqrt_fusion, f32[1024]{0:T(1024)S(1)} %broadcast_multiply_fusion.4), kind=kOutput, calls=%fused_computation.15 | convolution fusion | flops 4838129664 | bytes 14170112 | tf_op jit(solution)/shard_map/dot_general | solution.py:348
  388.1 9.7 %convolution_convert_fusion = bf16[3072,768]{1,0:T(8,128)(2,1)} fusion(bf16[1,1024,768]{2,1,0:T(8,128)(2,1)S(1)} %copy-done.24, f32[1024,3072]{1,0:T(8,128)S(1)} %bitcast.357, f32[3072]{0:T(1024)S(1)} %copy-done.33), kind=kOutput, calls=%fused_computation.14 | convolution fusion | flops 4865654784 | bytes 18886656 | tf_op jit(solution)/shard_map/dot_general | solution.py:348
  397.8 10.0 %fusion.49 = bf16[1,1024,768]{1,2,0:T(8,128)(2,1)} fusion(f32[768]{0:T(1024)S(1)} %copy-done.35, f32[1024,768]{0,1:T(8,128)S(1)} %get-tuple-element.120, bf16[3072,768]{1,0:T(8,128)(2,1)} %bitcast.367, f32[1024,3072]{1,0:T(8,128)S(1)} %bitcast.357, f32[3072]{0:T(1024)S(1)} %copy-done.33), kind=kOutput, calls=%fused_computation.97 | convolution fusion | flops 4865654784 | bytes 22035456 | tf_op jit(solution)/shard_map/dot_general | solution.py:348
  407.8 3.7 copy.48
  411.4 3.0 fusion.23
  420.3 4.0 fusion.38
  425.0 2.9 collective-permute-done.46
  435.0 2.7 collective-permute-start.48
  439.7 5.5 collective-permute-done.48
  445.3 2.0 dynamic-slice_bitcast_fusion
  447.4 3.0 collective-permute-done.49
  450.5 2.0 collective-permute-start.50
  452.5 3.2 collective-permute-done.50
  465.3 19.4 %collective-permute-done.39 = bf16[192,2304]{1,0:T(8,128)(2,1)S(1)} collective-permute-done((bf16[192,2304]{1,0:T(8,128)(2,1)S(1)}, bf16[192,2304]{1,0:T(8,128)(2,1)S(1)}, u32[]{:S(2)}, u32[]{:S(2)}) %collective-permute-start.39) | collective-permute-done | bytes 884768 | tf_op jit(solution)/shard_map/ppermute | solution.py:255
  489.2 7.4 %collective-permute-done.40 = bf16[96,2304]{1,0:T(8,128)(2,1)S(1)} collective-permute-done((bf16[96,2304]{1,0:T(8,128)(2,1)S(1)}, bf16[96,2304]{1,0:T(8,128)(2,1)S(1)}, u32[]{:S(2)}, u32[]{:S(2)}) %collective-permute-start.40) | collective-permute-done | bytes 442400 | tf_op jit(solution)/shard_map/ppermute | solution.py:194
  496.8 13.2 %collective-permute-done.53 = bf16[192,3072]{1,0:T(8,128)(2,1)S(1)} collective-permute-done((bf16[192,3072]{1,0:T(8,128)(2,1)S(1)}, bf16[192,3072]{1,0:T(8,128)(2,1)S(1)}, u32[]{:S(2)}, u32[]{:S(2)}) %collective-permute-start.53) | collective-permute-done | bytes 1179680 | tf_op jit(solution)/shard_map/ppermute | solution.py:255
  512.4 5.3 collective-permute-done.41
  517.9 17.1 %collective-permute-done.60 = bf16[768,768]{1,0:T(8,128)(2,1)S(1)} collective-permute-done((bf16[768,768]{1,0:T(8,128)(2,1)S(1)}, bf16[768,768]{1,0:T(8,128)(2,1)S(1)}, u32[]{:S(2)}, u32[]{:S(2)}) %collective-permute-start.60) | collective-permute-done | bytes 1179680 | tf_op jit(solution)/shard_map/ppermute | solution.py:255
  538.0 13.7 %collective-permute-done.61 = bf16[384,768]{1,0:T(8,128)(2,1)S(1)} collective-permute-done((bf16[384,768]{1,0:T(8,128)(2,1)S(1)}, bf16[384,768]{1,0:T(8,128)(2,1)S(1)}, u32[]{:S(2)}, u32[]{:S(2)}) %collective-permute-start.61) | collective-permute-done | bytes 589856 | tf_op jit(solution)/shard_map/ppermute | solution.py:194
  552.0 26.1 %collective-permute-done.55 = bf16[96,3072]{1,0:T(8,128)(2,1)S(1)} collective-permute-done((bf16[96,3072]{1,0:T(8,128)(2,1)S(1)}, bf16[96,3072]{1,0:T(8,128)(2,1)S(1)}, u32[]{:S(2)}, u32[]{:S(2)}) %collective-permute-start.55) | collective-permute-done | bytes 589856 | tf_op jit(solution)/shard_map/ppermute | solution.py:194
  578.4 12.3 %collective-permute-done.62 = bf16[384,768]{1,0:T(8,128)(2,1)S(1)} collective-permute-done((bf16[384,768]{1,0:T(8,128)(2,1)S(1)}, bf16[384,768]{1,0:T(8,128)(2,1)S(1)}, u32[]{:S(2)}, u32[]{:S(2)}) %collective-permute-start.62) | collective-permute-done | bytes 589856 | tf_op jit(solution)/shard_map/ppermute | solution.py:194
  591.0 12.4 %collective-permute-done.56 = bf16[96,3072]{1,0:T(8,128)(2,1)S(1)} collective-permute-done((bf16[96,3072]{1,0:T(8,128)(2,1)S(1)}, bf16[96,3072]{1,0:T(8,128)(2,1)S(1)}, u32[]{:S(2)}, u32[]{:S(2)}) %collective-permute-start.56) | collective-permute-done | bytes 589856 | tf_op jit(solution)/shard_map/ppermute | solution.py:194
  604.1 11.8 %collective-permute-done.63 = bf16[384,768]{1,0:T(8,128)(2,1)S(1)} collective-permute-done((bf16[384,768]{1,0:T(8,128)(2,1)S(1)}, bf16[384,768]{1,0:T(8,128)(2,1)S(1)}, u32[]{:S(2)}, u32[]{:S(2)}) %collective-permute-start.63) | collective-permute-done | bytes 589856 | tf_op jit(solution)/shard_map/ppermute | solution.py:194
  616.5 2.2 collective-permute-done.57
  619.1 2.1 convert_select_fusion.2
  621.2 10.1 %collective-permute-done.64 = bf16[384,768]{1,0:T(8,128)(2,1)S(1)} collective-permute-done((bf16[384,768]{1,0:T(8,128)(2,1)S(1)}, bf16[384,768]{1,0:T(8,128)(2,1)S(1)}, u32[]{:S(2)}, u32[]{:S(2)}) %collective-permute-start.64) | collective-permute-done | bytes 589856 | tf_op jit(solution)/shard_map/ppermute | solution.py:194
  631.8 2.8 convert_select_fusion.1
  634.7 2.6 convert_select_fusion
  (373 shorter events, 112.2 us)
Async XLA Ops:
  8.2 10.3 %collective-permute-start = (bf16[36,128]{1,0:T(8,128)(2,1)S(1)}, bf16[36,128]{1,0:T(8,128)(2,1)S(1)}, u32[]{:S(2)}, u32[]{:S(2)}) collective-permute-start(bf16[36,128]{1,0:T(8,128)(2,1)S(1)} %bitcast.404), channel_id=1, source_target_pairs={{0,2},{2,0},{4,6},{6,4},{8,10},{10,8},{12,14},{14,12},{16,18},{18,... | collective-permute-start | bytes 27656 | tf_op jit(solution)/shard_map/ppermute | solution.py:194
  10.9 52.2 %collective-permute-start.5 = (bf16[192,2304]{1,0:T(8,128)(2,1)}, bf16[192,2304]{1,0:T(8,128)(2,1)}, u32[]{:S(2)}, u32[]{:S(2)}) collective-permute-start(bf16[192,2304]{1,0:T(8,128)(2,1)} %dynamic-slice_bitcast_fusion.8), channel_id=1, source_target_pairs={{0,2},{2,0},{4,6},{6,4},{8,10},{10,8},{12,14},{14,12},{16,18},{18,... | collective-permute-start | bytes 2654216 | tf_op jit(solution)/shard_map/ppermute | solution.py:194
  12.7 21.5 %collective-permute-start.12 = (bf16[192,768]{1,0:T(8,128)(2,1)}, bf16[192,768]{1,0:T(8,128)(2,1)}, u32[]{:S(2)}, u32[]{:S(2)}) collective-permute-start(bf16[192,768]{1,0:T(8,128)(2,1)} %dynamic-slice_bitcast_fusion.17), channel_id=1, source_target_pairs={{0,2},{2,0},{4,6},{6,4},{8,10},{10,8},{12,14},{14,12},{16,18},{18,... | collective-permute-start | bytes 884744 | tf_op jit(solution)/shard_map/ppermute | solution.py:194
  14.2 55.3 %collective-permute-start.26 = (bf16[768,768]{1,0:T(8,128)(2,1)}, bf16[768,768]{1,0:T(8,128)(2,1)}, u32[]{:S(2)}, u32[]{:S(2)}) collective-permute-start(bf16[768,768]{1,0:T(8,128)(2,1)} %dynamic-slice_bitcast_fusion.5), channel_id=1, source_target_pairs={{0,2},{2,0},{4,6},{6,4},{8,10},{10,8},{12,14},{14,12},{16,18},{18,... | collective-permute-start | bytes 3538952 | tf_op jit(solution)/shard_map/ppermute | solution.py:194
  15.4 60.0 %collective-permute-start.19 = (bf16[192,3072]{1,0:T(8,128)(2,1)}, bf16[192,3072]{1,0:T(8,128)(2,1)}, u32[]{:S(2)}, u32[]{:S(2)}) collective-permute-start(bf16[192,3072]{1,0:T(8,128)(2,1)} %dynamic-slice_bitcast_fusion.6), channel_id=1, source_target_pairs={{0,2},{2,0},{4,6},{6,4},{8,10},{10,8},{12,14},{14,12},{16,18},{18,... | collective-permute-start | bytes 3538952 | tf_op jit(solution)/shard_map/ppermute | solution.py:194
  18.5 4.2 collective-permute-start.1
  22.7 4.7 collective-permute-start.2
  27.4 5.2 collective-permute-start.3
  32.7 4.3 collective-permute-start.4
  35.3 5.2 collective-permute-start.13
  40.6 7.7 %collective-permute-start.14 = (bf16[96,768]{1,0:T(8,128)(2,1)S(1)}, bf16[96,768]{1,0:T(8,128)(2,1)S(1)}, u32[]{:S(2)}, u32[]{:S(2)}) collective-permute-start(bf16[96,768]{1,0:T(8,128)(2,1)S(1)} %bitcast_select_fusion.7), channel_id=1, source_target_pairs={{0,16},{2,18},{4,20},{6,22},{8,24},{10,26},{12,28},{14,30},{16,0},... | collective-permute-start | bytes 442376 | tf_op jit(solution)/shard_map/ppermute | solution.py:194
  48.3 5.2 collective-permute-start.15
  53.5 8.0 %collective-permute-start.16 = (bf16[96,768]{1,0:T(8,128)(2,1)S(1)}, bf16[96,768]{1,0:T(8,128)(2,1)}, u32[]{:S(2)}, u32[]{:S(2)}) collective-permute-start(bf16[96,768]{1,0:T(8,128)(2,1)S(1)} %broadcast_select_fusion.7), channel_id=1, source_target_pairs={{0,4},{2,6},{4,0},{6,2},{8,12},{10,14},{12,8},{14,10},{16,20},{18,... | collective-permute-start | bytes 442376 | tf_op jit(solution)/shard_map/ppermute | solution.py:194
  62.5 6.8 %collective-permute-start.17 = (bf16[2,96,768]{2,1,0:T(8,128)(2,1)S(1)}, bf16[2,96,768]{2,1,0:T(8,128)(2,1)S(1)}, u32[]{:S(2)}, u32[]{:S(2)}) collective-permute-start(bf16[2,96,768]{2,1,0:T(8,128)(2,1)S(1)} %pad_maximum_fusion.14), channel_id=1, source_target_pairs={{0,1},{1,0},{2,3},{3,2},{4,5},{5,4},{6,7},{7,6},{8,9},{9,8},{10,11... | collective-permute-start | bytes 884744 | tf_op jit(solution)/shard_map/ppermute | solution.py:232
  64.5 8.4 %collective-permute-start.6 = (bf16[96,2304]{1,0:T(8,128)(2,1)S(1)}, bf16[96,2304]{1,0:T(8,128)(2,1)S(1)}, u32[]{:S(2)}, u32[]{:S(2)}) collective-permute-start(bf16[96,2304]{1,0:T(8,128)(2,1)S(1)} %dynamic-slice_bitcast_fusion.15), channel_id=1, source_target_pairs={{0,4},{2,6},{4,0},{6,2},{8,12},{10,14},{12,8},{14,10},{16,20},{18,... | collective-permute-start | bytes 1327112 | tf_op jit(solution)/shard_map/ppermute | solution.py:194
  69.4 31.3 %collective-permute-start.18 = (bf16[2,2,96,768]{3,2,1,0:T(8,128)(2,1)S(1)}, bf16[2,2,96,768]{3,2,1,0:T(8,128)(2,1)S(1)}, u32[]{:S(2)}, u32[]{:S(2)}) collective-permute-start(bf16[2,2,96,768]{3,2,1,0:T(8,128)(2,1)S(1)} %pad_maximum_fusion.13), channel_id=1, source_target_pairs={{0,2},{2,0},{4,6},{6,4},{8,10},{10,8},{12,14},{14,12},{16,18},{18,... | collective-permute-start | bytes 1769480 | tf_op jit(solution)/shard_map/ppermute | solution.py:194
  71.1 21.5 %collective-permute-start.27 = (bf16[384,768]{1,0:T(8,128)(2,1)S(1)}, bf16[384,768]{1,0:T(8,128)(2,1)S(1)}, u32[]{:S(2)}, u32[]{:S(2)}) collective-permute-start(bf16[384,768]{1,0:T(8,128)(2,1)S(1)} %dynamic-slice_bitcast_fusion.12), channel_id=1, source_target_pairs={{0,4},{2,6},{4,0},{6,2},{8,12},{10,14},{12,8},{14,10},{16,20},{18,... | collective-permute-start | bytes 1769480 | tf_op jit(solution)/shard_map/ppermute | solution.py:194
  72.9 19.6 %collective-permute-start.7 = (bf16[96,2304]{1,0:T(8,128)(2,1)S(1)}, bf16[96,2304]{1,0:T(8,128)(2,1)S(1)}, u32[]{:S(2)}, u32[]{:S(2)}) collective-permute-start(bf16[96,2304]{1,0:T(8,128)(2,1)S(1)} %bitcast_select_fusion.5), channel_id=1, source_target_pairs={{0,16},{2,18},{4,20},{6,22},{8,24},{10,26},{12,28},{14,30},{16,0},... | collective-permute-start | bytes 1327112 | tf_op jit(solution)/shard_map/ppermute | solution.py:194
  76.9 21.3 %collective-permute-start.20 = (bf16[96,3072]{1,0:T(8,128)(2,1)S(1)}, bf16[96,3072]{1,0:T(8,128)(2,1)S(1)}, u32[]{:S(2)}, u32[]{:S(2)}) collective-permute-start(bf16[96,3072]{1,0:T(8,128)(2,1)S(1)} %dynamic-slice_bitcast_fusion.13), channel_id=1, source_target_pairs={{0,4},{2,6},{4,0},{6,2},{8,12},{10,14},{12,8},{14,10},{16,20},{18,... | collective-permute-start | bytes 1769480 | tf_op jit(solution)/shard_map/ppermute | solution.py:194
  92.6 19.7 %collective-permute-start.8 = (bf16[96,2304]{1,0:T(8,128)(2,1)S(1)}, bf16[96,2304]{1,0:T(8,128)(2,1)S(1)}, u32[]{:S(2)}, u32[]{:S(2)}) collective-permute-start(bf16[96,2304]{1,0:T(8,128)(2,1)S(1)} %broadcast_select_fusion.4), channel_id=1, source_target_pairs={{0,8},{2,10},{4,12},{6,14},{8,0},{10,2},{12,4},{14,6},{16,24},{18,... | collective-permute-start | bytes 1327112 | tf_op jit(solution)/shard_map/ppermute | solution.py:194
  92.7 42.5 %collective-permute-start.28 = (bf16[384,768]{1,0:T(8,128)(2,1)S(1)}, bf16[384,768]{1,0:T(8,128)(2,1)S(1)}, u32[]{:S(2)}, u32[]{:S(2)}) collective-permute-start(bf16[384,768]{1,0:T(8,128)(2,1)S(1)} %bitcast_select_fusion.3), channel_id=1, source_target_pairs={{0,16},{2,18},{4,20},{6,22},{8,24},{10,26},{12,28},{14,30},{16,0},... | collective-permute-start | bytes 1769480 | tf_op jit(solution)/shard_map/ppermute | solution.py:194
  98.2 48.8 %collective-permute-start.21 = (bf16[96,3072]{1,0:T(8,128)(2,1)S(1)}, bf16[96,3072]{1,0:T(8,128)(2,1)S(1)}, u32[]{:S(2)}, u32[]{:S(2)}) collective-permute-start(bf16[96,3072]{1,0:T(8,128)(2,1)S(1)} %bitcast_select_fusion.4), channel_id=1, source_target_pairs={{0,16},{2,18},{4,20},{6,22},{8,24},{10,26},{12,28},{14,30},{16,0},... | collective-permute-start | bytes 1769480 | tf_op jit(solution)/shard_map/ppermute | solution.py:194
  112.3 34.8 %collective-permute-start.9 = (bf16[96,2304]{1,0:T(8,128)(2,1)S(1)}, bf16[96,2304]{1,0:T(8,128)(2,1)S(1)}, u32[]{:S(2)}, u32[]{:S(2)}) collective-permute-start(bf16[96,2304]{1,0:T(8,128)(2,1)S(1)} %broadcast_select_fusion.5), channel_id=1, source_target_pairs={{0,4},{2,6},{4,0},{6,2},{8,12},{10,14},{12,8},{14,10},{16,20},{18,... | collective-permute-start | bytes 1327112 | tf_op jit(solution)/shard_map/ppermute | solution.py:194
  135.3 24.4 %collective-permute-start.29 = (bf16[384,768]{1,0:T(8,128)(2,1)S(1)}, bf16[384,768]{1,0:T(8,128)(2,1)S(1)}, u32[]{:S(2)}, u32[]{:S(2)}) collective-permute-start(bf16[384,768]{1,0:T(8,128)(2,1)S(1)} %broadcast_select_fusion), channel_id=1, source_target_pairs={{0,8},{2,10},{4,12},{6,14},{8,0},{10,2},{12,4},{14,6},{16,24},{18,... | collective-permute-start | bytes 1769480 | tf_op jit(solution)/shard_map/ppermute | solution.py:194
  147.1 25.1 %collective-permute-start.22 = (bf16[96,3072]{1,0:T(8,128)(2,1)S(1)}, bf16[96,3072]{1,0:T(8,128)(2,1)S(1)}, u32[]{:S(2)}, u32[]{:S(2)}) collective-permute-start(bf16[96,3072]{1,0:T(8,128)(2,1)S(1)} %broadcast_select_fusion.2), channel_id=1, source_target_pairs={{0,8},{2,10},{4,12},{6,14},{8,0},{10,2},{12,4},{14,6},{16,24},{18,... | collective-permute-start | bytes 1769480 | tf_op jit(solution)/shard_map/ppermute | solution.py:194
  159.7 15.2 %collective-permute-start.30 = (bf16[384,768]{1,0:T(8,128)(2,1)S(1)}, bf16[384,768]{1,0:T(8,128)(2,1)S(1)}, u32[]{:S(2)}, u32[]{:S(2)}) collective-permute-start(bf16[384,768]{1,0:T(8,128)(2,1)S(1)} %broadcast_select_fusion.1), channel_id=1, source_target_pairs={{0,4},{2,6},{4,0},{6,2},{8,12},{10,14},{12,8},{14,10},{16,20},{18,... | collective-permute-start | bytes 1769480 | tf_op jit(solution)/shard_map/ppermute | solution.py:194
  172.3 15.3 %collective-permute-start.23 = (bf16[96,3072]{1,0:T(8,128)(2,1)S(1)}, bf16[96,3072]{1,0:T(8,128)(2,1)S(1)}, u32[]{:S(2)}, u32[]{:S(2)}) collective-permute-start(bf16[96,3072]{1,0:T(8,128)(2,1)S(1)} %broadcast_select_fusion.3), channel_id=1, source_target_pairs={{0,4},{2,6},{4,0},{6,2},{8,12},{10,14},{12,8},{14,10},{16,20},{18,... | collective-permute-start | bytes 1769480 | tf_op jit(solution)/shard_map/ppermute | solution.py:194
  173.9 22.6 %collective-permute-start.10 = (bf16[2,96,2304]{2,1,0:T(8,128)(2,1)S(1)}, bf16[2,96,2304]{2,1,0:T(8,128)(2,1)S(1)}, u32[]{:S(2)}, u32[]{:S(2)}) collective-permute-start(bf16[2,96,2304]{2,1,0:T(8,128)(2,1)S(1)} %pad_maximum_fusion.11), channel_id=1, source_target_pairs={{0,1},{1,0},{2,3},{3,2},{4,5},{5,4},{6,7},{7,6},{8,9},{9,8},{10,11... | collective-permute-start | bytes 2654216 | tf_op jit(solution)/shard_map/ppermute | solution.py:232
  175.2 46.6 %collective-permute-start.31 = (bf16[2,384,768]{2,1,0:T(8,128)(2,1)S(1)}, bf16[2,384,768]{2,1,0:T(8,128)(2,1)S(1)}, u32[]{:S(2)}, u32[]{:S(2)}) collective-permute-start(bf16[2,384,768]{2,1,0:T(8,128)(2,1)S(1)} %pad_maximum_fusion.8), channel_id=1, source_target_pairs={{0,1},{1,0},{2,3},{3,2},{4,5},{5,4},{6,7},{7,6},{8,9},{9,8},{10,11... | collective-permute-start | bytes 3538952 | tf_op jit(solution)/shard_map/ppermute | solution.py:232
  187.9 58.0 %collective-permute-start.24 = (bf16[2,96,3072]{2,1,0:T(8,128)(2,1)S(1)}, bf16[2,96,3072]{2,1,0:T(8,128)(2,1)S(1)}, u32[]{:S(2)}, u32[]{:S(2)}) collective-permute-start(bf16[2,96,3072]{2,1,0:T(8,128)(2,1)S(1)} %pad_maximum_fusion.7), channel_id=1, source_target_pairs={{0,1},{1,0},{2,3},{3,2},{4,5},{5,4},{6,7},{7,6},{8,9},{9,8},{10,11... | collective-permute-start | bytes 3538952 | tf_op jit(solution)/shard_map/ppermute | solution.py:232
  196.9 51.3 %collective-permute-start.11 = (bf16[2,2,96,2304]{3,2,1,0:T(8,128)(2,1)S(1)}, bf16[2,2,96,2304]{3,2,1,0:T(8,128)(2,1)S(1)}, u32[]{:S(2)}, u32[]{:S(2)}) collective-permute-start(bf16[2,2,96,2304]{3,2,1,0:T(8,128)(2,1)S(1)} %pad_maximum_fusion.5), channel_id=1, source_target_pairs={{0,2},{2,0},{4,6},{6,4},{8,10},{10,8},{12,14},{14,12},{16,18},{18,... | collective-permute-start | bytes 5308424 | tf_op jit(solution)/shard_map/ppermute | solution.py:194
  223.6 66.4 %collective-permute-start.32 = (bf16[2,2,384,768]{3,2,1,0:T(8,128)(2,1)}, bf16[2,2,384,768]{3,2,1,0:T(8,128)(2,1)}, u32[]{:S(2)}, u32[]{:S(2)}) collective-permute-start(bf16[2,2,384,768]{3,2,1,0:T(8,128)(2,1)} %pad_maximum_fusion.4), channel_id=1, source_target_pairs={{0,2},{2,0},{4,6},{6,4},{8,10},{10,8},{12,14},{14,12},{16,18},{18,... | collective-permute-start | bytes 7077896 | tf_op jit(solution)/shard_map/ppermute | solution.py:194
  248.2 46.4 %collective-permute-start.25 = (bf16[2,2,96,3072]{3,2,1,0:T(8,128)(2,1)}, bf16[2,2,96,3072]{3,2,1,0:T(8,128)(2,1)}, u32[]{:S(2)}, u32[]{:S(2)}) collective-permute-start(bf16[2,2,96,3072]{3,2,1,0:T(8,128)(2,1)} %pad_maximum_fusion.3), channel_id=1, source_target_pairs={{0,2},{2,0},{4,6},{6,4},{8,10},{10,8},{12,14},{14,12},{16,18},{18,... | collective-permute-start | bytes 7077896 | tf_op jit(solution)/shard_map/ppermute | solution.py:194
  416.9 7.4 %collective-permute-start.34 = (f32[36,128]{1,0:T(8,128)S(1)}, f32[36,128]{1,0:T(8,128)S(1)}, u32[]{:S(2)}, u32[]{:S(2)}) collective-permute-start(f32[36,128]{1,0:T(8,128)S(1)} %dynamic-slice_bitcast_fusion.20), channel_id=1, source_target_pairs={{0,1},{1,0},{2,3},{3,2},{4,5},{5,4},{6,7},{7,6},{8,9},{9,8},{10,11... | collective-permute-start | bytes 55304 | tf_op jit(solution)/shard_map/ppermute | solution.py:308
  418.8 9.1 %collective-permute-start.46 = (bf16[192,768]{1,0:T(8,128)(2,1)S(1)}, bf16[192,768]{1,0:T(8,128)(2,1)S(1)}, u32[]{:S(2)}, u32[]{:S(2)}) collective-permute-start(bf16[192,768]{1,0:T(8,128)(2,1)S(1)} %dynamic-slice_bitcast_fusion.16), channel_id=1, source_target_pairs={{0,1},{1,0},{2,3},{3,2},{4,5},{5,4},{6,7},{7,6},{8,9},{9,8},{10,11... | collective-permute-start | bytes 884744 | tf_op jit(solution)/shard_map/ppermute | solution.py:255
  424.4 9.3 %collective-permute-start.35 = (f32[36,128]{1,0:T(8,128)S(1)}, f32[36,128]{1,0:T(8,128)S(1)}, u32[]{:S(2)}, u32[]{:S(2)}) collective-permute-start(f32[36,128]{1,0:T(8,128)S(1)} %bitcast_add_fusion), channel_id=1, source_target_pairs={{0,4},{2,6},{4,0},{6,2},{8,12},{10,14},{12,8},{14,10},{16,20},{18,... | collective-permute-start | bytes 55304 | tf_op jit(solution)/shard_map/ppermute | solution.py:194
  428.6 5.5 collective-permute-start.47
  433.6 28.0 %collective-permute-start.38 = (bf16[2,192,2304]{2,1,0:T(8,128)(2,1)}, bf16[2,192,2304]{2,1,0:T(8,128)(2,1)S(1)}, u32[]{:S(2)}, u32[]{:S(2)}) collective-permute-start(bf16[2,192,2304]{2,1,0:T(8,128)(2,1)} %dynamic-slice_bitcast_fusion.2), channel_id=1, source_target_pairs={{0,2},{2,0},{4,6},{6,4},{8,10},{10,8},{12,14},{14,12},{16,18},{18,... | collective-permute-start | bytes 5308424 | tf_op jit(solution)/shard_map/ppermute | solution.py:194
  433.7 5.9 collective-permute-start.36
  435.0 10.2 %collective-permute-start.48 = (bf16[96,768]{1,0:T(8,128)(2,1)S(1)}, bf16[96,768]{1,0:T(8,128)(2,1)S(1)}, u32[]{:S(2)}, u32[]{:S(2)}) collective-permute-start(bf16[96,768]{1,0:T(8,128)(2,1)S(1)} %fusion.55), channel_id=1, source_target_pairs={{0,16},{2,18},{4,20},{6,22},{8,24},{10,26},{12,28},{14,30},{16,0},... | collective-permute-start | bytes 442376 | tf_op jit(solution)/shard_map/ppermute | solution.py:194
  439.5 24.6 %collective-permute-start.52 = (bf16[2,192,3072]{2,1,0:T(8,128)(2,1)S(1)}, bf16[2,192,3072]{2,1,0:T(8,128)(2,1)S(1)}, u32[]{:S(2)}, u32[]{:S(2)}) collective-permute-start(bf16[2,192,3072]{2,1,0:T(8,128)(2,1)S(1)} %dynamic-slice_bitcast_fusion.1), channel_id=1, source_target_pairs={{0,2},{2,0},{4,6},{6,4},{8,10},{10,8},{12,14},{14,12},{16,18},{18,... | collective-permute-start | bytes 7077896 | tf_op jit(solution)/shard_map/ppermute | solution.py:194
  439.6 7.8 %collective-permute-start.37 = (f32[36,128]{1,0:T(8,128)S(1)}, f32[36,128]{1,0:T(8,128)S(1)}, u32[]{:S(2)}, u32[]{:S(2)}) collective-permute-start(f32[36,128]{1,0:T(8,128)S(1)} %add.287), channel_id=1, source_target_pairs={{0,8},{2,10},{4,12},{6,14},{8,0},{10,2},{12,4},{14,6},{16,24},{18,... | collective-permute-start | bytes 55304 | tf_op jit(solution)/shard_map/ppermute | solution.py:194
  445.2 5.2 collective-permute-start.49
  447.3 39.6 %collective-permute-start.59 = (bf16[2,768,768]{2,1,0:T(8,128)(2,1)S(1)}, bf16[2,768,768]{2,1,0:T(8,128)(2,1)S(1)}, u32[]{:S(2)}, u32[]{:S(2)}) collective-permute-start(bf16[2,768,768]{2,1,0:T(8,128)(2,1)S(1)} %dynamic-slice_bitcast_fusion), channel_id=1, source_target_pairs={{0,2},{2,0},{4,6},{6,4},{8,10},{10,8},{12,14},{14,12},{16,18},{18,... | collective-permute-start | bytes 7077896 | tf_op jit(solution)/shard_map/ppermute | solution.py:194
  450.5 5.2 collective-permute-start.50
  455.8 4.7 collective-permute-start.51
  462.1 22.6 %collective-permute-start.39 = (bf16[192,2304]{1,0:T(8,128)(2,1)S(1)}, bf16[192,2304]{1,0:T(8,128)(2,1)S(1)}, u32[]{:S(2)}, u32[]{:S(2)}) collective-permute-start(bf16[192,2304]{1,0:T(8,128)(2,1)S(1)} %dynamic-slice_bitcast_fusion.7), channel_id=1, source_target_pairs={{0,1},{1,0},{2,3},{3,2},{4,5},{5,4},{6,7},{7,6},{8,9},{9,8},{10,11... | collective-permute-start | bytes 2654216 | tf_op jit(solution)/shard_map/ppermute | solution.py:255
  465.1 44.9 %collective-permute-start.53 = (bf16[192,3072]{1,0:T(8,128)(2,1)S(1)}, bf16[192,3072]{1,0:T(8,128)(2,1)S(1)}, u32[]{:S(2)}, u32[]{:S(2)}) collective-permute-start(bf16[192,3072]{1,0:T(8,128)(2,1)S(1)} %dynamic-slice_bitcast_fusion.4), channel_id=1, source_target_pairs={{0,1},{1,0},{2,3},{3,2},{4,5},{5,4},{6,7},{7,6},{8,9},{9,8},{10,11... | collective-permute-start | bytes 3538952 | tf_op jit(solution)/shard_map/ppermute | solution.py:255
  485.0 11.6 %collective-permute-start.40 = (bf16[96,2304]{1,0:T(8,128)(2,1)S(1)}, bf16[96,2304]{1,0:T(8,128)(2,1)S(1)}, u32[]{:S(2)}, u32[]{:S(2)}) collective-permute-start(bf16[96,2304]{1,0:T(8,128)(2,1)S(1)} %dynamic-slice_bitcast_fusion.14), channel_id=1, source_target_pairs={{0,4},{2,6},{4,0},{6,2},{8,12},{10,14},{12,8},{14,10},{16,20},{18,... | collective-permute-start | bytes 1327112 | tf_op jit(solution)/shard_map/ppermute | solution.py:194
  487.6 47.3 %collective-permute-start.60 = (bf16[768,768]{1,0:T(8,128)(2,1)S(1)}, bf16[768,768]{1,0:T(8,128)(2,1)S(1)}, u32[]{:S(2)}, u32[]{:S(2)}) collective-permute-start(bf16[768,768]{1,0:T(8,128)(2,1)S(1)} %dynamic-slice_bitcast_fusion.3), channel_id=1, source_target_pairs={{0,1},{1,0},{2,3},{3,2},{4,5},{5,4},{6,7},{7,6},{8,9},{9,8},{10,11... | collective-permute-start | bytes 3538952 | tf_op jit(solution)/shard_map/ppermute | solution.py:255
  496.7 21.0 %collective-permute-start.41 = (bf16[96,2304]{1,0:T(8,128)(2,1)S(1)}, bf16[96,2304]{1,0:T(8,128)(2,1)S(1)}, u32[]{:S(2)}, u32[]{:S(2)}) collective-permute-start(bf16[96,2304]{1,0:T(8,128)(2,1)S(1)} %fusion.53), channel_id=1, source_target_pairs={{0,16},{2,18},{4,20},{6,22},{8,24},{10,26},{12,28},{14,30},{16,0},... | collective-permute-start | bytes 1327112 | tf_op jit(solution)/shard_map/ppermute | solution.py:194
  510.5 26.7 %collective-permute-start.54 = (bf16[96,3072]{1,0:T(8,128)(2,1)S(1)}, bf16[96,3072]{1,0:T(8,128)(2,1)S(1)}, u32[]{:S(2)}, u32[]{:S(2)}) collective-permute-start(bf16[96,3072]{1,0:T(8,128)(2,1)S(1)} %dynamic-slice_bitcast_fusion.10), channel_id=1, source_target_pairs={{0,4},{2,6},{4,0},{6,2},{8,12},{10,14},{12,8},{14,10},{16,20},{18,... | collective-permute-start | bytes 1769480 | tf_op jit(solution)/shard_map/ppermute | solution.py:194
  517.8 19.7 %collective-permute-start.42 = (bf16[96,2304]{1,0:T(8,128)(2,1)S(1)}, bf16[96,2304]{1,0:T(8,128)(2,1)S(1)}, u32[]{:S(2)}, u32[]{:S(2)}) collective-permute-start(bf16[96,2304]{1,0:T(8,128)(2,1)S(1)} %add_convert_fusion.8), channel_id=1, source_target_pairs={{0,8},{2,10},{4,12},{6,14},{8,0},{10,2},{12,4},{14,6},{16,24},{18,... | collective-permute-start | bytes 1327112 | tf_op jit(solution)/shard_map/ppermute | solution.py:194
  535.3 16.3 %collective-permute-start.61 = (bf16[384,768]{1,0:T(8,128)(2,1)S(1)}, bf16[384,768]{1,0:T(8,128)(2,1)S(1)}, u32[]{:S(2)}, u32[]{:S(2)}) collective-permute-start(bf16[384,768]{1,0:T(8,128)(2,1)S(1)} %dynamic-slice_bitcast_fusion.9), channel_id=1, source_target_pairs={{0,4},{2,6},{4,0},{6,2},{8,12},{10,14},{12,8},{14,10},{16,20},{18,... | collective-permute-start | bytes 1769480 | tf_op jit(solution)/shard_map/ppermute | solution.py:194
  537.4 40.7 %collective-permute-start.55 = (bf16[96,3072]{1,0:T(8,128)(2,1)S(1)}, bf16[96,3072]{1,0:T(8,128)(2,1)S(1)}, u32[]{:S(2)}, u32[]{:S(2)}) collective-permute-start(bf16[96,3072]{1,0:T(8,128)(2,1)S(1)} %fusion.51), channel_id=1, source_target_pairs={{0,16},{2,18},{4,20},{6,22},{8,24},{10,26},{12,28},{14,30},{16,0},... | collective-permute-start | bytes 1769480 | tf_op jit(solution)/shard_map/ppermute | solution.py:194
  537.6 40.7 %collective-permute-start.43 = (bf16[96,2304]{1,0:T(8,128)(2,1)S(1)}, bf16[96,2304]{1,0:T(8,128)(2,1)S(1)}, u32[]{:S(2)}, u32[]{:S(2)}) collective-permute-start(bf16[96,2304]{1,0:T(8,128)(2,1)S(1)} %add_convert_fusion.7), channel_id=1, source_target_pairs={{0,4},{2,6},{4,0},{6,2},{8,12},{10,14},{12,8},{14,10},{16,20},{18,... | collective-permute-start | bytes 1327112 | tf_op jit(solution)/shard_map/ppermute | solution.py:194
  551.8 38.9 %collective-permute-start.62 = (bf16[384,768]{1,0:T(8,128)(2,1)S(1)}, bf16[384,768]{1,0:T(8,128)(2,1)S(1)}, u32[]{:S(2)}, u32[]{:S(2)}) collective-permute-start(bf16[384,768]{1,0:T(8,128)(2,1)S(1)} %fusion.50), channel_id=1, source_target_pairs={{0,16},{2,18},{4,20},{6,22},{8,24},{10,26},{12,28},{14,30},{16,0},... | collective-permute-start | bytes 1769480 | tf_op jit(solution)/shard_map/ppermute | solution.py:194
  578.2 25.1 %collective-permute-start.56 = (bf16[96,3072]{1,0:T(8,128)(2,1)S(1)}, bf16[96,3072]{1,0:T(8,128)(2,1)S(1)}, u32[]{:S(2)}, u32[]{:S(2)}) collective-permute-start(bf16[96,3072]{1,0:T(8,128)(2,1)S(1)} %add_convert_fusion.6), channel_id=1, source_target_pairs={{0,8},{2,10},{4,12},{6,14},{8,0},{10,2},{12,4},{14,6},{16,24},{18,... | collective-permute-start | bytes 1769480 | tf_op jit(solution)/shard_map/ppermute | solution.py:194
  590.9 25.0 %collective-permute-start.63 = (bf16[384,768]{1,0:T(8,128)(2,1)S(1)}, bf16[384,768]{1,0:T(8,128)(2,1)S(1)}, u32[]{:S(2)}, u32[]{:S(2)}) collective-permute-start(bf16[384,768]{1,0:T(8,128)(2,1)S(1)} %add_convert_fusion.4), channel_id=1, source_target_pairs={{0,8},{2,10},{4,12},{6,14},{8,0},{10,2},{12,4},{14,6},{16,24},{18,... | collective-permute-start | bytes 1769480 | tf_op jit(solution)/shard_map/ppermute | solution.py:194
  603.5 15.2 %collective-permute-start.57 = (bf16[96,3072]{1,0:T(8,128)(2,1)S(1)}, bf16[96,3072]{1,0:T(8,128)(2,1)S(1)}, u32[]{:S(2)}, u32[]{:S(2)}) collective-permute-start(bf16[96,3072]{1,0:T(8,128)(2,1)S(1)} %add_convert_fusion.5), channel_id=1, source_target_pairs={{0,4},{2,6},{4,0},{6,2},{8,12},{10,14},{12,8},{14,10},{16,20},{18,... | collective-permute-start | bytes 1769480 | tf_op jit(solution)/shard_map/ppermute | solution.py:194
  604.0 15.0 %collective-permute-start.44 = (bf16[2,96,2304]{2,1,0:T(8,128)(2,1)S(1)}, bf16[2,96,2304]{2,1,0:T(8,128)(2,1)S(1)}, u32[]{:S(2)}, u32[]{:S(2)}) collective-permute-start(bf16[2,96,2304]{2,1,0:T(8,128)(2,1)S(1)} %pad_maximum_fusion.12), channel_id=1, source_target_pairs={{0,2},{2,0},{4,6},{6,4},{8,10},{10,8},{12,14},{14,12},{16,18},{18,... | collective-permute-start | bytes 2654216 | tf_op jit(solution)/shard_map/ppermute | solution.py:194
  616.1 15.3 %collective-permute-start.64 = (bf16[384,768]{1,0:T(8,128)(2,1)S(1)}, bf16[384,768]{1,0:T(8,128)(2,1)S(1)}, u32[]{:S(2)}, u32[]{:S(2)}) collective-permute-start(bf16[384,768]{1,0:T(8,128)(2,1)S(1)} %add_convert_fusion.3), channel_id=1, source_target_pairs={{0,4},{2,6},{4,0},{6,2},{8,12},{10,14},{12,8},{14,10},{16,20},{18,... | collective-permute-start | bytes 1769480 | tf_op jit(solution)/shard_map/ppermute | solution.py:194
  618.9 12.7 %collective-permute-start.58 = (bf16[2,96,3072]{2,1,0:T(8,128)(2,1)S(1)}, bf16[2,96,3072]{2,1,0:T(8,128)(2,1)S(1)}, u32[]{:S(2)}, u32[]{:S(2)}) collective-permute-start(bf16[2,96,3072]{2,1,0:T(8,128)(2,1)S(1)} %pad_maximum_fusion.9), channel_id=1, source_target_pairs={{0,2},{2,0},{4,6},{6,4},{8,10},{10,8},{12,14},{14,12},{16,18},{18,... | collective-permute-start | bytes 3538952 | tf_op jit(solution)/shard_map/ppermute | solution.py:194
  631.6 3.0 collective-permute-start.65
  (49 other events, 663.1 us)

commit v2 on v1

v2 whole, which is shorter than its diff:
```python
import functools
import math

import jax
import jax.numpy as jnp
from jax import lax
from jax.experimental import pallas as pl
from jax.experimental.pallas import tpu as pltpu
from jax.sharding import PartitionSpec as P

H = 12
HD = 64
QB = 256
REACH = 512

epsilon = 1e-05
AXES = ("wide", "narrow")
VMEM = 56 * 1024 * 1024
TINY = pl.CostEstimate(flops=1000, bytes_accessed=1000, transcendentals=0)
f32 = jnp.float32
bf16 = jnp.bfloat16


def spans(length):
    out = []
    for b in range(length // QB):
        low = max(0, (b * QB - (REACH - 1)) // QB * QB)
        out.append((low, (b + 1) * QB))
    return out


def soft_rows(length):
    return sum(hi - lo for lo, hi in spans(length))


def attend_pair(doc, q, k, v, o_ref, p_ref):
    length = q.shape[0]
    lane = lax.broadcasted_iota(jnp.int32, (length, 128), 1)
    low = lane < HD
    hot = (lane & (HD - 1)) == doc
    q_side = jnp.where(hot, 1.0, 0.0)
    k_side = jnp.where(hot, 0.0, -1e9)
    q = q.astype(f32) * HD ** (-0.5)
    k = k.astype(f32)
    v_t = v.T
    sides = []
    for h in range(2):
        mine = low if h == 0 else jnp.logical_not(low)
        sides.append(
            (jnp.where(mine, q, q_side).astype(bf16), jnp.where(mine, k, k_side).astype(bf16))
        )
    rows = lax.broadcasted_iota(jnp.int32, (QB, QB), 0)
    tri = rows <= lax.broadcasted_iota(jnp.int32, (QB, QB), 1)
    at = 0
    for b, (lo, hi) in enumerate(spans(length)):
        n = hi - lo
        outs = []
        for h in range(2):
            qa, ka = sides[h]
            s = dot(ka[lo:hi], qa[b * QB : (b + 1) * QB], ((1,), (1,)))
            last = jnp.where(tri, s[n - QB :], -1e9)
            s = last if n == QB else jnp.concatenate([s[: n - QB], last], axis=0)
            e = jnp.exp(s - jnp.max(s, axis=0, keepdims=True))
            p = (e * (1.0 / jnp.sum(e, axis=0, keepdims=True))).astype(bf16)
            p_ref[h, at : at + n, :] = p
            outs.append(dot(v_t[h * HD : (h + 1) * HD, lo:hi], p))
        o_ref[b * QB : (b + 1) * QB, :] = jnp.concatenate(outs, axis=0).T.astype(bf16)
        at += n


def attend(place, doc, x, vec, weights, column, first, count, before):
    length, width = x.shape
    start = before is None
    packed = vec is None
    rows = soft_rows(length)
    n_p, n_v = len(weights.arrays), 0 if packed else 1
    n_a = 0 if start else 3

    def kernel(*refs):
        refs = list(refs)
        take = lambda n: [refs.pop(0) for _ in range(n)]
        place_ref, doc_ref, x_ref = take(3)
        vec_refs, pieces = take(n_v), take(n_p)
        take(n_a)
        mixed_ref, soft_ref, qkv_ref = take(3)
        if start:
            h1_ref, h1_t_ref, vec_out = take(3)
        w, sem = take(2)
        step = pl.program_id(0)

        @pl.when(step == 0)
        def _():
            weights.load(place_ref, pieces, w, sem)
            if start:
                if packed:
                    vec_out[...] = unpack_rows(w)
                else:
                    vec_out[...] = vec_refs[0][...]
                for at in range(0, length, 256):
                    here = slice(at, at + 256)
                    h1 = norm_rows(
                        x_ref[here, :].astype(f32), row_of(vec_out, GAIN1), row_of(vec_out, SHIFT1)
                    ).astype(bf16)
                    h1_ref[here, :] = h1
                    h1_t_ref[:, here] = h1.T

        h1 = (h1_ref if start else x_ref)[...]
        known = vec_out if start else vec_refs[0]
        cols = w[:, pl.ds(pl.multiple_of(column + step * 384, 128), 384)]
        bias = jnp.concatenate(
            [
                known[pl.ds(QV[0] + first + step, 1), :],
                jnp.zeros((1, 128), f32),
                known[pl.ds(QV[0] + 6 + first + step, 1), :],
            ],
            axis=1,
        )
        qkv = (dot(h1, cols) + bias).astype(bf16)
        qkv_ref[...] = qkv
        attend_pair(
            doc_ref[...], qkv[:, :128], qkv[:, 128:256], qkv[:, 256:], mixed_ref, soft_ref
        )

    full = lambda shape: pl.BlockSpec(shape, lambda i: (0,) * len(shape))
    anyplace = pl.BlockSpec(memory_space=pl.ANY)
    outs = [
        ((length, width), (length, 128), lambda i: (0, first + i), bf16),
        ((H, rows, QB), (2, rows, QB), lambda i: (first + i, 0, 0), bf16),
        ((length, 3 * width), (length, 384), lambda i: (0, first + i), bf16),
    ]
    if start:
        outs += [
            ((length, width), (length, width), lambda i: (0, 0), bf16),
            ((width, length), (width, length), lambda i: (0, 0), bf16),
            ((72, 128), (72, 128), lambda i: (0, 0), f32),
        ]
    given = [place.spot, doc, x] + ([] if packed else [vec]) + weights.arrays
    aliases = {}
    if not start:
        aliases = {len(given) + i: i for i in range(3)}
        given += before
    return pl.pallas_call(
        kernel,
        grid=(count,),
        in_specs=[pl.BlockSpec(memory_space=pltpu.SMEM), full((length, 1)), full(x.shape)]
        + [full((72, 128))] * n_v
        + [anyplace] * (n_p + n_a),
        out_specs=[pl.BlockSpec(block, index) for _, block, index, _ in outs],
        out_shape=[jax.ShapeDtypeStruct(shape, kind) for shape, _, _, kind in outs],
        scratch_shapes=[
            pltpu.VMEM((weights.rows, weights.width), bf16),
            pltpu.SemaphoreType.DMA((n_p,)),
        ],
        input_output_aliases=aliases,
        compiler_params=pltpu.CompilerParams(vmem_limit_bytes=VMEM),
        cost_estimate=TINY,
        name="attend",
    )(*given)


def lay_blocks(ref, place_ref, other, rows):
    out = []
    core = 1 - place_ref[0] if other else place_ref[0]
    for x in range(2):
        for y in range(2):
            at = pl.multiple_of((4 * x + 2 * core + y) * rows, 16)
            out.append(ref[pl.ds(at, rows), :])
    return jnp.concatenate(out, axis=0)


def attend_back_kernel(
    place_ref,
    q_ref,
    k_ref,
    v_ref,
    o_ref,
    do_ref,
    p_ref,
    h1_t_ref,
    *refs,
    length,
):
    out_ref, send_ref, keep_ref, dk_acc, dv_acc = refs[-5:]
    lane = lax.broadcasted_iota(jnp.int32, (length, 128), 1)
    low = lane < HD
    spot = lane & (HD - 1)
    q = q_ref[...].astype(f32) * HD ** (-0.5)
    do = do_ref[...].astype(f32)
    v = v_ref[...].astype(f32)
    product = do * o_ref[...].astype(f32)
    k_t = k_ref[...].T
    sides = []
    for h in range(2):
        mine = low if h == 0 else jnp.logical_not(low)
        center = jnp.sum(jnp.where(mine, product, 0.0), axis=1, keepdims=True)
        first = center.astype(bf16).astype(f32)
        second = (center - first).astype(bf16).astype(f32)
        third = center - first - second
        extra = jnp.where(
            spot == 0, -first, jnp.where(spot == 1, -second, jnp.where(spot == 2, -third, 0.0))
        )
        sides.append(
            (
                jnp.where(mine, do, extra).astype(bf16),
                jnp.where(mine, v, jnp.where(spot < 3, 1.0, 0.0)).astype(bf16),
                jnp.where(mine, do, 0.0).astype(bf16),
                jnp.where(mine, q, 0.0).astype(bf16),
            )
        )
    dk_acc[...] = jnp.zeros_like(dk_acc)
    dv_acc[...] = jnp.zeros_like(dv_acc)
    at = 0
    for b, (lo, hi) in enumerate(spans(length)):
        n = hi - lo
        here = slice(b * QB, (b + 1) * QB)
        dqs = []
        dk = dv = None
        for h in range(2):
            do_more, v_more, do_own, q_own = sides[h]
            p = p_ref[h, at : at + n, :]
            dp = dot(v_more[lo:hi], do_more[here], ((1,), (1,)))
            ds = (p.astype(f32) * dp).astype(bf16)
            dv_part = dot(p, do_own[here])
            dk_part = dot(ds, q_own[here])
            dv = dv_part if dv is None else dv + dv_part
            dk = dk_part if dk is None else dk + dk_part
            dqs.append(dot(k_t[h * HD : (h + 1) * HD, lo:hi], ds))
        dv_acc[lo:hi, :] += dv
        dk_acc[lo:hi, :] += dk
        out_ref[here, :128] = (jnp.concatenate(dqs, axis=0) * HD ** (-0.5)).T.astype(bf16)
        at += n
    out_ref[:, 128:256] = dk_acc[...].astype(bf16)
    out_ref[:, 256:] = dv_acc[...].astype(bf16)
    parts = out_ref[...]
    for other, ref in ((True, send_ref), (False, keep_ref)):
        rows = h1_t_ref.shape[0] // 8
        ref[...] = dot(lay_blocks(h1_t_ref, place_ref, other, rows), parts).astype(bf16)


def attend_back(place, qkv, mixed, grad_mixed, soft, h1_t, first, count, before):
    length, width = mixed.shape
    rows = soft_rows(length)
    col = lambda off: pl.BlockSpec((length, 128), lambda i: (0, 3 * (first + i) + off))
    pair = pl.BlockSpec((length, 128), lambda i: (0, first + i))
    terms = pl.BlockSpec((width // 2, 384), lambda i: (0, i))
    term = jax.ShapeDtypeStruct((width // 2, 384 * count), bf16)
    given = [place.spot, qkv, qkv, qkv, mixed, grad_mixed, soft, h1_t]
    aliases = {}
    if before is not None:
        aliases = {len(given): 0}
        given.append(before)
    return pl.pallas_call(
        functools.partial(attend_back_kernel, length=length),
        grid=(count,),
        in_specs=[
            pl.BlockSpec(memory_space=pltpu.SMEM),
            col(0),
            col(1),
            col(2),
            pair,
            pair,
            pl.BlockSpec((2, rows, QB), lambda i: (first + i, 0, 0)),
            pl.BlockSpec(h1_t.shape, lambda i: (0, 0)),
        ]
        + [pl.BlockSpec(memory_space=pl.ANY)] * len(aliases),
        out_specs=[pl.BlockSpec((length, 384), lambda i: (0, first + i)), terms, terms],
        out_shape=[jax.ShapeDtypeStruct(qkv.shape, bf16), term, term],
        scratch_shapes=[pltpu.VMEM((length, 128), f32)] * 2,
        input_output_aliases=aliases,
        compiler_params=pltpu.CompilerParams(vmem_limit_bytes=VMEM),
        cost_estimate=TINY,
        name="attend_back",
    )(*given)


def proj_terms(place, g_t, dout):
    hidden, length = g_t.shape
    width = dout.shape[1]
    rows = hidden // 8

    def kernel(place_ref, g_ref, dout_ref, send_ref, keep_ref):
        value = dot(g_ref[...], dout_ref[...]).astype(bf16)

        @pl.when(pl.program_id(0) < 4)
        def _():
            send_ref[...] = value

        @pl.when(pl.program_id(0) >= 4)
        def _():
            keep_ref[...] = value

    def block(i, place_ref):
        core = jnp.where(i < 4, 1 - place_ref[0], place_ref[0])
        j = i % 4
        return 4 * (j // 2) + 2 * core + j % 2, 0

    out = jax.ShapeDtypeStruct((hidden // 2, width), bf16)
    return pl.pallas_call(
        kernel,
        grid_spec=pltpu.PrefetchScalarGridSpec(
            num_scalar_prefetch=1,
            grid=(8,),
            in_specs=[
                pl.BlockSpec((rows, length), block),
                pl.BlockSpec((length, width), lambda i, p: (0, 0)),
            ],
            out_specs=[
                pl.BlockSpec((rows, width), lambda i, p: (jnp.minimum(i, 3), 0)),
                pl.BlockSpec((rows, width), lambda i, p: (jnp.maximum(i - 4, 0), 0)),
            ],
        ),
        out_shape=[out, out],
        compiler_params=pltpu.CompilerParams(vmem_limit_bytes=VMEM),
        cost_estimate=TINY,
        name="proj_terms",
    )(place.spot, g_t, dout)


def back_middle(place, dout, slope, y1, mixed, h2_t, vec, w_out, w_fc, w_proj):
    length, width = dout.shape
    hidden = w_fc.width
    step_rows, part = 256, 512
    steps = length // step_rows
    f_steps, rows = hidden // width, width // 8
    weights = (w_out, w_fc, w_proj)
    counts = [len(w.arrays) for w in weights]

    def kernel(*refs):
        refs = list(refs)
        take = lambda n: [refs.pop(0) for _ in range(n)]
        place_ref, dout_ref, slope_ref, y1_ref, mixed_ref, h2_t, vec_ref = take(7)
        pieces = [take(n) for n in counts]
        dmixed_ref, dy1_ref, send_ref, keep_ref = take(4)
        gain_ref, shift_ref, outb_ref, fcb_ref, projb_ref = sums = take(5)
        wo, wf, wp = buffers = take(3)
        sems = take(3)
        du_all, mixed_t, db1_all = take(3)
        i = pl.program_id(0)

        @pl.when(i == 0)
        def _():
            for w, own, buffer, sem in zip(weights, pieces, buffers, sems):
                w.load(place_ref, own, buffer, sem)
            for ref in sums:
                ref[...] = jnp.zeros_like(ref)

        @pl.when(i < steps)
        def _():
            here = pl.ds(pl.multiple_of(i * step_rows, step_rows), step_rows)
            dout = dout_ref[...]
            mixed_t[:, here] = mixed_ref[...].T
            dh2 = jnp.zeros((step_rows, width), f32)
            for c in range(0, hidden, part):
                cols = slice(c, c + part)
                du = dot(dout, wp[cols, :], ((1,), (1,))) * slope_ref[:, cols].astype(f32)
                du = du.astype(bf16)
                du_all[here, cols] = du
                fcb_ref[:, cols] += jnp.sum(du.astype(f32), axis=0, keepdims=True)
                dh2 = dh2 + dot(du, wf[:, cols], ((1,), (1,)))
            back, gain, shift = norm_back(y1_ref[...], row_of(vec_ref, GAIN2), dh2)
            wide_dout = dout.astype(f32)
            dy1 = wide_dout + back
            db1 = dy1.astype(bf16)
            dy1_ref[...] = dy1
            db1_all[here, :] = db1
            dmixed_ref[...] = dot(db1, wo[...], ((1,), (1,))).astype(bf16)
            gain_ref[...] += gain
            shift_ref[...] += shift
            outb_ref[...] += jnp.sum(db1.astype(f32), axis=0, keepdims=True)
            projb_ref[...] += jnp.sum(wide_dout, axis=0, keepdims=True)

        j = i - steps

        @pl.when((j >= 0) & (j < f_steps))
        def _():
            cols = pl.ds(pl.multiple_of(j * width, 128), width)
            for other, ref in ((True, send_ref), (False, keep_ref)):
                value = dot(lay_blocks(h2_t, place_ref, other, rows), du_all[:, cols])
                ref[...] = value.astype(bf16).reshape(ref.shape)

        @pl.when(j == f_steps)
        def _():
            for other, ref in ((True, send_ref), (False, keep_ref)):
                value = dot(lay_blocks(mixed_t, place_ref, other, rows), db1_all[...])
                ref[...] = value.astype(bf16).reshape(ref.shape)

    full = lambda shape: pl.BlockSpec(shape, lambda i: (0,) * len(shape))
    slab = lambda n: pl.BlockSpec((step_rows, n), lambda i: (jnp.minimum(i, steps - 1), 0))
    terms = pl.BlockSpec(
        (4, rows, width), lambda i: (0, jnp.clip(i - steps, 0, f_steps), 0)
    )
    like = jax.ShapeDtypeStruct
    one = (1, width)
    sum_shapes = [one, one, one, (1, hidden), one]
    return pl.pallas_call(
        kernel,
        grid=(steps + f_steps + 1,),
        in_specs=[
            pl.BlockSpec(memory_space=pltpu.SMEM),
            slab(width),
            slab(hidden),
            slab(width),
            slab(width),
            full(h2_t.shape),
            full((72, 128)),
        ]
        + [pl.BlockSpec(memory_space=pl.ANY)] * sum(counts),
        out_specs=[slab(width), slab(width), terms, terms] + [full(v) for v in sum_shapes],
        out_shape=[
            like((length, width), bf16),
            like((length, width), f32),
            like((4, rows * (f_steps + 1), width), bf16),
            like((4, rows * (f_steps + 1), width), bf16),
        ]
        + [like(v, f32) for v in sum_shapes],
        scratch_shapes=[pltpu.VMEM((w.rows, w.width), bf16) for w in weights]
        + [pltpu.SemaphoreType.DMA((n,)) for n in counts]
        + [
            pltpu.VMEM((length, hidden), bf16),
            pltpu.VMEM((width, length), bf16),
            pltpu.VMEM((length, width), bf16),
        ],
        compiler_params=pltpu.CompilerParams(vmem_limit_bytes=VMEM),
        cost_estimate=TINY,
        name="back_middle",
    )(place.spot, dout, slope, y1, mixed, h2_t, vec, *[v for w in weights for v in w.arrays])


class Place:
    def __init__(self, owner, wide, narrow, plain):
        self.wide, self.narrow = wide, narrow
        self.deep = wide // 4
        mine = lax.axis_index("wide")
        self.core, self.y, self.z = mine & 1, (mine >> 1) & 1, mine >> 2
        self.o_core, self.o_y, self.o_z = owner & 1, (owner >> 1) & 1, owner >> 2
        self.x = lax.axis_index("narrow")
        self.holder = mine == owner
        spot = jnp.stack([self.core, self.x, self.y]).astype(jnp.int32)
        self.spot = jnp.zeros_like(spot) if plain else spot

    def swap(self, value, flip):
        return lax.ppermute(value, "wide", [(i, i ^ flip) for i in range(self.wide)])

    def cross(self, value, flip):
        pairs = [(2 * i + j, 2 * (i ^ flip) + 1 - j) for i in range(self.wide) for j in range(2)]
        return lax.ppermute(value, AXES, pairs)

    def z_flips(self):
        step = self.deep // 2
        while step:
            yield step
            step //= 2


def pick(parts, index):
    return lax.dynamic_index_in_dim(parts, index, axis=0, keepdims=False)


def ordered(mine, other, index):
    first = index == 0
    return jnp.stack([jnp.where(first, mine, other), jnp.where(first, other, mine)])


def spread_plain(place, shard):
    now = jnp.where(place.core == place.o_core, shard, place.swap(shard, 1))
    now = jnp.where(place.y == place.o_y, now, place.swap(now, 2))
    for step in place.z_flips():
        other = place.swap(now, 4 * step)
        now = jnp.where((place.z & step) == (place.o_z & step), now, other)
    return lax.all_gather(now, "narrow", axis=0, tiled=True)


def spread_steps(place, shard):
    if isinstance(shard, tuple):
        keep, send = shard
    else:
        halves = shard.reshape(2, shard.shape[0] // 2, shard.shape[1])
        keep, send = pick(halves, place.core), pick(halves, 1 - place.core)
    rows, width = 2 * keep.shape[0], keep.shape[1]
    (other,) = yield [(send, 1)]
    now = jnp.where(place.core == place.o_core, keep, other)
    halves = now.reshape(2, rows // 4, width)
    (other,) = yield [(pick(halves, 1 - place.y), 2)]
    now = jnp.where(place.y == place.o_y, pick(halves, place.y), other)
    for step in place.z_flips():
        (other,) = yield [(now, 4 * step)]
        now = jnp.where((place.z & step) == (place.o_z & step), now, other)
    by_y, by_x = yield [(now, 2), (now, 0)]
    cut = rows // 8
    far_a, far_b = yield [(by_y[:cut], 0), (by_x[cut:], 2)]
    mine = [
        (now, (0, 0, 0), 0),
        (by_y, (0, 0, 1), 0),
        (by_x, (0, 1, 0), 0),
        (far_a, (0, 1, 1), 0),
        (far_b, (0, 1, 1), cut),
    ]
    theirs = yield [(piece, 1) for piece, _, _ in mine]
    return Pieces(
        mine + [(got, (1, x, y), row) for got, (_, (_, x, y), row) in zip(theirs, mine)]
    )


class Pieces:
    def __init__(self, found):
        self.arrays = [piece for piece, _, _ in found]
        self.spots = [(flips, row) for _, flips, row in found]
        self.block, self.width = self.arrays[0].shape
        self.rows = self.block if len(found) == 1 else 8 * self.block

    def over(self, arrays):
        return Pieces([(v, flips, row) for v, (flips, row) in zip(arrays, self.spots)])

    def load(self, place_ref, refs, buffer, sem):
        copies = []
        for ref, ((core, x, y), row) in zip(refs, self.spots):
            start = 0
            if len(refs) > 1:
                at = 4 * (place_ref[1] ^ x) + 2 * (place_ref[0] ^ core) + (place_ref[2] ^ y)
                start = pl.multiple_of(at * self.block + row, 16)
            target = buffer.at[pl.ds(start, ref.shape[0]), :]
            copies.append(pltpu.make_async_copy(ref, target, sem.at[len(copies)]))
        for copy in copies:
            copy.start()
        for copy in copies:
            copy.wait()


ROWS = 256


def by_rows(name, body, place, blocks, wholes, weights, out_blocks, out_sums):
    length = blocks[0].shape[0]
    n_b, n_w, n_o, n_s = len(blocks), len(wholes), len(out_blocks), len(out_sums)
    counts = [len(w.arrays) for w in weights]

    def kernel(*refs):
        refs = list(refs)
        take = lambda n: [refs.pop(0) for _ in range(n)]
        (place_ref,) = take(1)
        block_refs, whole_refs = take(n_b), take(n_w)
        piece_refs = [take(n) for n in counts]
        out_refs, sum_refs = take(n_o), take(n_s)
        buffers, sems = take(len(weights)), take(len(weights))

        @pl.when(pl.program_id(0) == 0)
        def _():
            for w, pieces, buffer, sem in zip(weights, piece_refs, buffers, sems):
                w.load(place_ref, pieces, buffer, sem)
            for ref in sum_refs:
                ref[...] = jnp.zeros_like(ref)

        body(block_refs, whole_refs, buffers, out_refs, sum_refs)

    full = lambda shape: pl.BlockSpec(shape, lambda i: (0,) * len(shape))
    slab = lambda shape: (
        pl.BlockSpec((ROWS, shape[1]), lambda i: (i, 0))
        if shape[0] == length
        else pl.BlockSpec((shape[0], ROWS), lambda i: (0, i))
    )
    return pl.pallas_call(
        kernel,
        grid=(length // ROWS,),
        in_specs=[pl.BlockSpec(memory_space=pltpu.SMEM)]
        + [slab(v.shape) for v in blocks]
        + [full(v.shape) for v in wholes]
        + [pl.BlockSpec(memory_space=pl.ANY)] * sum(counts),
        out_specs=[slab(shape) for shape, _ in out_blocks] + [full(s) for s in out_sums],
        out_shape=[jax.ShapeDtypeStruct(shape, kind) for shape, kind in out_blocks]
        + [jax.ShapeDtypeStruct(shape, f32) for shape in out_sums],
        scratch_shapes=[pltpu.VMEM((w.rows, w.width), bf16) for w in weights]
        + [pltpu.SemaphoreType.DMA((n,)) for n in counts],
        compiler_params=pltpu.CompilerParams(vmem_limit_bytes=VMEM),
        cost_estimate=TINY,
        name=name,
    )(place.spot, *blocks, *wholes, *[v for w in weights for v in w.arrays])


def tie(groups):
    flat, tree = jax.tree.flatten(groups)
    return jax.tree.unflatten(tree, lax.optimization_barrier(flat))


class Steps:
    def __init__(self, place):
        self.place = place
        self.asked, self.flips, self.chains, self.done, self.going = {}, {}, {}, {}, {}

    def ask(self, name, pairs):
        self.asked[name] = [value for value, _ in pairs]
        self.flips[name] = [flip for _, flip in pairs]

    def add(self, name, chain):
        self.chains[name] = chain
        self.ask(name, next(chain))

    def exchange(self, value, flip):
        if flip <= 0:
            return self.place.cross(value, -flip)
        return self.place.swap(value, flip)

    def slot(self, names="", hold="", work=None, given=()):
        names, hold = names.split(), hold.split()
        assert not set(names) & set(self.going)
        asked = {name: self.asked[name] for name in names if name in self.asked}
        held = tie({"asked": asked, "given": given})
        for name, values in held["asked"].items():
            self.going[name] = [
                self.exchange(value, flip) for value, flip in zip(values, self.flips[name])
            ]
        result = work(*held["given"]) if work else ()
        ready = {name: got for name, got in self.going.items() if name not in hold}
        ready, result, self.asked = tie((ready, result, self.asked))
        for name, got in ready.items():
            del self.going[name], self.asked[name]
            try:
                self.ask(name, self.chains[name].send(got))
            except StopIteration as stop:
                self.done[name] = stop.value
        return result


def collect_plain(place, keep, send):
    width = keep.shape[-1]
    parts = [v.reshape(2, 1, 2, -1, width) for v in (keep, send)]
    terms = jnp.concatenate(parts, axis=1).reshape(-1, width)
    now = lax.psum_scatter(terms, "narrow", scatter_dimension=0, tiled=True)
    return lax.psum(now, "wide")


def add(*values):
    return functools.reduce(lambda a, b: a + b, [v.astype(f32) for v in values]).astype(bf16)


def collect_steps(place, keep, send):
    width, deep = keep.shape[-1], place.deep
    (other,) = yield [(send, 1)]
    now = add(keep, other).reshape(4, -1, width)
    spot = 2 * place.x + place.y
    got = yield [(pick(now, spot ^ 2), 0), (pick(now, spot ^ 1), 2), (pick(now, spot ^ 3), -2)]
    now = add(pick(now, spot), *got).reshape(deep, -1, width)
    got = yield [(pick(now, place.z ^ i), 4 * i) for i in range(1, deep)]
    now = add(pick(now, place.z), *got)
    got = yield [(now, 4 * i) for i in range(1, deep)]
    now = jnp.stack(
        [lax.select_n(place.z ^ i, now, *got) for i in range(deep)]
    ).reshape(-1, width)
    (other,) = yield [(now, 2)]
    now = ordered(now, other, place.y)
    (other,) = yield [(now, 1)]
    return ordered(now, other, place.core).reshape(-1, width)


def unpack_vectors(now, sizes):
    now = now.reshape(1, -1)
    out, at = [], 0
    for size in sizes:
        out.append(now[:, at : at + size])
        at += size
    return out


def shares(vectors, narrow):
    out = []
    for i in range(narrow):
        for v in vectors:
            size = v.shape[1] // narrow
            out.append(v[:, i * size : (i + 1) * size])
    return jnp.concatenate(out, axis=1)


def collect_vectors_steps(place, vectors):
    now = shares(vectors, 2).reshape(2, -1, 128)
    (other,) = yield [(now, 1)]
    now = now + other
    (other,) = yield [(pick(now, 1 - place.x), 0)]
    now = pick(now, place.x) + other
    (other,) = yield [(now, 2)]
    now = now + other
    for step in place.z_flips():
        (other,) = yield [(now, 4 * step)]
        now = now + other
    return now


def collect_vectors_plain(place, vectors):
    now = shares(vectors, place.narrow).reshape(place.narrow, -1)
    now = lax.psum_scatter(now, "narrow", scatter_dimension=0, tiled=False)
    return lax.psum(now, "wide")


def norm_rows(values, gain, shift):
    center = values - jnp.mean(values, axis=-1, keepdims=True)
    spread_of = jnp.mean(center * center, axis=-1, keepdims=True)
    return center * lax.rsqrt(spread_of + epsilon) * gain + shift


def norm_back(values, gain, grad):
    center = values - jnp.mean(values, axis=-1, keepdims=True)
    inverse = lax.rsqrt(jnp.mean(center * center, axis=-1, keepdims=True) + epsilon)
    hat = center * inverse
    scaled = grad * gain
    inner = jnp.mean(scaled * hat, axis=-1, keepdims=True)
    back = inverse * (scaled - jnp.mean(scaled, axis=-1, keepdims=True) - hat * inner)
    return (
        back,
        jnp.sum(grad * hat, axis=0, keepdims=True),
        jnp.sum(grad, axis=0, keepdims=True),
    )


def gelu_both(u):
    c = math.sqrt(2.0 / math.pi)
    square = u * u
    half = 0.5 + 0.5 * jnp.tanh(u * (c + c * 0.044715 * square))
    g = u * half
    return g, half + g * (1.0 - half) * (2 * c + 6 * c * 0.044715 * square)


def dot(a, b, dims=((1,), (0,))):
    return lax.dot_general(a, b, (dims, ((), ())), preferred_element_type=f32)


GAIN1, SHIFT1, QV, OUTB = (0, 6), (6, 6), (12, 12), (24, 6)
GAIN2, SHIFT2, FCB, PROJB = (30, 6), (36, 6), (42, 24), (66, 6)


def row_of(vec, spot, first=0, count=None):
    start = spot[0] + first
    count = spot[1] if count is None else count
    return jnp.concatenate([vec[start + i : start + i + 1, :] for i in range(count)], axis=1)


def unpack_rows(w):
    shard = w.shape[0] // 2
    near = w[:64, w.shape[1] - 128 :].astype(f32)
    far = w[shard : shard + 64, w.shape[1] - 128 :].astype(f32)
    parts = []
    for start, count in (GAIN1, SHIFT1, QV, OUTB, GAIN2, SHIFT2, FCB, PROJB):
        rows = slice(start // 2, (start + count) // 2)
        parts += [near[rows], far[rows]]
    return jnp.concatenate(parts, axis=0)


def pack_kernel(core_ref, w_ref, *refs):
    vectors, outs, rows_ref = refs[:-5], refs[-5:-1], refs[-1]
    half, width = w_ref.shape[0] // 2, w_ref.shape[1] // 3
    rows_ref[...] = jnp.zeros_like(rows_ref)
    at = 0
    for ref in vectors:
        value = ref[...].astype(f32)
        for i in range(value.shape[1] // 128):
            rows_ref[at : at + 1, :] = value[:, i * 128 : (i + 1) * 128]
            at += 1
    pairs = width // 128
    for other in range(2):
        core = 1 - core_ref[0] if other else core_ref[0]
        w = w_ref[pl.ds(pl.multiple_of(core * half, 16), half), :]
        for part in range(2):
            ref = outs[2 * part + other]
            for p in range(pairs // 2):
                for j in range(3):
                    source = j * width + (part * (pairs // 2) + p) * 128
                    to = (3 * p + j) * 128
                    ref[:, to : to + 128] = w[:, source : source + 128]
            if part == 0:
                block = rows_ref[...].astype(bf16)
                ref[:, 3 * width // 2 :] = jnp.concatenate([block, block], axis=0)


def pack(place, w, vectors):
    rows, width = w.shape
    side = width // 2
    shape = lambda more: jax.ShapeDtypeStruct((rows // 2, side + more), bf16)
    vmem = pl.BlockSpec(memory_space=pltpu.VMEM)
    near, near_send, far, far_send = pl.pallas_call(
        pack_kernel,
        in_specs=[pl.BlockSpec(memory_space=pltpu.SMEM)] + [vmem] * (1 + len(vectors)),
        out_specs=[vmem] * 4,
        out_shape=[shape(128), shape(128), shape(0), shape(0)],
        scratch_shapes=[pltpu.VMEM((rows // 4, 128), f32)],
        compiler_params=pltpu.CompilerParams(vmem_limit_bytes=VMEM),
        cost_estimate=TINY,
        name="pack",
    )(place.spot, w, *vectors)
    return (near, near_send), (far, far_send)


def widen_body(blocks, wholes, weights, outs, sums):
    (x_ref, mixed_ref), (vec,), (w_out, w_fc) = blocks, wholes, weights
    y1_ref, slope_ref, h2_t_ref, g_t_ref = outs
    y1 = x_ref[...].astype(f32) + dot(mixed_ref[...], w_out[...]) + row_of(vec, OUTB)
    y1_ref[...] = y1
    h2 = norm_rows(y1, row_of(vec, GAIN2), row_of(vec, SHIFT2)).astype(bf16)
    h2_t_ref[...] = h2.T
    for at in range(0, w_fc.shape[1], 512):
        here = slice(at, at + 512)
        g, slope = gelu_both(dot(h2, w_fc[:, here]) + row_of(vec, FCB, at // 128, 4))
        g_t_ref[here, :] = g.astype(bf16).T
        slope_ref[:, here] = slope.astype(bf16)


def finish_body(blocks, wholes, weights, outs, sums):
    (y1_ref, g_t_ref), (vec,), (w,) = blocks, wholes, weights
    result = y1_ref[...] + dot(g_t_ref[...], w[...], ((0,), (0,))) + row_of(vec, PROJB)
    outs[0][...] = result.astype(bf16)


def back_first_body(blocks, wholes, weights, outs, sums):
    (dqkv_ref, x_ref, dy1_ref), (vec,), (w_a, w_b) = blocks, wholes, weights
    side = w_b.shape[1]
    dqkv = dqkv_ref[...]
    dh1 = dot(dqkv[:, :side], w_a[:, :side], ((1,), (1,)))
    dh1 = dh1 + dot(dqkv[:, side:], w_b[...], ((1,), (1,)))
    back, gain, shift = norm_back(x_ref[...].astype(f32), row_of(vec, GAIN1), dh1)
    outs[0][...] = (dy1_ref[...] + back).astype(bf16)
    total = jnp.sum(dqkv.astype(f32), axis=0, keepdims=True)
    parts = [total[:, p * 384 + j : p * 384 + j + 128] for j in (0, 256) for p in range(H // 2)]
    for ref, value in zip(sums, (gain, shift, jnp.concatenate(parts, axis=1))):
        ref[...] += value


def on_device(
    wide,
    narrow,
    tokens,
    doc_ids,
    cotangent,
    owner,
    ln1_gain,
    ln1_bias,
    qkv_weight,
    qv_bias,
    out_weight,
    out_bias,
    ln2_gain,
    ln2_bias,
    fc_weight,
    fc_bias,
    proj_weight,
    proj_bias,
):
    _, length, width = tokens.shape
    plain = narrow != 2 or ln1_gain.shape[1] % 128 != 0
    place = Place(owner[0], wide, narrow, plain)
    x = tokens[0]
    dout = cotangent[0]
    doc = doc_ids[0][:, None]
    pairs = H // 2
    half = pairs // 2

    def begin(name, shard):
        if plain:
            steps.done[name] = Pieces([(spread_plain(place, shard), (0, 0, 0), 0)])
        else:
            steps.add(name, spread_steps(place, shard))

    def end(name, keep, send):
        if plain:
            steps.done[name] = collect_plain(place, keep, send)
        else:
            steps.add(name, collect_steps(place, keep, send))

    steps = Steps(place)
    vectors = (ln1_gain, ln1_bias, qv_bias, out_bias, ln2_gain, ln2_bias, fc_bias, proj_bias)
    sizes = [v.shape[1] for v in vectors]
    vec = None
    if plain:
        rows = spread_plain(place, jnp.concatenate(vectors, axis=1))
        parts, at = [], 0
        for size in sizes:
            parts.append(rows[:, at : at + size].reshape(-1))
            at += size
        vec = jnp.concatenate(parts).reshape(-1, 128).astype(f32)
        order = [
            qkv_weight[0][:, j * width + p * 128 : j * width + (p + 1) * 128]
            for p in range(pairs)
            for j in range(3)
        ]
        near = jnp.concatenate(order[: 3 * half], axis=1)
        far = jnp.concatenate(order[3 * half :], axis=1)
    else:
        near, far = pack(place, qkv_weight[0], vectors)
    begin("qa", near)
    begin("qb", far)
    begin("o", out_weight[0])
    begin("f", fc_weight[0])
    begin("p", proj_weight[0])

    def attention(x, vec, name, column, first, count, before):
        weights = steps.done[name]

        def run(x, vec, arrays, before):
            return attend(place, doc, x, vec, weights.over(arrays), column, first, count, before)

        return dict(work=run, given=(x, vec, weights.arrays, before))

    def rows_work(name, body, blocks, wholes, weights, out_blocks, out_sums):
        def run(blocks, wholes, arrays):
            held = [w.over(own) for w, own in zip(weights, arrays)]
            return by_rows(name, body, place, blocks, wholes, held, out_blocks, out_sums)

        return dict(work=run, given=(blocks, wholes, [w.arrays for w in weights]))

    steps.slot("qa qb")
    steps.slot("qa o f p")
    steps.slot("qa qb o")
    steps.slot("qa qb f", hold="qb f")
    steps.slot("qa", hold="f")
    steps.slot("qa qb o")
    steps.slot("qa qb f p", hold="f p")
    state = steps.slot("qb o", **attention(x, vec, "qa", 0, 0, 2, None))
    state, (h1, h1_t, vec) = list(state[:3]), state[3:]
    state = steps.slot(
        "qb o f p", hold="p", **attention(h1, vec, "qa", 768, 2, 1, state)
    )
    state = steps.slot("o f", hold="", **attention(h1, vec, "qb", 0, 3, 2, list(state)))
    state = steps.slot("f o p", **attention(h1, vec, "qb", 768, 5, 1, list(state)))
    mixed, soft, qkv = state
    steps.slot("f p", hold="p")
    w_a, w_b, w_out, w_fc = [steps.done[name] for name in ("qa", "qb", "o", "f")]
    hidden = w_fc.width
    y1, slope, h2_t, g_t = steps.slot(
        "",
        **rows_work(
            "widen",
            widen_body,
            [x, mixed],
            [vec],
            [w_out, w_fc],
            [
                ((length, width), f32),
                ((length, hidden), bf16),
                ((width, length), bf16),
                ((hidden, length), bf16),
            ],
            [],
        ),
    )
    p_send, p_keep = steps.slot(
        "p", work=lambda g_t, dout: proj_terms(place, g_t, dout), given=(g_t, dout)
    )
    end("dp", p_keep, p_send)
    steps.slot("p dp")
    w_proj = steps.done["p"]

    def run(dout, slope, y1, mixed, h2_t, vec, arrays):
        held = [w.over(own) for w, own in zip((w_out, w_fc, w_proj), arrays)]
        return back_middle(place, dout, slope, y1, mixed, h2_t, vec, *held)

    found = steps.slot(
        "dp",
        work=run,
        given=(dout, slope, y1, mixed, h2_t, vec, [w.arrays for w in (w_out, w_fc, w_proj)]),
    )
    dmixed, dy1, f_send, f_keep, d_gain2, d_shift2, d_outb, d_fcb, d_projb = found
    end("df", f_keep, f_send)

    def heads_back(first, count, before):
        def run(qkv, mixed, dmixed, soft, h1_t, before):
            return attend_back(place, qkv, mixed, dmixed, soft, h1_t, first, count, before)

        return dict(work=run, given=(qkv, mixed, dmixed, soft, h1_t, before))

    steps.slot("df dp", hold="dp")
    dqkv, a_send, a_keep = steps.slot("df", hold="df", **heads_back(0, half, None))
    end("da", a_keep, a_send)
    steps.slot("da dp", hold="dp df")
    dqkv, b_send, b_keep = steps.slot("da", **heads_back(half, half, dqkv))
    end("db", b_keep, b_send)
    sums = [(1, width), (1, width), (1, 2 * width)]
    tokens_grad, d_gain1, d_shift1, d_qv = steps.slot(
        "db df dp da",
        **rows_work(
            "back_first",
            back_first_body,
            [dqkv, x, dy1],
            [vec],
            [w_a, w_b],
            [((length, width), bf16)],
            sums,
        ),
    )
    small = (d_gain1, d_shift1, d_qv, d_outb, d_gain2, d_shift2, d_fcb, d_projb)
    if plain:
        steps.done["dv"] = collect_vectors_plain(place, small)
    else:
        steps.add("dv", collect_vectors_steps(place, small))
    (block_out,) = steps.slot(
        "db df dp da dv",
        **rows_work(
            "finish", finish_body, [y1, g_t], [vec], [w_proj], [((length, width), bf16)], []
        ),
    )
    while steps.asked:
        steps.slot("db da df dp dv")

    put = lambda v: jnp.where(place.holder, v.astype(f32), 0.0)
    s_proj = put(steps.done["dp"])[None]
    block = width // 8
    found = steps.done["df"].reshape(-1, hidden // width + 1, block, width)
    fc = [found[:, i].reshape(-1, width) for i in range(hidden // width)]
    s_fc = put(jnp.concatenate(fc, axis=1))[None]
    s_out = put(found[:, -1].reshape(-1, width))[None]
    both = [
        v[:, (3 * p + j) * 128 : (3 * p + j + 1) * 128]
        for j in range(3)
        for v in (steps.done["da"], steps.done["db"])
        for p in range(half)
    ]
    s_qkv = put(jnp.concatenate(both, axis=1))[None]
    small = unpack_vectors(steps.done["dv"], [v.shape[1] // narrow for v in small])
    s_gain1, s_shift1, s_qv, s_outb, s_gain2, s_shift2, s_fcb, s_projb = [put(v) for v in small]
    return (
        block_out[None],
        tokens_grad[None],
        s_gain1,
        s_shift1,
        s_qkv,
        s_qv,
        s_out,
        s_outb,
        s_gain2,
        s_shift2,
        s_fc,
        s_fcb,
        s_proj,
        s_projb,
    )


def solution(mesh):
    rows = P(AXES, None, None)
    flat, deep = P("wide", "narrow"), P("wide", "narrow", None)
    in_specs = (
        rows,
        P(AXES, None),
        rows,
        P(),
        flat,
        flat,
        deep,
        flat,
        deep,
        flat,
        flat,
        flat,
        deep,
        flat,
        deep,
        flat,
    )
    out_specs = (
        rows,
        rows,
        flat,
        flat,
        deep,
        flat,
        deep,
        flat,
        flat,
        flat,
        deep,
        flat,
        deep,
        flat,
    )
    body = functools.partial(on_device, mesh.shape["wide"], mesh.shape["narrow"])
    return jax.shard_map(
        body, mesh=mesh, in_specs=in_specs, out_specs=out_specs, check_vma=False
    )
```

time: 647 us -> 480 us (0.74)
  waiting for transfers between devices: 341 us -> 105 us
  Pallas kernels: 51.4 us -> 177 us
  matrix products: 83.5 us -> 0 us
  starting transfers between devices: 54.2 us -> 115 us
  local copies, waits for them, and re-layouts: 46.8 us -> 27.1 us
  other arithmetic: 57.4 us -> 47.5 us
    ppermute x56 -> x99, waiting for transfers between devices: 229 us -> 92.8 us  [swap(): lax.ppermute(value, 'wide', [(i, i ^ flip) for i in range(self.wide)])]
    pallas_call x1 -> x10, Pallas kernels: 29.6 us -> 146 us  [the longest x4 52.3 us: attend(): pl.pallas_call(kernel, grid=(count,), in_specs=[pl.BlockSpec(memory_space...]
    ppermute x10 -> x19, waiting for transfers between devices: 111 us -> 12.2 us  [cross(): return lax.ppermute(value, AXES, pairs)]
    dot_general x12 -> x0, matrix products: 83.5 us -> none  [dot(): return lax.dot_general(a, b, (dims, ((), ())), preferred_element_type=f32)]
    ppermute x56 -> x99, starting transfers between devices: 44.1 us -> 92.3 us  [swap(): lax.ppermute(value, 'wide', [(i, i ^ flip) for i in range(self.wide)])]
    ppermute x10 -> x19, starting transfers between devices: 10.2 us -> 22.7 us  [cross(): return lax.ppermute(value, AXES, pairs)]
    convert_element_type x20 -> x12, other arithmetic: 6.31 us -> 17.4 us  [add(): functools.reduce(lambda a, b: a + b, [v.astype(f32) for v in values])]
    reduce_sum x7 -> x0, other arithmetic: 9.65 us -> none  [the longest x2 6.05 us: norm_back(): return (back, jnp.sum(grad * hat, axis=0), jnp.sum(grad, axis=0))]
  transfers between devices with their start and end apart: 66 -> 118, of which waited for: 37 -> 36; matrix products, arithmetic and copies ran while one was open for 12% -> 6% of each run, Pallas kernels for 5% -> 37%
where the time goes in v2:
time: 480 us; the launch traced here: 475 us
  Pallas kernels  177 us (37%)
  starting transfers between devices  115 us (24%)
  waiting for transfers between devices  105 us (22%)
  other arithmetic  47.5 us (10%)
  local copies, waits for them, and re-layouts  27.1 us (6%)
    ppermute x99, waiting for transfers between devices, swap(): lax.ppermute(value, 'wide', [(i, i ^ flip) for i in range(self.wide)])  92.8 us
    ppermute x99, starting transfers between devices, swap(): lax.ppermute(value, 'wide', [(i, i ^ flip) for i in range(self.wide)])  92.3 us
    pallas_call x4, Pallas kernels, attend(): pl.pallas_call(kernel, grid=(count,), in_specs=[pl.BlockSpec(memory_space...  52.3 us
    pallas_call x3, Pallas kernels, by_rows(): pl.pallas_call(kernel, grid=(length // ROWS,), in_specs=[pl.BlockSpec(mem...  44.5 us
    pallas_call x1, Pallas kernels, back_middle(): pl.pallas_call(kernel, grid=(steps + f_steps + 1,), in_specs=[pl.BlockSpe...  34.1 us
    pallas_call x2, Pallas kernels, attend_back(): pl.pallas_call(functools.partial(attend_back_kernel, length=length), grid...  31.2 us
    ppermute x19, starting transfers between devices, cross(): return lax.ppermute(value, AXES, pairs)  22.7 us
    convert_element_type x12, other arithmetic, add(): functools.reduce(lambda a, b: a + b, [v.astype(f32) for v in values])  17.4 us
  transfers between devices with their start and end apart: 118, of which 36 were waited for; matrix products, arithmetic and copies ran while one was open for 6% of the time, Pallas kernels for 37%

profile of v2, /device:TPU:0, one launch (start us, length us, event | category | flops | bytes accessed | tf_op | source)
XLA Modules:
  0.0 474.8 jit_solution(18226449872914334045)
XLA Ops:
  1.2 2.9 pack.1
  6.9 1.8 dynamic-slice_bitcast_fusion.10
  11.6 3.0 collective-permute-start.5
  15.7 5.4 %collective-permute-done.5 = bf16[96,1280]{1,0:T(8,128)(2,1)S(1)} collective-permute-done((bf16[96,1280]{1,0:T(8,128)(2,1)S(1)}, bf16[96,1280]{1,0:T(8,128)(2,1)S(1)}, u32[]{:S(2)}, u32[]{:S(2)}) %collective-permute-start.5) | collective-permute-done | bytes 245792 | tf_op jit(solution)/shard_map/ppermute | solution.py:442
  22.1 1.8 bitcast_select_fusion.1
  24.9 2.9 collective-permute-start.7
  32.1 5.2 %collective-permute-done.6 = bf16[96,768]{1,0:T(8,128)(2,1)S(1)} collective-permute-done((bf16[96,768]{1,0:T(8,128)(2,1)S(1)}, bf16[96,768]{1,0:T(8,128)(2,1)S(1)}, u32[]{:S(2)}, u32[]{:S(2)}) %collective-permute-start.6) | collective-permute-done | bytes 147488 | tf_op jit(solution)/shard_map/ppermute | solution.py:442
  39.3 6.1 %collective-permute-done.10 = bf16[96,1280]{1,0:T(8,128)(2,1)S(1)} collective-permute-done((bf16[96,1280]{1,0:T(8,128)(2,1)S(1)}, bf16[96,1280]{1,0:T(8,128)(2,1)S(1)}, u32[]{:S(2)}, u32[]{:S(2)}) %collective-permute-start.10) | collective-permute-done | bytes 245792 | tf_op jit(solution)/shard_map/ppermute | solution.py:442
  45.5 1.6 collective-permute-start.11
  48.6 3.4 collective-permute-start.13
  52.4 8.8 %collective-permute-done.13 = bf16[96,1152]{1,0:T(8,128)(2,1)S(1)} collective-permute-done((bf16[96,1152]{1,0:T(8,128)(2,1)S(1)}, bf16[96,1152]{1,0:T(8,128)(2,1)S(1)}, u32[]{:S(2)}, u32[]{:S(2)}) %collective-permute-start.13) | collective-permute-done | bytes 221216 | tf_op jit(solution)/shard_map/ppermute | solution.py:442
  62.0 3.4 collective-permute-start.14
  66.5 3.8 collective-permute-done.15.refs_6_.refs_7_.refs_8_
  73.1 1.7 collective-permute-start.18
  77.8 1.6 collective-permute-done.24.refs_5_.refs_16_
  82.7 3.2 collective-permute-start.26
  88.4 17.3 %attend.4 = (bf16[1024,768]{1,0:T(8,128)(2,1)}, bf16[12,2304,256]{2,1,0:T(8,128)(2,1)}, bf16[1024,2304]{1,0:T(8,128)(2,1)}, bf16[1024,768]{1,0:T(8,128)(2,1)}, b...) custom-call(s32[3]{0:T(128)} %pad_add_fusion.core_ref.refs_0_.place_ref, s32[1024,1]{1,0:T(8,128)} %copy.40.refs_1_, ...), custom_call_target="tpu_custom_call" | custom-call | flops 1000 | bytes 1000 | tf_op jit(solution)/shard_map/attend/pallas_call | solution.py:142
  107.6 2.1 collective-permute-start.31
  110.4 3.4 collective-permute-done.31.refs_5_.refs_8_
  115.3 9.9 %attend.5 = (bf16[1024,768]{1,0:T(8,128)(2,1)}, bf16[12,2304,256]{2,1,0:T(8,128)(2,1)}, bf16[1024,2304]{1,0:T(8,128)(2,1)}) custom-call(s32[3]{0:T(128)} %pad_add_fusion.core_ref.refs_0_.place_ref, s32[1024,1]{1,0:T(8,128)} %copy.40.refs_1_, ...), custom_call_target="tpu_custom_call", output_to_operand_aliasing={{0}: (14, {}), {1}: (15, {}), {2}: (16, {})} | custom-call | flops 1000 | bytes 1000 | tf_op jit(solution)/shard_map/attend/pallas_call | solution.py:142
  125.2 2.9 collective-permute-start.42
  128.3 1.8 collective-permute-start.38
  132.4 15.4 %attend.6 = (bf16[1024,768]{1,0:T(8,128)(2,1)}, bf16[12,2304,256]{2,1,0:T(8,128)(2,1)}, bf16[1024,2304]{1,0:T(8,128)(2,1)}) custom-call(s32[3]{0:T(128)} %pad_add_fusion.core_ref.refs_0_.place_ref, s32[1024,1]{1,0:T(8,128)} %copy.40.refs_1_, ...), custom_call_target="tpu_custom_call", output_to_operand_aliasing={{0}: (14, {}), {1}: (15, {}), {2}: (16, {})} | custom-call | flops 1000 | bytes 1000 | tf_op jit(solution)/shard_map/attend/pallas_call | solution.py:142
  147.8 5.7 %collective-permute-done.42 = bf16[384,768]{1,0:T(8,128)(2,1)S(1)} collective-permute-done((bf16[384,768]{1,0:T(8,128)(2,1)S(1)}, bf16[384,768]{1,0:T(8,128)(2,1)S(1)}, u32[]{:S(2)}, u32[]{:S(2)}) %collective-permute-start.42) | collective-permute-done | bytes 589856 | tf_op jit(solution)/shard_map/ppermute | solution.py:442
  158.8 9.8 %attend.7 = (bf16[1024,768]{1,0:T(8,128)(2,1)}, bf16[12,2304,256]{2,1,0:T(8,128)(2,1)}, bf16[1024,2304]{1,0:T(8,128)(2,1)}) custom-call(s32[3]{0:T(128)} %pad_add_fusion.core_ref.refs_0_.place_ref, s32[1024,1]{1,0:T(8,128)} %copy.40.refs_1_, ...), custom_call_target="tpu_custom_call", output_to_operand_aliasing={{0}: (14, {}), {1}: (15, {}), {2}: (16, {})} | custom-call | flops 1000 | bytes 1000 | tf_op jit(solution)/shard_map/attend/pallas_call | solution.py:142
  174.5 21.0 %widen.1 = (f32[1024,768]{1,0:T(8,128)}, bf16[1024,3072]{1,0:T(8,128)(2,1)}, bf16[768,1024]{1,0:T(8,128)(2,1)}, bf16[3072,1024]{1,0:T(8,128)(2,1)}) custom-call(s32[3]{0:T(128)} %pad_add_fusion.core_ref.refs_0_.place_ref, bf16[1024,768]{1,0:T(8,128)(2,1)} %bitcast.301, bf16[1024,768]{1,0:T(8,128)(2,1)} %get-tuple-element.868.refs_2_.refs_4_.o_ref, ...), custom_call_target="tpu_custom_call" | custom-call | flops 1000 | bytes 1000 | tf_op jit(solution)/shard_map/widen/pallas_call | solution.py:561
  197.6 11.8 %proj_terms.1 = (bf16[1536,768]{1,0:T(8,128)(2,1)}, bf16[1536,768]{1,0:T(8,128)(2,1)}) custom-call(s32[3]{0:T(128)} %pad_add_fusion.core_ref.refs_0_.place_ref, bf16[3072,1024]{1,0:T(8,128)(2,1)} %get-tuple-element.953.g_ref.refs_2_, bf16[1024,768]{1,0:T(8,128)(2,1)} %bitcast.307), custom_call_target="tpu_custom_call" | custom-call | flops 1000 | bytes 1000 | tf_op jit(solution)/shard_map/proj_terms/pallas_call | solution.py:298
  210.6 3.5 collective-permute-done.64.refs_35_.refs_12_
  215.2 2.6 collective-permute-done.65.refs_36_.refs_13_
  218.6 3.0 add_convert_fusion.1
  226.3 34.1 %back_middle.1 = (bf16[1024,768]{1,0:T(8,128)(2,1)}, f32[1024,768]{1,0:T(8,128)}, bf16[4,480,768]{2,1,0:T(8,128)(2,1)}, bf16[4,480,768]{2,1,0:T(8,128)(2,1)}, f3...) custom-call(s32[3]{0:T(128)} %pad_add_fusion.core_ref.refs_0_.place_ref, ...), custom_call_target="tpu_custom_call" | custom-call | flops 1000 | bytes 1000 | tf_op jit(solution)/shard_map/back_middle/pallas_call | solution.py:395
  260.4 1.5 fusion.5
  264.0 3.0 collective-permute-start.70
  268.4 3.4 add_convert_fusion
  273.1 15.5 %attend_back.2 = (bf16[1024,2304]{1,0:T(8,128)(2,1)}, bf16[384,1152]{1,0:T(8,128)(2,1)}, bf16[384,1152]{1,0:T(8,128)(2,1)}) custom-call(s32[3]{0:T(128)} %pad_add_fusion.core_ref.refs_0_.place_ref, bf16[1024,2304]{1,0:T(8,128)(2,1)} %get-tuple-element.867.q_ref.k_ref.v_ref, bf16[1024,2304]{1,0:T(8,128)(2,1)} %get-tuple-element.867.q_ref.k_ref.v_ref, ...), custom_call_target="tpu_custom_call" | custom-call | flops 1000 | bytes 1000 | tf_op jit(solution)/shard_map/attend_back/pallas_call | solution.py:252
  290.3 3.0 collective-permute-start.81
  295.3 1.5 collective-permute-start.79
  302.0 3.5 collective-permute-done.82
  307.0 5.7 %collective-permute-done.77 = bf16[480,768]{1,0:T(8,128)(2,1)S(1)} collective-permute-done((bf16[480,768]{1,0:T(8,128)(2,1)S(1)}, bf16[480,768]{1,0:T(8,128)(2,1)S(1)}, u32[]{:S(2)}, u32[]{:S(2)}) %collective-permute-start.77) | collective-permute-done | bytes 737312 | tf_op jit(solution)/shard_map/ppermute | solution.py:446
  315.0 15.6 %attend_back.3 = (bf16[1024,2304]{1,0:T(8,128)(2,1)}, bf16[384,1152]{1,0:T(8,128)(2,1)}, bf16[384,1152]{1,0:T(8,128)(2,1)}) custom-call(s32[3]{0:T(128)} %pad_add_fusion.core_ref.refs_0_.place_ref, bf16[1024,2304]{1,0:T(8,128)(2,1)} %get-tuple-element.867.q_ref.k_ref.v_ref, ...), custom_call_target="tpu_custom_call", output_to_operand_aliasing={{0}: (8, {})} | custom-call | flops 1000 | bytes 1000 | tf_op jit(solution)/shard_map/attend_back/pallas_call | solution.py:252
  330.6 2.7 collective-permute-done.74
  333.3 4.8 %collective-permute-done.75 = bf16[96,1152]{1,0:T(8,128)(2,1)S(1)} collective-permute-done((bf16[96,1152]{1,0:T(8,128)(2,1)}, bf16[96,1152]{1,0:T(8,128)(2,1)S(1)}, u32[]{:S(2)}, u32[]{:S(2)}) %collective-permute-start.75) | collective-permute-done | bytes 221216 | tf_op jit(solution)/shard_map/ppermute | solution.py:442
  338.1 1.7 fusion.2
  345.2 2.9 collective-permute-start.85
  349.4 2.8 collective-permute-done.84
  352.2 2.5 collective-permute-start.89
  354.7 12.2 %back_first.1 = (bf16[1024,768]{1,0:T(8,128)(2,1)}, f32[1,768]{1,0:T(1,128)}, f32[1,768]{1,0:T(1,128)}, f32[1,1536]{1,0:T(1,128)}) custom-call(s32[3]{0:T(128)} %pad_add_fusion.core_ref.refs_0_.place_ref, bf16[1024,2304]{1,0:T(8,128)(2,1)} %get-tuple-element.896.refs_1_, bf16[1024,768]{1,0:T(8,128)(2,1)} %bitcast.302, ...), custom_call_target="tpu_custom_call" | custom-call | flops 1000 | bytes 1000 | tf_op jit(solution)/shard_map/back_first/pallas_call | solution.py:561
  377.8 3.8 collective-permute-start.97
  383.7 2.1 collective-permute-start.92
  385.8 5.9 %collective-permute-done.91 = bf16[24,1152]{1,0:T(8,128)(2,1)S(1)} collective-permute-done((bf16[24,1152]{1,0:T(8,128)(2,1)S(1)}, bf16[24,1152]{1,0:T(8,128)(2,1)S(1)}, u32[]{:S(2)}, u32[]{:S(2)}) %collective-permute-start.91) | collective-permute-done | bytes 55328 | tf_op jit(solution)/shard_map/ppermute | solution.py:442
  392.4 3.8 collective-permute-done.92
  401.7 11.3 %finish.1 = bf16[1024,768]{1,0:T(8,128)(2,1)} custom-call(s32[3]{0:T(128)} %pad_add_fusion.core_ref.refs_0_.place_ref, f32[1024,768]{1,0:T(8,128)} %get-tuple-element.952.refs_3_.refs_1_, bf16[3072,1024]{1,0:T(8,128)(2,1)} %get-tuple-element.953.g_ref.refs_2_, f32[72,128]{1,0:T(8,128)} %get-tuple-element.954.refs_3_.refs_6_.refs_4_, ...), custom_call_target="tpu_custom_call" | custom-call | flops 1000 | bytes 1000 | tf_op jit(solution)/shard_map/finish/pallas_call | solution.py:561
  419.8 3.3 collective-permute-start.104
  423.1 2.3 collective-permute-start.105
  425.5 3.6 collective-permute-done.105
  429.1 8.5 %collective-permute-done.102 = bf16[96,1152]{1,0:T(8,128)(2,1)S(1)} collective-permute-done((bf16[96,1152]{1,0:T(8,128)(2,1)S(1)}, bf16[96,1152]{1,0:T(8,128)(2,1)S(1)}, u32[]{:S(2)}, u32[]{:S(2)}) %collective-permute-start.102) | collective-permute-done | bytes 221216 | tf_op jit(solution)/shard_map/ppermute | solution.py:442
  446.9 2.4 collective-permute-start.110
  450.3 2.6 convert_select_fusion
  452.9 2.3 collective-permute-done.111
  455.2 1.6 select_bitcast_fusion.1
  459.4 3.2 collective-permute-done.115
  463.1 2.8 convert_select_fusion.1
  467.0 2.7 collective-permute-done.117
  472.5 2.0 convert_select_fusion.2
  (514 shorter events, 124.1 us)
Async XLA Ops:
  10.9 10.2 %collective-permute-start.2 = (bf16[192,3072]{1,0:T(8,128)(2,1)}, bf16[192,3072]{1,0:T(8,128)(2,1)S(1)}, u32[]{:S(2)}, u32[]{:S(2)}) collective-permute-start(bf16[192,3072]{1,0:T(8,128)(2,1)} %dynamic-slice_bitcast_fusion.1), channel_id=1, source_target_pairs={{0,2},{2,0},{4,6},{6,4},{8,10},{10,8},{12,14},{14,12},{16,18},{18,... | collective-permute-start | bytes 3538952 | tf_op jit(solution)/shard_map/ppermute | solution.py:442
  11.0 11.1 %collective-permute-start.4 = (bf16[768,768]{1,0:T(8,128)(2,1)S(1)}, bf16[768,768]{1,0:T(8,128)(2,1)}, u32[]{:S(2)}, u32[]{:S(2)}) collective-permute-start(bf16[768,768]{1,0:T(8,128)(2,1)S(1)} %dynamic-slice_bitcast_fusion), channel_id=1, source_target_pairs={{0,2},{2,0},{4,6},{6,4},{8,10},{10,8},{12,14},{14,12},{16,18},{18,... | collective-permute-start | bytes 3538952 | tf_op jit(solution)/shard_map/ppermute | solution.py:442
  11.5 9.6 %collective-permute-start.3 = (bf16[192,768]{1,0:T(8,128)(2,1)}, bf16[192,768]{1,0:T(8,128)(2,1)S(1)}, u32[]{:S(2)}, u32[]{:S(2)}) collective-permute-start(bf16[192,768]{1,0:T(8,128)(2,1)} %dynamic-slice_bitcast_fusion.10), channel_id=1, source_target_pairs={{0,2},{2,0},{4,6},{6,4},{8,10},{10,8},{12,14},{14,12},{16,18},{18,... | collective-permute-start | bytes 884744 | tf_op jit(solution)/shard_map/ppermute | solution.py:442
  24.9 13.6 %collective-permute-start.7 = (bf16[96,1280]{1,0:T(8,128)(2,1)S(1)}, bf16[96,1280]{1,0:T(8,128)(2,1)S(1)}, u32[]{:S(2)}, u32[]{:S(2)}) collective-permute-start(bf16[96,1280]{1,0:T(8,128)(2,1)S(1)} %bitcast_select_fusion.5), channel_id=1, source_target_pairs={{0,16},{2,18},{4,20},{6,22},{8,24},{10,26},{12,28},{14,30},{16,0},... | collective-permute-start | bytes 737288 | tf_op jit(solution)/shard_map/ppermute | solution.py:442
  45.5 15.7 %collective-permute-start.11 = (bf16[96,1280]{1,0:T(8,128)(2,1)S(1)}, bf16[96,1280]{1,0:T(8,128)(2,1)S(1)}, u32[]{:S(2)}, u32[]{:S(2)}) collective-permute-start(bf16[96,1280]{1,0:T(8,128)(2,1)S(1)} %broadcast_select_fusion.6.refs_3_.refs_4_.refs_5_), channel_id=1, source_target_pairs={{0,4},{2,6},{4,0},{6,2},{8,12},{10,14},{12,8},{14,10},{16,20},{18,... | collective-permute-start | bytes 737288 | tf_op jit(solution)/shard_map/ppermute | solution.py:442
  47.1 14.1 %collective-permute-start.12 = (bf16[96,1280]{1,0:T(8,128)(2,1)S(1)}, bf16[96,1280]{1,0:T(8,128)(2,1)S(1)}, u32[]{:S(2)}, u32[]{:S(2)}) collective-permute-start(bf16[96,1280]{1,0:T(8,128)(2,1)S(1)} %broadcast_select_fusion.6.refs_3_.refs_4_.refs_5_), channel_id=1, source_target_pairs={{0,1},{1,0},{2,3},{3,2},{4,5},{5,4},{6,7},{7,6},{8,9},{9,8},{10,11... | collective-permute-start | bytes 737288 | tf_op jit(solution)/shard_map/ppermute | solution.py:446
  48.6 12.6 %collective-permute-start.13 = (bf16[96,1152]{1,0:T(8,128)(2,1)S(1)}, bf16[96,1152]{1,0:T(8,128)(2,1)S(1)}, u32[]{:S(2)}, u32[]{:S(2)}) collective-permute-start(bf16[96,1152]{1,0:T(8,128)(2,1)S(1)} %bitcast_select_fusion.6), channel_id=1, source_target_pairs={{0,16},{2,18},{4,20},{6,22},{8,24},{10,26},{12,28},{14,30},{16,0},... | collective-permute-start | bytes 663560 | tf_op jit(solution)/shard_map/ppermute | solution.py:442
  51.9 14.5 %collective-permute-start.9 = (bf16[96,3072]{1,0:T(8,128)(2,1)}, bf16[96,3072]{1,0:T(8,128)(2,1)S(1)}, u32[]{:S(2)}, u32[]{:S(2)}) collective-permute-start(bf16[96,3072]{1,0:T(8,128)(2,1)} %dynamic-slice_bitcast_fusion.9), channel_id=1, source_target_pairs={{0,4},{2,6},{4,0},{6,2},{8,12},{10,14},{12,8},{14,10},{16,20},{18,... | collective-permute-start | bytes 1769480 | tf_op jit(solution)/shard_map/ppermute | solution.py:442
  61.3 9.6 %collective-permute-start.17 = (bf16[96,1152]{1,0:T(8,128)(2,1)S(1)}, bf16[96,1152]{1,0:T(8,128)(2,1)S(1)}, u32[]{:S(2)}, u32[]{:S(2)}) collective-permute-start(bf16[96,1152]{1,0:T(8,128)(2,1)S(1)} %broadcast_select_fusion.9), channel_id=1, source_target_pairs={{0,8},{2,10},{4,12},{6,14},{8,0},{10,2},{12,4},{14,6},{16,24},{18,... | collective-permute-start | bytes 663560 | tf_op jit(solution)/shard_map/ppermute | solution.py:442
  73.1 32.6 %collective-permute-start.18 = (bf16[96,3072]{1,0:T(8,128)(2,1)S(1)}, bf16[96,3072]{1,0:T(8,128)(2,1)}, u32[]{:S(2)}, u32[]{:S(2)}) collective-permute-start(bf16[96,3072]{1,0:T(8,128)(2,1)S(1)} %bitcast_select_fusion.3), channel_id=1, source_target_pairs={{0,16},{2,18},{4,20},{6,22},{8,24},{10,26},{12,28},{14,30},{16,0},... | collective-permute-start | bytes 1769480 | tf_op jit(solution)/shard_map/ppermute | solution.py:442
  74.8 30.9 %collective-permute-start.27 = (bf16[384,768]{1,0:T(8,128)(2,1)}, bf16[384,768]{1,0:T(8,128)(2,1)}, u32[]{:S(2)}, u32[]{:S(2)}) collective-permute-start(bf16[384,768]{1,0:T(8,128)(2,1)} %dynamic-slice_bitcast_fusion.8), channel_id=1, source_target_pairs={{0,4},{2,6},{4,0},{6,2},{8,12},{10,14},{12,8},{14,10},{16,20},{18,... | collective-permute-start | bytes 1769480 | tf_op jit(solution)/shard_map/ppermute | solution.py:442
  82.7 23.1 %collective-permute-start.26 = (bf16[96,768]{1,0:T(8,128)(2,1)}, bf16[96,768]{1,0:T(8,128)(2,1)}, u32[]{:S(2)}, u32[]{:S(2)}) collective-permute-start(bf16[96,768]{1,0:T(8,128)(2,1)} %broadcast_select_fusion.11), channel_id=1, source_target_pairs={{0,8},{2,10},{4,12},{6,14},{8,0},{10,2},{12,4},{14,6},{16,24},{18,... | collective-permute-start | bytes 442376 | tf_op jit(solution)/shard_map/ppermute | solution.py:442
  85.9 19.8 %collective-permute-start.28 = (bf16[48,1152]{1,0:T(8,128)(2,1)}, bf16[48,1152]{1,0:T(8,128)(2,1)}, u32[]{:S(2)}, u32[]{:S(2)}) collective-permute-start(bf16[48,1152]{1,0:T(8,128)(2,1)} %slice.173), channel_id=1, source_target_pairs={{0,1},{1,0},{2,3},{3,2},{4,5},{5,4},{6,7},{7,6},{8,9},{9,8},{10,11... | collective-permute-start | bytes 331784 | tf_op jit(solution)/shard_map/ppermute | solution.py:446
  86.4 19.3 %collective-permute-start.29 = (bf16[48,1152]{1,0:T(8,128)(2,1)}, bf16[48,1152]{1,0:T(8,128)(2,1)}, u32[]{:S(2)}, u32[]{:S(2)}) collective-permute-start(bf16[48,1152]{1,0:T(8,128)(2,1)} %slice.174), channel_id=1, source_target_pairs={{0,4},{2,6},{4,0},{6,2},{8,12},{10,14},{12,8},{14,10},{16,20},{18,... | collective-permute-start | bytes 331784 | tf_op jit(solution)/shard_map/ppermute | solution.py:442
  106.9 21.3 %collective-permute-start.30 = (bf16[96,3072]{1,0:T(8,128)(2,1)S(1)}, bf16[96,3072]{1,0:T(8,128)(2,1)S(1)}, u32[]{:S(2)}, u32[]{:S(2)}) collective-permute-start(bf16[96,3072]{1,0:T(8,128)(2,1)S(1)} %broadcast_select_fusion.2), channel_id=1, source_target_pairs={{0,8},{2,10},{4,12},{6,14},{8,0},{10,2},{12,4},{14,6},{16,24},{18,... | collective-permute-start | bytes 1769480 | tf_op jit(solution)/shard_map/ppermute | solution.py:442
  109.7 18.4 %collective-permute-start.33 = (bf16[96,1152]{1,0:T(8,128)(2,1)S(1)}, bf16[96,1152]{1,0:T(8,128)(2,1)S(1)}, u32[]{:S(2)}, u32[]{:S(2)}) collective-permute-start(bf16[96,1152]{1,0:T(8,128)(2,1)S(1)} %broadcast_select_fusion.8.refs_4_.refs_15_), channel_id=1, source_target_pairs={{0,2},{2,0},{4,6},{6,4},{8,10},{10,8},{12,14},{14,12},{16,18},{18,... | collective-permute-start | bytes 663560 | tf_op jit(solution)/shard_map/ppermute | solution.py:442
  109.7 18.4 %collective-permute-start.34 = (bf16[96,1152]{1,0:T(8,128)(2,1)S(1)}, bf16[96,1152]{1,0:T(8,128)(2,1)S(1)}, u32[]{:S(2)}, u32[]{:S(2)}) collective-permute-start(bf16[96,1152]{1,0:T(8,128)(2,1)S(1)} %collective-permute-done.24.refs_5_.refs_16_), channel_id=1, source_target_pairs={{0,2},{2,0},{4,6},{6,4},{8,10},{10,8},{12,14},{14,12},{16,18},{18,... | collective-permute-start | bytes 663560 | tf_op jit(solution)/shard_map/ppermute | solution.py:442
  110.3 17.9 %collective-permute-start.35 = (bf16[96,1152]{1,0:T(8,128)(2,1)S(1)}, bf16[96,1152]{1,0:T(8,128)(2,1)S(1)}, u32[]{:S(2)}, u32[]{:S(2)}) collective-permute-start(bf16[96,1152]{1,0:T(8,128)(2,1)S(1)} %collective-permute-done.25.refs_6_.refs_17_), channel_id=1, source_target_pairs={{0,2},{2,0},{4,6},{6,4},{8,10},{10,8},{12,14},{14,12},{16,18},{18,... | collective-permute-start | bytes 663560 | tf_op jit(solution)/shard_map/ppermute | solution.py:442
  113.8 11.4 %collective-permute-start.32 = (bf16[96,768]{1,0:T(8,128)(2,1)S(1)}, bf16[96,768]{1,0:T(8,128)(2,1)S(1)}, u32[]{:S(2)}, u32[]{:S(2)}) collective-permute-start(bf16[96,768]{1,0:T(8,128)(2,1)S(1)} %broadcast_select_fusion.10.refs_4_.refs_7_), channel_id=1, source_target_pairs={{0,1},{1,0},{2,3},{3,2},{4,5},{5,4},{6,7},{7,6},{8,9},{9,8},{10,11... | collective-permute-start | bytes 442376 | tf_op jit(solution)/shard_map/ppermute | solution.py:446
  125.2 28.3 %collective-permute-start.42 = (bf16[384,768]{1,0:T(8,128)(2,1)S(1)}, bf16[384,768]{1,0:T(8,128)(2,1)S(1)}, u32[]{:S(2)}, u32[]{:S(2)}) collective-permute-start(bf16[384,768]{1,0:T(8,128)(2,1)S(1)} %bitcast_select_fusion.2), channel_id=1, source_target_pairs={{0,16},{2,18},{4,20},{6,22},{8,24},{10,26},{12,28},{14,30},{16,0},... | collective-permute-start | bytes 1769480 | tf_op jit(solution)/shard_map/ppermute | solution.py:442
  128.3 25.2 %collective-permute-start.38 = (bf16[96,3072]{1,0:T(8,128)(2,1)S(1)}, bf16[96,3072]{1,0:T(8,128)(2,1)S(1)}, u32[]{:S(2)}, u32[]{:S(2)}) collective-permute-start(bf16[96,3072]{1,0:T(8,128)(2,1)S(1)} %broadcast_select_fusion.3.refs_14_.refs_17_), channel_id=1, source_target_pairs={{0,4},{2,6},{4,0},{6,2},{8,12},{10,14},{12,8},{14,10},{16,20},{18,... | collective-permute-start | bytes 1769480 | tf_op jit(solution)/shard_map/ppermute | solution.py:442
  130.1 23.5 %collective-permute-start.39 = (bf16[96,3072]{1,0:T(8,128)(2,1)S(1)}, bf16[96,3072]{1,0:T(8,128)(2,1)S(1)}, u32[]{:S(2)}, u32[]{:S(2)}) collective-permute-start(bf16[96,3072]{1,0:T(8,128)(2,1)S(1)} %broadcast_select_fusion.3.refs_14_.refs_17_), channel_id=1, source_target_pairs={{0,1},{1,0},{2,3},{3,2},{4,5},{5,4},{6,7},{7,6},{8,9},{9,8},{10,11... | collective-permute-start | bytes 1769480 | tf_op jit(solution)/shard_map/ppermute | solution.py:446
  130.6 22.9 %collective-permute-start.40 = (bf16[48,768]{1,0:T(8,128)(2,1)S(1)}, bf16[48,768]{1,0:T(8,128)(2,1)S(1)}, u32[]{:S(2)}, u32[]{:S(2)}) collective-permute-start(bf16[48,768]{1,0:T(8,128)(2,1)S(1)} %slice.175), channel_id=1, source_target_pairs={{0,1},{1,0},{2,3},{3,2},{4,5},{5,4},{6,7},{7,6},{8,9},{9,8},{10,11... | collective-permute-start | bytes 221192 | tf_op jit(solution)/shard_map/ppermute | solution.py:446
  132.1 21.4 %collective-permute-start.41 = (bf16[48,768]{1,0:T(8,128)(2,1)S(1)}, bf16[48,768]{1,0:T(8,128)(2,1)S(1)}, u32[]{:S(2)}, u32[]{:S(2)}) collective-permute-start(bf16[48,768]{1,0:T(8,128)(2,1)S(1)} %slice.176), channel_id=1, source_target_pairs={{0,4},{2,6},{4,0},{6,2},{8,12},{10,14},{12,8},{14,10},{16,20},{18,... | collective-permute-start | bytes 221192 | tf_op jit(solution)/shard_map/ppermute | solution.py:442
  153.7 15.1 %collective-permute-start.50 = (bf16[384,768]{1,0:T(8,128)(2,1)S(1)}, bf16[384,768]{1,0:T(8,128)(2,1)S(1)}, u32[]{:S(2)}, u32[]{:S(2)}) collective-permute-start(bf16[384,768]{1,0:T(8,128)(2,1)S(1)} %broadcast_select_fusion.1), channel_id=1, source_target_pairs={{0,8},{2,10},{4,12},{6,14},{8,0},{10,2},{12,4},{14,6},{16,24},{18,... | collective-permute-start | bytes 1769480 | tf_op jit(solution)/shard_map/ppermute | solution.py:442
  155.0 13.7 %collective-permute-start.43 = (bf16[48,3072]{1,0:T(8,128)(2,1)S(1)}, bf16[48,3072]{1,0:T(8,128)(2,1)S(1)}, u32[]{:S(2)}, u32[]{:S(2)}) collective-permute-start(bf16[48,3072]{1,0:T(8,128)(2,1)S(1)} %slice.177), channel_id=1, source_target_pairs={{0,1},{1,0},{2,3},{3,2},{4,5},{5,4},{6,7},{7,6},{8,9},{9,8},{10,11... | collective-permute-start | bytes 884744 | tf_op jit(solution)/shard_map/ppermute | solution.py:446
  155.6 13.2 %collective-permute-start.44 = (bf16[48,3072]{1,0:T(8,128)(2,1)S(1)}, bf16[48,3072]{1,0:T(8,128)(2,1)S(1)}, u32[]{:S(2)}, u32[]{:S(2)}) collective-permute-start(bf16[48,3072]{1,0:T(8,128)(2,1)S(1)} %slice.178), channel_id=1, source_target_pairs={{0,4},{2,6},{4,0},{6,2},{8,12},{10,14},{12,8},{14,10},{16,20},{18,... | collective-permute-start | bytes 884744 | tf_op jit(solution)/shard_map/ppermute | solution.py:442
  158.3 10.4 %collective-permute-start.46 = (bf16[96,768]{1,0:T(8,128)(2,1)S(1)}, bf16[96,768]{1,0:T(8,128)(2,1)S(1)}, u32[]{:S(2)}, u32[]{:S(2)}) collective-permute-start(bf16[96,768]{1,0:T(8,128)(2,1)S(1)} %collective-permute-done.31.refs_5_.refs_8_), channel_id=1, source_target_pairs={{0,2},{2,0},{4,6},{6,4},{8,10},{10,8},{12,14},{14,12},{16,18},{18,... | collective-permute-start | bytes 442376 | tf_op jit(solution)/shard_map/ppermute | solution.py:442
  158.4 10.3 %collective-permute-start.47 = (bf16[96,768]{1,0:T(8,128)(2,1)S(1)}, bf16[96,768]{1,0:T(8,128)(2,1)S(1)}, u32[]{:S(2)}, u32[]{:S(2)}) collective-permute-start(bf16[96,768]{1,0:T(8,128)(2,1)S(1)} %collective-permute-done.32.refs_6_.refs_9_), channel_id=1, source_target_pairs={{0,2},{2,0},{4,6},{6,4},{8,10},{10,8},{12,14},{14,12},{16,18},{18,... | collective-permute-start | bytes 442376 | tf_op jit(solution)/shard_map/ppermute | solution.py:442
  170.5 25.0 %collective-permute-start.51 = (bf16[384,768]{1,0:T(8,128)(2,1)S(1)}, bf16[384,768]{1,0:T(8,128)(2,1)S(1)}, u32[]{:S(2)}, u32[]{:S(2)}) collective-permute-start(bf16[384,768]{1,0:T(8,128)(2,1)S(1)} %broadcast_select_fusion.refs_27_.refs_4_), channel_id=1, source_target_pairs={{0,4},{2,6},{4,0},{6,2},{8,12},{10,14},{12,8},{14,10},{16,20},{18,... | collective-permute-start | bytes 1769480 | tf_op jit(solution)/shard_map/ppermute | solution.py:442
  171.2 24.3 %collective-permute-start.52 = (bf16[384,768]{1,0:T(8,128)(2,1)S(1)}, bf16[384,768]{1,0:T(8,128)(2,1)S(1)}, u32[]{:S(2)}, u32[]{:S(2)}) collective-permute-start(bf16[384,768]{1,0:T(8,128)(2,1)S(1)} %broadcast_select_fusion.refs_27_.refs_4_), channel_id=1, source_target_pairs={{0,1},{1,0},{2,3},{3,2},{4,5},{5,4},{6,7},{7,6},{8,9},{9,8},{10,11... | collective-permute-start | bytes 1769480 | tf_op jit(solution)/shard_map/ppermute | solution.py:446
  195.6 13.8 %collective-permute-start.58 = (bf16[192,768]{1,0:T(8,128)(2,1)S(1)}, bf16[192,768]{1,0:T(8,128)(2,1)S(1)}, u32[]{:S(2)}, u32[]{:S(2)}) collective-permute-start(bf16[192,768]{1,0:T(8,128)(2,1)S(1)} %slice.179), channel_id=1, source_target_pairs={{0,1},{1,0},{2,3},{3,2},{4,5},{5,4},{6,7},{7,6},{8,9},{9,8},{10,11... | collective-permute-start | bytes 884744 | tf_op jit(solution)/shard_map/ppermute | solution.py:446
  197.0 12.4 %collective-permute-start.59 = (bf16[192,768]{1,0:T(8,128)(2,1)S(1)}, bf16[192,768]{1,0:T(8,128)(2,1)}, u32[]{:S(2)}, u32[]{:S(2)}) collective-permute-start(bf16[192,768]{1,0:T(8,128)(2,1)S(1)} %slice.180), channel_id=1, source_target_pairs={{0,4},{2,6},{4,0},{6,2},{8,12},{10,14},{12,8},{14,10},{16,20},{18,... | collective-permute-start | bytes 884744 | tf_op jit(solution)/shard_map/ppermute | solution.py:442
  222.8 37.6 %collective-permute-start.66 = (bf16[384,768]{1,0:T(8,128)(2,1)}, bf16[384,768]{1,0:T(8,128)(2,1)S(1)}, u32[]{:S(2)}, u32[]{:S(2)}) collective-permute-start(bf16[384,768]{1,0:T(8,128)(2,1)} %get-tuple-element.780), channel_id=1, source_target_pairs={{0,1},{1,0},{2,3},{3,2},{4,5},{5,4},{6,7},{7,6},{8,9},{9,8},{10,11... | collective-permute-start | bytes 1769480 | tf_op jit(solution)/shard_map/ppermute | solution.py:446
  224.3 36.1 %collective-permute-start.67 = (bf16[384,768]{1,0:T(8,128)(2,1)}, bf16[384,768]{1,0:T(8,128)(2,1)}, u32[]{:S(2)}, u32[]{:S(2)}) collective-permute-start(bf16[384,768]{1,0:T(8,128)(2,1)} %get-tuple-element.781), channel_id=1, source_target_pairs={{0,4},{2,6},{4,0},{6,2},{8,12},{10,14},{12,8},{14,10},{16,20},{18,... | collective-permute-start | bytes 1769480 | tf_op jit(solution)/shard_map/ppermute | solution.py:442
  224.9 35.5 %collective-permute-start.68 = (bf16[384,768]{1,0:T(8,128)(2,1)S(1)}, bf16[384,768]{1,0:T(8,128)(2,1)}, u32[]{:S(2)}, u32[]{:S(2)}) collective-permute-start(bf16[384,768]{1,0:T(8,128)(2,1)S(1)} %get-tuple-element.782), channel_id=1, source_target_pairs={{0,5},{1,4},{2,7},{3,6},{4,1},{5,0},{6,3},{7,2},{8,13},{9,12},{10,... | collective-permute-start | bytes 1769480 | tf_op jit(solution)/shard_map/ppermute | solution.py:446
  262.7 25.9 %collective-permute-start.69 = (bf16[96,768]{1,0:T(8,128)(2,1)}, bf16[96,768]{1,0:T(8,128)(2,1)S(1)}, u32[]{:S(2)}, u32[]{:S(2)}) collective-permute-start(bf16[96,768]{1,0:T(8,128)(2,1)} %get-tuple-element.832), channel_id=1, source_target_pairs={{0,8},{2,10},{4,12},{6,14},{8,0},{10,2},{12,4},{14,6},{16,24},{18,... | collective-permute-start | bytes 442376 | tf_op jit(solution)/shard_map/ppermute | solution.py:442
  264.0 24.6 %collective-permute-start.70 = (bf16[96,768]{1,0:T(8,128)(2,1)}, bf16[96,768]{1,0:T(8,128)(2,1)S(1)}, u32[]{:S(2)}, u32[]{:S(2)}) collective-permute-start(bf16[96,768]{1,0:T(8,128)(2,1)} %get-tuple-element.833), channel_id=1, source_target_pairs={{0,16},{2,18},{4,20},{6,22},{8,24},{10,26},{12,28},{14,30},{16,0},... | collective-permute-start | bytes 442376 | tf_op jit(solution)/shard_map/ppermute | solution.py:442
  267.0 21.6 %collective-permute-start.71 = (bf16[96,768]{1,0:T(8,128)(2,1)}, bf16[96,768]{1,0:T(8,128)(2,1)S(1)}, u32[]{:S(2)}, u32[]{:S(2)}) collective-permute-start(bf16[96,768]{1,0:T(8,128)(2,1)} %get-tuple-element.834), channel_id=1, source_target_pairs={{0,24},{2,26},{4,28},{6,30},{8,16},{10,18},{12,20},{14,22},{16,8},... | collective-permute-start | bytes 442376 | tf_op jit(solution)/shard_map/ppermute | solution.py:442
  290.3 10.3 %collective-permute-start.81 = (bf16[96,768]{1,0:T(8,128)(2,1)S(1)}, bf16[96,768]{1,0:T(8,128)(2,1)}, u32[]{:S(2)}, u32[]{:S(2)}) collective-permute-start(bf16[96,768]{1,0:T(8,128)(2,1)S(1)} %fusion.17), channel_id=1, source_target_pairs={{0,16},{2,18},{4,20},{6,22},{8,24},{10,26},{12,28},{14,30},{16,0},... | collective-permute-start | bytes 442376 | tf_op jit(solution)/shard_map/ppermute | solution.py:442
  293.3 19.4 %collective-permute-start.77 = (bf16[480,768]{1,0:T(8,128)(2,1)S(1)}, bf16[480,768]{1,0:T(8,128)(2,1)S(1)}, u32[]{:S(2)}, u32[]{:S(2)}) collective-permute-start(bf16[480,768]{1,0:T(8,128)(2,1)S(1)} %get-tuple-element.861), channel_id=1, source_target_pairs={{0,1},{1,0},{2,3},{3,2},{4,5},{5,4},{6,7},{7,6},{8,9},{9,8},{10,11... | collective-permute-start | bytes 2211848 | tf_op jit(solution)/shard_map/ppermute | solution.py:446
  294.7 35.9 %collective-permute-start.78 = (bf16[480,768]{1,0:T(8,128)(2,1)}, bf16[480,768]{1,0:T(8,128)(2,1)}, u32[]{:S(2)}, u32[]{:S(2)}) collective-permute-start(bf16[480,768]{1,0:T(8,128)(2,1)} %get-tuple-element.862), channel_id=1, source_target_pairs={{0,4},{2,6},{4,0},{6,2},{8,12},{10,14},{12,8},{14,10},{16,20},{18,... | collective-permute-start | bytes 2211848 | tf_op jit(solution)/shard_map/ppermute | solution.py:442
  295.3 35.3 %collective-permute-start.79 = (bf16[480,768]{1,0:T(8,128)(2,1)}, bf16[480,768]{1,0:T(8,128)(2,1)}, u32[]{:S(2)}, u32[]{:S(2)}) collective-permute-start(bf16[480,768]{1,0:T(8,128)(2,1)} %get-tuple-element.863), channel_id=1, source_target_pairs={{0,5},{1,4},{2,7},{3,6},{4,1},{5,0},{6,3},{7,2},{8,13},{9,12},{10,... | collective-permute-start | bytes 2211848 | tf_op jit(solution)/shard_map/ppermute | solution.py:446
  300.6 32.6 %collective-permute-start.74 = (bf16[96,1152]{1,0:T(8,128)(2,1)}, bf16[96,1152]{1,0:T(8,128)(2,1)S(1)}, u32[]{:S(2)}, u32[]{:S(2)}) collective-permute-start(bf16[96,1152]{1,0:T(8,128)(2,1)} %get-tuple-element.858), channel_id=1, source_target_pairs={{0,1},{1,0},{2,3},{3,2},{4,5},{5,4},{6,7},{7,6},{8,9},{9,8},{10,11... | collective-permute-start | bytes 663560 | tf_op jit(solution)/shard_map/ppermute | solution.py:446
  305.6 32.5 %collective-permute-start.75 = (bf16[96,1152]{1,0:T(8,128)(2,1)}, bf16[96,1152]{1,0:T(8,128)(2,1)S(1)}, u32[]{:S(2)}, u32[]{:S(2)}) collective-permute-start(bf16[96,1152]{1,0:T(8,128)(2,1)} %get-tuple-element.859), channel_id=1, source_target_pairs={{0,4},{2,6},{4,0},{6,2},{8,12},{10,14},{12,8},{14,10},{16,20},{18,... | collective-permute-start | bytes 663560 | tf_op jit(solution)/shard_map/ppermute | solution.py:442
  313.6 24.5 %collective-permute-start.76 = (bf16[96,1152]{1,0:T(8,128)(2,1)}, bf16[96,1152]{1,0:T(8,128)(2,1)}, u32[]{:S(2)}, u32[]{:S(2)}) collective-permute-start(bf16[96,1152]{1,0:T(8,128)(2,1)} %get-tuple-element.860), channel_id=1, source_target_pairs={{0,5},{1,4},{2,7},{3,6},{4,1},{5,0},{6,3},{7,2},{8,13},{9,12},{10,... | collective-permute-start | bytes 663560 | tf_op jit(solution)/shard_map/ppermute | solution.py:446
  343.0 24.1 %collective-permute-start.86 = (bf16[384,1152]{1,0:T(8,128)(2,1)}, bf16[384,1152]{1,0:T(8,128)(2,1)S(1)}, u32[]{:S(2)}, u32[]{:S(2)}) collective-permute-start(bf16[384,1152]{1,0:T(8,128)(2,1)} %get-tuple-element.891), channel_id=1, source_target_pairs={{0,2},{2,0},{4,6},{6,4},{8,10},{10,8},{12,14},{14,12},{16,18},{18,... | collective-permute-start | bytes 2654216 | tf_op jit(solution)/shard_map/ppermute | solution.py:442
  343.1 24.0 %collective-permute-start.90 = (bf16[384,768]{1,0:T(8,128)(2,1)S(1)}, bf16[384,768]{1,0:T(8,128)(2,1)S(1)}, u32[]{:S(2)}, u32[]{:S(2)}) collective-permute-start(bf16[384,768]{1,0:T(8,128)(2,1)S(1)} %bitcast.343), channel_id=1, source_target_pairs={{0,4},{2,6},{4,0},{6,2},{8,12},{10,14},{12,8},{14,10},{16,20},{18,... | collective-permute-start | bytes 1769480 | tf_op jit(solution)/shard_map/ppermute | solution.py:442
  348.1 18.9 %collective-permute-start.87 = (bf16[120,768]{1,0:T(8,128)(2,1)}, bf16[120,768]{1,0:T(8,128)(2,1)}, u32[]{:S(2)}, u32[]{:S(2)}) collective-permute-start(bf16[120,768]{1,0:T(8,128)(2,1)} %get-tuple-element.892), channel_id=1, source_target_pairs={{0,8},{2,10},{4,12},{6,14},{8,0},{10,2},{12,4},{14,6},{16,24},{18,... | collective-permute-start | bytes 552968 | tf_op jit(solution)/shard_map/ppermute | solution.py:442
  352.2 14.8 %collective-permute-start.88 = (bf16[120,768]{1,0:T(8,128)(2,1)S(1)}, bf16[120,768]{1,0:T(8,128)(2,1)}, u32[]{:S(2)}, u32[]{:S(2)}) collective-permute-start(bf16[120,768]{1,0:T(8,128)(2,1)S(1)} %get-tuple-element.893), channel_id=1, source_target_pairs={{0,16},{2,18},{4,20},{6,22},{8,24},{10,26},{12,28},{14,30},{16,0},... | collective-permute-start | bytes 552968 | tf_op jit(solution)/shard_map/ppermute | solution.py:442
  352.2 14.8 %collective-permute-start.89 = (bf16[120,768]{1,0:T(8,128)(2,1)S(1)}, bf16[120,768]{1,0:T(8,128)(2,1)}, u32[]{:S(2)}, u32[]{:S(2)}) collective-permute-start(bf16[120,768]{1,0:T(8,128)(2,1)S(1)} %get-tuple-element.894), channel_id=1, source_target_pairs={{0,24},{2,26},{4,28},{6,30},{8,16},{10,18},{12,20},{14,22},{16,8},... | collective-permute-start | bytes 552968 | tf_op jit(solution)/shard_map/ppermute | solution.py:442
  377.7 35.3 %collective-permute-start.100 = (bf16[2,384,768]{2,1,0:T(8,128)(2,1)}, bf16[2,384,768]{2,1,0:T(8,128)(2,1)}, u32[]{:S(2)}, u32[]{:S(2)}) collective-permute-start(bf16[2,384,768]{2,1,0:T(8,128)(2,1)} %pad_maximum_fusion.2), channel_id=1, source_target_pairs={{0,2},{2,0},{4,6},{6,4},{8,10},{10,8},{12,14},{14,12},{16,18},{18,... | collective-permute-start | bytes 3538952 | tf_op jit(solution)/shard_map/ppermute | solution.py:442
  377.8 21.4 %collective-permute-start.97 = (bf16[120,768]{1,0:T(8,128)(2,1)S(1)}, bf16[120,768]{1,0:T(8,128)(2,1)S(1)}, u32[]{:S(2)}, u32[]{:S(2)}) collective-permute-start(bf16[120,768]{1,0:T(8,128)(2,1)S(1)} %fusion.14), channel_id=1, source_target_pairs={{0,8},{2,10},{4,12},{6,14},{8,0},{10,2},{12,4},{14,6},{16,24},{18,... | collective-permute-start | bytes 552968 | tf_op jit(solution)/shard_map/ppermute | solution.py:442
  381.6 18.7 %collective-permute-start.98 = (bf16[120,768]{1,0:T(8,128)(2,1)S(1)}, bf16[120,768]{1,0:T(8,128)(2,1)S(1)}, u32[]{:S(2)}, u32[]{:S(2)}) collective-permute-start(bf16[120,768]{1,0:T(8,128)(2,1)S(1)} %fusion.14), channel_id=1, source_target_pairs={{0,16},{2,18},{4,20},{6,22},{8,24},{10,26},{12,28},{14,30},{16,0},... | collective-permute-start | bytes 552968 | tf_op jit(solution)/shard_map/ppermute | solution.py:442
  381.6 10.1 %collective-permute-start.91 = (bf16[24,1152]{1,0:T(8,128)(2,1)S(1)}, bf16[24,1152]{1,0:T(8,128)(2,1)S(1)}, u32[]{:S(2)}, u32[]{:S(2)}) collective-permute-start(bf16[24,1152]{1,0:T(8,128)(2,1)S(1)} %fusion.23), channel_id=1, source_target_pairs={{0,8},{2,10},{4,12},{6,14},{8,0},{10,2},{12,4},{14,6},{16,24},{18,... | collective-permute-start | bytes 165896 | tf_op jit(solution)/shard_map/ppermute | solution.py:442
  383.7 12.5 %collective-permute-start.92 = (bf16[24,1152]{1,0:T(8,128)(2,1)S(1)}, bf16[24,1152]{1,0:T(8,128)(2,1)S(1)}, u32[]{:S(2)}, u32[]{:S(2)}) collective-permute-start(bf16[24,1152]{1,0:T(8,128)(2,1)S(1)} %fusion.23), channel_id=1, source_target_pairs={{0,16},{2,18},{4,20},{6,22},{8,24},{10,26},{12,28},{14,30},{16,0},... | collective-permute-start | bytes 165896 | tf_op jit(solution)/shard_map/ppermute | solution.py:442
  396.2 16.8 %collective-permute-start.94 = (bf16[96,1152]{1,0:T(8,128)(2,1)S(1)}, bf16[96,1152]{1,0:T(8,128)(2,1)S(1)}, u32[]{:S(2)}, u32[]{:S(2)}) collective-permute-start(bf16[96,1152]{1,0:T(8,128)(2,1)S(1)} %get-tuple-element.944), channel_id=1, source_target_pairs={{0,1},{1,0},{2,3},{3,2},{4,5},{5,4},{6,7},{7,6},{8,9},{9,8},{10,11... | collective-permute-start | bytes 663560 | tf_op jit(solution)/shard_map/ppermute | solution.py:446
  397.7 15.3 %collective-permute-start.95 = (bf16[96,1152]{1,0:T(8,128)(2,1)S(1)}, bf16[96,1152]{1,0:T(8,128)(2,1)}, u32[]{:S(2)}, u32[]{:S(2)}) collective-permute-start(bf16[96,1152]{1,0:T(8,128)(2,1)S(1)} %get-tuple-element.945), channel_id=1, source_target_pairs={{0,4},{2,6},{4,0},{6,2},{8,12},{10,14},{12,8},{14,10},{16,20},{18,... | collective-permute-start | bytes 663560 | tf_op jit(solution)/shard_map/ppermute | solution.py:442
  399.1 13.9 %collective-permute-start.96 = (bf16[96,1152]{1,0:T(8,128)(2,1)S(1)}, bf16[96,1152]{1,0:T(8,128)(2,1)}, u32[]{:S(2)}, u32[]{:S(2)}) collective-permute-start(bf16[96,1152]{1,0:T(8,128)(2,1)S(1)} %get-tuple-element.946), channel_id=1, source_target_pairs={{0,5},{1,4},{2,7},{3,6},{4,1},{5,0},{6,3},{7,2},{8,13},{9,12},{10,... | collective-permute-start | bytes 663560 | tf_op jit(solution)/shard_map/ppermute | solution.py:446
  401.0 12.0 %collective-permute-start.99 = (bf16[120,768]{1,0:T(8,128)(2,1)S(1)}, bf16[120,768]{1,0:T(8,128)(2,1)}, u32[]{:S(2)}, u32[]{:S(2)}) collective-permute-start(bf16[120,768]{1,0:T(8,128)(2,1)S(1)} %fusion.14), channel_id=1, source_target_pairs={{0,24},{2,26},{4,28},{6,30},{8,16},{10,18},{12,20},{14,22},{16,8},... | collective-permute-start | bytes 552968 | tf_op jit(solution)/shard_map/ppermute | solution.py:442
  416.4 21.9 %collective-permute-start.106 = (bf16[480,768]{1,0:T(8,128)(2,1)S(1)}, bf16[480,768]{1,0:T(8,128)(2,1)}, u32[]{:S(2)}, u32[]{:S(2)}) collective-permute-start(bf16[480,768]{1,0:T(8,128)(2,1)S(1)} %bitcast.336), channel_id=1, source_target_pairs={{0,4},{2,6},{4,0},{6,2},{8,12},{10,14},{12,8},{14,10},{16,20},{18,... | collective-permute-start | bytes 2211848 | tf_op jit(solution)/shard_map/ppermute | solution.py:442
  417.1 20.5 %collective-permute-start.102 = (bf16[96,1152]{1,0:T(8,128)(2,1)S(1)}, bf16[96,1152]{1,0:T(8,128)(2,1)S(1)}, u32[]{:S(2)}, u32[]{:S(2)}) collective-permute-start(bf16[96,1152]{1,0:T(8,128)(2,1)S(1)} %bitcast.359), channel_id=1, source_target_pairs={{0,4},{2,6},{4,0},{6,2},{8,12},{10,14},{12,8},{14,10},{16,20},{18,... | collective-permute-start | bytes 663560 | tf_op jit(solution)/shard_map/ppermute | solution.py:442
  443.1 12.1 %collective-permute-start.112 = (bf16[2,480,768]{2,1,0:T(8,128)(2,1)}, bf16[2,480,768]{2,1,0:T(8,128)(2,1)}, u32[]{:S(2)}, u32[]{:S(2)}) collective-permute-start(bf16[2,480,768]{2,1,0:T(8,128)(2,1)} %pad_maximum_fusion.1), channel_id=1, source_target_pairs={{0,2},{2,0},{4,6},{6,4},{8,10},{10,8},{12,14},{14,12},{16,18},{18,... | collective-permute-start | bytes 4423688 | tf_op jit(solution)/shard_map/ppermute | solution.py:442
  443.1 12.1 %collective-permute-start.108 = (bf16[2,96,1152]{2,1,0:T(8,128)(2,1)S(1)}, bf16[2,96,1152]{2,1,0:T(8,128)(2,1)S(1)}, u32[]{:S(2)}, u32[]{:S(2)}) collective-permute-start(bf16[2,96,1152]{2,1,0:T(8,128)(2,1)S(1)} %pad_maximum_fusion.7), channel_id=1, source_target_pairs={{0,2},{2,0},{4,6},{6,4},{8,10},{10,8},{12,14},{14,12},{16,18},{18,... | collective-permute-start | bytes 1327112 | tf_op jit(solution)/shard_map/ppermute | solution.py:442
  (152 other events, 1324.1 us)

commit v3 on v2

--- a/solution.py
+++ b/solution.py
@@ -276,37 +276,36 @@
 def proj_terms(place, g_t, dout):
     hidden, length = g_t.shape
     width = dout.shape[1]
-    rows = hidden // 8
+    rows = hidden // 4
 
     def kernel(place_ref, g_ref, dout_ref, send_ref, keep_ref):
         value = dot(g_ref[...], dout_ref[...]).astype(bf16)
 
-        @pl.when(pl.program_id(0) < 4)
+        @pl.when(pl.program_id(0) < 2)
         def _():
             send_ref[...] = value
 
-        @pl.when(pl.program_id(0) >= 4)
+        @pl.when(pl.program_id(0) >= 2)
         def _():
             keep_ref[...] = value
 
     def block(i, place_ref):
-        core = jnp.where(i < 4, 1 - place_ref[0], place_ref[0])
-        j = i % 4
-        return 4 * (j // 2) + 2 * core + j % 2, 0
+        core = jnp.where(i < 2, 1 - place_ref[0], place_ref[0])
+        return 2 * (i % 2) + core, 0
 
     out = jax.ShapeDtypeStruct((hidden // 2, width), bf16)
     return pl.pallas_call(
         kernel,
         grid_spec=pltpu.PrefetchScalarGridSpec(
             num_scalar_prefetch=1,
-            grid=(8,),
+            grid=(4,),
             in_specs=[
                 pl.BlockSpec((rows, length), block),
                 pl.BlockSpec((length, width), lambda i, p: (0, 0)),
             ],
             out_specs=[
-                pl.BlockSpec((rows, width), lambda i, p: (jnp.minimum(i, 3), 0)),
-                pl.BlockSpec((rows, width), lambda i, p: (jnp.maximum(i - 4, 0), 0)),
+                pl.BlockSpec((rows, width), lambda i, p: (jnp.minimum(i, 1), 0)),
+                pl.BlockSpec((rows, width), lambda i, p: (jnp.maximum(i - 2, 0), 0)),
             ],
         ),
         out_shape=[out, out],
@@ -319,7 +318,7 @@
 def back_middle(place, dout, slope, y1, mixed, h2_t, vec, w_out, w_fc, w_proj):
     length, width = dout.shape
     hidden = w_fc.width
-    step_rows, part = 256, 512
+    step_rows, part = 256, PART
     steps = length // step_rows
     f_steps, rows = hidden // width, width // 8
     weights = (w_out, w_fc, w_proj)
@@ -435,7 +434,7 @@
         self.o_core, self.o_y, self.o_z = owner & 1, (owner >> 1) & 1, owner >> 2
         self.x = lax.axis_index("narrow")
         self.holder = mine == owner
-        spot = jnp.stack([self.core, self.x, self.y]).astype(jnp.int32)
+        spot = jnp.stack([self.core, self.x, self.y, self.holder]).astype(jnp.int32)
         self.spot = jnp.zeros_like(spot) if plain else spot
 
     def swap(self, value, flip):
@@ -444,6 +443,30 @@
     def cross(self, value, flip):
         pairs = [(2 * i + j, 2 * (i ^ flip) + 1 - j) for i in range(self.wide) for j in range(2)]
         return lax.ppermute(value, AXES, pairs)
+
+    def shift(self, value, pairs):
+        places = [(4 * a + low, 4 * b + low) for a, b in pairs for low in range(4)]
+        return lax.ppermute(value, "wide", places)
+
+    def z_pairs(self):
+        last = self.deep - 1
+        return [((i, i + 1), (last - i, last - i - 1)) for i in range(self.deep // 2 - 1)]
+
+    def deal(self, value, kind):
+        if kind == "plane":
+            groups = [
+                [2 * (4 * z + 2 * y + core) + x for x in range(2) for y in range(2)]
+                for z in range(self.deep)
+                for core in range(2)
+            ]
+            return lax.all_to_all(
+                value, AXES, 0, 0, axis_index_groups=groups, tiled=True
+            )
+        groups = [
+            [4 * z + 2 * y + core for y in range(2) for z in range(self.deep)]
+            for core in range(2)
+        ]
+        return lax.all_to_all(value, "wide", 0, 0, axis_index_groups=groups, tiled=True)
 
     def z_flips(self):
         step = self.deep // 2
@@ -527,6 +550,7 @@
 
 
 ROWS = 256
+PART = 1024
 
 
 def by_rows(name, body, place, blocks, wholes, weights, out_blocks, out_sums):
@@ -595,19 +619,26 @@
         self.ask(name, next(chain))
 
     def exchange(self, value, flip):
+        if isinstance(flip, tuple):
+            return self.place.shift(value, flip)
+        if isinstance(flip, str):
+            return self.place.deal(value, flip)
         if flip <= 0:
             return self.place.cross(value, -flip)
         return self.place.swap(value, flip)
 
-    def slot(self, names="", hold="", work=None, given=()):
-        names, hold = names.split(), hold.split()
+    def slot(self, names="", hold="", work=None, given=(), strict=False):
+        names = list(self.asked) if names == "all" else names.replace(",", " ").split()
+        hold = hold.split()
         assert not set(names) & set(self.going)
         asked = {name: self.asked[name] for name in names if name in self.asked}
-        held = tie({"asked": asked, "given": given})
-        for name, values in held["asked"].items():
+        if strict:
+            asked = tie(asked)
+        for name, values in asked.items():
             self.going[name] = [
                 self.exchange(value, flip) for value, flip in zip(values, self.flips[name])
             ]
+        held = tie({"asked": asked, "given": given})
         result = work(*held["given"]) if work else ()
         ready = {name: got for name, got in self.going.items() if name not in hold}
         ready, result, self.asked = tie((ready, result, self.asked))
@@ -632,23 +663,125 @@
     return functools.reduce(lambda a, b: a + b, [v.astype(f32) for v in values]).astype(bf16)
 
 
-def collect_steps(place, keep, send):
-    width, deep = keep.shape[-1], place.deep
+def collect_steps(place, keep, send, plane, line):
+    width = keep.shape[-1]
     (other,) = yield [(send, 1)]
-    now = add(keep, other).reshape(4, -1, width)
-    spot = 2 * place.x + place.y
-    got = yield [(pick(now, spot ^ 2), 0), (pick(now, spot ^ 1), 2), (pick(now, spot ^ 3), -2)]
-    now = add(pick(now, spot), *got).reshape(deep, -1, width)
-    got = yield [(pick(now, place.z ^ i), 4 * i) for i in range(1, deep)]
-    now = add(pick(now, place.z), *got)
-    got = yield [(now, 4 * i) for i in range(1, deep)]
-    now = jnp.stack(
-        [lax.select_n(place.z ^ i, now, *got) for i in range(deep)]
-    ).reshape(-1, width)
+    if plane == "deal":
+        (got,) = yield [(add(keep, other).reshape(-1, width), "plane")]
+        now = add(*got.reshape(4, -1, width))
+    else:
+        terms = [v.reshape(2, 2, -1, width) for v in (keep, other)]
+        at_x = lambda v, i: pick(v, place.x ^ i)
+        at_y = lambda v, i: lax.dynamic_index_in_dim(v, place.y ^ i, axis=1, keepdims=False)
+        if plane == "turn":
+            (other,) = yield [(add(*[at_x(v, 1) for v in terms]), 0)]
+            terms = [at_x(v, 0) for v in terms] + [other]
+            part = lambda i: add(*[pick(v, place.y ^ i) for v in terms])
+            (other,) = yield [(part(1), 2)]
+            now = add(part(0), other)
+        else:
+            cut = terms[0].shape[2] // 2
+            upper = [v[:, :, :cut] for v in terms]
+            lower = [v[:, :, cut:] for v in terms]
+            by_x, by_y = yield [
+                (add(*[at_x(v, 1) for v in upper]), 0),
+                (add(*[at_y(v, 1) for v in lower]), 2),
+            ]
+            upper = [at_x(v, 0) for v in upper] + [by_x]
+            lower = [at_y(v, 0) for v in lower] + [by_y]
+            top = lambda i: add(*[pick(v, place.y ^ i) for v in upper])
+            low = lambda i: add(*[pick(v, place.x ^ i) for v in lower])
+            by_y, by_x = yield [(top(1), 2), (low(1), 0)]
+            now = jnp.concatenate([add(top(0), by_y), add(low(0), by_x)], axis=0)
+    if line:
+        inward = place.z_pairs()
+        for pairs in inward:
+            (other,) = yield [(now, pairs)]
+            now = add(now, other)
+        half = place.deep // 2
+        (other,) = yield [(now, ((half - 1, half), (half, half - 1)))]
+        now = add(now, other)
+        for pairs in reversed(inward):
+            (other,) = yield [(now, tuple((b, a) for a, b in pairs))]
+            got = (place.z == pairs[0][0]) | (place.z == pairs[1][0])
+            now = jnp.where(got, other, now)
+    else:
+        for step in reversed(list(place.z_flips())):
+            (other,) = yield [(now, 4 * step)]
+            now = add(now, other)
     (other,) = yield [(now, 2)]
-    now = ordered(now, other, place.y)
-    (other,) = yield [(now, 1)]
-    return ordered(now, other, place.core).reshape(-1, width)
+    far, far_other = yield [(now, 1), (other, 1)]
+    return [now, other, far, far_other]
+
+
+def put_kernel(place_ref, *refs, counts, bodies):
+    refs = list(refs)
+    take = lambda n: [refs.pop(0) for _ in range(n)]
+    pieces = [take(4) for _ in range(counts[0])]
+    outs = take(counts[1])
+    buffers, sem = take(counts[0]), refs[0]
+    copies = []
+    for group, buffer in zip(pieces, buffers):
+        for i, ref in enumerate(group):
+            rows = ref.shape[0]
+            at = 2 * (place_ref[0] ^ (i // 2)) + (place_ref[2] ^ (i % 2))
+            target = buffer.at[pl.ds(pl.multiple_of(at * rows, 16), rows), :]
+            copies.append(pltpu.make_async_copy(ref, target, sem.at[len(copies)]))
+    for copy in copies:
+        copy.start()
+    for copy in copies:
+        copy.wait()
+    holder = place_ref[3] == 1
+    bodies(buffers, outs, lambda v: jnp.where(holder, v.astype(f32), 0.0))
+
+
+def put(place, groups, bodies, shapes, name):
+    flat = [v for group in groups for v in group]
+    return pl.pallas_call(
+        functools.partial(put_kernel, counts=(len(groups), len(shapes)), bodies=bodies),
+        in_specs=[pl.BlockSpec(memory_space=pltpu.SMEM)]
+        + [pl.BlockSpec(memory_space=pl.ANY)] * len(flat),
+        out_specs=[pl.BlockSpec(memory_space=pltpu.VMEM)] * len(shapes),
+        out_shape=[jax.ShapeDtypeStruct(v, f32) for v in shapes],
+        scratch_shapes=[
+            pltpu.VMEM((4 * group[0].shape[0], group[0].shape[1]), bf16) for group in groups
+        ]
+        + [pltpu.SemaphoreType.DMA((len(flat),))],
+        compiler_params=pltpu.CompilerParams(vmem_limit_bytes=VMEM),
+        cost_estimate=TINY,
+        name=name,
+    )(place.spot, *flat)
+
+
+def put_rows(buffers, outs, mask):
+    outs[0][...] = mask(buffers[0][...])
+
+
+def put_wide(buffers, outs, mask):
+    wide, narrow = outs
+    rows = narrow.shape[0] // 4
+    width = narrow.shape[1]
+    blocks = wide.shape[1] // width
+    for quarter in range(4):
+        here = slice(quarter * rows, (quarter + 1) * rows)
+        for i in range(blocks + 1):
+            start = (quarter * (blocks + 1) + i) * rows
+            value = mask(buffers[0][start : start + rows, :])
+            if i < blocks:
+                wide[here, i * width : (i + 1) * width] = value
+            else:
+                narrow[here, :] = value
+
+
+def put_pairs(buffers, outs, mask):
+    width = outs[0].shape[1] // 3
+    for part, buffer in enumerate(buffers):
+        pairs = buffer.shape[1] // 384
+        for p in range(pairs):
+            for j in range(3):
+                at = j * width + (part * pairs + p) * 128
+                source = (3 * p + j) * 128
+                outs[0][:, at : at + 128] = mask(buffer[:, source : source + 128])
 
 
 def unpack_vectors(now, sizes):
@@ -669,8 +802,7 @@
     return jnp.concatenate(out, axis=1)
 
 
-def collect_vectors_steps(place, vectors):
-    now = shares(vectors, 2).reshape(2, -1, 128)
+def collect_vectors_steps(place, now):
     (other,) = yield [(now, 1)]
     now = now + other
     (other,) = yield [(pick(now, 1 - place.x), 0)]
@@ -793,9 +925,9 @@
     y1_ref[...] = y1
     h2 = norm_rows(y1, row_of(vec, GAIN2), row_of(vec, SHIFT2)).astype(bf16)
     h2_t_ref[...] = h2.T
-    for at in range(0, w_fc.shape[1], 512):
-        here = slice(at, at + 512)
-        g, slope = gelu_both(dot(h2, w_fc[:, here]) + row_of(vec, FCB, at // 128, 4))
+    for at in range(0, w_fc.shape[1], PART):
+        here = slice(at, at + PART)
+        g, slope = gelu_both(dot(h2, w_fc[:, here]) + row_of(vec, FCB, at // 128, PART // 128))
         g_t_ref[here, :] = g.astype(bf16).T
         slope_ref[:, here] = slope.astype(bf16)
 
@@ -807,7 +939,7 @@
 
 
 def back_first_body(blocks, wholes, weights, outs, sums):
-    (dqkv_ref, x_ref, dy1_ref), (vec,), (w_a, w_b) = blocks, wholes, weights
+    (dqkv_ref, x_ref, dy1_ref), (vec, *more), (w_a, w_b) = blocks, wholes, weights
     side = w_b.shape[1]
     dqkv = dqkv_ref[...]
     dh1 = dot(dqkv[:, :side], w_a[:, :side], ((1,), (1,)))
@@ -818,6 +950,18 @@
     parts = [total[:, p * 384 + j : p * 384 + j + 128] for j in (0, 256) for p in range(H // 2)]
     for ref, value in zip(sums, (gain, shift, jnp.concatenate(parts, axis=1))):
         ref[...] += value
+
+    @pl.when(pl.program_id(0) == pl.num_programs(0) - 1)
+    def _():
+        found = sums[:3] + more
+        at = 0
+        for half in range(2):
+            for ref in found:
+                count = ref.shape[1] // 256
+                for i in range(count):
+                    start = (half * count + i) * 128
+                    sums[3][at : at + 1, :] = ref[:, start : start + 128]
+                    at += 1
 
 
 def on_device(
@@ -855,11 +999,11 @@
         else:
             steps.add(name, spread_steps(place, shard))
 
-    def end(name, keep, send):
+    def end(name, keep, send, plane, line):
         if plain:
             steps.done[name] = collect_plain(place, keep, send)
         else:
-            steps.add(name, collect_steps(place, keep, send))
+            steps.add(name, collect_steps(place, keep, send, plane, line))
 
     steps = Steps(place)
     vectors = (ln1_gain, ln1_bias, qv_bias, out_bias, ln2_gain, ln2_bias, fc_bias, proj_bias)
@@ -902,13 +1046,13 @@
 
         return dict(work=run, given=(blocks, wholes, [w.arrays for w in weights]))
 
-    steps.slot("qa qb")
-    steps.slot("qa o f p")
-    steps.slot("qa qb o")
-    steps.slot("qa qb f", hold="qb f")
-    steps.slot("qa", hold="f")
-    steps.slot("qa qb o")
-    steps.slot("qa qb f p", hold="f p")
+    steps.slot("qa qb", strict=True)
+    steps.slot("qa", strict=True)
+    steps.slot("qa,qb,o,f,p", strict=True)
+    steps.slot("qa qb o f", hold="qb f", strict=True)
+    steps.slot("qa", hold="f", strict=True)
+    steps.slot("qa qb o", strict=True)
+    steps.slot("qa qb f p", hold="f p", strict=True)
     state = steps.slot("qb o", **attention(x, vec, "qa", 0, 0, 2, None))
     state, (h1, h1_t, vec) = list(state[:3]), state[3:]
     state = steps.slot(
@@ -940,7 +1084,7 @@
     p_send, p_keep = steps.slot(
         "p", work=lambda g_t, dout: proj_terms(place, g_t, dout), given=(g_t, dout)
     )
-    end("dp", p_keep, p_send)
+    end("dp", p_keep, p_send, "deal", True)
     steps.slot("p dp")
     w_proj = steps.done["p"]
 
@@ -954,7 +1098,7 @@
         given=(dout, slope, y1, mixed, h2_t, vec, [w.arrays for w in (w_out, w_fc, w_proj)]),
     )
     dmixed, dy1, f_send, f_keep, d_gain2, d_shift2, d_outb, d_fcb, d_projb = found
-    end("df", f_keep, f_send)
+    end("df", f_keep, f_send, "halves", True)
 
     def heads_back(first, count, before):
         def run(qkv, mixed, dmixed, soft, h1_t, before):
@@ -962,20 +1106,18 @@
 
         return dict(work=run, given=(qkv, mixed, dmixed, soft, h1_t, before))
 
-    steps.slot("df dp", hold="dp")
-    dqkv, a_send, a_keep = steps.slot("df", hold="df", **heads_back(0, half, None))
-    end("da", a_keep, a_send)
-    steps.slot("da dp", hold="dp df")
-    dqkv, b_send, b_keep = steps.slot("da", **heads_back(half, half, dqkv))
-    end("db", b_keep, b_send)
-    sums = [(1, width), (1, width), (1, 2 * width)]
-    tokens_grad, d_gain1, d_shift1, d_qv = steps.slot(
-        "db df dp da",
+    dqkv, a_send, a_keep = steps.slot("df dp", **heads_back(0, half, None))
+    end("da", a_keep, a_send, "turn", False)
+    dqkv, b_send, b_keep = steps.slot("da df dp", **heads_back(half, half, dqkv))
+    end("db", b_keep, b_send, "turn", False)
+    sums = [(1, width), (1, width), (1, 2 * width), (72, 128)]
+    tokens_grad, d_gain1, d_shift1, d_qv, packed = steps.slot(
+        "all",
         **rows_work(
             "back_first",
             back_first_body,
             [dqkv, x, dy1],
-            [vec],
+            [vec, d_outb, d_gain2, d_shift2, d_fcb, d_projb],
             [w_a, w_b],
             [((length, width), bf16)],
             sums,
@@ -985,32 +1127,53 @@
     if plain:
         steps.done["dv"] = collect_vectors_plain(place, small)
     else:
-        steps.add("dv", collect_vectors_steps(place, small))
+        steps.add("dv", collect_vectors_steps(place, packed.reshape(2, -1, 128)))
     (block_out,) = steps.slot(
-        "db df dp da dv",
+        "all",
         **rows_work(
             "finish", finish_body, [y1, g_t], [vec], [w_proj], [((length, width), bf16)], []
         ),
     )
+    rows = width // 2
+    placed = {}
+    makers = {
+        "dp": (put_rows, [(hidden // 2, width)], "put_proj"),
+        "df": (put_wide, [(rows, hidden), (rows, width)], "put_fc"),
+    }
     while steps.asked:
-        steps.slot("db da df dp dv")
-
-    put = lambda v: jnp.where(place.holder, v.astype(f32), 0.0)
-    s_proj = put(steps.done["dp"])[None]
-    block = width // 8
-    found = steps.done["df"].reshape(-1, hidden // width + 1, block, width)
-    fc = [found[:, i].reshape(-1, width) for i in range(hidden // width)]
-    s_fc = put(jnp.concatenate(fc, axis=1))[None]
-    s_out = put(found[:, -1].reshape(-1, width))[None]
-    both = [
-        v[:, (3 * p + j) * 128 : (3 * p + j + 1) * 128]
-        for j in range(3)
-        for v in (steps.done["da"], steps.done["db"])
-        for p in range(half)
-    ]
-    s_qkv = put(jnp.concatenate(both, axis=1))[None]
+        ready = [n for n in makers if n in steps.done and n not in placed and not plain]
+        if ready:
+            found = steps.done[ready[0]]
+            run = lambda *v: put(place, [v], *makers[ready[0]])
+            placed[ready[0]] = steps.slot("all", work=run, given=found)
+        else:
+            steps.slot("all")
+
+    held = lambda v: jnp.where(place.holder, v.astype(f32), 0.0)
+    if plain:
+        s_proj = held(steps.done["dp"])
+        found = steps.done["df"].reshape(-1, hidden // width + 1, width // 8, width)
+        fc = [found[:, i].reshape(-1, width) for i in range(hidden // width)]
+        s_fc = held(jnp.concatenate(fc, axis=1))
+        s_out = held(found[:, -1].reshape(-1, width))
+        both = [
+            v[:, (3 * p + j) * 128 : (3 * p + j + 1) * 128]
+            for j in range(3)
+            for v in (steps.done["da"], steps.done["db"])
+            for p in range(half)
+        ]
+        s_qkv = held(jnp.concatenate(both, axis=1))
+    else:
+        for name in makers:
+            if name not in placed:
+                placed[name] = put(place, [steps.done[name]], *makers[name])
+        (s_proj,), (s_fc, s_out) = placed["dp"], placed["df"]
+        parts = [steps.done["da"], steps.done["db"]]
+        (s_qkv,) = put(place, parts, put_pairs, [(rows, 3 * width)], "put_qkv")
+    s_proj, s_fc, s_out, s_qkv = s_proj[None], s_fc[None], s_out[None], s_qkv[None]
     small = unpack_vectors(steps.done["dv"], [v.shape[1] // narrow for v in small])
-    s_gain1, s_shift1, s_qv, s_outb, s_gain2, s_shift2, s_fcb, s_projb = [put(v) for v in small]
+    small = [held(v) for v in small]
+    s_gain1, s_shift1, s_qv, s_outb, s_gain2, s_shift2, s_fcb, s_projb = small
     return (
         block_out[None],
         tokens_grad[None],

time: 480 us -> 451 us (0.940)
  other arithmetic: 47.5 us -> 32.5 us
  Pallas kernels: 177 us -> 189 us
  local copies, waits for them, and re-layouts: 27.1 us -> 16 us
  starting transfers between devices: 115 us -> 104 us
    ppermute x99 -> x83, starting transfers between devices: 92.3 us -> 71.6 us  [swap(): lax.ppermute(value, 'wide', [(i, i ^ flip) for i in range(self.wide)])]
    pallas_call x0 -> x3, Pallas kernels: none -> 14.5 us  [put(): pl.pallas_call(functools.partial(put_kernel, counts=(len(groups), len(sha...]
    ppermute x0 -> x6, starting transfers between devices: none -> 13.2 us  [shift(): return lax.ppermute(value, 'wide', places)]
    another operation x23 -> x1, other arithmetic: 10.8 us -> 0.65 us  [__init__(): spot = jnp.stack([self.core, self.x, self.y, self.holder]).astype(jnp.int32)]
    unnamed x229 -> x169, local copies, waits for them, and re-layouts: 12.2 us -> 2.91 us
    convert_element_type x12 -> x21, other arithmetic: 17.4 us -> 25.2 us  [add(): functools.reduce(lambda a, b: a + b, [v.astype(f32) for v in values])]
    ppermute x19 -> x15, starting transfers between devices: 22.7 us -> 15.2 us  [cross(): return lax.ppermute(value, AXES, pairs)]
    select_n x7 -> x5, other arithmetic: 10.3 us -> 3.12 us  [the longest x3 1.88 us: on_device(): held = lambda v: jnp.where(place.holder, v.astype(f32), 0.0)]
  transfers between devices with their start and end apart: 118 -> 105, of which waited for: 36 -> 34; matrix products, arithmetic and copies ran while one was open for 6% -> 8% of each run, Pallas kernels for 37% -> 41%
where the time goes in v3:
time: 451 us; the launch traced here: 447 us
  Pallas kernels  189 us (42%)
  starting transfers between devices  104 us (23%)
  waiting for transfers between devices  102 us (23%)
  other arithmetic  32.5 us (7%)
  local copies, waits for them, and re-layouts  16 us (4%)
    ppermute x83, waiting for transfers between devices, swap(): lax.ppermute(value, 'wide', [(i, i ^ flip) for i in range(self.wide)])  91.1 us
    ppermute x83, starting transfers between devices, swap(): lax.ppermute(value, 'wide', [(i, i ^ flip) for i in range(self.wide)])  71.6 us
    pallas_call x4, Pallas kernels, attend(): pl.pallas_call(kernel, grid=(count,), in_specs=[pl.BlockSpec(memory_space...  52.8 us
    pallas_call x3, Pallas kernels, by_rows(): pl.pallas_call(kernel, grid=(length // ROWS,), in_specs=[pl.BlockSpec(mem...  44 us
    pallas_call x1, Pallas kernels, back_middle(): pl.pallas_call(kernel, grid=(steps + f_steps + 1,), in_specs=[pl.BlockSpe...  33 us
    pallas_call x2, Pallas kernels, attend_back(): pl.pallas_call(functools.partial(attend_back_kernel, length=length), grid...  31.3 us
    convert_element_type x21, other arithmetic, add(): functools.reduce(lambda a, b: a + b, [v.astype(f32) for v in values])  25.2 us
    ppermute x15, starting transfers between devices, cross(): return lax.ppermute(value, AXES, pairs)  15.2 us
  transfers between devices with their start and end apart: 105, of which 34 were waited for; matrix products, arithmetic and copies ran while one was open for 8% of the time, Pallas kernels for 41%

profile of v3, /device:TPU:0, one launch (start us, length us, event | category | flops | bytes accessed | tf_op | source)
XLA Modules:
  0.0 446.5 jit_solution(9639614116971099934)
XLA Ops:
  2.0 2.9 pack.1
  5.4 2.5 dynamic-slice_bitcast_fusion
  9.8 3.0 collective-permute-start.2
  13.6 5.4 %collective-permute-done.2 = bf16[96,1280]{1,0:T(8,128)(2,1)S(1)} collective-permute-done((bf16[96,1280]{1,0:T(8,128)(2,1)S(1)}, bf16[96,1280]{1,0:T(8,128)(2,1)S(1)}, u32[]{:S(2)}, u32[]{:S(2)}) %collective-permute-start.2) | collective-permute-done | bytes 245792 | tf_op jit(solution)/shard_map/ppermute | solution.py:441
  19.7 2.8 collective-permute-start.6
  22.6 1.5 collective-permute-start.7
  24.1 6.3 %collective-permute-done.7 = bf16[96,1152]{1,0:T(8,128)(2,1)} collective-permute-done((bf16[96,1152]{1,0:T(8,128)(2,1)}, bf16[96,1152]{1,0:T(8,128)(2,1)}, u32[]{:S(2)}, u32[]{:S(2)}) %collective-permute-start.7) | collective-permute-done | bytes 221216 | tf_op jit(solution)/shard_map/ppermute | solution.py:441
  30.4 4.1 collective-permute-done.6
  36.4 2.4 collective-permute-start.9
  39.9 3.3 collective-permute-done.9
  44.0 2.4 collective-permute-start.11
  47.9 3.8 collective-permute-start.13
  51.8 9.8 %collective-permute-done.13 = bf16[96,1152]{1,0:T(8,128)(2,1)S(1)} collective-permute-done((bf16[96,1152]{1,0:T(8,128)(2,1)S(1)}, bf16[96,1152]{1,0:T(8,128)(2,1)S(1)}, u32[]{:S(2)}, u32[]{:S(2)}) %collective-permute-start.13) | collective-permute-done | bytes 221216 | tf_op jit(solution)/shard_map/ppermute | solution.py:441
  62.4 3.4 collective-permute-start.14
  66.7 4.0 collective-permute-done.15.refs_6_.refs_7_.refs_13_
  73.4 1.8 collective-permute-start.18
  75.2 1.6 collective-permute-start.27
  81.7 3.3 collective-permute-start.26
  88.8 17.4 %attend.4 = (bf16[1024,768]{1,0:T(8,128)(2,1)}, bf16[12,2304,256]{2,1,0:T(8,128)(2,1)}, bf16[1024,2304]{1,0:T(8,128)(2,1)}, bf16[1024,768]{1,0:T(8,128)(2,1)}, b...) custom-call(s32[4]{0:T(128)} %pad_add_fusion.core_ref.refs_0_.place_ref, s32[1024,1]{1,0:T(8,128)} %copy.40.refs_1_, ...), custom_call_target="tpu_custom_call" | custom-call | flops 1000 | bytes 1000 | tf_op jit(solution)/shard_map/attend/pallas_call | solution.py:142
  111.4 9.9 %attend.5 = (bf16[1024,768]{1,0:T(8,128)(2,1)}, bf16[12,2304,256]{2,1,0:T(8,128)(2,1)}, bf16[1024,2304]{1,0:T(8,128)(2,1)}) custom-call(s32[4]{0:T(128)} %pad_add_fusion.core_ref.refs_0_.place_ref, s32[1024,1]{1,0:T(8,128)} %copy.40.refs_1_, ...), custom_call_target="tpu_custom_call", output_to_operand_aliasing={{0}: (14, {}), {1}: (15, {}), {2}: (16, {})} | custom-call | flops 1000 | bytes 1000 | tf_op jit(solution)/shard_map/attend/pallas_call | solution.py:142
  121.3 2.9 collective-permute-start.42
  124.3 2.1 collective-permute-start.38
  127.0 1.6 collective-permute-start.40
  128.6 15.7 %attend.6 = (bf16[1024,768]{1,0:T(8,128)(2,1)}, bf16[12,2304,256]{2,1,0:T(8,128)(2,1)}, bf16[1024,2304]{1,0:T(8,128)(2,1)}) custom-call(s32[4]{0:T(128)} %pad_add_fusion.core_ref.refs_0_.place_ref, s32[1024,1]{1,0:T(8,128)} %copy.40.refs_1_, ...), custom_call_target="tpu_custom_call", output_to_operand_aliasing={{0}: (14, {}), {1}: (15, {}), {2}: (16, {})} | custom-call | flops 1000 | bytes 1000 | tf_op jit(solution)/shard_map/attend/pallas_call | solution.py:142
  144.3 6.1 %collective-permute-done.42 = bf16[384,768]{1,0:T(8,128)(2,1)S(1)} collective-permute-done((bf16[384,768]{1,0:T(8,128)(2,1)S(1)}, bf16[384,768]{1,0:T(8,128)(2,1)S(1)}, u32[]{:S(2)}, u32[]{:S(2)}) %collective-permute-start.42) | collective-permute-done | bytes 589856 | tf_op jit(solution)/shard_map/ppermute | solution.py:441
  152.0 2.1 collective-permute-start.44
  157.3 9.8 %attend.7 = (bf16[1024,768]{1,0:T(8,128)(2,1)}, bf16[12,2304,256]{2,1,0:T(8,128)(2,1)}, bf16[1024,2304]{1,0:T(8,128)(2,1)}) custom-call(s32[4]{0:T(128)} %pad_add_fusion.core_ref.refs_0_.place_ref, s32[1024,1]{1,0:T(8,128)} %copy.40.refs_1_, ...), custom_call_target="tpu_custom_call", output_to_operand_aliasing={{0}: (14, {}), {1}: (15, {}), {2}: (16, {})} | custom-call | flops 1000 | bytes 1000 | tf_op jit(solution)/shard_map/attend/pallas_call | solution.py:142
  172.2 20.8 %widen.1 = (f32[1024,768]{1,0:T(8,128)}, bf16[1024,3072]{1,0:T(8,128)(2,1)}, bf16[768,1024]{1,0:T(8,128)(2,1)}, bf16[3072,1024]{1,0:T(8,128)(2,1)}) custom-call(s32[4]{0:T(128)} %pad_add_fusion.core_ref.refs_0_.place_ref, bf16[1024,768]{1,0:T(8,128)(2,1)} %bitcast.136, bf16[1024,768]{1,0:T(8,128)(2,1)} %get-tuple-element.715.refs_2_.refs_4_.o_ref, ...), custom_call_target="tpu_custom_call" | custom-call | flops 1000 | bytes 1000 | tf_op jit(solution)/shard_map/widen/pallas_call | solution.py:585
  194.0 1.6 collective-permute-start.59
  195.6 10.4 %proj_terms.1 = (bf16[1536,768]{1,0:T(8,128)(2,1)}, bf16[1536,768]{1,0:T(8,128)(2,1)}) custom-call(s32[4]{0:T(128)} %pad_add_fusion.core_ref.refs_0_.place_ref, bf16[3072,1024]{1,0:T(8,128)(2,1)} %get-tuple-element.774.g_ref.refs_2_, bf16[1024,768]{1,0:T(8,128)(2,1)} %bitcast.139), custom_call_target="tpu_custom_call" | custom-call | flops 1000 | bytes 1000 | tf_op jit(solution)/shard_map/proj_terms/pallas_call | solution.py:297
  207.2 3.9 collective-permute-done.61.refs_32_.refs_9_
  214.0 3.8 add_convert_fusion
  217.8 3.6 all-to-all-start
  221.5 33.0 %back_middle.1 = (bf16[1024,768]{1,0:T(8,128)(2,1)}, f32[1024,768]{1,0:T(8,128)}, bf16[4,480,768]{2,1,0:T(8,128)(2,1)}, bf16[4,480,768]{2,1,0:T(8,128)(2,1)}, f3...) custom-call(s32[4]{0:T(128)} %pad_add_fusion.core_ref.refs_0_.place_ref, ...), custom_call_target="tpu_custom_call" | custom-call | flops 1000 | bytes 1000 | tf_op jit(solution)/shard_map/back_middle/pallas_call | solution.py:394
  255.0 3.5 collective-permute-start.67
  258.5 15.7 %attend_back.2 = (bf16[1024,2304]{1,0:T(8,128)(2,1)}, bf16[384,1152]{1,0:T(8,128)(2,1)}, bf16[384,1152]{1,0:T(8,128)(2,1)}) custom-call(s32[4]{0:T(128)} %pad_add_fusion.core_ref.refs_0_.place_ref, bf16[1024,2304]{1,0:T(8,128)(2,1)} %get-tuple-element.714.q_ref.k_ref.v_ref, bf16[1024,2304]{1,0:T(8,128)(2,1)} %get-tuple-element.714.q_ref.k_ref.v_ref, ...), custom_call_target="tpu_custom_call" | custom-call | flops 1000 | bytes 1000 | tf_op jit(solution)/shard_map/attend_back/pallas_call | solution.py:252
  274.5 3.0 fusion.13
  278.8 1.8 collective-permute-start.70
  284.2 15.6 %attend_back.3 = (bf16[1024,2304]{1,0:T(8,128)(2,1)}, bf16[384,1152]{1,0:T(8,128)(2,1)}, bf16[384,1152]{1,0:T(8,128)(2,1)}) custom-call(s32[4]{0:T(128)} %pad_add_fusion.core_ref.refs_0_.place_ref, bf16[1024,2304]{1,0:T(8,128)(2,1)} %get-tuple-element.714.q_ref.k_ref.v_ref, ...), custom_call_target="tpu_custom_call", output_to_operand_aliasing={{0}: (8, {})} | custom-call | flops 1000 | bytes 1000 | tf_op jit(solution)/shard_map/attend_back/pallas_call | solution.py:252
  303.2 2.0 fusion.4
  306.7 1.9 fusion.6
  309.2 2.0 fusion.5
  311.5 11.9 %back_first.1 = (bf16[1024,768]{1,0:T(8,128)(2,1)}, f32[1,768]{1,0:T(1,128)}, f32[1,768]{1,0:T(1,128)}, f32[1,1536]{1,0:T(1,128)}, f32[72,128]{1,0:T(8,128)}) custom-call(s32[4]{0:T(128)} %pad_add_fusion.core_ref.refs_0_.place_ref, bf16[1024,2304]{1,0:T(8,128)(2,1)} %get-tuple-element.735.refs_1_, bf16[1024,768]{1,0:T(8,128)(2,1)} %bitcast.137, ...), custom_call_target="tpu_custom_call" | custom-call | flops 1000 | bytes 1000 | tf_op jit(solution)/shard_map/back_first/pallas_call | solution.py:585
  323.4 2.6 collective-permute-done.72
  326.1 1.9 add_convert_fusion.10
  328.1 5.6 %collective-permute-start.79 = (bf16[480,768]{1,0:T(8,128)(2,1)S(1)}, bf16[480,768]{1,0:T(8,128)(2,1)S(1)}, u32[]{:S(2)}, u32[]{:S(2)}) collective-permute-start(bf16[480,768]{1,0:T(8,128)(2,1)S(1)} %pad_maximum_fusion), channel_id=1, source_target_pairs={{0,8},{2,10},{4,12},{6,14},{24,16},{26,18},{28,20},{30,22},{1,9},{... | collective-permute-start | bytes 2211848 | tf_op jit(solution)/shard_map/ppermute | solution.py:449
  335.5 1.9 fusion.7
  338.7 1.9 fusion.11
  343.5 11.3 %finish.1 = bf16[1024,768]{1,0:T(8,128)(2,1)} custom-call(s32[4]{0:T(128)} %pad_add_fusion.core_ref.refs_0_.place_ref, f32[1024,768]{1,0:T(8,128)} %get-tuple-element.773.refs_3_.refs_1_, bf16[3072,1024]{1,0:T(8,128)(2,1)} %get-tuple-element.774.g_ref.refs_2_, f32[72,128]{1,0:T(8,128)} %get-tuple-element.775.refs_3_.refs_6_.refs_4_, ...), custom_call_target="tpu_custom_call" | custom-call | flops 1000 | bytes 1000 | tf_op jit(solution)/shard_map/finish/pallas_call | solution.py:585
  356.3 1.8 fusion.9
  360.1 3.2 collective-permute-start.82
  364.5 3.5 collective-permute-done.87
  368.0 1.6 collective-permute-done.82
  372.2 6.7 %collective-permute-start.89 = (bf16[96,1152]{1,0:T(8,128)(2,1)S(1)}, bf16[96,1152]{1,0:T(8,128)(2,1)S(1)}, u32[]{:S(2)}, u32[]{:S(2)}) collective-permute-start(bf16[96,1152]{1,0:T(8,128)(2,1)S(1)} %add_convert_fusion.15), channel_id=1, source_target_pairs={{0,8},{2,10},{4,12},{6,14},{8,0},{10,2},{12,4},{14,6},{16,24},{18,... | collective-permute-start | bytes 663560 | tf_op jit(solution)/shard_map/ppermute | solution.py:441
  381.8 4.8 %put_proj.1 = f32[1536,768]{1,0:T(8,128)} custom-call(s32[4]{0:T(128)} %pad_add_fusion.core_ref.refs_0_.place_ref, bf16[384,768]{1,0:T(8,128)(2,1)} %copy-done.25, bf16[384,768]{1,0:T(8,128)(2,1)} %collective-permute-done.80.refs_1_, bf16[384,768]{1,0:T(8,128)(2,1)} %collective-permute-done.85.refs_2_, bf16[384,768]{1,0:T(8,128)(2,1)} %collective-permute-done.86.refs_3_), custom_call_target="tpu_custom_call" | custom-call | flops 1000 | bytes 1000 | tf_op jit(solution)/shard_map/put_proj/pallas_call | solution.py:740
  386.6 16.7 %collective-permute-done.89 = bf16[96,1152]{1,0:T(8,128)(2,1)S(1)} collective-permute-done((bf16[96,1152]{1,0:T(8,128)(2,1)S(1)}, bf16[96,1152]{1,0:T(8,128)(2,1)S(1)}, u32[]{:S(2)}, u32[]{:S(2)}) %collective-permute-start.89) | collective-permute-done | bytes 221216 | tf_op jit(solution)/shard_map/ppermute | solution.py:441
  404.7 1.5 collective-permute-start.92
  406.2 2.5 collective-permute-start.95
  408.7 7.3 %collective-permute-done.95 = f32[36,128]{1,0:T(8,128)S(1)} collective-permute-done((f32[36,128]{1,0:T(8,128)S(1)}, f32[36,128]{1,0:T(8,128)S(1)}, u32[]{:S(2)}, u32[]{:S(2)}) %collective-permute-start.95) | collective-permute-done | bytes 18464 | tf_op jit(solution)/shard_map/ppermute | solution.py:441
  416.0 9.5 %collective-permute-done.92.refs_1_ = bf16[96,1152]{1,0:T(8,128)(2,1)S(1)} collective-permute-done((bf16[96,1152]{1,0:T(8,128)(2,1)S(1)}, bf16[96,1152]{1,0:T(8,128)(2,1)S(1)}, u32[]{:S(2)}, u32[]{:S(2)}) %collective-permute-start.92) | collective-permute-done | bytes 221216 | tf_op jit(solution)/shard_map/ppermute | solution.py:441
  428.4 3.6 collective-permute-done.101
  431.9 1.7 collective-permute-done.98.refs_5_
  435.1 5.4 %put_fc.1 = (f32[384,3072]{1,0:T(8,128)}, f32[384,768]{1,0:T(8,128)}) custom-call(s32[4]{0:T(128)} %pad_add_fusion.core_ref.refs_0_.place_ref, bf16[480,768]{1,0:T(8,128)(2,1)} %copy-done.18, bf16[480,768]{1,0:T(8,128)(2,1)} %copy-done.59, bf16[480,768]{1,0:T(8,128)(2,1)} %copy-done.60, bf16[480,768]{1,0:T(8,128)(2,1)} %copy-done.61), custom_call_target="tpu_custom_call" | custom-call | flops 1000 | bytes 1000 | tf_op jit(solution)/shard_map/put_fc/pallas_call | solution.py:740
  441.9 4.3 put_qkv.1
  (406 shorter events, 77.5 us)
Async XLA Ops:
  19.1 15.4 %collective-permute-start.3 = (bf16[192,3072]{1,0:T(8,128)(2,1)}, bf16[192,3072]{1,0:T(8,128)(2,1)}, u32[]{:S(2)}, u32[]{:S(2)}) collective-permute-start(bf16[192,3072]{1,0:T(8,128)(2,1)} %dynamic-slice_bitcast_fusion.1), channel_id=1, source_target_pairs={{0,2},{2,0},{4,6},{6,4},{8,10},{10,8},{12,14},{14,12},{16,18},{18,... | collective-permute-start | bytes 3538952 | tf_op jit(solution)/shard_map/ppermute | solution.py:441
  19.2 15.3 %collective-permute-start.5 = (bf16[768,768]{1,0:T(8,128)(2,1)}, bf16[768,768]{1,0:T(8,128)(2,1)}, u32[]{:S(2)}, u32[]{:S(2)}) collective-permute-start(bf16[768,768]{1,0:T(8,128)(2,1)} %dynamic-slice_bitcast_fusion), channel_id=1, source_target_pairs={{0,2},{2,0},{4,6},{6,4},{8,10},{10,8},{12,14},{14,12},{16,18},{18,... | collective-permute-start | bytes 3538952 | tf_op jit(solution)/shard_map/ppermute | solution.py:441
  19.7 14.8 %collective-permute-start.4 = (bf16[192,768]{1,0:T(8,128)(2,1)}, bf16[192,768]{1,0:T(8,128)(2,1)S(1)}, u32[]{:S(2)}, u32[]{:S(2)}) collective-permute-start(bf16[192,768]{1,0:T(8,128)(2,1)} %dynamic-slice_bitcast_fusion.4), channel_id=1, source_target_pairs={{0,2},{2,0},{4,6},{6,4},{8,10},{10,8},{12,14},{14,12},{16,18},{18,... | collective-permute-start | bytes 884744 | tf_op jit(solution)/shard_map/ppermute | solution.py:441
  19.7 14.7 %collective-permute-start.6 = (bf16[96,1280]{1,0:T(8,128)(2,1)S(1)}, bf16[96,1280]{1,0:T(8,128)(2,1)}, u32[]{:S(2)}, u32[]{:S(2)}) collective-permute-start(bf16[96,1280]{1,0:T(8,128)(2,1)S(1)} %bitcast_select_fusion.5), channel_id=1, source_target_pairs={{0,16},{2,18},{4,20},{6,22},{8,24},{10,26},{12,28},{14,30},{16,0},... | collective-permute-start | bytes 737288 | tf_op jit(solution)/shard_map/ppermute | solution.py:441
  44.0 17.6 %collective-permute-start.11 = (bf16[96,1280]{1,0:T(8,128)(2,1)S(1)}, bf16[96,1280]{1,0:T(8,128)(2,1)S(1)}, u32[]{:S(2)}, u32[]{:S(2)}) collective-permute-start(bf16[96,1280]{1,0:T(8,128)(2,1)S(1)} %broadcast_select_fusion.8.refs_3_.refs_4_.refs_10_), channel_id=1, source_target_pairs={{0,4},{2,6},{4,0},{6,2},{8,12},{10,14},{12,8},{14,10},{16,20},{18,... | collective-permute-start | bytes 737288 | tf_op jit(solution)/shard_map/ppermute | solution.py:441
  46.4 15.2 %collective-permute-start.12 = (bf16[96,1280]{1,0:T(8,128)(2,1)S(1)}, bf16[96,1280]{1,0:T(8,128)(2,1)S(1)}, u32[]{:S(2)}, u32[]{:S(2)}) collective-permute-start(bf16[96,1280]{1,0:T(8,128)(2,1)S(1)} %broadcast_select_fusion.8.refs_3_.refs_4_.refs_10_), channel_id=1, source_target_pairs={{0,1},{1,0},{2,3},{3,2},{4,5},{5,4},{6,7},{7,6},{8,9},{9,8},{10,11... | collective-permute-start | bytes 737288 | tf_op jit(solution)/shard_map/ppermute | solution.py:445
  47.9 13.7 %collective-permute-start.13 = (bf16[96,1152]{1,0:T(8,128)(2,1)S(1)}, bf16[96,1152]{1,0:T(8,128)(2,1)S(1)}, u32[]{:S(2)}, u32[]{:S(2)}) collective-permute-start(bf16[96,1152]{1,0:T(8,128)(2,1)S(1)} %bitcast_select_fusion.6), channel_id=1, source_target_pairs={{0,16},{2,18},{4,20},{6,22},{8,24},{10,26},{12,28},{14,30},{16,0},... | collective-permute-start | bytes 663560 | tf_op jit(solution)/shard_map/ppermute | solution.py:441
  51.7 15.0 %collective-permute-start.8 = (bf16[96,3072]{1,0:T(8,128)(2,1)S(1)}, bf16[96,3072]{1,0:T(8,128)(2,1)S(1)}, u32[]{:S(2)}, u32[]{:S(2)}) collective-permute-start(bf16[96,3072]{1,0:T(8,128)(2,1)S(1)} %dynamic-slice_bitcast_fusion.3), channel_id=1, source_target_pairs={{0,4},{2,6},{4,0},{6,2},{8,12},{10,14},{12,8},{14,10},{16,20},{18,... | collective-permute-start | bytes 1769480 | tf_op jit(solution)/shard_map/ppermute | solution.py:441
  61.7 9.6 %collective-permute-start.17 = (bf16[96,1152]{1,0:T(8,128)(2,1)S(1)}, bf16[96,1152]{1,0:T(8,128)(2,1)S(1)}, u32[]{:S(2)}, u32[]{:S(2)}) collective-permute-start(bf16[96,1152]{1,0:T(8,128)(2,1)S(1)} %broadcast_select_fusion.11), channel_id=1, source_target_pairs={{0,8},{2,10},{4,12},{6,14},{8,0},{10,2},{12,4},{14,6},{16,24},{18,... | collective-permute-start | bytes 663560 | tf_op jit(solution)/shard_map/ppermute | solution.py:441
  73.4 32.9 %collective-permute-start.18 = (bf16[96,3072]{1,0:T(8,128)(2,1)S(1)}, bf16[96,3072]{1,0:T(8,128)(2,1)}, u32[]{:S(2)}, u32[]{:S(2)}) collective-permute-start(bf16[96,3072]{1,0:T(8,128)(2,1)S(1)} %bitcast_select_fusion.2), channel_id=1, source_target_pairs={{0,16},{2,18},{4,20},{6,22},{8,24},{10,26},{12,28},{14,30},{16,0},... | collective-permute-start | bytes 1769480 | tf_op jit(solution)/shard_map/ppermute | solution.py:441
  75.2 31.1 %collective-permute-start.27 = (bf16[384,768]{1,0:T(8,128)(2,1)}, bf16[384,768]{1,0:T(8,128)(2,1)}, u32[]{:S(2)}, u32[]{:S(2)}) collective-permute-start(bf16[384,768]{1,0:T(8,128)(2,1)} %dynamic-slice_bitcast_fusion.2), channel_id=1, source_target_pairs={{0,4},{2,6},{4,0},{6,2},{8,12},{10,14},{12,8},{14,10},{16,20},{18,... | collective-permute-start | bytes 1769480 | tf_op jit(solution)/shard_map/ppermute | solution.py:441
  81.7 24.6 %collective-permute-start.26 = (bf16[96,768]{1,0:T(8,128)(2,1)}, bf16[96,768]{1,0:T(8,128)(2,1)}, u32[]{:S(2)}, u32[]{:S(2)}) collective-permute-start(bf16[96,768]{1,0:T(8,128)(2,1)} %broadcast_select_fusion.13), channel_id=1, source_target_pairs={{0,8},{2,10},{4,12},{6,14},{8,0},{10,2},{12,4},{14,6},{16,24},{18,... | collective-permute-start | bytes 442376 | tf_op jit(solution)/shard_map/ppermute | solution.py:441
  86.3 19.9 %collective-permute-start.28 = (bf16[48,1152]{1,0:T(8,128)(2,1)}, bf16[48,1152]{1,0:T(8,128)(2,1)S(1)}, u32[]{:S(2)}, u32[]{:S(2)}) collective-permute-start(bf16[48,1152]{1,0:T(8,128)(2,1)} %slice.72), channel_id=1, source_target_pairs={{0,1},{1,0},{2,3},{3,2},{4,5},{5,4},{6,7},{7,6},{8,9},{9,8},{10,11... | collective-permute-start | bytes 331784 | tf_op jit(solution)/shard_map/ppermute | solution.py:445
  86.8 19.4 %collective-permute-start.29 = (bf16[48,1152]{1,0:T(8,128)(2,1)}, bf16[48,1152]{1,0:T(8,128)(2,1)S(1)}, u32[]{:S(2)}, u32[]{:S(2)}) collective-permute-start(bf16[48,1152]{1,0:T(8,128)(2,1)} %slice.73), channel_id=1, source_target_pairs={{0,4},{2,6},{4,0},{6,2},{8,12},{10,14},{12,8},{14,10},{16,20},{18,... | collective-permute-start | bytes 331784 | tf_op jit(solution)/shard_map/ppermute | solution.py:441
  106.4 17.8 %collective-permute-start.30 = (bf16[96,3072]{1,0:T(8,128)(2,1)S(1)}, bf16[96,3072]{1,0:T(8,128)(2,1)S(1)}, u32[]{:S(2)}, u32[]{:S(2)}) collective-permute-start(bf16[96,3072]{1,0:T(8,128)(2,1)S(1)} %broadcast_select_fusion.2), channel_id=1, source_target_pairs={{0,8},{2,10},{4,12},{6,14},{8,0},{10,2},{12,4},{14,6},{16,24},{18,... | collective-permute-start | bytes 1769480 | tf_op jit(solution)/shard_map/ppermute | solution.py:441
  108.1 16.1 %collective-permute-start.31 = (bf16[96,768]{1,0:T(8,128)(2,1)S(1)}, bf16[96,768]{1,0:T(8,128)(2,1)S(1)}, u32[]{:S(2)}, u32[]{:S(2)}) collective-permute-start(bf16[96,768]{1,0:T(8,128)(2,1)S(1)} %broadcast_select_fusion.12.refs_4_.refs_7_), channel_id=1, source_target_pairs={{0,4},{2,6},{4,0},{6,2},{8,12},{10,14},{12,8},{14,10},{16,20},{18,... | collective-permute-start | bytes 442376 | tf_op jit(solution)/shard_map/ppermute | solution.py:441
  109.3 15.0 %collective-permute-start.32 = (bf16[96,768]{1,0:T(8,128)(2,1)S(1)}, bf16[96,768]{1,0:T(8,128)(2,1)S(1)}, u32[]{:S(2)}, u32[]{:S(2)}) collective-permute-start(bf16[96,768]{1,0:T(8,128)(2,1)S(1)} %broadcast_select_fusion.12.refs_4_.refs_7_), channel_id=1, source_target_pairs={{0,1},{1,0},{2,3},{3,2},{4,5},{5,4},{6,7},{7,6},{8,9},{9,8},{10,11... | collective-permute-start | bytes 442376 | tf_op jit(solution)/shard_map/ppermute | solution.py:445
  110.8 10.5 %collective-permute-start.36 = (bf16[48,1152]{1,0:T(8,128)(2,1)S(1)}, bf16[48,1152]{1,0:T(8,128)(2,1)S(1)}, u32[]{:S(2)}, u32[]{:S(2)}) collective-permute-start(bf16[48,1152]{1,0:T(8,128)(2,1)S(1)} %collective-permute-done.28.refs_7_.refs_23_), channel_id=1, source_target_pairs={{0,2},{2,0},{4,6},{6,4},{8,10},{10,8},{12,14},{14,12},{16,18},{18,... | collective-permute-start | bytes 331784 | tf_op jit(solution)/shard_map/ppermute | solution.py:441
  110.8 13.4 %collective-permute-start.37 = (bf16[48,1152]{1,0:T(8,128)(2,1)S(1)}, bf16[48,1152]{1,0:T(8,128)(2,1)S(1)}, u32[]{:S(2)}, u32[]{:S(2)}) collective-permute-start(bf16[48,1152]{1,0:T(8,128)(2,1)S(1)} %collective-permute-done.29.refs_8_.refs_24_), channel_id=1, source_target_pairs={{0,2},{2,0},{4,6},{6,4},{8,10},{10,8},{12,14},{14,12},{16,18},{18,... | collective-permute-start | bytes 331784 | tf_op jit(solution)/shard_map/ppermute | solution.py:441
  121.3 29.1 %collective-permute-start.42 = (bf16[384,768]{1,0:T(8,128)(2,1)S(1)}, bf16[384,768]{1,0:T(8,128)(2,1)S(1)}, u32[]{:S(2)}, u32[]{:S(2)}) collective-permute-start(bf16[384,768]{1,0:T(8,128)(2,1)S(1)} %bitcast_select_fusion.3), channel_id=1, source_target_pairs={{0,16},{2,18},{4,20},{6,22},{8,24},{10,26},{12,28},{14,30},{16,0},... | collective-permute-start | bytes 1769480 | tf_op jit(solution)/shard_map/ppermute | solution.py:441
  124.3 26.1 %collective-permute-start.38 = (bf16[96,3072]{1,0:T(8,128)(2,1)S(1)}, bf16[96,3072]{1,0:T(8,128)(2,1)S(1)}, u32[]{:S(2)}, u32[]{:S(2)}) collective-permute-start(bf16[96,3072]{1,0:T(8,128)(2,1)S(1)} %broadcast_select_fusion.3.refs_14_.refs_17_), channel_id=1, source_target_pairs={{0,4},{2,6},{4,0},{6,2},{8,12},{10,14},{12,8},{14,10},{16,20},{18,... | collective-permute-start | bytes 1769480 | tf_op jit(solution)/shard_map/ppermute | solution.py:441
  126.4 24.0 %collective-permute-start.39 = (bf16[96,3072]{1,0:T(8,128)(2,1)S(1)}, bf16[96,3072]{1,0:T(8,128)(2,1)S(1)}, u32[]{:S(2)}, u32[]{:S(2)}) collective-permute-start(bf16[96,3072]{1,0:T(8,128)(2,1)S(1)} %broadcast_select_fusion.3.refs_14_.refs_17_), channel_id=1, source_target_pairs={{0,1},{1,0},{2,3},{3,2},{4,5},{5,4},{6,7},{7,6},{8,9},{9,8},{10,11... | collective-permute-start | bytes 1769480 | tf_op jit(solution)/shard_map/ppermute | solution.py:445
  127.0 23.4 %collective-permute-start.40 = (bf16[48,768]{1,0:T(8,128)(2,1)S(1)}, bf16[48,768]{1,0:T(8,128)(2,1)S(1)}, u32[]{:S(2)}, u32[]{:S(2)}) collective-permute-start(bf16[48,768]{1,0:T(8,128)(2,1)S(1)} %slice.74), channel_id=1, source_target_pairs={{0,1},{1,0},{2,3},{3,2},{4,5},{5,4},{6,7},{7,6},{8,9},{9,8},{10,11... | collective-permute-start | bytes 221192 | tf_op jit(solution)/shard_map/ppermute | solution.py:445
  128.5 21.9 %collective-permute-start.41 = (bf16[48,768]{1,0:T(8,128)(2,1)S(1)}, bf16[48,768]{1,0:T(8,128)(2,1)S(1)}, u32[]{:S(2)}, u32[]{:S(2)}) collective-permute-start(bf16[48,768]{1,0:T(8,128)(2,1)S(1)} %slice.75), channel_id=1, source_target_pairs={{0,4},{2,6},{4,0},{6,2},{8,12},{10,14},{12,8},{14,10},{16,20},{18,... | collective-permute-start | bytes 221192 | tf_op jit(solution)/shard_map/ppermute | solution.py:441
  150.5 16.9 %collective-permute-start.50 = (bf16[384,768]{1,0:T(8,128)(2,1)S(1)}, bf16[384,768]{1,0:T(8,128)(2,1)S(1)}, u32[]{:S(2)}, u32[]{:S(2)}) collective-permute-start(bf16[384,768]{1,0:T(8,128)(2,1)S(1)} %broadcast_select_fusion.4), channel_id=1, source_target_pairs={{0,8},{2,10},{4,12},{6,14},{8,0},{10,2},{12,4},{14,6},{16,24},{18,... | collective-permute-start | bytes 1769480 | tf_op jit(solution)/shard_map/ppermute | solution.py:441
  151.4 15.8 %collective-permute-start.43 = (bf16[48,3072]{1,0:T(8,128)(2,1)S(1)}, bf16[48,3072]{1,0:T(8,128)(2,1)S(1)}, u32[]{:S(2)}, u32[]{:S(2)}) collective-permute-start(bf16[48,3072]{1,0:T(8,128)(2,1)S(1)} %slice.76), channel_id=1, source_target_pairs={{0,1},{1,0},{2,3},{3,2},{4,5},{5,4},{6,7},{7,6},{8,9},{9,8},{10,11... | collective-permute-start | bytes 884744 | tf_op jit(solution)/shard_map/ppermute | solution.py:445
  152.0 15.4 %collective-permute-start.44 = (bf16[48,3072]{1,0:T(8,128)(2,1)S(1)}, bf16[48,3072]{1,0:T(8,128)(2,1)S(1)}, u32[]{:S(2)}, u32[]{:S(2)}) collective-permute-start(bf16[48,3072]{1,0:T(8,128)(2,1)S(1)} %slice.77), channel_id=1, source_target_pairs={{0,4},{2,6},{4,0},{6,2},{8,12},{10,14},{12,8},{14,10},{16,20},{18,... | collective-permute-start | bytes 884744 | tf_op jit(solution)/shard_map/ppermute | solution.py:441
  156.7 12.5 %collective-permute-start.53 = (bf16[96,3072]{1,0:T(8,128)(2,1)S(1)}, bf16[96,3072]{1,0:T(8,128)(2,1)S(1)}, u32[]{:S(2)}, u32[]{:S(2)}) collective-permute-start(bf16[96,3072]{1,0:T(8,128)(2,1)S(1)} %broadcast_select_fusion.3.refs_14_.refs_17_), channel_id=1, source_target_pairs={{0,2},{2,0},{4,6},{6,4},{8,10},{10,8},{12,14},{14,12},{16,18},{18,... | collective-permute-start | bytes 1769480 | tf_op jit(solution)/shard_map/ppermute | solution.py:441
  156.9 12.3 %collective-permute-start.54 = (bf16[96,3072]{1,0:T(8,128)(2,1)S(1)}, bf16[96,3072]{1,0:T(8,128)(2,1)S(1)}, u32[]{:S(2)}, u32[]{:S(2)}) collective-permute-start(bf16[96,3072]{1,0:T(8,128)(2,1)S(1)} %collective-permute-done.38.refs_15_.refs_18_), channel_id=1, source_target_pairs={{0,2},{2,0},{4,6},{6,4},{8,10},{10,8},{12,14},{14,12},{16,18},{18,... | collective-permute-start | bytes 1769480 | tf_op jit(solution)/shard_map/ppermute | solution.py:441
  167.5 25.5 %collective-permute-start.51 = (bf16[384,768]{1,0:T(8,128)(2,1)S(1)}, bf16[384,768]{1,0:T(8,128)(2,1)S(1)}, u32[]{:S(2)}, u32[]{:S(2)}) collective-permute-start(bf16[384,768]{1,0:T(8,128)(2,1)S(1)} %broadcast_select_fusion.5.refs_27_.refs_4_), channel_id=1, source_target_pairs={{0,4},{2,6},{4,0},{6,2},{8,12},{10,14},{12,8},{14,10},{16,20},{18,... | collective-permute-start | bytes 1769480 | tf_op jit(solution)/shard_map/ppermute | solution.py:441
  168.0 25.1 %collective-permute-start.52 = (bf16[384,768]{1,0:T(8,128)(2,1)S(1)}, bf16[384,768]{1,0:T(8,128)(2,1)S(1)}, u32[]{:S(2)}, u32[]{:S(2)}) collective-permute-start(bf16[384,768]{1,0:T(8,128)(2,1)S(1)} %broadcast_select_fusion.5.refs_27_.refs_4_), channel_id=1, source_target_pairs={{0,1},{1,0},{2,3},{3,2},{4,5},{5,4},{6,7},{7,6},{8,9},{9,8},{10,11... | collective-permute-start | bytes 1769480 | tf_op jit(solution)/shard_map/ppermute | solution.py:445
  193.1 12.8 %collective-permute-start.58 = (bf16[192,768]{1,0:T(8,128)(2,1)S(1)}, bf16[192,768]{1,0:T(8,128)(2,1)S(1)}, u32[]{:S(2)}, u32[]{:S(2)}) collective-permute-start(bf16[192,768]{1,0:T(8,128)(2,1)S(1)} %slice.78), channel_id=1, source_target_pairs={{0,1},{1,0},{2,3},{3,2},{4,5},{5,4},{6,7},{7,6},{8,9},{9,8},{10,11... | collective-permute-start | bytes 884744 | tf_op jit(solution)/shard_map/ppermute | solution.py:445
  194.0 12.0 %collective-permute-start.59 = (bf16[192,768]{1,0:T(8,128)(2,1)S(1)}, bf16[192,768]{1,0:T(8,128)(2,1)S(1)}, u32[]{:S(2)}, u32[]{:S(2)}) collective-permute-start(bf16[192,768]{1,0:T(8,128)(2,1)S(1)} %slice.79), channel_id=1, source_target_pairs={{0,4},{2,6},{4,0},{6,2},{8,12},{10,14},{12,8},{14,10},{16,20},{18,... | collective-permute-start | bytes 884744 | tf_op jit(solution)/shard_map/ppermute | solution.py:441
  217.8 36.7 %all-to-all-start = ((bf16[4,384,768]{2,1,0:T(8,128)(2,1)}), bf16[4,384,768]{2,1,0:T(8,128)(2,1)S(1)}, u32[]{:S(2)}, u32[]{:S(2)}) async-start(bf16[4,384,768]{2,1,0:T(8,128)(2,1)} %bitcast.138), calls=%async_computation | async-start | bytes 4718592 | tf_op jit(solution)/shard_map/all_to_all | solution.py:462
  254.5 19.9 %collective-permute-start.66 = (bf16[4,480,768]{2,1,0:T(8,128)(2,1)}, bf16[4,480,768]{2,1,0:T(8,128)(2,1)}, u32[]{:S(2)}, u32[]{:S(2)}) collective-permute-start(bf16[4,480,768]{2,1,0:T(8,128)(2,1)} %get-tuple-element.694), channel_id=1, source_target_pairs={{0,2},{2,0},{4,6},{6,4},{8,10},{10,8},{12,14},{14,12},{16,18},{18,... | collective-permute-start | bytes 8847368 | tf_op jit(solution)/shard_map/ppermute | solution.py:441
  255.0 19.4 %collective-permute-start.67 = (bf16[384,768]{1,0:T(8,128)(2,1)S(1)}, bf16[384,768]{1,0:T(8,128)(2,1)S(1)}, u32[]{:S(2)}, u32[]{:S(2)}) collective-permute-start(bf16[384,768]{1,0:T(8,128)(2,1)S(1)} %add_convert_fusion.7), channel_id=1, source_target_pairs={{0,8},{2,10},{4,12},{6,14},{24,16},{26,18},{28,20},{30,22},{1,9},{... | collective-permute-start | bytes 1769480 | tf_op jit(solution)/shard_map/ppermute | solution.py:449
  278.8 21.0 %collective-permute-start.70 = (bf16[2,240,768]{2,1,0:T(8,128)(2,1)}, bf16[2,240,768]{2,1,0:T(8,128)(2,1)}, u32[]{:S(2)}, u32[]{:S(2)}) collective-permute-start(bf16[2,240,768]{2,1,0:T(8,128)(2,1)} %fusion.1), channel_id=1, source_target_pairs={{0,4},{2,6},{4,0},{6,2},{8,12},{10,14},{12,8},{14,10},{16,20},{18,... | collective-permute-start | bytes 2211848 | tf_op jit(solution)/shard_map/ppermute | solution.py:441
  280.6 20.3 %collective-permute-start.68 = (bf16[384,1152]{1,0:T(8,128)(2,1)}, bf16[384,1152]{1,0:T(8,128)(2,1)}, u32[]{:S(2)}, u32[]{:S(2)}) collective-permute-start(bf16[384,1152]{1,0:T(8,128)(2,1)} %get-tuple-element.709), channel_id=1, source_target_pairs={{0,2},{2,0},{4,6},{6,4},{8,10},{10,8},{12,14},{14,12},{16,18},{18,... | collective-permute-start | bytes 2654216 | tf_op jit(solution)/shard_map/ppermute | solution.py:441
  281.6 19.2 %collective-permute-start.69 = (bf16[2,240,768]{2,1,0:T(8,128)(2,1)}, bf16[2,240,768]{2,1,0:T(8,128)(2,1)}, u32[]{:S(2)}, u32[]{:S(2)}) collective-permute-start(bf16[2,240,768]{2,1,0:T(8,128)(2,1)} %fusion), channel_id=1, source_target_pairs={{0,1},{1,0},{2,3},{3,2},{4,5},{5,4},{6,7},{7,6},{8,9},{9,8},{10,11... | collective-permute-start | bytes 2211848 | tf_op jit(solution)/shard_map/ppermute | solution.py:445
  283.4 16.4 %collective-permute-start.71 = (bf16[384,768]{1,0:T(8,128)(2,1)S(1)}, bf16[384,768]{1,0:T(8,128)(2,1)S(1)}, u32[]{:S(2)}, u32[]{:S(2)}) collective-permute-start(bf16[384,768]{1,0:T(8,128)(2,1)S(1)} %add_convert_fusion.6), channel_id=1, source_target_pairs={{8,16},{10,18},{12,20},{14,22},{16,8},{18,10},{20,12},{22,14},{9,1... | collective-permute-start | bytes 1769480 | tf_op jit(solution)/shard_map/ppermute | solution.py:449
  300.9 25.2 %collective-permute-start.73 = (bf16[384,1152]{1,0:T(8,128)(2,1)}, bf16[384,1152]{1,0:T(8,128)(2,1)}, u32[]{:S(2)}, u32[]{:S(2)}) collective-permute-start(bf16[384,1152]{1,0:T(8,128)(2,1)} %get-tuple-element.724), channel_id=1, source_target_pairs={{0,2},{2,0},{4,6},{6,4},{8,10},{10,8},{12,14},{14,12},{16,18},{18,... | collective-permute-start | bytes 2654216 | tf_op jit(solution)/shard_map/ppermute | solution.py:441
  301.8 24.2 %collective-permute-start.76 = (bf16[384,768]{1,0:T(8,128)(2,1)}, bf16[384,768]{1,0:T(8,128)(2,1)}, u32[]{:S(2)}, u32[]{:S(2)}) collective-permute-start(bf16[384,768]{1,0:T(8,128)(2,1)} %add_convert_fusion.5), channel_id=1, source_target_pairs={{8,0},{10,2},{12,4},{14,6},{16,24},{18,26},{20,28},{22,30},{9,1},{... | collective-permute-start | bytes 1769480 | tf_op jit(solution)/shard_map/ppermute | solution.py:449
  305.2 18.2 %collective-permute-start.75 = (bf16[240,768]{1,0:T(8,128)(2,1)}, bf16[240,768]{1,0:T(8,128)(2,1)S(1)}, u32[]{:S(2)}, u32[]{:S(2)}) collective-permute-start(bf16[240,768]{1,0:T(8,128)(2,1)} %fusion.4), channel_id=1, source_target_pairs={{0,1},{1,0},{2,3},{3,2},{4,5},{5,4},{6,7},{7,6},{8,9},{9,8},{10,11... | collective-permute-start | bytes 1105928 | tf_op jit(solution)/shard_map/ppermute | solution.py:445
  308.6 17.5 %collective-permute-start.72 = (bf16[2,96,1152]{2,1,0:T(8,128)(2,1)}, bf16[2,96,1152]{2,1,0:T(8,128)(2,1)}, u32[]{:S(2)}, u32[]{:S(2)}) collective-permute-start(bf16[2,96,1152]{2,1,0:T(8,128)(2,1)} %fusion.6), channel_id=1, source_target_pairs={{0,1},{1,0},{2,3},{3,2},{4,5},{5,4},{6,7},{7,6},{8,9},{9,8},{10,11... | collective-permute-start | bytes 1327112 | tf_op jit(solution)/shard_map/ppermute | solution.py:445
  311.2 12.3 %collective-permute-start.74 = (bf16[240,768]{1,0:T(8,128)(2,1)}, bf16[240,768]{1,0:T(8,128)(2,1)}, u32[]{:S(2)}, u32[]{:S(2)}) collective-permute-start(bf16[240,768]{1,0:T(8,128)(2,1)} %fusion.5), channel_id=1, source_target_pairs={{0,4},{2,6},{4,0},{6,2},{8,12},{10,14},{12,8},{14,10},{16,20},{18,... | collective-permute-start | bytes 1105928 | tf_op jit(solution)/shard_map/ppermute | solution.py:441
  328.1 27.3 %collective-permute-start.79 = (bf16[480,768]{1,0:T(8,128)(2,1)S(1)}, bf16[480,768]{1,0:T(8,128)(2,1)S(1)}, u32[]{:S(2)}, u32[]{:S(2)}) collective-permute-start(bf16[480,768]{1,0:T(8,128)(2,1)S(1)} %pad_maximum_fusion), channel_id=1, source_target_pairs={{0,8},{2,10},{4,12},{6,14},{24,16},{26,18},{28,20},{30,22},{1,9},{... | collective-permute-start | bytes 2211848 | tf_op jit(solution)/shard_map/ppermute | solution.py:449
  334.8 20.5 %collective-permute-start.80 = (bf16[384,768]{1,0:T(8,128)(2,1)S(1)}, bf16[384,768]{1,0:T(8,128)(2,1)}, u32[]{:S(2)}, u32[]{:S(2)}) collective-permute-start(bf16[384,768]{1,0:T(8,128)(2,1)S(1)} %broadcast_select_fusion.1.refs_0_), channel_id=1, source_target_pairs={{0,4},{2,6},{4,0},{6,2},{8,12},{10,14},{12,8},{14,10},{16,20},{18,... | collective-permute-start | bytes 1769480 | tf_op jit(solution)/shard_map/ppermute | solution.py:441
  337.4 18.0 %collective-permute-start.78 = (bf16[2,96,1152]{2,1,0:T(8,128)(2,1)}, bf16[2,96,1152]{2,1,0:T(8,128)(2,1)}, u32[]{:S(2)}, u32[]{:S(2)}) collective-permute-start(bf16[2,96,1152]{2,1,0:T(8,128)(2,1)} %fusion.7), channel_id=1, source_target_pairs={{0,1},{1,0},{2,3},{3,2},{4,5},{5,4},{6,7},{7,6},{8,9},{9,8},{10,11... | collective-permute-start | bytes 1327112 | tf_op jit(solution)/shard_map/ppermute | solution.py:445
  340.7 14.7 %collective-permute-start.77 = (bf16[96,1152]{1,0:T(8,128)(2,1)}, bf16[96,1152]{1,0:T(8,128)(2,1)S(1)}, u32[]{:S(2)}, u32[]{:S(2)}) collective-permute-start(bf16[96,1152]{1,0:T(8,128)(2,1)} %fusion.11), channel_id=1, source_target_pairs={{0,4},{2,6},{4,0},{6,2},{8,12},{10,14},{12,8},{14,10},{16,20},{18,... | collective-permute-start | bytes 663560 | tf_op jit(solution)/shard_map/ppermute | solution.py:441
  343.5 11.3 %collective-permute-start.81 = (f32[2,36,128]{2,1,0:T(8,128)}, f32[2,36,128]{2,1,0:T(8,128)S(1)}, u32[]{:S(2)}, u32[]{:S(2)}) collective-permute-start(f32[2,36,128]{2,1,0:T(8,128)} %reshape.177), channel_id=1, source_target_pairs={{0,2},{2,0},{4,6},{6,4},{8,10},{10,8},{12,14},{14,12},{16,18},{18,... | collective-permute-start | bytes 110600 | tf_op jit(solution)/shard_map/ppermute | solution.py:441
  354.8 9.3 %collective-permute-start.85 = (bf16[384,768]{1,0:T(8,128)(2,1)S(1)}, bf16[384,768]{1,0:T(8,128)(2,1)}, u32[]{:S(2)}, u32[]{:S(2)}) collective-permute-start(bf16[384,768]{1,0:T(8,128)(2,1)S(1)} %broadcast_select_fusion.1.refs_0_), channel_id=1, source_target_pairs={{0,2},{2,0},{4,6},{6,4},{8,10},{10,8},{12,14},{14,12},{16,18},{18,... | collective-permute-start | bytes 1769480 | tf_op jit(solution)/shard_map/ppermute | solution.py:441
  355.6 14.0 %collective-permute-start.84 = (bf16[480,768]{1,0:T(8,128)(2,1)S(1)}, bf16[480,768]{1,0:T(8,128)(2,1)S(1)}, u32[]{:S(2)}, u32[]{:S(2)}) collective-permute-start(bf16[480,768]{1,0:T(8,128)(2,1)S(1)} %add_convert_fusion.2), channel_id=1, source_target_pairs={{8,16},{10,18},{12,20},{14,22},{16,8},{18,10},{20,12},{22,14},{9,1... | collective-permute-start | bytes 2211848 | tf_op jit(solution)/shard_map/ppermute | solution.py:449
  358.2 9.9 %collective-permute-start.83 = (bf16[96,1152]{1,0:T(8,128)(2,1)}, bf16[96,1152]{1,0:T(8,128)(2,1)S(1)}, u32[]{:S(2)}, u32[]{:S(2)}) collective-permute-start(bf16[96,1152]{1,0:T(8,128)(2,1)} %fusion.9), channel_id=1, source_target_pairs={{0,4},{2,6},{4,0},{6,2},{8,12},{10,14},{12,8},{14,10},{16,20},{18,... | collective-permute-start | bytes 663560 | tf_op jit(solution)/shard_map/ppermute | solution.py:441
  358.7 10.8 %collective-permute-start.86 = (bf16[384,768]{1,0:T(8,128)(2,1)}, bf16[384,768]{1,0:T(8,128)(2,1)}, u32[]{:S(2)}, u32[]{:S(2)}) collective-permute-start(bf16[384,768]{1,0:T(8,128)(2,1)} %collective-permute-done.80.refs_1_), channel_id=1, source_target_pairs={{0,2},{2,0},{4,6},{6,4},{8,10},{10,8},{12,14},{14,12},{16,18},{18,... | collective-permute-start | bytes 1769480 | tf_op jit(solution)/shard_map/ppermute | solution.py:441
  360.1 9.4 %collective-permute-start.82 = (bf16[96,1152]{1,0:T(8,128)(2,1)S(1)}, bf16[96,1152]{1,0:T(8,128)(2,1)}, u32[]{:S(2)}, u32[]{:S(2)}) collective-permute-start(bf16[96,1152]{1,0:T(8,128)(2,1)S(1)} %add_convert_fusion.17), channel_id=1, source_target_pairs={{0,8},{2,10},{4,12},{6,14},{8,0},{10,2},{12,4},{14,6},{16,24},{18,... | collective-permute-start | bytes 663560 | tf_op jit(solution)/shard_map/ppermute | solution.py:441
  369.8 33.5 %collective-permute-start.90 = (bf16[480,768]{1,0:T(8,128)(2,1)S(1)}, bf16[480,768]{1,0:T(8,128)(2,1)S(1)}, u32[]{:S(2)}, u32[]{:S(2)}) collective-permute-start(bf16[480,768]{1,0:T(8,128)(2,1)S(1)} %add_convert_fusion.1), channel_id=1, source_target_pairs={{8,0},{10,2},{12,4},{14,6},{16,24},{18,26},{20,28},{22,30},{9,1},{... | collective-permute-start | bytes 2211848 | tf_op jit(solution)/shard_map/ppermute | solution.py:449
  372.2 31.1 %collective-permute-start.89 = (bf16[96,1152]{1,0:T(8,128)(2,1)S(1)}, bf16[96,1152]{1,0:T(8,128)(2,1)S(1)}, u32[]{:S(2)}, u32[]{:S(2)}) collective-permute-start(bf16[96,1152]{1,0:T(8,128)(2,1)S(1)} %add_convert_fusion.15), channel_id=1, source_target_pairs={{0,8},{2,10},{4,12},{6,14},{8,0},{10,2},{12,4},{14,6},{16,24},{18,... | collective-permute-start | bytes 663560 | tf_op jit(solution)/shard_map/ppermute | solution.py:441
  379.9 23.4 %collective-permute-start.88 = (bf16[96,1152]{1,0:T(8,128)(2,1)S(1)}, bf16[96,1152]{1,0:T(8,128)(2,1)S(1)}, u32[]{:S(2)}, u32[]{:S(2)}) collective-permute-start(bf16[96,1152]{1,0:T(8,128)(2,1)S(1)} %add_convert_fusion.16), channel_id=1, source_target_pairs={{0,16},{2,18},{4,20},{6,22},{8,24},{10,26},{12,28},{14,30},{16,0},... | collective-permute-start | bytes 663560 | tf_op jit(solution)/shard_map/ppermute | solution.py:441
  403.4 22.1 %collective-permute-start.94 = (bf16[480,768]{1,0:T(8,128)(2,1)S(1)}, bf16[480,768]{1,0:T(8,128)(2,1)S(1)}, u32[]{:S(2)}, u32[]{:S(2)}) collective-permute-start(bf16[480,768]{1,0:T(8,128)(2,1)S(1)} %broadcast_select_fusion.refs_0_), channel_id=1, source_target_pairs={{0,4},{2,6},{4,0},{6,2},{8,12},{10,14},{12,8},{14,10},{16,20},{18,... | collective-permute-start | bytes 2211848 | tf_op jit(solution)/shard_map/ppermute | solution.py:441
  404.2 11.9 %collective-permute-start.93 = (bf16[96,1152]{1,0:T(8,128)(2,1)S(1)}, bf16[96,1152]{1,0:T(8,128)(2,1)S(1)}, u32[]{:S(2)}, u32[]{:S(2)}) collective-permute-start(bf16[96,1152]{1,0:T(8,128)(2,1)S(1)} %add_convert_fusion.13), channel_id=1, source_target_pairs={{0,16},{2,18},{4,20},{6,22},{8,24},{10,26},{12,28},{14,30},{16,0},... | collective-permute-start | bytes 663560 | tf_op jit(solution)/shard_map/ppermute | solution.py:441
  404.7 20.9 %collective-permute-start.92 = (bf16[96,1152]{1,0:T(8,128)(2,1)S(1)}, bf16[96,1152]{1,0:T(8,128)(2,1)S(1)}, u32[]{:S(2)}, u32[]{:S(2)}) collective-permute-start(bf16[96,1152]{1,0:T(8,128)(2,1)S(1)} %add_convert_fusion.14.refs_0_), channel_id=1, source_target_pairs={{0,4},{2,6},{4,0},{6,2},{8,12},{10,14},{12,8},{14,10},{16,20},{18,... | collective-permute-start | bytes 663560 | tf_op jit(solution)/shard_map/ppermute | solution.py:441
  406.2 9.9 %collective-permute-start.95 = (f32[36,128]{1,0:T(8,128)S(1)}, f32[36,128]{1,0:T(8,128)S(1)}, u32[]{:S(2)}, u32[]{:S(2)}) collective-permute-start(f32[36,128]{1,0:T(8,128)S(1)} %add.356), channel_id=1, source_target_pairs={{0,16},{2,18},{4,20},{6,22},{8,24},{10,26},{12,28},{14,30},{16,0},... | collective-permute-start | bytes 55304 | tf_op jit(solution)/shard_map/ppermute | solution.py:441
  408.7 19.5 %collective-permute-start.99 = (bf16[480,768]{1,0:T(8,128)(2,1)S(1)}, bf16[480,768]{1,0:T(8,128)(2,1)S(1)}, u32[]{:S(2)}, u32[]{:S(2)}) collective-permute-start(bf16[480,768]{1,0:T(8,128)(2,1)S(1)} %broadcast_select_fusion.refs_0_), channel_id=1, source_target_pairs={{0,2},{2,0},{4,6},{6,4},{8,10},{10,8},{12,14},{14,12},{16,18},{18,... | collective-permute-start | bytes 2211848 | tf_op jit(solution)/shard_map/ppermute | solution.py:441
  428.2 12.9 %collective-permute-start.102 = (bf16[96,1152]{1,0:T(8,128)(2,1)S(1)}, bf16[96,1152]{1,0:T(8,128)(2,1)S(1)}, u32[]{:S(2)}, u32[]{:S(2)}) collective-permute-start(bf16[96,1152]{1,0:T(8,128)(2,1)S(1)} %add_convert_fusion.12.refs_4_), channel_id=1, source_target_pairs={{0,2},{2,0},{4,6},{6,4},{8,10},{10,8},{12,14},{14,12},{16,18},{18,... | collective-permute-start | bytes 663560 | tf_op jit(solution)/shard_map/ppermute | solution.py:441
  (125 other events, 1113.1 us)

commit v4 on v3

--- a/solution.py
+++ b/solution.py
@@ -1084,7 +1084,7 @@
     p_send, p_keep = steps.slot(
         "p", work=lambda g_t, dout: proj_terms(place, g_t, dout), given=(g_t, dout)
     )
-    end("dp", p_keep, p_send, "deal", True)
+    end("dp", p_keep, p_send, "deal", False)
     steps.slot("p dp")
     w_proj = steps.done["p"]
 
@@ -1098,7 +1098,7 @@
         given=(dout, slope, y1, mixed, h2_t, vec, [w.arrays for w in (w_out, w_fc, w_proj)]),
     )
     dmixed, dy1, f_send, f_keep, d_gain2, d_shift2, d_outb, d_fcb, d_projb = found
-    end("df", f_keep, f_send, "halves", True)
+    end("df", f_keep, f_send, "deal", False)
 
     def heads_back(first, count, before):
         def run(qkv, mixed, dmixed, soft, h1_t, before):

time: 451 us -> 443 us (0.982)
  starting transfers between devices: 104 us -> 90.1 us
  waiting for transfers between devices: 102 us -> 113 us
    ppermute x83 -> x85, waiting for transfers between devices: 91.1 us -> 107 us  [swap(): lax.ppermute(value, 'wide', [(i, i ^ flip) for i in range(self.wide)])]
    ppermute x6 -> x0, starting transfers between devices: 13.2 us -> none  [shift(): return lax.ppermute(value, 'wide', places)]
    ppermute x15 -> x13, waiting for transfers between devices: 11.1 us -> 3.63 us  [cross(): return lax.ppermute(value, AXES, pairs)]
    all_to_all x1 -> x2, starting transfers between devices: 3.64 us -> 8.61 us  [deal(): lax.all_to_all(value, AXES, 0, 0, axis_index_groups=groups, tiled=True)]
    ppermute x83 -> x85, starting transfers between devices: 71.6 us -> 67.6 us  [swap(): lax.ppermute(value, 'wide', [(i, i ^ flip) for i in range(self.wide)])]
    ppermute x15 -> x13, starting transfers between devices: 15.2 us -> 13.9 us  [cross(): return lax.ppermute(value, AXES, pairs)]
    convert_element_type x21 -> x18, other arithmetic: 25.2 us -> 25.2 us  [add(): functools.reduce(lambda a, b: a + b, [v.astype(f32) for v in values])]
  transfers between devices with their start and end apart: 105 -> 100, of which waited for: 34 -> 38; matrix products, arithmetic and copies ran while one was open for 8% -> 6% of each run, Pallas kernels for 41% -> 41%
where the time goes in v4:
time: 443 us; the launch traced here: 440 us
  Pallas kernels  189 us (43%)
  waiting for transfers between devices  113 us (26%)
  starting transfers between devices  90.1 us (20%)
  other arithmetic  32.4 us (7%)
  local copies, waits for them, and re-layouts  13 us (3%)
    ppermute x85, waiting for transfers between devices, swap(): lax.ppermute(value, 'wide', [(i, i ^ flip) for i in range(self.wide)])  107 us
    ppermute x85, starting transfers between devices, swap(): lax.ppermute(value, 'wide', [(i, i ^ flip) for i in range(self.wide)])  67.6 us
    pallas_call x4, Pallas kernels, attend(): pl.pallas_call(kernel, grid=(count,), in_specs=[pl.BlockSpec(memory_space...  52.6 us
    pallas_call x3, Pallas kernels, by_rows(): pl.pallas_call(kernel, grid=(length // ROWS,), in_specs=[pl.BlockSpec(mem...  43.9 us
    pallas_call x1, Pallas kernels, back_middle(): pl.pallas_call(kernel, grid=(steps + f_steps + 1,), in_specs=[pl.BlockSpe...  33.1 us
    pallas_call x2, Pallas kernels, attend_back(): pl.pallas_call(functools.partial(attend_back_kernel, length=length), grid...  31.3 us
    convert_element_type x18, other arithmetic, add(): functools.reduce(lambda a, b: a + b, [v.astype(f32) for v in values])  25.2 us
    pallas_call x3, Pallas kernels, put(): pl.pallas_call(functools.partial(put_kernel, counts=(len(groups), len(sha...  14.5 us
  transfers between devices with their start and end apart: 100, of which 38 were waited for; matrix products, arithmetic and copies ran while one was open for 6% of the time, Pallas kernels for 41%

profile of v4, /device:TPU:0, one launch (start us, length us, event | category | flops | bytes accessed | tf_op | source)
XLA Modules:
  0.0 440.4 jit_solution(17652451175040463424)
XLA Ops:
  1.9 3.0 pack.1
  5.4 2.5 dynamic-slice_bitcast_fusion
  9.9 3.0 collective-permute-start.2
  13.7 5.8 %collective-permute-done.2 = bf16[96,1280]{1,0:T(8,128)(2,1)S(1)} collective-permute-done((bf16[96,1280]{1,0:T(8,128)(2,1)S(1)}, bf16[96,1280]{1,0:T(8,128)(2,1)S(1)}, u32[]{:S(2)}, u32[]{:S(2)}) %collective-permute-start.2) | collective-permute-done | bytes 245792 | tf_op jit(solution)/shard_map/ppermute | solution.py:441
  20.2 3.3 collective-permute-start.6
  23.5 1.5 collective-permute-start.7
  25.0 6.3 %collective-permute-done.7 = bf16[96,1152]{1,0:T(8,128)(2,1)} collective-permute-done((bf16[96,1152]{1,0:T(8,128)(2,1)}, bf16[96,1152]{1,0:T(8,128)(2,1)}, u32[]{:S(2)}, u32[]{:S(2)}) %collective-permute-start.7) | collective-permute-done | bytes 221216 | tf_op jit(solution)/shard_map/ppermute | solution.py:441
  31.3 4.1 collective-permute-done.6
  39.9 4.4 %collective-permute-done.9 = bf16[96,768]{1,0:T(8,128)(2,1)S(1)} collective-permute-done((bf16[96,768]{1,0:T(8,128)(2,1)S(1)}, bf16[96,768]{1,0:T(8,128)(2,1)S(1)}, u32[]{:S(2)}, u32[]{:S(2)}) %collective-permute-start.9) | collective-permute-done | bytes 147488 | tf_op jit(solution)/shard_map/ppermute | solution.py:441
  44.3 1.5 collective-permute-done.10
  47.9 3.8 collective-permute-start.13
  53.1 8.4 %collective-permute-done.13 = bf16[96,1152]{1,0:T(8,128)(2,1)S(1)} collective-permute-done((bf16[96,1152]{1,0:T(8,128)(2,1)S(1)}, bf16[96,1152]{1,0:T(8,128)(2,1)S(1)}, u32[]{:S(2)}, u32[]{:S(2)}) %collective-permute-start.13) | collective-permute-done | bytes 221216 | tf_op jit(solution)/shard_map/ppermute | solution.py:441
  62.5 3.4 collective-permute-start.14
  67.8 2.9 collective-permute-done.15.refs_6_.refs_7_.refs_13_
  71.5 1.5 collective-permute-start.24
  74.5 1.7 collective-permute-start.18
  82.0 3.3 collective-permute-start.26
  89.3 17.6 %attend.4 = (bf16[1024,768]{1,0:T(8,128)(2,1)}, bf16[12,2304,256]{2,1,0:T(8,128)(2,1)}, bf16[1024,2304]{1,0:T(8,128)(2,1)}, bf16[1024,768]{1,0:T(8,128)(2,1)}, b...) custom-call(s32[4]{0:T(128)} %pad_add_fusion.core_ref.refs_0_.place_ref, s32[1024,1]{1,0:T(8,128)} %copy.40.refs_1_, ...), custom_call_target="tpu_custom_call" | custom-call | flops 1000 | bytes 1000 | tf_op jit(solution)/shard_map/attend/pallas_call | solution.py:142
  109.8 1.5 collective-permute-start.32
  113.0 9.9 %attend.5 = (bf16[1024,768]{1,0:T(8,128)(2,1)}, bf16[12,2304,256]{2,1,0:T(8,128)(2,1)}, bf16[1024,2304]{1,0:T(8,128)(2,1)}) custom-call(s32[4]{0:T(128)} %pad_add_fusion.core_ref.refs_0_.place_ref, s32[1024,1]{1,0:T(8,128)} %copy.40.refs_1_, ...), custom_call_target="tpu_custom_call", output_to_operand_aliasing={{0}: (14, {}), {1}: (15, {}), {2}: (16, {})} | custom-call | flops 1000 | bytes 1000 | tf_op jit(solution)/shard_map/attend/pallas_call | solution.py:142
  122.9 2.9 collective-permute-start.42
  126.6 1.6 collective-permute-start.40
  128.2 1.9 collective-permute-start.41
  130.1 15.3 %attend.6 = (bf16[1024,768]{1,0:T(8,128)(2,1)}, bf16[12,2304,256]{2,1,0:T(8,128)(2,1)}, bf16[1024,2304]{1,0:T(8,128)(2,1)}) custom-call(s32[4]{0:T(128)} %pad_add_fusion.core_ref.refs_0_.place_ref, s32[1024,1]{1,0:T(8,128)} %copy.40.refs_1_, ...), custom_call_target="tpu_custom_call", output_to_operand_aliasing={{0}: (14, {}), {1}: (15, {}), {2}: (16, {})} | custom-call | flops 1000 | bytes 1000 | tf_op jit(solution)/shard_map/attend/pallas_call | solution.py:142
  145.4 6.6 %collective-permute-done.42 = bf16[384,768]{1,0:T(8,128)(2,1)S(1)} collective-permute-done((bf16[384,768]{1,0:T(8,128)(2,1)S(1)}, bf16[384,768]{1,0:T(8,128)(2,1)S(1)}, u32[]{:S(2)}, u32[]{:S(2)}) %collective-permute-start.42) | collective-permute-done | bytes 589856 | tf_op jit(solution)/shard_map/ppermute | solution.py:441
  157.1 9.8 %attend.7 = (bf16[1024,768]{1,0:T(8,128)(2,1)}, bf16[12,2304,256]{2,1,0:T(8,128)(2,1)}, bf16[1024,2304]{1,0:T(8,128)(2,1)}) custom-call(s32[4]{0:T(128)} %pad_add_fusion.core_ref.refs_0_.place_ref, s32[1024,1]{1,0:T(8,128)} %copy.40.refs_1_, ...), custom_call_target="tpu_custom_call", output_to_operand_aliasing={{0}: (14, {}), {1}: (15, {}), {2}: (16, {})} | custom-call | flops 1000 | bytes 1000 | tf_op jit(solution)/shard_map/attend/pallas_call | solution.py:142
  167.6 1.7 collective-permute-start.51
  173.8 20.6 %widen.1 = (f32[1024,768]{1,0:T(8,128)}, bf16[1024,3072]{1,0:T(8,128)(2,1)}, bf16[768,1024]{1,0:T(8,128)(2,1)}, bf16[3072,1024]{1,0:T(8,128)(2,1)}) custom-call(s32[4]{0:T(128)} %pad_add_fusion.core_ref.refs_0_.place_ref, bf16[1024,768]{1,0:T(8,128)(2,1)} %bitcast.110, bf16[1024,768]{1,0:T(8,128)(2,1)} %get-tuple-element.710.refs_2_.refs_4_.o_ref, ...), custom_call_target="tpu_custom_call" | custom-call | flops 1000 | bytes 1000 | tf_op jit(solution)/shard_map/widen/pallas_call | solution.py:585
  195.5 10.4 %proj_terms.1 = (bf16[1536,768]{1,0:T(8,128)(2,1)}, bf16[1536,768]{1,0:T(8,128)(2,1)}) custom-call(s32[4]{0:T(128)} %pad_add_fusion.core_ref.refs_0_.place_ref, bf16[3072,1024]{1,0:T(8,128)(2,1)} %get-tuple-element.767.g_ref.refs_2_, bf16[1024,768]{1,0:T(8,128)(2,1)} %bitcast.113), custom_call_target="tpu_custom_call" | custom-call | flops 1000 | bytes 1000 | tf_op jit(solution)/shard_map/proj_terms/pallas_call | solution.py:297
  207.1 3.9 collective-permute-done.61.refs_32_.refs_9_
  213.9 3.8 add_convert_fusion.1
  217.7 4.0 all-to-all-start
  221.7 33.1 %back_middle.1 = (bf16[1024,768]{1,0:T(8,128)(2,1)}, f32[1024,768]{1,0:T(8,128)}, bf16[4,480,768]{2,1,0:T(8,128)(2,1)}, bf16[4,480,768]{2,1,0:T(8,128)(2,1)}, f3...) custom-call(s32[4]{0:T(128)} %pad_add_fusion.core_ref.refs_0_.place_ref, ...), custom_call_target="tpu_custom_call" | custom-call | flops 1000 | bytes 1000 | tf_op jit(solution)/shard_map/back_middle/pallas_call | solution.py:394
  256.6 15.7 %attend_back.2 = (bf16[1024,2304]{1,0:T(8,128)(2,1)}, bf16[384,1152]{1,0:T(8,128)(2,1)}, bf16[384,1152]{1,0:T(8,128)(2,1)}) custom-call(s32[4]{0:T(128)} %pad_add_fusion.core_ref.refs_0_.place_ref, bf16[1024,2304]{1,0:T(8,128)(2,1)} %get-tuple-element.709.q_ref.k_ref.v_ref, bf16[1024,2304]{1,0:T(8,128)(2,1)} %get-tuple-element.709.q_ref.k_ref.v_ref, ...), custom_call_target="tpu_custom_call" | custom-call | flops 1000 | bytes 1000 | tf_op jit(solution)/shard_map/attend_back/pallas_call | solution.py:252
  273.1 4.2 add_convert_fusion
  277.3 4.6 %all-to-all-start.1 = ((bf16[4,480,768]{2,1,0:T(8,128)(2,1)}), bf16[4,480,768]{2,1,0:T(8,128)(2,1)S(1)}, u32[]{:S(2)}, u32[]{:S(2)}) async-start(bf16[4,480,768]{2,1,0:T(8,128)(2,1)} %add_convert_fusion), calls=%async_computation.1 | async-start | bytes 5898240 | tf_op jit(solution)/shard_map/all_to_all | solution.py:462
  282.0 2.1 add_convert_fusion.6
  284.1 2.7 collective-permute-start.69
  286.8 15.6 %attend_back.3 = (bf16[1024,2304]{1,0:T(8,128)(2,1)}, bf16[384,1152]{1,0:T(8,128)(2,1)}, bf16[384,1152]{1,0:T(8,128)(2,1)}) custom-call(s32[4]{0:T(128)} %pad_add_fusion.core_ref.refs_0_.place_ref, bf16[1024,2304]{1,0:T(8,128)(2,1)} %get-tuple-element.709.q_ref.k_ref.v_ref, ...), custom_call_target="tpu_custom_call", output_to_operand_aliasing={{0}: (8, {})} | custom-call | flops 1000 | bytes 1000 | tf_op jit(solution)/shard_map/attend_back/pallas_call | solution.py:252
  302.4 11.1 %collective-permute-done.69 = bf16[384,768]{1,0:T(8,128)(2,1)} collective-permute-done((bf16[384,768]{1,0:T(8,128)(2,1)S(1)}, bf16[384,768]{1,0:T(8,128)(2,1)}, u32[]{:S(2)}, u32[]{:S(2)}) %collective-permute-start.69) | collective-permute-done | bytes 589856 | tf_op jit(solution)/shard_map/ppermute | solution.py:441
  313.6 2.8 all-to-all-done.1
  318.9 1.5 collective-permute-start.73
  322.1 11.9 %back_first.1 = (bf16[1024,768]{1,0:T(8,128)(2,1)}, f32[1,768]{1,0:T(1,128)}, f32[1,768]{1,0:T(1,128)}, f32[1,1536]{1,0:T(1,128)}, f32[72,128]{1,0:T(8,128)}) custom-call(s32[4]{0:T(128)} %pad_add_fusion.core_ref.refs_0_.place_ref, bf16[1024,2304]{1,0:T(8,128)(2,1)} %get-tuple-element.729.refs_1_, bf16[1024,768]{1,0:T(8,128)(2,1)} %bitcast.111, ...), custom_call_target="tpu_custom_call" | custom-call | flops 1000 | bytes 1000 | tf_op jit(solution)/shard_map/back_first/pallas_call | solution.py:585
  335.9 3.4 collective-permute-start.76
  339.8 2.1 fusion.1
  343.3 1.9 fusion.5
  346.6 11.4 %finish.1 = bf16[1024,768]{1,0:T(8,128)(2,1)} custom-call(s32[4]{0:T(128)} %pad_add_fusion.core_ref.refs_0_.place_ref, f32[1024,768]{1,0:T(8,128)} %get-tuple-element.766.refs_3_.refs_1_, bf16[3072,1024]{1,0:T(8,128)(2,1)} %get-tuple-element.767.g_ref.refs_2_, f32[72,128]{1,0:T(8,128)} %get-tuple-element.768.refs_3_.refs_6_.refs_4_, ...), custom_call_target="tpu_custom_call" | custom-call | flops 1000 | bytes 1000 | tf_op jit(solution)/shard_map/finish/pallas_call | solution.py:585
  358.1 13.6 %collective-permute-done.76 = bf16[480,768]{1,0:T(8,128)(2,1)S(1)} collective-permute-done((bf16[480,768]{1,0:T(8,128)(2,1)}, bf16[480,768]{1,0:T(8,128)(2,1)S(1)}, u32[]{:S(2)}, u32[]{:S(2)}) %collective-permute-start.76) | collective-permute-done | bytes 737312 | tf_op jit(solution)/shard_map/ppermute | solution.py:441
  374.5 1.7 fusion.3
  378.2 1.6 collective-permute-start.83
  379.8 4.8 %put_proj.1 = f32[1536,768]{1,0:T(8,128)} custom-call(s32[4]{0:T(128)} %pad_add_fusion.core_ref.refs_0_.place_ref, bf16[384,768]{1,0:T(8,128)(2,1)} %copy-done.18, bf16[384,768]{1,0:T(8,128)(2,1)} %copy-done.58, bf16[384,768]{1,0:T(8,128)(2,1)} %copy-done.59, bf16[384,768]{1,0:T(8,128)(2,1)} %collective-permute-done.78.refs_3_), custom_call_target="tpu_custom_call" | custom-call | flops 1000 | bytes 1000 | tf_op jit(solution)/shard_map/put_proj/pallas_call | solution.py:740
  384.6 11.7 %collective-permute-done.81 = bf16[96,1152]{1,0:T(8,128)(2,1)} collective-permute-done((bf16[96,1152]{1,0:T(8,128)(2,1)}, bf16[96,1152]{1,0:T(8,128)(2,1)}, u32[]{:S(2)}, u32[]{:S(2)}) %collective-permute-start.81) | collective-permute-done | bytes 221216 | tf_op jit(solution)/shard_map/ppermute | solution.py:441
  398.8 2.3 collective-permute-start.84
  402.6 2.3 collective-permute-done.88
  404.9 3.3 collective-permute-done.85
  408.2 4.0 collective-permute-done.84
  412.4 1.5 collective-permute-start.89
  414.0 2.8 collective-permute-start.91
  416.8 5.4 %put_fc.1 = (f32[384,3072]{1,0:T(8,128)}, f32[384,768]{1,0:T(8,128)}) custom-call(s32[4]{0:T(128)} %pad_add_fusion.core_ref.refs_0_.place_ref, bf16[480,768]{1,0:T(8,128)(2,1)} %copy-done.12, bf16[480,768]{1,0:T(8,128)(2,1)} %copy-done.55, bf16[480,768]{1,0:T(8,128)(2,1)} %copy-done.56, bf16[480,768]{1,0:T(8,128)(2,1)} %copy-done.57), custom_call_target="tpu_custom_call" | custom-call | flops 1000 | bytes 1000 | tf_op jit(solution)/shard_map/put_fc/pallas_call | solution.py:740
  422.2 2.6 collective-permute-done.91
  424.9 1.5 collective-permute-start.94
  427.0 3.3 collective-permute-done.95
  430.3 2.1 collective-permute-done.94.refs_5_
  435.9 4.3 put_qkv.1
  (388 shorter events, 72.7 us)
Async XLA Ops:
  9.9 9.6 %collective-permute-start.2 = (bf16[96,1280]{1,0:T(8,128)(2,1)S(1)}, bf16[96,1280]{1,0:T(8,128)(2,1)S(1)}, u32[]{:S(2)}, u32[]{:S(2)}) collective-permute-start(bf16[96,1280]{1,0:T(8,128)(2,1)S(1)} %dynamic-slice_bitcast_fusion.5), channel_id=1, source_target_pairs={{0,4},{2,6},{4,0},{6,2},{8,12},{10,14},{12,8},{14,10},{16,20},{18,... | collective-permute-start | bytes 737288 | tf_op jit(solution)/shard_map/ppermute | solution.py:441
  19.5 15.9 %collective-permute-start.3 = (bf16[192,3072]{1,0:T(8,128)(2,1)}, bf16[192,3072]{1,0:T(8,128)(2,1)}, u32[]{:S(2)}, u32[]{:S(2)}) collective-permute-start(bf16[192,3072]{1,0:T(8,128)(2,1)} %dynamic-slice_bitcast_fusion.1), channel_id=1, source_target_pairs={{0,2},{2,0},{4,6},{6,4},{8,10},{10,8},{12,14},{14,12},{16,18},{18,... | collective-permute-start | bytes 3538952 | tf_op jit(solution)/shard_map/ppermute | solution.py:441
  19.7 15.7 %collective-permute-start.5 = (bf16[768,768]{1,0:T(8,128)(2,1)}, bf16[768,768]{1,0:T(8,128)(2,1)}, u32[]{:S(2)}, u32[]{:S(2)}) collective-permute-start(bf16[768,768]{1,0:T(8,128)(2,1)} %dynamic-slice_bitcast_fusion), channel_id=1, source_target_pairs={{0,2},{2,0},{4,6},{6,4},{8,10},{10,8},{12,14},{14,12},{16,18},{18,... | collective-permute-start | bytes 3538952 | tf_op jit(solution)/shard_map/ppermute | solution.py:441
  20.1 15.3 %collective-permute-start.4 = (bf16[192,768]{1,0:T(8,128)(2,1)}, bf16[192,768]{1,0:T(8,128)(2,1)S(1)}, u32[]{:S(2)}, u32[]{:S(2)}) collective-permute-start(bf16[192,768]{1,0:T(8,128)(2,1)} %dynamic-slice_bitcast_fusion.4), channel_id=1, source_target_pairs={{0,2},{2,0},{4,6},{6,4},{8,10},{10,8},{12,14},{14,12},{16,18},{18,... | collective-permute-start | bytes 884744 | tf_op jit(solution)/shard_map/ppermute | solution.py:441
  20.2 15.2 %collective-permute-start.6 = (bf16[96,1280]{1,0:T(8,128)(2,1)S(1)}, bf16[96,1280]{1,0:T(8,128)(2,1)}, u32[]{:S(2)}, u32[]{:S(2)}) collective-permute-start(bf16[96,1280]{1,0:T(8,128)(2,1)S(1)} %bitcast_select_fusion.5), channel_id=1, source_target_pairs={{0,16},{2,18},{4,20},{6,22},{8,24},{10,26},{12,28},{14,30},{16,0},... | collective-permute-start | bytes 737288 | tf_op jit(solution)/shard_map/ppermute | solution.py:441
  37.6 8.3 %collective-permute-start.10 = (bf16[96,1280]{1,0:T(8,128)(2,1)S(1)}, bf16[96,1280]{1,0:T(8,128)(2,1)S(1)}, u32[]{:S(2)}, u32[]{:S(2)}) collective-permute-start(bf16[96,1280]{1,0:T(8,128)(2,1)S(1)} %broadcast_select_fusion.7), channel_id=1, source_target_pairs={{0,8},{2,10},{4,12},{6,14},{8,0},{10,2},{12,4},{14,6},{16,24},{18,... | collective-permute-start | bytes 737288 | tf_op jit(solution)/shard_map/ppermute | solution.py:441
  45.9 15.7 %collective-permute-start.11 = (bf16[96,1280]{1,0:T(8,128)(2,1)S(1)}, bf16[96,1280]{1,0:T(8,128)(2,1)S(1)}, u32[]{:S(2)}, u32[]{:S(2)}) collective-permute-start(bf16[96,1280]{1,0:T(8,128)(2,1)S(1)} %broadcast_select_fusion.6.refs_3_.refs_4_.refs_10_), channel_id=1, source_target_pairs={{0,4},{2,6},{4,0},{6,2},{8,12},{10,14},{12,8},{14,10},{16,20},{18,... | collective-permute-start | bytes 737288 | tf_op jit(solution)/shard_map/ppermute | solution.py:441
  46.4 15.2 %collective-permute-start.12 = (bf16[96,1280]{1,0:T(8,128)(2,1)S(1)}, bf16[96,1280]{1,0:T(8,128)(2,1)S(1)}, u32[]{:S(2)}, u32[]{:S(2)}) collective-permute-start(bf16[96,1280]{1,0:T(8,128)(2,1)S(1)} %broadcast_select_fusion.6.refs_3_.refs_4_.refs_10_), channel_id=1, source_target_pairs={{0,1},{1,0},{2,3},{3,2},{4,5},{5,4},{6,7},{7,6},{8,9},{9,8},{10,11... | collective-permute-start | bytes 737288 | tf_op jit(solution)/shard_map/ppermute | solution.py:445
  47.9 13.7 %collective-permute-start.13 = (bf16[96,1152]{1,0:T(8,128)(2,1)S(1)}, bf16[96,1152]{1,0:T(8,128)(2,1)S(1)}, u32[]{:S(2)}, u32[]{:S(2)}) collective-permute-start(bf16[96,1152]{1,0:T(8,128)(2,1)S(1)} %bitcast_select_fusion.6), channel_id=1, source_target_pairs={{0,16},{2,18},{4,20},{6,22},{8,24},{10,26},{12,28},{14,30},{16,0},... | collective-permute-start | bytes 663560 | tf_op jit(solution)/shard_map/ppermute | solution.py:441
  51.7 16.1 %collective-permute-start.8 = (bf16[96,3072]{1,0:T(8,128)(2,1)S(1)}, bf16[96,3072]{1,0:T(8,128)(2,1)S(1)}, u32[]{:S(2)}, u32[]{:S(2)}) collective-permute-start(bf16[96,3072]{1,0:T(8,128)(2,1)S(1)} %dynamic-slice_bitcast_fusion.3), channel_id=1, source_target_pairs={{0,4},{2,6},{4,0},{6,2},{8,12},{10,14},{12,8},{14,10},{16,20},{18,... | collective-permute-start | bytes 1769480 | tf_op jit(solution)/shard_map/ppermute | solution.py:441
  61.7 9.6 %collective-permute-start.17 = (bf16[96,1152]{1,0:T(8,128)(2,1)S(1)}, bf16[96,1152]{1,0:T(8,128)(2,1)S(1)}, u32[]{:S(2)}, u32[]{:S(2)}) collective-permute-start(bf16[96,1152]{1,0:T(8,128)(2,1)S(1)} %broadcast_select_fusion.9), channel_id=1, source_target_pairs={{0,8},{2,10},{4,12},{6,14},{8,0},{10,2},{12,4},{14,6},{16,24},{18,... | collective-permute-start | bytes 663560 | tf_op jit(solution)/shard_map/ppermute | solution.py:441
  62.5 8.8 %collective-permute-start.14 = (bf16[96,768]{1,0:T(8,128)(2,1)S(1)}, bf16[96,768]{1,0:T(8,128)(2,1)S(1)}, u32[]{:S(2)}, u32[]{:S(2)}) collective-permute-start(bf16[96,768]{1,0:T(8,128)(2,1)S(1)} %bitcast_select_fusion.7), channel_id=1, source_target_pairs={{0,16},{2,18},{4,20},{6,22},{8,24},{10,26},{12,28},{14,30},{16,0},... | collective-permute-start | bytes 442376 | tf_op jit(solution)/shard_map/ppermute | solution.py:441
  71.5 8.3 %collective-permute-start.24 = (bf16[96,1152]{1,0:T(8,128)(2,1)S(1)}, bf16[96,1152]{1,0:T(8,128)(2,1)S(1)}, u32[]{:S(2)}, u32[]{:S(2)}) collective-permute-start(bf16[96,1152]{1,0:T(8,128)(2,1)S(1)} %broadcast_select_fusion.8.refs_4_.refs_20_), channel_id=1, source_target_pairs={{0,4},{2,6},{4,0},{6,2},{8,12},{10,14},{12,8},{14,10},{16,20},{18,... | collective-permute-start | bytes 663560 | tf_op jit(solution)/shard_map/ppermute | solution.py:441
  74.5 32.5 %collective-permute-start.18 = (bf16[96,3072]{1,0:T(8,128)(2,1)S(1)}, bf16[96,3072]{1,0:T(8,128)(2,1)}, u32[]{:S(2)}, u32[]{:S(2)}) collective-permute-start(bf16[96,3072]{1,0:T(8,128)(2,1)S(1)} %bitcast_select_fusion.2), channel_id=1, source_target_pairs={{0,16},{2,18},{4,20},{6,22},{8,24},{10,26},{12,28},{14,30},{16,0},... | collective-permute-start | bytes 1769480 | tf_op jit(solution)/shard_map/ppermute | solution.py:441
  76.2 30.8 %collective-permute-start.27 = (bf16[384,768]{1,0:T(8,128)(2,1)}, bf16[384,768]{1,0:T(8,128)(2,1)}, u32[]{:S(2)}, u32[]{:S(2)}) collective-permute-start(bf16[384,768]{1,0:T(8,128)(2,1)} %dynamic-slice_bitcast_fusion.2), channel_id=1, source_target_pairs={{0,4},{2,6},{4,0},{6,2},{8,12},{10,14},{12,8},{14,10},{16,20},{18,... | collective-permute-start | bytes 1769480 | tf_op jit(solution)/shard_map/ppermute | solution.py:441
  82.0 25.0 %collective-permute-start.26 = (bf16[96,768]{1,0:T(8,128)(2,1)}, bf16[96,768]{1,0:T(8,128)(2,1)}, u32[]{:S(2)}, u32[]{:S(2)}) collective-permute-start(bf16[96,768]{1,0:T(8,128)(2,1)} %broadcast_select_fusion.11), channel_id=1, source_target_pairs={{0,8},{2,10},{4,12},{6,14},{8,0},{10,2},{12,4},{14,6},{16,24},{18,... | collective-permute-start | bytes 442376 | tf_op jit(solution)/shard_map/ppermute | solution.py:441
  86.6 20.3 %collective-permute-start.28 = (bf16[48,1152]{1,0:T(8,128)(2,1)}, bf16[48,1152]{1,0:T(8,128)(2,1)}, u32[]{:S(2)}, u32[]{:S(2)}) collective-permute-start(bf16[48,1152]{1,0:T(8,128)(2,1)} %slice.64), channel_id=1, source_target_pairs={{0,1},{1,0},{2,3},{3,2},{4,5},{5,4},{6,7},{7,6},{8,9},{9,8},{10,11... | collective-permute-start | bytes 331784 | tf_op jit(solution)/shard_map/ppermute | solution.py:445
  87.2 19.8 %collective-permute-start.29 = (bf16[48,1152]{1,0:T(8,128)(2,1)}, bf16[48,1152]{1,0:T(8,128)(2,1)S(1)}, u32[]{:S(2)}, u32[]{:S(2)}) collective-permute-start(bf16[48,1152]{1,0:T(8,128)(2,1)} %slice.65), channel_id=1, source_target_pairs={{0,4},{2,6},{4,0},{6,2},{8,12},{10,14},{12,8},{14,10},{16,20},{18,... | collective-permute-start | bytes 331784 | tf_op jit(solution)/shard_map/ppermute | solution.py:441
  107.1 18.7 %collective-permute-start.30 = (bf16[96,3072]{1,0:T(8,128)(2,1)S(1)}, bf16[96,3072]{1,0:T(8,128)(2,1)S(1)}, u32[]{:S(2)}, u32[]{:S(2)}) collective-permute-start(bf16[96,3072]{1,0:T(8,128)(2,1)S(1)} %broadcast_select_fusion), channel_id=1, source_target_pairs={{0,8},{2,10},{4,12},{6,14},{8,0},{10,2},{12,4},{14,6},{16,24},{18,... | collective-permute-start | bytes 1769480 | tf_op jit(solution)/shard_map/ppermute | solution.py:441
  108.8 17.0 %collective-permute-start.31 = (bf16[96,768]{1,0:T(8,128)(2,1)S(1)}, bf16[96,768]{1,0:T(8,128)(2,1)S(1)}, u32[]{:S(2)}, u32[]{:S(2)}) collective-permute-start(bf16[96,768]{1,0:T(8,128)(2,1)S(1)} %broadcast_select_fusion.10.refs_4_.refs_7_), channel_id=1, source_target_pairs={{0,4},{2,6},{4,0},{6,2},{8,12},{10,14},{12,8},{14,10},{16,20},{18,... | collective-permute-start | bytes 442376 | tf_op jit(solution)/shard_map/ppermute | solution.py:441
  109.8 16.0 %collective-permute-start.32 = (bf16[96,768]{1,0:T(8,128)(2,1)S(1)}, bf16[96,768]{1,0:T(8,128)(2,1)S(1)}, u32[]{:S(2)}, u32[]{:S(2)}) collective-permute-start(bf16[96,768]{1,0:T(8,128)(2,1)S(1)} %broadcast_select_fusion.10.refs_4_.refs_7_), channel_id=1, source_target_pairs={{0,1},{1,0},{2,3},{3,2},{4,5},{5,4},{6,7},{7,6},{8,9},{9,8},{10,11... | collective-permute-start | bytes 442376 | tf_op jit(solution)/shard_map/ppermute | solution.py:445
  111.3 11.6 %collective-permute-start.36 = (bf16[48,1152]{1,0:T(8,128)(2,1)}, bf16[48,1152]{1,0:T(8,128)(2,1)S(1)}, u32[]{:S(2)}, u32[]{:S(2)}) collective-permute-start(bf16[48,1152]{1,0:T(8,128)(2,1)} %collective-permute-done.28.refs_7_.refs_23_), channel_id=1, source_target_pairs={{0,2},{2,0},{4,6},{6,4},{8,10},{10,8},{12,14},{14,12},{16,18},{18,... | collective-permute-start | bytes 331784 | tf_op jit(solution)/shard_map/ppermute | solution.py:441
  111.3 14.4 %collective-permute-start.37 = (bf16[48,1152]{1,0:T(8,128)(2,1)S(1)}, bf16[48,1152]{1,0:T(8,128)(2,1)S(1)}, u32[]{:S(2)}, u32[]{:S(2)}) collective-permute-start(bf16[48,1152]{1,0:T(8,128)(2,1)S(1)} %collective-permute-done.29.refs_8_.refs_24_), channel_id=1, source_target_pairs={{0,2},{2,0},{4,6},{6,4},{8,10},{10,8},{12,14},{14,12},{16,18},{18,... | collective-permute-start | bytes 331784 | tf_op jit(solution)/shard_map/ppermute | solution.py:441
  122.9 29.1 %collective-permute-start.42 = (bf16[384,768]{1,0:T(8,128)(2,1)S(1)}, bf16[384,768]{1,0:T(8,128)(2,1)S(1)}, u32[]{:S(2)}, u32[]{:S(2)}) collective-permute-start(bf16[384,768]{1,0:T(8,128)(2,1)S(1)} %bitcast_select_fusion.3), channel_id=1, source_target_pairs={{0,16},{2,18},{4,20},{6,22},{8,24},{10,26},{12,28},{14,30},{16,0},... | collective-permute-start | bytes 1769480 | tf_op jit(solution)/shard_map/ppermute | solution.py:441
  125.9 26.1 %collective-permute-start.38 = (bf16[96,3072]{1,0:T(8,128)(2,1)S(1)}, bf16[96,3072]{1,0:T(8,128)(2,1)S(1)}, u32[]{:S(2)}, u32[]{:S(2)}) collective-permute-start(bf16[96,3072]{1,0:T(8,128)(2,1)S(1)} %broadcast_select_fusion.1.refs_14_.refs_17_), channel_id=1, source_target_pairs={{0,4},{2,6},{4,0},{6,2},{8,12},{10,14},{12,8},{14,10},{16,20},{18,... | collective-permute-start | bytes 1769480 | tf_op jit(solution)/shard_map/ppermute | solution.py:441
  126.0 26.1 %collective-permute-start.39 = (bf16[96,3072]{1,0:T(8,128)(2,1)S(1)}, bf16[96,3072]{1,0:T(8,128)(2,1)S(1)}, u32[]{:S(2)}, u32[]{:S(2)}) collective-permute-start(bf16[96,3072]{1,0:T(8,128)(2,1)S(1)} %broadcast_select_fusion.1.refs_14_.refs_17_), channel_id=1, source_target_pairs={{0,1},{1,0},{2,3},{3,2},{4,5},{5,4},{6,7},{7,6},{8,9},{9,8},{10,11... | collective-permute-start | bytes 1769480 | tf_op jit(solution)/shard_map/ppermute | solution.py:445
  126.6 25.4 %collective-permute-start.40 = (bf16[48,768]{1,0:T(8,128)(2,1)S(1)}, bf16[48,768]{1,0:T(8,128)(2,1)S(1)}, u32[]{:S(2)}, u32[]{:S(2)}) collective-permute-start(bf16[48,768]{1,0:T(8,128)(2,1)S(1)} %slice.66), channel_id=1, source_target_pairs={{0,1},{1,0},{2,3},{3,2},{4,5},{5,4},{6,7},{7,6},{8,9},{9,8},{10,11... | collective-permute-start | bytes 221192 | tf_op jit(solution)/shard_map/ppermute | solution.py:445
  128.2 23.9 %collective-permute-start.41 = (bf16[48,768]{1,0:T(8,128)(2,1)S(1)}, bf16[48,768]{1,0:T(8,128)(2,1)S(1)}, u32[]{:S(2)}, u32[]{:S(2)}) collective-permute-start(bf16[48,768]{1,0:T(8,128)(2,1)S(1)} %slice.67), channel_id=1, source_target_pairs={{0,4},{2,6},{4,0},{6,2},{8,12},{10,14},{12,8},{14,10},{16,20},{18,... | collective-permute-start | bytes 221192 | tf_op jit(solution)/shard_map/ppermute | solution.py:441
  152.2 15.3 %collective-permute-start.50 = (bf16[384,768]{1,0:T(8,128)(2,1)S(1)}, bf16[384,768]{1,0:T(8,128)(2,1)S(1)}, u32[]{:S(2)}, u32[]{:S(2)}) collective-permute-start(bf16[384,768]{1,0:T(8,128)(2,1)S(1)} %broadcast_select_fusion.2), channel_id=1, source_target_pairs={{0,8},{2,10},{4,12},{6,14},{8,0},{10,2},{12,4},{14,6},{16,24},{18,... | collective-permute-start | bytes 1769480 | tf_op jit(solution)/shard_map/ppermute | solution.py:441
  153.0 14.0 %collective-permute-start.43 = (bf16[48,3072]{1,0:T(8,128)(2,1)S(1)}, bf16[48,3072]{1,0:T(8,128)(2,1)S(1)}, u32[]{:S(2)}, u32[]{:S(2)}) collective-permute-start(bf16[48,3072]{1,0:T(8,128)(2,1)S(1)} %slice.68), channel_id=1, source_target_pairs={{0,1},{1,0},{2,3},{3,2},{4,5},{5,4},{6,7},{7,6},{8,9},{9,8},{10,11... | collective-permute-start | bytes 884744 | tf_op jit(solution)/shard_map/ppermute | solution.py:445
  153.6 13.9 %collective-permute-start.44 = (bf16[48,3072]{1,0:T(8,128)(2,1)S(1)}, bf16[48,3072]{1,0:T(8,128)(2,1)S(1)}, u32[]{:S(2)}, u32[]{:S(2)}) collective-permute-start(bf16[48,3072]{1,0:T(8,128)(2,1)S(1)} %slice.69), channel_id=1, source_target_pairs={{0,4},{2,6},{4,0},{6,2},{8,12},{10,14},{12,8},{14,10},{16,20},{18,... | collective-permute-start | bytes 884744 | tf_op jit(solution)/shard_map/ppermute | solution.py:441
  156.4 14.3 %collective-permute-start.53 = (bf16[96,3072]{1,0:T(8,128)(2,1)S(1)}, bf16[96,3072]{1,0:T(8,128)(2,1)S(1)}, u32[]{:S(2)}, u32[]{:S(2)}) collective-permute-start(bf16[96,3072]{1,0:T(8,128)(2,1)S(1)} %broadcast_select_fusion.1.refs_14_.refs_17_), channel_id=1, source_target_pairs={{0,2},{2,0},{4,6},{6,4},{8,10},{10,8},{12,14},{14,12},{16,18},{18,... | collective-permute-start | bytes 1769480 | tf_op jit(solution)/shard_map/ppermute | solution.py:441
  157.0 13.8 %collective-permute-start.54 = (bf16[96,3072]{1,0:T(8,128)(2,1)S(1)}, bf16[96,3072]{1,0:T(8,128)(2,1)S(1)}, u32[]{:S(2)}, u32[]{:S(2)}) collective-permute-start(bf16[96,3072]{1,0:T(8,128)(2,1)S(1)} %collective-permute-done.38.refs_15_.refs_18_), channel_id=1, source_target_pairs={{0,2},{2,0},{4,6},{6,4},{8,10},{10,8},{12,14},{14,12},{16,18},{18,... | collective-permute-start | bytes 1769480 | tf_op jit(solution)/shard_map/ppermute | solution.py:441
  167.6 26.8 %collective-permute-start.51 = (bf16[384,768]{1,0:T(8,128)(2,1)S(1)}, bf16[384,768]{1,0:T(8,128)(2,1)S(1)}, u32[]{:S(2)}, u32[]{:S(2)}) collective-permute-start(bf16[384,768]{1,0:T(8,128)(2,1)S(1)} %broadcast_select_fusion.3.refs_27_.refs_4_), channel_id=1, source_target_pairs={{0,4},{2,6},{4,0},{6,2},{8,12},{10,14},{12,8},{14,10},{16,20},{18,... | collective-permute-start | bytes 1769480 | tf_op jit(solution)/shard_map/ppermute | solution.py:441
  169.2 25.2 %collective-permute-start.52 = (bf16[384,768]{1,0:T(8,128)(2,1)S(1)}, bf16[384,768]{1,0:T(8,128)(2,1)S(1)}, u32[]{:S(2)}, u32[]{:S(2)}) collective-permute-start(bf16[384,768]{1,0:T(8,128)(2,1)S(1)} %broadcast_select_fusion.3.refs_27_.refs_4_), channel_id=1, source_target_pairs={{0,1},{1,0},{2,3},{3,2},{4,5},{5,4},{6,7},{7,6},{8,9},{9,8},{10,11... | collective-permute-start | bytes 1769480 | tf_op jit(solution)/shard_map/ppermute | solution.py:445
  194.5 11.4 %collective-permute-start.58 = (bf16[192,768]{1,0:T(8,128)(2,1)S(1)}, bf16[192,768]{1,0:T(8,128)(2,1)S(1)}, u32[]{:S(2)}, u32[]{:S(2)}) collective-permute-start(bf16[192,768]{1,0:T(8,128)(2,1)S(1)} %slice.70), channel_id=1, source_target_pairs={{0,1},{1,0},{2,3},{3,2},{4,5},{5,4},{6,7},{7,6},{8,9},{9,8},{10,11... | collective-permute-start | bytes 884744 | tf_op jit(solution)/shard_map/ppermute | solution.py:445
  195.1 10.8 %collective-permute-start.59 = (bf16[192,768]{1,0:T(8,128)(2,1)S(1)}, bf16[192,768]{1,0:T(8,128)(2,1)S(1)}, u32[]{:S(2)}, u32[]{:S(2)}) collective-permute-start(bf16[192,768]{1,0:T(8,128)(2,1)S(1)} %slice.71), channel_id=1, source_target_pairs={{0,4},{2,6},{4,0},{6,2},{8,12},{10,14},{12,8},{14,10},{16,20},{18,... | collective-permute-start | bytes 884744 | tf_op jit(solution)/shard_map/ppermute | solution.py:441
  205.9 8.0 %collective-permute-start.60 = (bf16[1536,768]{1,0:T(8,128)(2,1)}, bf16[1536,768]{1,0:T(8,128)(2,1)S(1)}, u32[]{:S(2)}, u32[]{:S(2)}) collective-permute-start(bf16[1536,768]{1,0:T(8,128)(2,1)} %get-tuple-element.632), channel_id=1, source_target_pairs={{0,2},{2,0},{4,6},{6,4},{8,10},{10,8},{12,14},{14,12},{16,18},{18,... | collective-permute-start | bytes 7077896 | tf_op jit(solution)/shard_map/ppermute | solution.py:441
  217.7 37.1 %all-to-all-start = ((bf16[4,384,768]{2,1,0:T(8,128)(2,1)}), bf16[4,384,768]{2,1,0:T(8,128)(2,1)S(1)}, u32[]{:S(2)}, u32[]{:S(2)}) async-start(bf16[4,384,768]{2,1,0:T(8,128)(2,1)} %bitcast.112), calls=%async_computation | async-start | bytes 4718592 | tf_op jit(solution)/shard_map/all_to_all | solution.py:462
  254.8 18.2 %collective-permute-start.66 = (bf16[4,480,768]{2,1,0:T(8,128)(2,1)}, bf16[4,480,768]{2,1,0:T(8,128)(2,1)}, u32[]{:S(2)}, u32[]{:S(2)}) collective-permute-start(bf16[4,480,768]{2,1,0:T(8,128)(2,1)} %get-tuple-element.689), channel_id=1, source_target_pairs={{0,2},{2,0},{4,6},{6,4},{8,10},{10,8},{12,14},{14,12},{16,18},{18,... | collective-permute-start | bytes 8847368 | tf_op jit(solution)/shard_map/ppermute | solution.py:441
  255.2 17.0 %collective-permute-start.67 = (bf16[384,768]{1,0:T(8,128)(2,1)S(1)}, bf16[384,768]{1,0:T(8,128)(2,1)S(1)}, u32[]{:S(2)}, u32[]{:S(2)}) collective-permute-start(bf16[384,768]{1,0:T(8,128)(2,1)S(1)} %add_convert_fusion.7), channel_id=1, source_target_pairs={{0,8},{2,10},{4,12},{6,14},{8,0},{10,2},{12,4},{14,6},{16,24},{18,... | collective-permute-start | bytes 1769480 | tf_op jit(solution)/shard_map/ppermute | solution.py:441
  277.3 39.0 %all-to-all-start.1 = ((bf16[4,480,768]{2,1,0:T(8,128)(2,1)}), bf16[4,480,768]{2,1,0:T(8,128)(2,1)S(1)}, u32[]{:S(2)}, u32[]{:S(2)}) async-start(bf16[4,480,768]{2,1,0:T(8,128)(2,1)} %add_convert_fusion), calls=%async_computation.1 | async-start | bytes 5898240 | tf_op jit(solution)/shard_map/all_to_all | solution.py:462
  281.9 31.7 %collective-permute-start.68 = (bf16[384,1152]{1,0:T(8,128)(2,1)}, bf16[384,1152]{1,0:T(8,128)(2,1)}, u32[]{:S(2)}, u32[]{:S(2)}) collective-permute-start(bf16[384,1152]{1,0:T(8,128)(2,1)} %get-tuple-element.704), channel_id=1, source_target_pairs={{0,2},{2,0},{4,6},{6,4},{8,10},{10,8},{12,14},{14,12},{16,18},{18,... | collective-permute-start | bytes 2654216 | tf_op jit(solution)/shard_map/ppermute | solution.py:441
  284.1 29.4 %collective-permute-start.69 = (bf16[384,768]{1,0:T(8,128)(2,1)S(1)}, bf16[384,768]{1,0:T(8,128)(2,1)}, u32[]{:S(2)}, u32[]{:S(2)}) collective-permute-start(bf16[384,768]{1,0:T(8,128)(2,1)S(1)} %add_convert_fusion.6), channel_id=1, source_target_pairs={{0,16},{2,18},{4,20},{6,22},{8,24},{10,26},{12,28},{14,30},{16,0},... | collective-permute-start | bytes 1769480 | tf_op jit(solution)/shard_map/ppermute | solution.py:441
  316.7 17.9 %collective-permute-start.72 = (bf16[480,768]{1,0:T(8,128)(2,1)S(1)}, bf16[480,768]{1,0:T(8,128)(2,1)S(1)}, u32[]{:S(2)}, u32[]{:S(2)}) collective-permute-start(bf16[480,768]{1,0:T(8,128)(2,1)S(1)} %add_convert_fusion.4), channel_id=1, source_target_pairs={{0,8},{2,10},{4,12},{6,14},{8,0},{10,2},{12,4},{14,6},{16,24},{18,... | collective-permute-start | bytes 2211848 | tf_op jit(solution)/shard_map/ppermute | solution.py:441
  317.5 17.0 %collective-permute-start.71 = (bf16[384,1152]{1,0:T(8,128)(2,1)S(1)}, bf16[384,1152]{1,0:T(8,128)(2,1)S(1)}, u32[]{:S(2)}, u32[]{:S(2)}) collective-permute-start(bf16[384,1152]{1,0:T(8,128)(2,1)S(1)} %copy-done.83), channel_id=1, source_target_pairs={{0,2},{2,0},{4,6},{6,4},{8,10},{10,8},{12,14},{14,12},{16,18},{18,... | collective-permute-start | bytes 2654216 | tf_op jit(solution)/shard_map/ppermute | solution.py:441
  318.9 15.7 %collective-permute-start.73 = (bf16[384,768]{1,0:T(8,128)(2,1)S(1)}, bf16[384,768]{1,0:T(8,128)(2,1)S(1)}, u32[]{:S(2)}, u32[]{:S(2)}) collective-permute-start(bf16[384,768]{1,0:T(8,128)(2,1)S(1)} %add_convert_fusion.5.refs_0_), channel_id=1, source_target_pairs={{0,4},{2,6},{4,0},{6,2},{8,12},{10,14},{12,8},{14,10},{16,20},{18,... | collective-permute-start | bytes 1769480 | tf_op jit(solution)/shard_map/ppermute | solution.py:441
  321.5 12.6 %collective-permute-start.70 = (bf16[2,96,1152]{2,1,0:T(8,128)(2,1)S(1)}, bf16[2,96,1152]{2,1,0:T(8,128)(2,1)S(1)}, u32[]{:S(2)}, u32[]{:S(2)}) collective-permute-start(bf16[2,96,1152]{2,1,0:T(8,128)(2,1)S(1)} %fusion), channel_id=1, source_target_pairs={{0,1},{1,0},{2,3},{3,2},{4,5},{5,4},{6,7},{7,6},{8,9},{9,8},{10,11... | collective-permute-start | bytes 1327112 | tf_op jit(solution)/shard_map/ppermute | solution.py:445
  335.9 35.8 %collective-permute-start.76 = (bf16[480,768]{1,0:T(8,128)(2,1)}, bf16[480,768]{1,0:T(8,128)(2,1)S(1)}, u32[]{:S(2)}, u32[]{:S(2)}) collective-permute-start(bf16[480,768]{1,0:T(8,128)(2,1)} %add_convert_fusion.3), channel_id=1, source_target_pairs={{0,16},{2,18},{4,20},{6,22},{8,24},{10,26},{12,28},{14,30},{16,0},... | collective-permute-start | bytes 2211848 | tf_op jit(solution)/shard_map/ppermute | solution.py:441
  339.3 18.8 %collective-permute-start.78 = (bf16[384,768]{1,0:T(8,128)(2,1)}, bf16[384,768]{1,0:T(8,128)(2,1)}, u32[]{:S(2)}, u32[]{:S(2)}) collective-permute-start(bf16[384,768]{1,0:T(8,128)(2,1)} %copy-done.58), channel_id=1, source_target_pairs={{0,2},{2,0},{4,6},{6,4},{8,10},{10,8},{12,14},{14,12},{16,18},{18,... | collective-permute-start | bytes 1769480 | tf_op jit(solution)/shard_map/ppermute | solution.py:441
  341.9 16.2 %collective-permute-start.75 = (bf16[2,96,1152]{2,1,0:T(8,128)(2,1)}, bf16[2,96,1152]{2,1,0:T(8,128)(2,1)}, u32[]{:S(2)}, u32[]{:S(2)}) collective-permute-start(bf16[2,96,1152]{2,1,0:T(8,128)(2,1)} %fusion.1), channel_id=1, source_target_pairs={{0,1},{1,0},{2,3},{3,2},{4,5},{5,4},{6,7},{7,6},{8,9},{9,8},{10,11... | collective-permute-start | bytes 1327112 | tf_op jit(solution)/shard_map/ppermute | solution.py:445
  345.2 12.9 %collective-permute-start.74 = (bf16[96,1152]{1,0:T(8,128)(2,1)}, bf16[96,1152]{1,0:T(8,128)(2,1)S(1)}, u32[]{:S(2)}, u32[]{:S(2)}) collective-permute-start(bf16[96,1152]{1,0:T(8,128)(2,1)} %fusion.5), channel_id=1, source_target_pairs={{0,4},{2,6},{4,0},{6,2},{8,12},{10,14},{12,8},{14,10},{16,20},{18,... | collective-permute-start | bytes 663560 | tf_op jit(solution)/shard_map/ppermute | solution.py:441
  345.8 12.2 %collective-permute-start.79 = (f32[2,36,128]{2,1,0:T(8,128)S(1)}, f32[2,36,128]{2,1,0:T(8,128)S(1)}, u32[]{:S(2)}, u32[]{:S(2)}) collective-permute-start(f32[2,36,128]{2,1,0:T(8,128)S(1)} %reshape.141), channel_id=1, source_target_pairs={{0,2},{2,0},{4,6},{6,4},{8,10},{10,8},{12,14},{14,12},{16,18},{18,... | collective-permute-start | bytes 110600 | tf_op jit(solution)/shard_map/ppermute | solution.py:441
  373.0 23.3 %collective-permute-start.82 = (bf16[480,768]{1,0:T(8,128)(2,1)S(1)}, bf16[480,768]{1,0:T(8,128)(2,1)S(1)}, u32[]{:S(2)}, u32[]{:S(2)}) collective-permute-start(bf16[480,768]{1,0:T(8,128)(2,1)S(1)} %add_convert_fusion.2.refs_0_), channel_id=1, source_target_pairs={{0,4},{2,6},{4,0},{6,2},{8,12},{10,14},{12,8},{14,10},{16,20},{18,... | collective-permute-start | bytes 2211848 | tf_op jit(solution)/shard_map/ppermute | solution.py:441
  376.2 20.1 %collective-permute-start.81 = (bf16[96,1152]{1,0:T(8,128)(2,1)}, bf16[96,1152]{1,0:T(8,128)(2,1)}, u32[]{:S(2)}, u32[]{:S(2)}) collective-permute-start(bf16[96,1152]{1,0:T(8,128)(2,1)} %fusion.3), channel_id=1, source_target_pairs={{0,4},{2,6},{4,0},{6,2},{8,12},{10,14},{12,8},{14,10},{16,20},{18,... | collective-permute-start | bytes 663560 | tf_op jit(solution)/shard_map/ppermute | solution.py:441
  378.1 18.2 %collective-permute-start.80 = (bf16[96,1152]{1,0:T(8,128)(2,1)S(1)}, bf16[96,1152]{1,0:T(8,128)(2,1)}, u32[]{:S(2)}, u32[]{:S(2)}) collective-permute-start(bf16[96,1152]{1,0:T(8,128)(2,1)S(1)} %add_convert_fusion.15), channel_id=1, source_target_pairs={{0,8},{2,10},{4,12},{6,14},{8,0},{10,2},{12,4},{14,6},{16,24},{18,... | collective-permute-start | bytes 663560 | tf_op jit(solution)/shard_map/ppermute | solution.py:441
  379.8 22.8 %collective-permute-start.86 = (bf16[480,768]{1,0:T(8,128)(2,1)S(1)}, bf16[480,768]{1,0:T(8,128)(2,1)S(1)}, u32[]{:S(2)}, u32[]{:S(2)}) collective-permute-start(bf16[480,768]{1,0:T(8,128)(2,1)S(1)} %add_convert_fusion.2.refs_0_), channel_id=1, source_target_pairs={{0,2},{2,0},{4,6},{6,4},{8,10},{10,8},{12,14},{14,12},{16,18},{18,... | collective-permute-start | bytes 2211848 | tf_op jit(solution)/shard_map/ppermute | solution.py:441
  396.3 15.9 %collective-permute-start.87 = (bf16[480,768]{1,0:T(8,128)(2,1)S(1)}, bf16[480,768]{1,0:T(8,128)(2,1)S(1)}, u32[]{:S(2)}, u32[]{:S(2)}) collective-permute-start(bf16[480,768]{1,0:T(8,128)(2,1)S(1)} %collective-permute-done.82.refs_1_), channel_id=1, source_target_pairs={{0,2},{2,0},{4,6},{6,4},{8,10},{10,8},{12,14},{14,12},{16,18},{18,... | collective-permute-start | bytes 2211848 | tf_op jit(solution)/shard_map/ppermute | solution.py:441
  397.8 10.4 %collective-permute-start.85 = (bf16[96,1152]{1,0:T(8,128)(2,1)S(1)}, bf16[96,1152]{1,0:T(8,128)(2,1)S(1)}, u32[]{:S(2)}, u32[]{:S(2)}) collective-permute-start(bf16[96,1152]{1,0:T(8,128)(2,1)S(1)} %add_convert_fusion.13), channel_id=1, source_target_pairs={{0,8},{2,10},{4,12},{6,14},{8,0},{10,2},{12,4},{14,6},{16,24},{18,... | collective-permute-start | bytes 663560 | tf_op jit(solution)/shard_map/ppermute | solution.py:441
  398.8 13.4 %collective-permute-start.84 = (bf16[96,1152]{1,0:T(8,128)(2,1)S(1)}, bf16[96,1152]{1,0:T(8,128)(2,1)S(1)}, u32[]{:S(2)}, u32[]{:S(2)}) collective-permute-start(bf16[96,1152]{1,0:T(8,128)(2,1)S(1)} %add_convert_fusion.14), channel_id=1, source_target_pairs={{0,16},{2,18},{4,20},{6,22},{8,24},{10,26},{12,28},{14,30},{16,0},... | collective-permute-start | bytes 663560 | tf_op jit(solution)/shard_map/ppermute | solution.py:441
  412.4 12.4 %collective-permute-start.90 = (bf16[96,1152]{1,0:T(8,128)(2,1)S(1)}, bf16[96,1152]{1,0:T(8,128)(2,1)S(1)}, u32[]{:S(2)}, u32[]{:S(2)}) collective-permute-start(bf16[96,1152]{1,0:T(8,128)(2,1)S(1)} %add_convert_fusion.11), channel_id=1, source_target_pairs={{0,16},{2,18},{4,20},{6,22},{8,24},{10,26},{12,28},{14,30},{16,0},... | collective-permute-start | bytes 663560 | tf_op jit(solution)/shard_map/ppermute | solution.py:441
  412.4 12.4 %collective-permute-start.89 = (bf16[96,1152]{1,0:T(8,128)(2,1)S(1)}, bf16[96,1152]{1,0:T(8,128)(2,1)S(1)}, u32[]{:S(2)}, u32[]{:S(2)}) collective-permute-start(bf16[96,1152]{1,0:T(8,128)(2,1)S(1)} %add_convert_fusion.12.refs_0_), channel_id=1, source_target_pairs={{0,4},{2,6},{4,0},{6,2},{8,12},{10,14},{12,8},{14,10},{16,20},{18,... | collective-permute-start | bytes 663560 | tf_op jit(solution)/shard_map/ppermute | solution.py:441
  414.0 10.8 %collective-permute-start.91 = (f32[36,128]{1,0:T(8,128)S(1)}, f32[36,128]{1,0:T(8,128)S(1)}, u32[]{:S(2)}, u32[]{:S(2)}) collective-permute-start(f32[36,128]{1,0:T(8,128)S(1)} %add.251), channel_id=1, source_target_pairs={{0,16},{2,18},{4,20},{6,22},{8,24},{10,26},{12,28},{14,30},{16,0},... | collective-permute-start | bytes 55304 | tf_op jit(solution)/shard_map/ppermute | solution.py:441
  416.8 10.2 %collective-permute-start.92 = (bf16[96,1152]{1,0:T(8,128)(2,1)S(1)}, bf16[96,1152]{1,0:T(8,128)(2,1)S(1)}, u32[]{:S(2)}, u32[]{:S(2)}) collective-permute-start(bf16[96,1152]{1,0:T(8,128)(2,1)S(1)} %add_convert_fusion.12.refs_0_), channel_id=1, source_target_pairs={{0,2},{2,0},{4,6},{6,4},{8,10},{10,8},{12,14},{14,12},{16,18},{18,... | collective-permute-start | bytes 663560 | tf_op jit(solution)/shard_map/ppermute | solution.py:441
  (120 other events, 1104.6 us)

commit v5 on v4

--- a/solution.py
+++ b/solution.py
@@ -1098,7 +1098,7 @@
         given=(dout, slope, y1, mixed, h2_t, vec, [w.arrays for w in (w_out, w_fc, w_proj)]),
     )
     dmixed, dy1, f_send, f_keep, d_gain2, d_shift2, d_outb, d_fcb, d_projb = found
-    end("df", f_keep, f_send, "deal", False)
+    end("df", f_keep, f_send, "deal", True)
 
     def heads_back(first, count, before):
         def run(qkv, mixed, dmixed, soft, h1_t, before):
@@ -1108,7 +1108,15 @@
 
     dqkv, a_send, a_keep = steps.slot("df dp", **heads_back(0, half, None))
     end("da", a_keep, a_send, "turn", False)
-    dqkv, b_send, b_keep = steps.slot("da df dp", **heads_back(half, half, dqkv))
+    heads = heads_back(half, half, dqkv)
+    last = rows_work(
+        "finish", finish_body, [y1, g_t], [vec], [w_proj], [((length, width), bf16)], []
+    )
+    (dqkv, b_send, b_keep), (block_out,) = steps.slot(
+        "da df dp",
+        work=lambda a, b: (heads["work"](*a), last["work"](*b)),
+        given=(heads["given"], last["given"]),
+    )
     end("db", b_keep, b_send, "turn", False)
     sums = [(1, width), (1, width), (1, 2 * width), (72, 128)]
     tokens_grad, d_gain1, d_shift1, d_qv, packed = steps.slot(
@@ -1128,12 +1136,6 @@
         steps.done["dv"] = collect_vectors_plain(place, small)
     else:
         steps.add("dv", collect_vectors_steps(place, packed.reshape(2, -1, 128)))
-    (block_out,) = steps.slot(
-        "all",
-        **rows_work(
-            "finish", finish_body, [y1, g_t], [vec], [w_proj], [((length, width), bf16)], []
-        ),
-    )
     rows = width // 2
     placed = {}
     makers = {

time: 443 us -> 430 us (0.971)
  waiting for transfers between devices: 113 us -> 91.5 us
  other arithmetic: 32.4 us -> 37.3 us
    ppermute x85 -> x83, waiting for transfers between devices: 107 us -> 83 us  [swap(): lax.ppermute(value, 'wide', [(i, i ^ flip) for i in range(self.wide)])]
    ppermute x0 -> x3, starting transfers between devices: none -> 5.53 us  [shift(): return lax.ppermute(value, 'wide', places)]
    select_n x5, other arithmetic: 0.45 us -> 5.13 us  [spread_steps(): now = jnp.where(place.core == place.o_core, keep, other)]
    ppermute x85 -> x83, starting transfers between devices: 67.6 us -> 64.2 us  [swap(): lax.ppermute(value, 'wide', [(i, i ^ flip) for i in range(self.wide)])]
  transfers between devices with their start and end apart: 100 -> 101, of which waited for: 38 -> 35; matrix products, arithmetic and copies ran while one was open for 6% -> 7% of each run, Pallas kernels for 41% -> 43%
where the time goes in v5:
time: 430 us; the launch traced here: 423 us
  Pallas kernels  189 us (44%)
  starting transfers between devices  91.7 us (21%)
  waiting for transfers between devices  91.5 us (21%)
  other arithmetic  37.3 us (9%)
  local copies, waits for them, and re-layouts  11.3 us (3%)
    ppermute x83, waiting for transfers between devices, swap(): lax.ppermute(value, 'wide', [(i, i ^ flip) for i in range(self.wide)])  83 us
    ppermute x83, starting transfers between devices, swap(): lax.ppermute(value, 'wide', [(i, i ^ flip) for i in range(self.wide)])  64.2 us
    pallas_call x4, Pallas kernels, attend(): pl.pallas_call(kernel, grid=(count,), in_specs=[pl.BlockSpec(memory_space...  52.7 us
    pallas_call x3, Pallas kernels, by_rows(): pl.pallas_call(kernel, grid=(length // ROWS,), in_specs=[pl.BlockSpec(mem...  43.8 us
    pallas_call x1, Pallas kernels, back_middle(): pl.pallas_call(kernel, grid=(steps + f_steps + 1,), in_specs=[pl.BlockSpe...  33.1 us
    pallas_call x2, Pallas kernels, attend_back(): pl.pallas_call(functools.partial(attend_back_kernel, length=length), grid...  31.3 us
    convert_element_type x18, other arithmetic, add(): functools.reduce(lambda a, b: a + b, [v.astype(f32) for v in values])  24.4 us
    pallas_call x3, Pallas kernels, put(): pl.pallas_call(functools.partial(put_kernel, counts=(len(groups), len(sha...  14.5 us
  transfers between devices with their start and end apart: 101, of which 35 were waited for; matrix products, arithmetic and copies ran while one was open for 7% of the time, Pallas kernels for 43%

profile of v5, /device:TPU:0, one launch (start us, length us, event | category | flops | bytes accessed | tf_op | source)
XLA Modules:
  0.0 423.4 jit_solution(3589729954060806858)
XLA Ops:
  1.9 3.0 pack.1
  5.4 2.5 dynamic-slice_bitcast_fusion
  11.0 3.0 collective-permute-start.2
  15.8 3.1 collective-permute-done.2
  19.6 2.8 collective-permute-start.6
  22.4 1.5 collective-permute-start.7
  24.0 6.3 %collective-permute-done.7 = bf16[96,1152]{1,0:T(8,128)(2,1)} collective-permute-done((bf16[96,1152]{1,0:T(8,128)(2,1)}, bf16[96,1152]{1,0:T(8,128)(2,1)}, u32[]{:S(2)}, u32[]{:S(2)}) %collective-permute-start.7) | collective-permute-done | bytes 221216 | tf_op jit(solution)/shard_map/ppermute | solution.py:441
  30.3 4.1 collective-permute-done.6
  37.9 2.4 collective-permute-start.9
  44.3 2.4 collective-permute-start.11
  46.8 1.5 collective-permute-start.12
  48.2 1.8 collective-permute-start.13
  50.1 8.6 %collective-permute-done.13 = bf16[96,1152]{1,0:T(8,128)(2,1)S(1)} collective-permute-done((bf16[96,1152]{1,0:T(8,128)(2,1)S(1)}, bf16[96,1152]{1,0:T(8,128)(2,1)S(1)}, u32[]{:S(2)}, u32[]{:S(2)}) %collective-permute-start.13) | collective-permute-done | bytes 221216 | tf_op jit(solution)/shard_map/ppermute | solution.py:441
  59.6 3.4 collective-permute-start.14
  63.9 4.0 collective-permute-done.15.refs_6_.refs_7_.refs_13_
  70.6 1.9 collective-permute-start.18
  75.5 1.5 collective-permute-done.24.refs_5_.refs_21_
  78.8 3.2 collective-permute-start.26
  85.8 17.6 %attend.4 = (bf16[1024,768]{1,0:T(8,128)(2,1)}, bf16[12,2304,256]{2,1,0:T(8,128)(2,1)}, bf16[1024,2304]{1,0:T(8,128)(2,1)}, bf16[1024,768]{1,0:T(8,128)(2,1)}, b...) custom-call(s32[4]{0:T(128)} %pad_add_fusion.core_ref.refs_0_.place_ref, s32[1024,1]{1,0:T(8,128)} %copy.40.refs_1_, ...), custom_call_target="tpu_custom_call" | custom-call | flops 1000 | bytes 1000 | tf_op jit(solution)/shard_map/attend/pallas_call | solution.py:142
  107.6 1.5 collective-permute-start.32
  109.7 9.9 %attend.5 = (bf16[1024,768]{1,0:T(8,128)(2,1)}, bf16[12,2304,256]{2,1,0:T(8,128)(2,1)}, bf16[1024,2304]{1,0:T(8,128)(2,1)}) custom-call(s32[4]{0:T(128)} %pad_add_fusion.core_ref.refs_0_.place_ref, s32[1024,1]{1,0:T(8,128)} %copy.40.refs_1_, ...), custom_call_target="tpu_custom_call", output_to_operand_aliasing={{0}: (14, {}), {1}: (15, {}), {2}: (16, {})} | custom-call | flops 1000 | bytes 1000 | tf_op jit(solution)/shard_map/attend/pallas_call | solution.py:142
  120.5 2.1 collective-permute-start.38
  123.1 1.6 collective-permute-start.40
  124.7 15.3 %attend.6 = (bf16[1024,768]{1,0:T(8,128)(2,1)}, bf16[12,2304,256]{2,1,0:T(8,128)(2,1)}, bf16[1024,2304]{1,0:T(8,128)(2,1)}) custom-call(s32[4]{0:T(128)} %pad_add_fusion.core_ref.refs_0_.place_ref, s32[1024,1]{1,0:T(8,128)} %copy.40.refs_1_, ...), custom_call_target="tpu_custom_call", output_to_operand_aliasing={{0}: (14, {}), {1}: (15, {}), {2}: (16, {})} | custom-call | flops 1000 | bytes 1000 | tf_op jit(solution)/shard_map/attend/pallas_call | solution.py:142
  140.1 8.5 %collective-permute-done.42 = bf16[384,768]{1,0:T(8,128)(2,1)S(1)} collective-permute-done((bf16[384,768]{1,0:T(8,128)(2,1)S(1)}, bf16[384,768]{1,0:T(8,128)(2,1)S(1)}, u32[]{:S(2)}, u32[]{:S(2)}) %collective-permute-start.42) | collective-permute-done | bytes 589856 | tf_op jit(solution)/shard_map/ppermute | solution.py:441
  149.5 2.1 collective-permute-start.44
  154.8 9.8 %attend.7 = (bf16[1024,768]{1,0:T(8,128)(2,1)}, bf16[12,2304,256]{2,1,0:T(8,128)(2,1)}, bf16[1024,2304]{1,0:T(8,128)(2,1)}) custom-call(s32[4]{0:T(128)} %pad_add_fusion.core_ref.refs_0_.place_ref, s32[1024,1]{1,0:T(8,128)} %copy.40.refs_1_, ...), custom_call_target="tpu_custom_call", output_to_operand_aliasing={{0}: (14, {}), {1}: (15, {}), {2}: (16, {})} | custom-call | flops 1000 | bytes 1000 | tf_op jit(solution)/shard_map/attend/pallas_call | solution.py:142
  169.7 20.6 %widen.1 = (f32[1024,768]{1,0:T(8,128)}, bf16[1024,3072]{1,0:T(8,128)(2,1)}, bf16[768,1024]{1,0:T(8,128)(2,1)}, bf16[3072,1024]{1,0:T(8,128)(2,1)}) custom-call(s32[4]{0:T(128)} %pad_add_fusion.core_ref.refs_0_.place_ref, bf16[1024,768]{1,0:T(8,128)(2,1)} %bitcast.110, bf16[1024,768]{1,0:T(8,128)(2,1)} %get-tuple-element.710.refs_2_.refs_4_.o_ref, ...), custom_call_target="tpu_custom_call" | custom-call | flops 1000 | bytes 1000 | tf_op jit(solution)/shard_map/widen/pallas_call | solution.py:585
  191.3 1.6 collective-permute-start.59
  193.0 10.4 %proj_terms.1 = (bf16[1536,768]{1,0:T(8,128)(2,1)}, bf16[1536,768]{1,0:T(8,128)(2,1)}) custom-call(s32[4]{0:T(128)} %pad_add_fusion.core_ref.refs_0_.place_ref, bf16[3072,1024]{1,0:T(8,128)(2,1)} %get-tuple-element.719.g_ref.refs_2_, bf16[1024,768]{1,0:T(8,128)(2,1)} %bitcast.113), custom_call_target="tpu_custom_call" | custom-call | flops 1000 | bytes 1000 | tf_op jit(solution)/shard_map/proj_terms/pallas_call | solution.py:297
  204.5 3.9 collective-permute-done.61.refs_32_.refs_9_
  211.3 3.8 add_convert_fusion.1
  215.2 3.9 all-to-all-start
  219.0 33.1 %back_middle.1 = (bf16[1024,768]{1,0:T(8,128)(2,1)}, f32[1024,768]{1,0:T(8,128)}, bf16[4,480,768]{2,1,0:T(8,128)(2,1)}, bf16[4,480,768]{2,1,0:T(8,128)(2,1)}, f3...) custom-call(s32[4]{0:T(128)} %pad_add_fusion.core_ref.refs_0_.place_ref, ...), custom_call_target="tpu_custom_call" | custom-call | flops 1000 | bytes 1000 | tf_op jit(solution)/shard_map/back_middle/pallas_call | solution.py:394
  252.6 2.0 collective-permute-start.67
  254.6 15.7 %attend_back.2 = (bf16[1024,2304]{1,0:T(8,128)(2,1)}, bf16[384,1152]{1,0:T(8,128)(2,1)}, bf16[384,1152]{1,0:T(8,128)(2,1)}) custom-call(s32[4]{0:T(128)} %pad_add_fusion.core_ref.refs_0_.place_ref, bf16[1024,2304]{1,0:T(8,128)(2,1)} %get-tuple-element.709.q_ref.k_ref.v_ref, bf16[1024,2304]{1,0:T(8,128)(2,1)} %get-tuple-element.709.q_ref.k_ref.v_ref, ...), custom_call_target="tpu_custom_call" | custom-call | flops 1000 | bytes 1000 | tf_op jit(solution)/shard_map/attend_back/pallas_call | solution.py:252
  271.1 4.2 add_convert_fusion
  275.3 4.5 %all-to-all-start.1 = ((bf16[4,480,768]{2,1,0:T(8,128)(2,1)}), bf16[4,480,768]{2,1,0:T(8,128)(2,1)S(1)}, u32[]{:S(2)}, u32[]{:S(2)}) async-start(bf16[4,480,768]{2,1,0:T(8,128)(2,1)} %add_convert_fusion), calls=%async_computation.1 | async-start | bytes 5898240 | tf_op jit(solution)/shard_map/all_to_all | solution.py:462
  279.8 2.1 add_convert_fusion.6
  282.4 15.6 %attend_back.3 = (bf16[1024,2304]{1,0:T(8,128)(2,1)}, bf16[384,1152]{1,0:T(8,128)(2,1)}, bf16[384,1152]{1,0:T(8,128)(2,1)}) custom-call(s32[4]{0:T(128)} %pad_add_fusion.core_ref.refs_0_.place_ref, bf16[1024,2304]{1,0:T(8,128)(2,1)} %get-tuple-element.709.q_ref.k_ref.v_ref, ...), custom_call_target="tpu_custom_call", output_to_operand_aliasing={{0}: (8, {})} | custom-call | flops 1000 | bytes 1000 | tf_op jit(solution)/shard_map/attend_back/pallas_call | solution.py:252
  298.0 11.3 %finish.1 = bf16[1024,768]{1,0:T(8,128)(2,1)} custom-call(s32[4]{0:T(128)} %pad_add_fusion.core_ref.refs_0_.place_ref, f32[1024,768]{1,0:T(8,128)} %get-tuple-element.718.refs_3_.refs_1_, bf16[3072,1024]{1,0:T(8,128)(2,1)} %get-tuple-element.719.g_ref.refs_2_, f32[72,128]{1,0:T(8,128)} %get-tuple-element.747.refs_3_.refs_6_.refs_4_, ...), custom_call_target="tpu_custom_call" | custom-call | flops 1000 | bytes 1000 | tf_op jit(solution)/shard_map/finish/pallas_call | solution.py:585
  309.3 1.8 collective-permute-done.69
  311.1 3.0 all-to-all-done.1
  314.5 2.4 collective-permute-start.72
  318.2 1.6 collective-permute-start.73
  321.5 11.9 %back_first.1 = (bf16[1024,768]{1,0:T(8,128)(2,1)}, f32[1,768]{1,0:T(1,128)}, f32[1,768]{1,0:T(1,128)}, f32[1,1536]{1,0:T(1,128)}, f32[72,128]{1,0:T(8,128)}) custom-call(s32[4]{0:T(128)} %pad_add_fusion.core_ref.refs_0_.place_ref, bf16[1024,2304]{1,0:T(8,128)(2,1)} %get-tuple-element.744.refs_1_, bf16[1024,768]{1,0:T(8,128)(2,1)} %bitcast.111, ...), custom_call_target="tpu_custom_call" | custom-call | flops 1000 | bytes 1000 | tf_op jit(solution)/shard_map/back_first/pallas_call | solution.py:585
  335.4 1.7 collective-permute-start.76
  340.3 1.9 fusion.5
  344.1 5.4 %collective-permute-done.74 = bf16[96,1152]{1,0:T(8,128)(2,1)} collective-permute-done((bf16[96,1152]{1,0:T(8,128)(2,1)}, bf16[96,1152]{1,0:T(8,128)(2,1)}, u32[]{:S(2)}, u32[]{:S(2)}) %collective-permute-start.74) | collective-permute-done | bytes 221216 | tf_op jit(solution)/shard_map/ppermute | solution.py:441
  349.6 1.5 collective-permute-done.75
  351.1 1.5 add_convert_fusion.2
  352.6 1.5 collective-permute-start.82
  354.1 1.7 fusion.3
  355.9 1.5 collective-permute-start.81
  358.6 4.2 collective-permute-start.80
  364.9 4.8 %put_proj.1 = f32[1536,768]{1,0:T(8,128)} custom-call(s32[4]{0:T(128)} %pad_add_fusion.core_ref.refs_0_.place_ref, bf16[384,768]{1,0:T(8,128)(2,1)} %copy-done.18, bf16[384,768]{1,0:T(8,128)(2,1)} %copy-done.58, bf16[384,768]{1,0:T(8,128)(2,1)} %copy-done.59, bf16[384,768]{1,0:T(8,128)(2,1)} %collective-permute-done.78.refs_3_), custom_call_target="tpu_custom_call" | custom-call | flops 1000 | bytes 1000 | tf_op jit(solution)/shard_map/put_proj/pallas_call | solution.py:740
  369.7 7.5 %collective-permute-done.80 = bf16[96,1152]{1,0:T(8,128)(2,1)} collective-permute-done((bf16[96,1152]{1,0:T(8,128)(2,1)S(1)}, bf16[96,1152]{1,0:T(8,128)(2,1)}, u32[]{:S(2)}, u32[]{:S(2)}) %collective-permute-start.80) | collective-permute-done | bytes 221216 | tf_op jit(solution)/shard_map/ppermute | solution.py:441
  377.4 1.5 collective-permute-start.86
  381.1 2.2 collective-permute-start.84
  384.4 8.9 %collective-permute-done.87 = f32[36,128]{1,0:T(8,128)S(1)} collective-permute-done((f32[36,128]{1,0:T(8,128)S(1)}, f32[36,128]{1,0:T(8,128)S(1)}, u32[]{:S(2)}, u32[]{:S(2)}) %collective-permute-start.87) | collective-permute-done | bytes 18464 | tf_op jit(solution)/shard_map/ppermute | solution.py:441
  395.1 2.9 collective-permute-start.92
  398.0 9.8 %collective-permute-done.92 = f32[36,128]{1,0:T(8,128)S(1)} collective-permute-done((f32[36,128]{1,0:T(8,128)S(1)}, f32[36,128]{1,0:T(8,128)S(1)}, u32[]{:S(2)}, u32[]{:S(2)}) %collective-permute-start.92) | collective-permute-done | bytes 18464 | tf_op jit(solution)/shard_map/ppermute | solution.py:441
  409.0 5.4 %put_fc.1 = (f32[384,3072]{1,0:T(8,128)}, f32[384,768]{1,0:T(8,128)}) custom-call(s32[4]{0:T(128)} %pad_add_fusion.core_ref.refs_0_.place_ref, bf16[480,768]{1,0:T(8,128)(2,1)} %copy-done.11, bf16[480,768]{1,0:T(8,128)(2,1)} %copy-done.55, bf16[480,768]{1,0:T(8,128)(2,1)} %copy-done.56, bf16[480,768]{1,0:T(8,128)(2,1)} %copy-done.57), custom_call_target="tpu_custom_call" | custom-call | flops 1000 | bytes 1000 | tf_op jit(solution)/shard_map/put_fc/pallas_call | solution.py:740
  418.9 4.3 %put_qkv.1 = f32[384,2304]{1,0:T(8,128)} custom-call(s32[4]{0:T(128)} %pad_add_fusion.core_ref.refs_0_.place_ref, bf16[96,1152]{1,0:T(8,128)(2,1)} %copy-done.53, bf16[96,1152]{1,0:T(8,128)(2,1)} %copy-done.74, bf16[96,1152]{1,0:T(8,128)(2,1)} %copy-done.75, bf16[96,1152]{1,0:T(8,128)(2,1)} %copy-done.77, bf16[96,1152]{1,0:T(8,128)(2,1)} %copy-done.54, ...), custom_call_target="tpu_custom_call" | custom-call | flops 1000 | bytes 1000 | tf_op jit(solution)/shard_map/put_qkv/pallas_call | solution.py:740
  (395 shorter events, 73.7 us)
Async XLA Ops:
  11.0 8.0 %collective-permute-start.2 = (bf16[96,1280]{1,0:T(8,128)(2,1)S(1)}, bf16[96,1280]{1,0:T(8,128)(2,1)S(1)}, u32[]{:S(2)}, u32[]{:S(2)}) collective-permute-start(bf16[96,1280]{1,0:T(8,128)(2,1)S(1)} %dynamic-slice_bitcast_fusion.5), channel_id=1, source_target_pairs={{0,4},{2,6},{4,0},{6,2},{8,12},{10,14},{12,8},{14,10},{16,20},{18,... | collective-permute-start | bytes 737288 | tf_op jit(solution)/shard_map/ppermute | solution.py:441
  19.0 15.4 %collective-permute-start.3 = (bf16[192,3072]{1,0:T(8,128)(2,1)}, bf16[192,3072]{1,0:T(8,128)(2,1)}, u32[]{:S(2)}, u32[]{:S(2)}) collective-permute-start(bf16[192,3072]{1,0:T(8,128)(2,1)} %dynamic-slice_bitcast_fusion.1), channel_id=1, source_target_pairs={{0,2},{2,0},{4,6},{6,4},{8,10},{10,8},{12,14},{14,12},{16,18},{18,... | collective-permute-start | bytes 3538952 | tf_op jit(solution)/shard_map/ppermute | solution.py:441
  19.1 15.3 %collective-permute-start.5 = (bf16[768,768]{1,0:T(8,128)(2,1)}, bf16[768,768]{1,0:T(8,128)(2,1)}, u32[]{:S(2)}, u32[]{:S(2)}) collective-permute-start(bf16[768,768]{1,0:T(8,128)(2,1)} %dynamic-slice_bitcast_fusion), channel_id=1, source_target_pairs={{0,2},{2,0},{4,6},{6,4},{8,10},{10,8},{12,14},{14,12},{16,18},{18,... | collective-permute-start | bytes 3538952 | tf_op jit(solution)/shard_map/ppermute | solution.py:441
  19.5 14.8 %collective-permute-start.4 = (bf16[192,768]{1,0:T(8,128)(2,1)}, bf16[192,768]{1,0:T(8,128)(2,1)S(1)}, u32[]{:S(2)}, u32[]{:S(2)}) collective-permute-start(bf16[192,768]{1,0:T(8,128)(2,1)} %dynamic-slice_bitcast_fusion.4), channel_id=1, source_target_pairs={{0,2},{2,0},{4,6},{6,4},{8,10},{10,8},{12,14},{14,12},{16,18},{18,... | collective-permute-start | bytes 884744 | tf_op jit(solution)/shard_map/ppermute | solution.py:441
  19.6 14.7 %collective-permute-start.6 = (bf16[96,1280]{1,0:T(8,128)(2,1)S(1)}, bf16[96,1280]{1,0:T(8,128)(2,1)}, u32[]{:S(2)}, u32[]{:S(2)}) collective-permute-start(bf16[96,1280]{1,0:T(8,128)(2,1)S(1)} %bitcast_select_fusion.5), channel_id=1, source_target_pairs={{0,16},{2,18},{4,20},{6,22},{8,24},{10,26},{12,28},{14,30},{16,0},... | collective-permute-start | bytes 737288 | tf_op jit(solution)/shard_map/ppermute | solution.py:441
  44.3 14.4 %collective-permute-start.11 = (bf16[96,1280]{1,0:T(8,128)(2,1)S(1)}, bf16[96,1280]{1,0:T(8,128)(2,1)S(1)}, u32[]{:S(2)}, u32[]{:S(2)}) collective-permute-start(bf16[96,1280]{1,0:T(8,128)(2,1)S(1)} %broadcast_select_fusion.7.refs_3_.refs_4_.refs_10_), channel_id=1, source_target_pairs={{0,4},{2,6},{4,0},{6,2},{8,12},{10,14},{12,8},{14,10},{16,20},{18,... | collective-permute-start | bytes 737288 | tf_op jit(solution)/shard_map/ppermute | solution.py:441
  46.8 12.0 %collective-permute-start.12 = (bf16[96,1280]{1,0:T(8,128)(2,1)S(1)}, bf16[96,1280]{1,0:T(8,128)(2,1)S(1)}, u32[]{:S(2)}, u32[]{:S(2)}) collective-permute-start(bf16[96,1280]{1,0:T(8,128)(2,1)S(1)} %broadcast_select_fusion.7.refs_3_.refs_4_.refs_10_), channel_id=1, source_target_pairs={{0,1},{1,0},{2,3},{3,2},{4,5},{5,4},{6,7},{7,6},{8,9},{9,8},{10,11... | collective-permute-start | bytes 737288 | tf_op jit(solution)/shard_map/ppermute | solution.py:445
  48.2 10.5 %collective-permute-start.13 = (bf16[96,1152]{1,0:T(8,128)(2,1)S(1)}, bf16[96,1152]{1,0:T(8,128)(2,1)S(1)}, u32[]{:S(2)}, u32[]{:S(2)}) collective-permute-start(bf16[96,1152]{1,0:T(8,128)(2,1)S(1)} %bitcast_select_fusion.6), channel_id=1, source_target_pairs={{0,16},{2,18},{4,20},{6,22},{8,24},{10,26},{12,28},{14,30},{16,0},... | collective-permute-start | bytes 663560 | tf_op jit(solution)/shard_map/ppermute | solution.py:441
  50.0 13.9 %collective-permute-start.8 = (bf16[96,3072]{1,0:T(8,128)(2,1)S(1)}, bf16[96,3072]{1,0:T(8,128)(2,1)S(1)}, u32[]{:S(2)}, u32[]{:S(2)}) collective-permute-start(bf16[96,3072]{1,0:T(8,128)(2,1)S(1)} %dynamic-slice_bitcast_fusion.3), channel_id=1, source_target_pairs={{0,4},{2,6},{4,0},{6,2},{8,12},{10,14},{12,8},{14,10},{16,20},{18,... | collective-permute-start | bytes 1769480 | tf_op jit(solution)/shard_map/ppermute | solution.py:441
  58.9 9.6 %collective-permute-start.17 = (bf16[96,1152]{1,0:T(8,128)(2,1)S(1)}, bf16[96,1152]{1,0:T(8,128)(2,1)S(1)}, u32[]{:S(2)}, u32[]{:S(2)}) collective-permute-start(bf16[96,1152]{1,0:T(8,128)(2,1)S(1)} %broadcast_select_fusion.10), channel_id=1, source_target_pairs={{0,8},{2,10},{4,12},{6,14},{8,0},{10,2},{12,4},{14,6},{16,24},{18,... | collective-permute-start | bytes 663560 | tf_op jit(solution)/shard_map/ppermute | solution.py:441
  59.6 8.8 %collective-permute-start.14 = (bf16[96,768]{1,0:T(8,128)(2,1)S(1)}, bf16[96,768]{1,0:T(8,128)(2,1)S(1)}, u32[]{:S(2)}, u32[]{:S(2)}) collective-permute-start(bf16[96,768]{1,0:T(8,128)(2,1)S(1)} %bitcast_select_fusion.7), channel_id=1, source_target_pairs={{0,16},{2,18},{4,20},{6,22},{8,24},{10,26},{12,28},{14,30},{16,0},... | collective-permute-start | bytes 442376 | tf_op jit(solution)/shard_map/ppermute | solution.py:441
  68.6 8.3 %collective-permute-start.24 = (bf16[96,1152]{1,0:T(8,128)(2,1)S(1)}, bf16[96,1152]{1,0:T(8,128)(2,1)S(1)}, u32[]{:S(2)}, u32[]{:S(2)}) collective-permute-start(bf16[96,1152]{1,0:T(8,128)(2,1)S(1)} %broadcast_select_fusion.9.refs_4_.refs_20_), channel_id=1, source_target_pairs={{0,4},{2,6},{4,0},{6,2},{8,12},{10,14},{12,8},{14,10},{16,20},{18,... | collective-permute-start | bytes 663560 | tf_op jit(solution)/shard_map/ppermute | solution.py:441
  70.6 33.0 %collective-permute-start.18 = (bf16[96,3072]{1,0:T(8,128)(2,1)S(1)}, bf16[96,3072]{1,0:T(8,128)(2,1)}, u32[]{:S(2)}, u32[]{:S(2)}) collective-permute-start(bf16[96,3072]{1,0:T(8,128)(2,1)S(1)} %bitcast_select_fusion.2), channel_id=1, source_target_pairs={{0,16},{2,18},{4,20},{6,22},{8,24},{10,26},{12,28},{14,30},{16,0},... | collective-permute-start | bytes 1769480 | tf_op jit(solution)/shard_map/ppermute | solution.py:441
  72.4 31.1 %collective-permute-start.27 = (bf16[384,768]{1,0:T(8,128)(2,1)}, bf16[384,768]{1,0:T(8,128)(2,1)}, u32[]{:S(2)}, u32[]{:S(2)}) collective-permute-start(bf16[384,768]{1,0:T(8,128)(2,1)} %dynamic-slice_bitcast_fusion.2), channel_id=1, source_target_pairs={{0,4},{2,6},{4,0},{6,2},{8,12},{10,14},{12,8},{14,10},{16,20},{18,... | collective-permute-start | bytes 1769480 | tf_op jit(solution)/shard_map/ppermute | solution.py:441
  78.8 24.7 %collective-permute-start.26 = (bf16[96,768]{1,0:T(8,128)(2,1)}, bf16[96,768]{1,0:T(8,128)(2,1)}, u32[]{:S(2)}, u32[]{:S(2)}) collective-permute-start(bf16[96,768]{1,0:T(8,128)(2,1)} %broadcast_select_fusion.12), channel_id=1, source_target_pairs={{0,8},{2,10},{4,12},{6,14},{8,0},{10,2},{12,4},{14,6},{16,24},{18,... | collective-permute-start | bytes 442376 | tf_op jit(solution)/shard_map/ppermute | solution.py:441
  83.3 20.2 %collective-permute-start.28 = (bf16[48,1152]{1,0:T(8,128)(2,1)}, bf16[48,1152]{1,0:T(8,128)(2,1)}, u32[]{:S(2)}, u32[]{:S(2)}) collective-permute-start(bf16[48,1152]{1,0:T(8,128)(2,1)} %slice.64), channel_id=1, source_target_pairs={{0,1},{1,0},{2,3},{3,2},{4,5},{5,4},{6,7},{7,6},{8,9},{9,8},{10,11... | collective-permute-start | bytes 331784 | tf_op jit(solution)/shard_map/ppermute | solution.py:445
  83.8 19.6 %collective-permute-start.29 = (bf16[48,1152]{1,0:T(8,128)(2,1)}, bf16[48,1152]{1,0:T(8,128)(2,1)S(1)}, u32[]{:S(2)}, u32[]{:S(2)}) collective-permute-start(bf16[48,1152]{1,0:T(8,128)(2,1)} %slice.65), channel_id=1, source_target_pairs={{0,4},{2,6},{4,0},{6,2},{8,12},{10,14},{12,8},{14,10},{16,20},{18,... | collective-permute-start | bytes 331784 | tf_op jit(solution)/shard_map/ppermute | solution.py:441
  104.7 15.7 %collective-permute-start.30 = (bf16[96,3072]{1,0:T(8,128)(2,1)S(1)}, bf16[96,3072]{1,0:T(8,128)(2,1)S(1)}, u32[]{:S(2)}, u32[]{:S(2)}) collective-permute-start(bf16[96,3072]{1,0:T(8,128)(2,1)S(1)} %broadcast_select_fusion.1), channel_id=1, source_target_pairs={{0,8},{2,10},{4,12},{6,14},{8,0},{10,2},{12,4},{14,6},{16,24},{18,... | collective-permute-start | bytes 1769480 | tf_op jit(solution)/shard_map/ppermute | solution.py:441
  106.4 13.9 %collective-permute-start.31 = (bf16[96,768]{1,0:T(8,128)(2,1)S(1)}, bf16[96,768]{1,0:T(8,128)(2,1)S(1)}, u32[]{:S(2)}, u32[]{:S(2)}) collective-permute-start(bf16[96,768]{1,0:T(8,128)(2,1)S(1)} %broadcast_select_fusion.11.refs_4_.refs_7_), channel_id=1, source_target_pairs={{0,4},{2,6},{4,0},{6,2},{8,12},{10,14},{12,8},{14,10},{16,20},{18,... | collective-permute-start | bytes 442376 | tf_op jit(solution)/shard_map/ppermute | solution.py:441
  107.6 12.8 %collective-permute-start.32 = (bf16[96,768]{1,0:T(8,128)(2,1)S(1)}, bf16[96,768]{1,0:T(8,128)(2,1)S(1)}, u32[]{:S(2)}, u32[]{:S(2)}) collective-permute-start(bf16[96,768]{1,0:T(8,128)(2,1)S(1)} %broadcast_select_fusion.11.refs_4_.refs_7_), channel_id=1, source_target_pairs={{0,1},{1,0},{2,3},{3,2},{4,5},{5,4},{6,7},{7,6},{8,9},{9,8},{10,11... | collective-permute-start | bytes 442376 | tf_op jit(solution)/shard_map/ppermute | solution.py:445
  109.1 10.5 %collective-permute-start.36 = (bf16[48,1152]{1,0:T(8,128)(2,1)}, bf16[48,1152]{1,0:T(8,128)(2,1)S(1)}, u32[]{:S(2)}, u32[]{:S(2)}) collective-permute-start(bf16[48,1152]{1,0:T(8,128)(2,1)} %collective-permute-done.28.refs_7_.refs_23_), channel_id=1, source_target_pairs={{0,2},{2,0},{4,6},{6,4},{8,10},{10,8},{12,14},{14,12},{16,18},{18,... | collective-permute-start | bytes 331784 | tf_op jit(solution)/shard_map/ppermute | solution.py:441
  109.1 11.3 %collective-permute-start.37 = (bf16[48,1152]{1,0:T(8,128)(2,1)S(1)}, bf16[48,1152]{1,0:T(8,128)(2,1)S(1)}, u32[]{:S(2)}, u32[]{:S(2)}) collective-permute-start(bf16[48,1152]{1,0:T(8,128)(2,1)S(1)} %collective-permute-done.29.refs_8_.refs_24_), channel_id=1, source_target_pairs={{0,2},{2,0},{4,6},{6,4},{8,10},{10,8},{12,14},{14,12},{16,18},{18,... | collective-permute-start | bytes 331784 | tf_op jit(solution)/shard_map/ppermute | solution.py:441
  119.6 28.9 %collective-permute-start.42 = (bf16[384,768]{1,0:T(8,128)(2,1)S(1)}, bf16[384,768]{1,0:T(8,128)(2,1)S(1)}, u32[]{:S(2)}, u32[]{:S(2)}) collective-permute-start(bf16[384,768]{1,0:T(8,128)(2,1)S(1)} %bitcast_select_fusion.3), channel_id=1, source_target_pairs={{0,16},{2,18},{4,20},{6,22},{8,24},{10,26},{12,28},{14,30},{16,0},... | collective-permute-start | bytes 1769480 | tf_op jit(solution)/shard_map/ppermute | solution.py:441
  120.5 28.1 %collective-permute-start.38 = (bf16[96,3072]{1,0:T(8,128)(2,1)S(1)}, bf16[96,3072]{1,0:T(8,128)(2,1)S(1)}, u32[]{:S(2)}, u32[]{:S(2)}) collective-permute-start(bf16[96,3072]{1,0:T(8,128)(2,1)S(1)} %broadcast_select_fusion.2.refs_14_.refs_17_), channel_id=1, source_target_pairs={{0,4},{2,6},{4,0},{6,2},{8,12},{10,14},{12,8},{14,10},{16,20},{18,... | collective-permute-start | bytes 1769480 | tf_op jit(solution)/shard_map/ppermute | solution.py:441
  122.6 26.0 %collective-permute-start.39 = (bf16[96,3072]{1,0:T(8,128)(2,1)S(1)}, bf16[96,3072]{1,0:T(8,128)(2,1)S(1)}, u32[]{:S(2)}, u32[]{:S(2)}) collective-permute-start(bf16[96,3072]{1,0:T(8,128)(2,1)S(1)} %broadcast_select_fusion.2.refs_14_.refs_17_), channel_id=1, source_target_pairs={{0,1},{1,0},{2,3},{3,2},{4,5},{5,4},{6,7},{7,6},{8,9},{9,8},{10,11... | collective-permute-start | bytes 1769480 | tf_op jit(solution)/shard_map/ppermute | solution.py:445
  123.1 25.4 %collective-permute-start.40 = (bf16[48,768]{1,0:T(8,128)(2,1)S(1)}, bf16[48,768]{1,0:T(8,128)(2,1)S(1)}, u32[]{:S(2)}, u32[]{:S(2)}) collective-permute-start(bf16[48,768]{1,0:T(8,128)(2,1)S(1)} %slice.66), channel_id=1, source_target_pairs={{0,1},{1,0},{2,3},{3,2},{4,5},{5,4},{6,7},{7,6},{8,9},{9,8},{10,11... | collective-permute-start | bytes 221192 | tf_op jit(solution)/shard_map/ppermute | solution.py:445
  124.7 23.9 %collective-permute-start.41 = (bf16[48,768]{1,0:T(8,128)(2,1)S(1)}, bf16[48,768]{1,0:T(8,128)(2,1)S(1)}, u32[]{:S(2)}, u32[]{:S(2)}) collective-permute-start(bf16[48,768]{1,0:T(8,128)(2,1)S(1)} %slice.67), channel_id=1, source_target_pairs={{0,4},{2,6},{4,0},{6,2},{8,12},{10,14},{12,8},{14,10},{16,20},{18,... | collective-permute-start | bytes 221192 | tf_op jit(solution)/shard_map/ppermute | solution.py:441
  148.7 16.3 %collective-permute-start.50 = (bf16[384,768]{1,0:T(8,128)(2,1)S(1)}, bf16[384,768]{1,0:T(8,128)(2,1)S(1)}, u32[]{:S(2)}, u32[]{:S(2)}) collective-permute-start(bf16[384,768]{1,0:T(8,128)(2,1)S(1)} %broadcast_select_fusion.3), channel_id=1, source_target_pairs={{0,8},{2,10},{4,12},{6,14},{8,0},{10,2},{12,4},{14,6},{16,24},{18,... | collective-permute-start | bytes 1769480 | tf_op jit(solution)/shard_map/ppermute | solution.py:441
  148.9 15.8 %collective-permute-start.43 = (bf16[48,3072]{1,0:T(8,128)(2,1)S(1)}, bf16[48,3072]{1,0:T(8,128)(2,1)S(1)}, u32[]{:S(2)}, u32[]{:S(2)}) collective-permute-start(bf16[48,3072]{1,0:T(8,128)(2,1)S(1)} %slice.68), channel_id=1, source_target_pairs={{0,1},{1,0},{2,3},{3,2},{4,5},{5,4},{6,7},{7,6},{8,9},{9,8},{10,11... | collective-permute-start | bytes 884744 | tf_op jit(solution)/shard_map/ppermute | solution.py:445
  149.5 15.5 %collective-permute-start.44 = (bf16[48,3072]{1,0:T(8,128)(2,1)S(1)}, bf16[48,3072]{1,0:T(8,128)(2,1)S(1)}, u32[]{:S(2)}, u32[]{:S(2)}) collective-permute-start(bf16[48,3072]{1,0:T(8,128)(2,1)S(1)} %slice.69), channel_id=1, source_target_pairs={{0,4},{2,6},{4,0},{6,2},{8,12},{10,14},{12,8},{14,10},{16,20},{18,... | collective-permute-start | bytes 884744 | tf_op jit(solution)/shard_map/ppermute | solution.py:441
  154.2 12.5 %collective-permute-start.53 = (bf16[96,3072]{1,0:T(8,128)(2,1)S(1)}, bf16[96,3072]{1,0:T(8,128)(2,1)S(1)}, u32[]{:S(2)}, u32[]{:S(2)}) collective-permute-start(bf16[96,3072]{1,0:T(8,128)(2,1)S(1)} %broadcast_select_fusion.2.refs_14_.refs_17_), channel_id=1, source_target_pairs={{0,2},{2,0},{4,6},{6,4},{8,10},{10,8},{12,14},{14,12},{16,18},{18,... | collective-permute-start | bytes 1769480 | tf_op jit(solution)/shard_map/ppermute | solution.py:441
  154.4 12.3 %collective-permute-start.54 = (bf16[96,3072]{1,0:T(8,128)(2,1)S(1)}, bf16[96,3072]{1,0:T(8,128)(2,1)S(1)}, u32[]{:S(2)}, u32[]{:S(2)}) collective-permute-start(bf16[96,3072]{1,0:T(8,128)(2,1)S(1)} %collective-permute-done.38.refs_15_.refs_18_), channel_id=1, source_target_pairs={{0,2},{2,0},{4,6},{6,4},{8,10},{10,8},{12,14},{14,12},{16,18},{18,... | collective-permute-start | bytes 1769480 | tf_op jit(solution)/shard_map/ppermute | solution.py:441
  165.0 25.3 %collective-permute-start.51 = (bf16[384,768]{1,0:T(8,128)(2,1)S(1)}, bf16[384,768]{1,0:T(8,128)(2,1)S(1)}, u32[]{:S(2)}, u32[]{:S(2)}) collective-permute-start(bf16[384,768]{1,0:T(8,128)(2,1)S(1)} %broadcast_select_fusion.4.refs_27_.refs_4_), channel_id=1, source_target_pairs={{0,4},{2,6},{4,0},{6,2},{8,12},{10,14},{12,8},{14,10},{16,20},{18,... | collective-permute-start | bytes 1769480 | tf_op jit(solution)/shard_map/ppermute | solution.py:441
  165.5 24.9 %collective-permute-start.52 = (bf16[384,768]{1,0:T(8,128)(2,1)S(1)}, bf16[384,768]{1,0:T(8,128)(2,1)S(1)}, u32[]{:S(2)}, u32[]{:S(2)}) collective-permute-start(bf16[384,768]{1,0:T(8,128)(2,1)S(1)} %broadcast_select_fusion.4.refs_27_.refs_4_), channel_id=1, source_target_pairs={{0,1},{1,0},{2,3},{3,2},{4,5},{5,4},{6,7},{7,6},{8,9},{9,8},{10,11... | collective-permute-start | bytes 1769480 | tf_op jit(solution)/shard_map/ppermute | solution.py:445
  190.5 12.9 %collective-permute-start.58 = (bf16[192,768]{1,0:T(8,128)(2,1)S(1)}, bf16[192,768]{1,0:T(8,128)(2,1)S(1)}, u32[]{:S(2)}, u32[]{:S(2)}) collective-permute-start(bf16[192,768]{1,0:T(8,128)(2,1)S(1)} %slice.70), channel_id=1, source_target_pairs={{0,1},{1,0},{2,3},{3,2},{4,5},{5,4},{6,7},{7,6},{8,9},{9,8},{10,11... | collective-permute-start | bytes 884744 | tf_op jit(solution)/shard_map/ppermute | solution.py:445
  191.3 12.0 %collective-permute-start.59 = (bf16[192,768]{1,0:T(8,128)(2,1)S(1)}, bf16[192,768]{1,0:T(8,128)(2,1)S(1)}, u32[]{:S(2)}, u32[]{:S(2)}) collective-permute-start(bf16[192,768]{1,0:T(8,128)(2,1)S(1)} %slice.71), channel_id=1, source_target_pairs={{0,4},{2,6},{4,0},{6,2},{8,12},{10,14},{12,8},{14,10},{16,20},{18,... | collective-permute-start | bytes 884744 | tf_op jit(solution)/shard_map/ppermute | solution.py:441
  203.4 8.0 %collective-permute-start.60 = (bf16[1536,768]{1,0:T(8,128)(2,1)}, bf16[1536,768]{1,0:T(8,128)(2,1)S(1)}, u32[]{:S(2)}, u32[]{:S(2)}) collective-permute-start(bf16[1536,768]{1,0:T(8,128)(2,1)} %get-tuple-element.633), channel_id=1, source_target_pairs={{0,2},{2,0},{4,6},{6,4},{8,10},{10,8},{12,14},{14,12},{16,18},{18,... | collective-permute-start | bytes 7077896 | tf_op jit(solution)/shard_map/ppermute | solution.py:441
  215.2 36.9 %all-to-all-start = ((bf16[4,384,768]{2,1,0:T(8,128)(2,1)}), bf16[4,384,768]{2,1,0:T(8,128)(2,1)S(1)}, u32[]{:S(2)}, u32[]{:S(2)}) async-start(bf16[4,384,768]{2,1,0:T(8,128)(2,1)} %bitcast.112), calls=%async_computation | async-start | bytes 4718592 | tf_op jit(solution)/shard_map/all_to_all | solution.py:462
  252.1 19.0 %collective-permute-start.66 = (bf16[4,480,768]{2,1,0:T(8,128)(2,1)}, bf16[4,480,768]{2,1,0:T(8,128)(2,1)}, u32[]{:S(2)}, u32[]{:S(2)}) collective-permute-start(bf16[4,480,768]{2,1,0:T(8,128)(2,1)} %get-tuple-element.690), channel_id=1, source_target_pairs={{0,2},{2,0},{4,6},{6,4},{8,10},{10,8},{12,14},{14,12},{16,18},{18,... | collective-permute-start | bytes 8847368 | tf_op jit(solution)/shard_map/ppermute | solution.py:441
  252.6 17.7 %collective-permute-start.67 = (bf16[384,768]{1,0:T(8,128)(2,1)S(1)}, bf16[384,768]{1,0:T(8,128)(2,1)S(1)}, u32[]{:S(2)}, u32[]{:S(2)}) collective-permute-start(bf16[384,768]{1,0:T(8,128)(2,1)S(1)} %add_convert_fusion.7), channel_id=1, source_target_pairs={{0,8},{2,10},{4,12},{6,14},{8,0},{10,2},{12,4},{14,6},{16,24},{18,... | collective-permute-start | bytes 1769480 | tf_op jit(solution)/shard_map/ppermute | solution.py:441
  275.3 38.8 %all-to-all-start.1 = ((bf16[4,480,768]{2,1,0:T(8,128)(2,1)}), bf16[4,480,768]{2,1,0:T(8,128)(2,1)S(1)}, u32[]{:S(2)}, u32[]{:S(2)}) async-start(bf16[4,480,768]{2,1,0:T(8,128)(2,1)} %add_convert_fusion), calls=%async_computation.1 | async-start | bytes 5898240 | tf_op jit(solution)/shard_map/all_to_all | solution.py:462
  279.7 31.4 %collective-permute-start.68 = (bf16[384,1152]{1,0:T(8,128)(2,1)}, bf16[384,1152]{1,0:T(8,128)(2,1)}, u32[]{:S(2)}, u32[]{:S(2)}) collective-permute-start(bf16[384,1152]{1,0:T(8,128)(2,1)} %get-tuple-element.704), channel_id=1, source_target_pairs={{0,2},{2,0},{4,6},{6,4},{8,10},{10,8},{12,14},{14,12},{16,18},{18,... | collective-permute-start | bytes 2654216 | tf_op jit(solution)/shard_map/ppermute | solution.py:441
  282.0 29.1 %collective-permute-start.69 = (bf16[384,768]{1,0:T(8,128)(2,1)S(1)}, bf16[384,768]{1,0:T(8,128)(2,1)}, u32[]{:S(2)}, u32[]{:S(2)}) collective-permute-start(bf16[384,768]{1,0:T(8,128)(2,1)S(1)} %add_convert_fusion.6), channel_id=1, source_target_pairs={{0,16},{2,18},{4,20},{6,22},{8,24},{10,26},{12,28},{14,30},{16,0},... | collective-permute-start | bytes 1769480 | tf_op jit(solution)/shard_map/ppermute | solution.py:441
  314.5 19.5 %collective-permute-start.72 = (bf16[480,768]{1,0:T(8,128)(2,1)S(1)}, bf16[480,768]{1,0:T(8,128)(2,1)S(1)}, u32[]{:S(2)}, u32[]{:S(2)}) collective-permute-start(bf16[480,768]{1,0:T(8,128)(2,1)S(1)} %add_convert_fusion.4), channel_id=1, source_target_pairs={{0,8},{2,10},{4,12},{6,14},{24,16},{26,18},{28,20},{30,22},{1,9},{... | collective-permute-start | bytes 2211848 | tf_op jit(solution)/shard_map/ppermute | solution.py:449
  316.9 17.1 %collective-permute-start.71 = (bf16[384,1152]{1,0:T(8,128)(2,1)S(1)}, bf16[384,1152]{1,0:T(8,128)(2,1)S(1)}, u32[]{:S(2)}, u32[]{:S(2)}) collective-permute-start(bf16[384,1152]{1,0:T(8,128)(2,1)S(1)} %copy-done.85), channel_id=1, source_target_pairs={{0,2},{2,0},{4,6},{6,4},{8,10},{10,8},{12,14},{14,12},{16,18},{18,... | collective-permute-start | bytes 2654216 | tf_op jit(solution)/shard_map/ppermute | solution.py:441
  318.2 15.8 %collective-permute-start.73 = (bf16[384,768]{1,0:T(8,128)(2,1)S(1)}, bf16[384,768]{1,0:T(8,128)(2,1)S(1)}, u32[]{:S(2)}, u32[]{:S(2)}) collective-permute-start(bf16[384,768]{1,0:T(8,128)(2,1)S(1)} %add_convert_fusion.5.refs_0_), channel_id=1, source_target_pairs={{0,4},{2,6},{4,0},{6,2},{8,12},{10,14},{12,8},{14,10},{16,20},{18,... | collective-permute-start | bytes 1769480 | tf_op jit(solution)/shard_map/ppermute | solution.py:441
  320.9 12.5 %collective-permute-start.70 = (bf16[2,96,1152]{2,1,0:T(8,128)(2,1)S(1)}, bf16[2,96,1152]{2,1,0:T(8,128)(2,1)S(1)}, u32[]{:S(2)}, u32[]{:S(2)}) collective-permute-start(bf16[2,96,1152]{2,1,0:T(8,128)(2,1)S(1)} %fusion), channel_id=1, source_target_pairs={{0,1},{1,0},{2,3},{3,2},{4,5},{5,4},{6,7},{7,6},{8,9},{9,8},{10,11... | collective-permute-start | bytes 1327112 | tf_op jit(solution)/shard_map/ppermute | solution.py:445
  335.4 15.7 %collective-permute-start.76 = (bf16[480,768]{1,0:T(8,128)(2,1)}, bf16[480,768]{1,0:T(8,128)(2,1)}, u32[]{:S(2)}, u32[]{:S(2)}) collective-permute-start(bf16[480,768]{1,0:T(8,128)(2,1)} %add_convert_fusion.3), channel_id=1, source_target_pairs={{8,16},{10,18},{12,20},{14,22},{16,8},{18,10},{20,12},{22,14},{9,1... | collective-permute-start | bytes 2211848 | tf_op jit(solution)/shard_map/ppermute | solution.py:449
  337.1 14.0 %collective-permute-start.78 = (bf16[384,768]{1,0:T(8,128)(2,1)}, bf16[384,768]{1,0:T(8,128)(2,1)}, u32[]{:S(2)}, u32[]{:S(2)}) collective-permute-start(bf16[384,768]{1,0:T(8,128)(2,1)} %copy-done.58), channel_id=1, source_target_pairs={{0,2},{2,0},{4,6},{6,4},{8,10},{10,8},{12,14},{14,12},{16,18},{18,... | collective-permute-start | bytes 1769480 | tf_op jit(solution)/shard_map/ppermute | solution.py:441
  338.8 12.2 %collective-permute-start.75 = (bf16[2,96,1152]{2,1,0:T(8,128)(2,1)S(1)}, bf16[2,96,1152]{2,1,0:T(8,128)(2,1)}, u32[]{:S(2)}, u32[]{:S(2)}) collective-permute-start(bf16[2,96,1152]{2,1,0:T(8,128)(2,1)S(1)} %fusion.1), channel_id=1, source_target_pairs={{0,1},{1,0},{2,3},{3,2},{4,5},{5,4},{6,7},{7,6},{8,9},{9,8},{10,11... | collective-permute-start | bytes 1327112 | tf_op jit(solution)/shard_map/ppermute | solution.py:445
  352.6 24.6 %collective-permute-start.82 = (bf16[480,768]{1,0:T(8,128)(2,1)S(1)}, bf16[480,768]{1,0:T(8,128)(2,1)S(1)}, u32[]{:S(2)}, u32[]{:S(2)}) collective-permute-start(bf16[480,768]{1,0:T(8,128)(2,1)S(1)} %add_convert_fusion.2), channel_id=1, source_target_pairs={{8,0},{10,2},{12,4},{14,6},{16,24},{18,26},{20,28},{22,30},{9,1},{... | collective-permute-start | bytes 2211848 | tf_op jit(solution)/shard_map/ppermute | solution.py:449
  355.9 13.8 %collective-permute-start.81 = (bf16[96,1152]{1,0:T(8,128)(2,1)}, bf16[96,1152]{1,0:T(8,128)(2,1)}, u32[]{:S(2)}, u32[]{:S(2)}) collective-permute-start(bf16[96,1152]{1,0:T(8,128)(2,1)} %fusion.3), channel_id=1, source_target_pairs={{0,4},{2,6},{4,0},{6,2},{8,12},{10,14},{12,8},{14,10},{16,20},{18,... | collective-permute-start | bytes 663560 | tf_op jit(solution)/shard_map/ppermute | solution.py:441
  358.6 18.6 %collective-permute-start.80 = (bf16[96,1152]{1,0:T(8,128)(2,1)S(1)}, bf16[96,1152]{1,0:T(8,128)(2,1)}, u32[]{:S(2)}, u32[]{:S(2)}) collective-permute-start(bf16[96,1152]{1,0:T(8,128)(2,1)S(1)} %add_convert_fusion.15), channel_id=1, source_target_pairs={{0,8},{2,10},{4,12},{6,14},{8,0},{10,2},{12,4},{14,6},{16,24},{18,... | collective-permute-start | bytes 663560 | tf_op jit(solution)/shard_map/ppermute | solution.py:441
  377.4 15.9 %collective-permute-start.86 = (bf16[480,768]{1,0:T(8,128)(2,1)S(1)}, bf16[480,768]{1,0:T(8,128)(2,1)S(1)}, u32[]{:S(2)}, u32[]{:S(2)}) collective-permute-start(bf16[480,768]{1,0:T(8,128)(2,1)S(1)} %broadcast_select_fusion.refs_0_), channel_id=1, source_target_pairs={{0,4},{2,6},{4,0},{6,2},{8,12},{10,14},{12,8},{14,10},{16,20},{18,... | collective-permute-start | bytes 2211848 | tf_op jit(solution)/shard_map/ppermute | solution.py:441
  380.0 13.2 %collective-permute-start.85 = (bf16[96,1152]{1,0:T(8,128)(2,1)S(1)}, bf16[96,1152]{1,0:T(8,128)(2,1)S(1)}, u32[]{:S(2)}, u32[]{:S(2)}) collective-permute-start(bf16[96,1152]{1,0:T(8,128)(2,1)S(1)} %add_convert_fusion.13), channel_id=1, source_target_pairs={{0,8},{2,10},{4,12},{6,14},{8,0},{10,2},{12,4},{14,6},{16,24},{18,... | collective-permute-start | bytes 663560 | tf_op jit(solution)/shard_map/ppermute | solution.py:441
  381.1 12.2 %collective-permute-start.84 = (bf16[96,1152]{1,0:T(8,128)(2,1)S(1)}, bf16[96,1152]{1,0:T(8,128)(2,1)S(1)}, u32[]{:S(2)}, u32[]{:S(2)}) collective-permute-start(bf16[96,1152]{1,0:T(8,128)(2,1)S(1)} %add_convert_fusion.14), channel_id=1, source_target_pairs={{0,16},{2,18},{4,20},{6,22},{8,24},{10,26},{12,28},{14,30},{16,0},... | collective-permute-start | bytes 663560 | tf_op jit(solution)/shard_map/ppermute | solution.py:441
  383.3 10.0 %collective-permute-start.87 = (f32[36,128]{1,0:T(8,128)S(1)}, f32[36,128]{1,0:T(8,128)S(1)}, u32[]{:S(2)}, u32[]{:S(2)}) collective-permute-start(f32[36,128]{1,0:T(8,128)S(1)} %bitcast_add_fusion), channel_id=1, source_target_pairs={{0,4},{2,6},{4,0},{6,2},{8,12},{10,14},{12,8},{14,10},{16,20},{18,... | collective-permute-start | bytes 55304 | tf_op jit(solution)/shard_map/ppermute | solution.py:441
  384.4 13.6 %collective-permute-start.90 = (bf16[480,768]{1,0:T(8,128)(2,1)S(1)}, bf16[480,768]{1,0:T(8,128)(2,1)S(1)}, u32[]{:S(2)}, u32[]{:S(2)}) collective-permute-start(bf16[480,768]{1,0:T(8,128)(2,1)S(1)} %broadcast_select_fusion.refs_0_), channel_id=1, source_target_pairs={{0,2},{2,0},{4,6},{6,4},{8,10},{10,8},{12,14},{14,12},{16,18},{18,... | collective-permute-start | bytes 2211848 | tf_op jit(solution)/shard_map/ppermute | solution.py:441
  393.3 14.5 %collective-permute-start.91 = (bf16[480,768]{1,0:T(8,128)(2,1)S(1)}, bf16[480,768]{1,0:T(8,128)(2,1)S(1)}, u32[]{:S(2)}, u32[]{:S(2)}) collective-permute-start(bf16[480,768]{1,0:T(8,128)(2,1)S(1)} %collective-permute-done.86.refs_1_), channel_id=1, source_target_pairs={{0,2},{2,0},{4,6},{6,4},{8,10},{10,8},{12,14},{14,12},{16,18},{18,... | collective-permute-start | bytes 2211848 | tf_op jit(solution)/shard_map/ppermute | solution.py:441
  393.4 14.4 %collective-permute-start.89 = (bf16[96,1152]{1,0:T(8,128)(2,1)S(1)}, bf16[96,1152]{1,0:T(8,128)(2,1)S(1)}, u32[]{:S(2)}, u32[]{:S(2)}) collective-permute-start(bf16[96,1152]{1,0:T(8,128)(2,1)S(1)} %add_convert_fusion.11), channel_id=1, source_target_pairs={{0,16},{2,18},{4,20},{6,22},{8,24},{10,26},{12,28},{14,30},{16,0},... | collective-permute-start | bytes 663560 | tf_op jit(solution)/shard_map/ppermute | solution.py:441
  394.3 13.5 %collective-permute-start.88 = (bf16[96,1152]{1,0:T(8,128)(2,1)S(1)}, bf16[96,1152]{1,0:T(8,128)(2,1)S(1)}, u32[]{:S(2)}, u32[]{:S(2)}) collective-permute-start(bf16[96,1152]{1,0:T(8,128)(2,1)S(1)} %add_convert_fusion.12.refs_0_), channel_id=1, source_target_pairs={{0,4},{2,6},{4,0},{6,2},{8,12},{10,14},{12,8},{14,10},{16,20},{18,... | collective-permute-start | bytes 663560 | tf_op jit(solution)/shard_map/ppermute | solution.py:441
  395.1 12.7 %collective-permute-start.92 = (f32[36,128]{1,0:T(8,128)S(1)}, f32[36,128]{1,0:T(8,128)S(1)}, u32[]{:S(2)}, u32[]{:S(2)}) collective-permute-start(f32[36,128]{1,0:T(8,128)S(1)} %add.251), channel_id=1, source_target_pairs={{0,16},{2,18},{4,20},{6,22},{8,24},{10,26},{12,28},{14,30},{16,0},... | collective-permute-start | bytes 55304 | tf_op jit(solution)/shard_map/ppermute | solution.py:441
  398.0 16.5 %collective-permute-start.93 = (bf16[96,1152]{1,0:T(8,128)(2,1)S(1)}, bf16[96,1152]{1,0:T(8,128)(2,1)S(1)}, u32[]{:S(2)}, u32[]{:S(2)}) collective-permute-start(bf16[96,1152]{1,0:T(8,128)(2,1)S(1)} %add_convert_fusion.12.refs_0_), channel_id=1, source_target_pairs={{0,2},{2,0},{4,6},{6,4},{8,10},{10,8},{12,14},{14,12},{16,18},{18,... | collective-permute-start | bytes 663560 | tf_op jit(solution)/shard_map/ppermute | solution.py:441
  408.5 8.8 %collective-permute-start.97 = (bf16[96,1152]{1,0:T(8,128)(2,1)S(1)}, bf16[96,1152]{1,0:T(8,128)(2,1)S(1)}, u32[]{:S(2)}, u32[]{:S(2)}) collective-permute-start(bf16[96,1152]{1,0:T(8,128)(2,1)S(1)} %add_convert_fusion.10.refs_4_), channel_id=1, source_target_pairs={{0,2},{2,0},{4,6},{6,4},{8,10},{10,8},{12,14},{14,12},{16,18},{18,... | collective-permute-start | bytes 663560 | tf_op jit(solution)/shard_map/ppermute | solution.py:441
  (123 other events, 1128.8 us)
